TPU v7x, 512 devices: a whole 4x4x16 slice. The times are simulated.
512 devices in a mesh: req: 32 (over z, core), tensor: 16 (over y, x).
Axes of the slice: x: 4, y: 4, z: 16, core: 2. Of those that a mesh axis runs over, the one named last changes fastest.
Arguments:
- x_in: bfloat16 [36864, 8192], P(('req', 'tensor')), may hold values from -6 to 6
- dt_raw: bfloat16 [36864, 128], P(('req', 'tensor')), may hold values from -4 to 4
- b_in: bfloat16 [36864, 512], P(('req', 'tensor')), may hold values from -1 to 1
- c_in: bfloat16 [36864, 512], P(('req', 'tensor')), may hold values from -1 to 1
- a_log: float32 [128], P('tensor')
- dt_bias: float32 [128], P('tensor'), may hold values from -1 to 0
- d_skip: float32 [128], P('tensor'), may hold values from 0.5 to 1.5
- state_cache: bfloat16 [192, 128, 64, 128], P('req', 'tensor'), may hold values from -6 to 6
- group_sessions: int32 [32, 6], replicated, may hold values from 0 to 191, as said below
- owners: int32 [192], replicated, may hold values from 0 to 31, as said below
- cache_slots: int32 [192], replicated, may hold values from 0 to 5, as said below
- lengths: int32 [192], replicated, may hold values from 64 to 192, as said below
Outputs:
- y_out: bfloat16 [36864, 8192], P(('req', 'tensor'))
- new_cache: bfloat16 [192, 128, 64, 128], P('req', 'tensor')
Inputs may be any that keep to these rules, and one draw needn't show every extreme that they name: `group_sessions`: every session number stands exactly once. `owners`: each owner holds exactly 6 sessions. No two sessions of one request group have the same owner. `cache_slots`: no two sessions share both owner and cache slot. `lengths`: some session has exactly 192 new tokens and some exactly 64.
All inputs are finite; a program needn't handle non-finite values.
Results may differ from a plain program's by a relative error of at most 0.0035.
Values may be sent and summed in bfloat16 or wider, within the bound.
No kernel may reach another device: no remote copies, remote signals or barrier semaphores. Data moves between devices by JAX's collectives and lax.ppermute only.
A program may use at most 64 MiB of HBM per device.

v0:
```python
import jax
import jax.numpy as jnp
import numpy as np
from jax import lax
from jax.sharding import PartitionSpec as P

HEADS = 128
HEAD_DIM = 64
STATE = 128
GROUPS = 4
MAXLEN = 192


def session_mixed(pieces, skip_gain):
    values, out_proj, in_proj, initial, step_size, cumulative, is_live = pieces
    steps_total = values.shape[0]
    places = jnp.arange(steps_total, dtype=jnp.int32)
    affinity = jnp.einsum("tn,un->tu", out_proj, in_proj, preferred_element_type=jnp.float32)
    causal = places[:, None] >= places[None, :]
    spread = cumulative.T[:, :, None] - cumulative.T[:, None, :]
    damping = jnp.exp(jnp.where(causal[None], spread, -jnp.inf))
    weights = (affinity[None] * damping * step_size.T[:, None, :]).astype(jnp.bfloat16)
    local_mix = jnp.einsum("htu,uhp->thp", weights, values, preferred_element_type=jnp.float32)
    carried = jnp.einsum("hpn,tn->thp", initial, out_proj, preferred_element_type=jnp.float32)
    mixed = (
        local_mix
        + jnp.exp(cumulative)[:, :, None] * carried
        + skip_gain[None, :, None] * values.astype(jnp.float32)
    )
    return jnp.where(is_live[:, None, None], mixed, jnp.float32(0.0)).astype(jnp.bfloat16)


def session_closing(pieces):
    values, in_proj, initial, step_size, cumulative = pieces
    to_end = jnp.exp(cumulative[-1][None, :] - cumulative) * step_size
    scaled = (values.astype(jnp.float32) * to_end[:, :, None]).astype(jnp.bfloat16)
    closing = jnp.exp(cumulative[-1])[:, None, None] * initial.astype(jnp.float32) + jnp.einsum(
        "thp,tn->hpn", scaled, in_proj, preferred_element_type=jnp.float32
    )
    return closing.astype(jnp.bfloat16)


def per_device(
    x_in,
    dt_raw,
    b_in,
    c_in,
    a_log,
    dt_bias,
    d_skip,
    state_cache,
    group_sessions,
    owners,
    cache_slots,
    lengths,
):
    tensor_size = lax.axis_size("tensor")
    req_size = lax.axis_size("req")
    req_index = lax.axis_index("req")
    local_heads = a_log.shape[0]
    slot_count = state_cache.shape[0]
    shard_rows = x_in.shape[0]
    per_group = HEADS // GROUPS
    capacity = (slot_count + req_size - 1) // req_size
    head_values, head_steps = (
        lax.all_to_all(x_in, "tensor", split_axis=1, concat_axis=0, tiled=True),
        lax.all_to_all(dt_raw, "tensor", split_axis=1, concat_axis=0, tiled=True),
    )
    chosen = np.arange(tensor_size) * local_heads // per_group
    b_chosen = b_in.reshape(shard_rows, GROUPS, STATE)[:, chosen, :]
    c_chosen = c_in.reshape(shard_rows, GROUPS, STATE)[:, chosen, :]
    head_inputs, head_readout = (
        lax.all_to_all(b_chosen, "tensor", split_axis=1, concat_axis=0, tiled=True),
        lax.all_to_all(c_chosen, "tensor", split_axis=1, concat_axis=0, tiled=True),
    )
    owner_grid = owners[group_sessions]
    slot_grid = cache_slots[group_sessions]
    columns = jnp.arange(slot_count, dtype=jnp.int32)
    same_owner = owner_grid[:, :, None] == owner_grid[:, None, :]
    order_rank = jnp.sum(same_owner & (columns[None, None, :] < columns[None, :, None]), axis=2)
    my_sessions = lax.dynamic_index_in_dim(group_sessions, req_index, 0, keepdims=False)
    my_owner = lax.dynamic_index_in_dim(owner_grid, req_index, 0, keepdims=False)
    my_rank = lax.dynamic_index_in_dim(order_rank, req_index, 0, keepdims=False)
    my_lengths = lengths[my_sessions]
    held_here = owner_grid == req_index
    wanted = held_here[:, :, None] & (
        order_rank[:, :, None] == jnp.arange(capacity, dtype=jnp.int32)[None, None, :]
    )
    source = jnp.sum(jnp.where(wanted, slot_grid[:, :, None], 0), axis=1)
    filled = jnp.any(wanted, axis=1)
    outgoing = jnp.where(
        filled[:, :, None, None, None], state_cache[source], jnp.zeros((), jnp.bfloat16)
    )
    incoming = lax.all_to_all(outgoing, "req", split_axis=0, concat_axis=0, tiled=True)
    flat_incoming = incoming.reshape((req_size * capacity,) + state_cache.shape[1:])
    target = my_owner * capacity + my_rank
    starting = flat_incoming[target]
    decay_rate = -jnp.exp(a_log)
    session_values = head_values.reshape(slot_count, MAXLEN, local_heads, HEAD_DIM)
    session_steps = head_steps.reshape(slot_count, MAXLEN, local_heads)
    session_inputs = head_inputs.reshape(slot_count, MAXLEN, STATE)
    session_readout = head_readout.reshape(slot_count, MAXLEN, STATE)
    places = jnp.arange(MAXLEN, dtype=jnp.int32)
    live_rows = places[None, :] < my_lengths[:, None]
    step_size = jnp.where(
        live_rows[:, :, None],
        jax.nn.softplus(session_steps.astype(jnp.float32) + dt_bias[None, None, :]),
        jnp.float32(0.0),
    )
    cumulative = jnp.cumsum(step_size * decay_rate[None, None, :], axis=1)
    mixed = lax.map(
        lambda pieces: session_mixed(pieces, d_skip),
        (
            session_values,
            session_readout,
            session_inputs,
            starting,
            step_size,
            cumulative,
            live_rows,
        ),
    )
    mixed_rows = mixed.reshape(slot_count * MAXLEN, local_heads * HEAD_DIM)
    closing_states = lax.map(
        session_closing, (session_values, session_inputs, starting, step_size, cumulative)
    )
    route_table = (
        jnp.arange(req_size * capacity, dtype=jnp.int32)[:, None] == target[None, :]
    ).astype(jnp.bfloat16)
    packed = jnp.dot(
        route_table, closing_states.reshape(slot_count, -1), preferred_element_type=jnp.float32
    ).astype(jnp.bfloat16)
    packed = packed.reshape((req_size, capacity) + closing_states.shape[1:])
    returned = lax.all_to_all(packed, "req", split_axis=0, concat_axis=0, tiled=True)
    y_out = lax.all_to_all(mixed_rows, "tensor", split_axis=0, concat_axis=1, tiled=True)
    flat_back = returned.reshape((req_size * capacity,) + state_cache.shape[1:])
    matches = held_here[None] & (slot_grid[None] == columns[:, None, None])
    arrival = jnp.arange(req_size, dtype=jnp.int32)[:, None] * capacity + order_rank
    placement = jnp.sum(jnp.where(matches, arrival[None], 0), axis=(1, 2))
    new_cache = flat_back[placement]
    return (y_out, new_cache)


def solution(mesh):
    placed = (
        P(("req", "tensor"), None),
        P(("req", "tensor"), None),
        P(("req", "tensor"), None),
        P(("req", "tensor"), None),
        P("tensor"),
        P("tensor"),
        P("tensor"),
        P("req", "tensor", None, None),
        P(),
        P(),
        P(),
        P(),
    )
    return jax.shard_map(
        per_device,
        mesh=mesh,
        in_specs=placed,
        out_specs=(P(("req", "tensor"), None), P("req", "tensor", None, None)),
        check_vma=False,
    )
```

profile of v0, /device:TPU:1, one launch (start us, length us, event | category | flops | bytes accessed | tf_op | source)
XLA Modules:
  0.0 516.4 jit_solution(13135449833546529265)
XLA Ops:
  2.2 7.6 %all-to-all-start.3 = ((bf16[72,16,8]{0,2,1:T(8,128)(2,1)}), bf16[72,16,8]{0,2,1:T(8,128)(2,1)S(1)}, u32[]{:S(2)}, u32[]{:S(2)}) async-start(bf16[72,16,8]{0,2,1:T(8,128)(2,1)} %bitcast.30), calls=%async_computation.3 | async-start | bytes 65536 | tf_op jit(solution)/shard_map/all_to_all | solution.py:67
  13.5 2.7 all-to-all-done.3
  16.2 4.0 all-to-all-start.2
  20.2 1.6 gather_fusion.3
  25.5 2.4 all-to-all-done.2
  27.9 4.3 all-to-all-start
  32.8 3.1 gather_fusion.5
  35.9 4.5 bitcast_select_fusion
  40.4 6.7 %all-to-all-done = bf16[72,16,512]{2,0,1:T(8,128)(2,1)S(1)} async-done(((bf16[72,16,512]{2,0,1:T(8,128)(2,1)}), bf16[72,16,512]{2,0,1:T(8,128)(2,1)S(1)}, u32[]{:S(2)}, u32[]{:S(2)}) %all-to-all-start) | async-done | bytes 1179680 | tf_op jit(solution)/shard_map/all_to_all | solution.py:66
  48.1 20.4 %all-to-all-start.4 = ((bf16[32,1,8,64,128]{4,3,2,1,0:T(8,128)(2,1)}), bf16[32,1,8,64,128]{4,3,2,1,0:T(8,128)(2,1)}, u32[]{:S(2)}, u32[]{:S(2)}) async-start(bf16[32,1,8,64,128]{4,3,2,1,0:T(8,128)(2,1)} %bitcast_select_fusion), calls=%async_computation.4 | async-start | bytes 8388608 | tf_op jit(solution)/shard_map/all_to_all | solution.py:94
  71.1 3.4 reduce-window.6
  74.5 177.2 %all-to-all-done.4 = bf16[32,1,8,64,128]{4,3,2,1,0:T(8,128)(2,1)} async-done(((bf16[32,1,8,64,128]{4,3,2,1,0:T(8,128)(2,1)}), bf16[32,1,8,64,128]{4,3,2,1,0:T(8,128)(2,1)}, u32[]{:S(2)}, u32[]{:S(2)}) %all-to-all-start.4) | async-done | bytes 4194336 | tf_op jit(solution)/shard_map/all_to_all | solution.py:94
  251.7 3.5 all-to-all-start.1
  255.6 3.0 reshape.280
  258.6 2.5 copy.124
  261.1 2.9 gather_fusion.6
  264.0 22.2 %while.20 = (s32[]{:T(128)}, bf16[6,192,8,64]{1,3,2,0:T(8,128)(2,1)}, pred[6,192]{1,0:T(8,128)(4,1)S(1)}, bf16[6,192,8,64]{1,3,2,0:T(8,128)(2,1)}, bf16[6,192,12...) while((s32[]{:T(128)}, ...), condition=%wide.region_6.7_spmd, body=%wide.region_5.6_spmd.sunk | while | flops 74551296 | bytes 2486777 | solution.py:111
  265.4 2.4 fusion.68
  269.1 2.4 fusion.68
  272.8 2.4 fusion.68
  276.5 2.4 fusion.68
  280.2 2.3 fusion.68
  283.9 2.4 fusion.68
  287.2 2.9 copy.126
  290.1 2.4 all_to_all.76
  292.5 6.7 %all-to-all-start.5 = ((bf16[16,72,512]{2,1,0:T(8,128)(2,1)}), bf16[16,72,512]{2,1,0:T(8,128)(2,1)S(1)}, u32[]{:S(2)}, u32[]{:S(2)}) async-start(bf16[16,72,512]{2,1,0:T(8,128)(2,1)} %all_to_all.76), calls=%async_computation.5 | async-start | bytes 2359296 | tf_op jit(solution)/shard_map/all_to_all | solution.py:135
  299.3 9.1 %while.21 = (s32[]{:T(128)}, bf16[6,8,64,128]{3,2,1,0:T(8,128)(2,1)S(1)}, f32[6,192,8]{1,2,0:T(8,128)S(1)}, bf16[6,8,64,128]{3,2,1,0:T(8,128)(2,1)}, bf16[6,192,...) while((s32[]{:T(128)}, ...), condition=%wide.region_8.9_spmd, body=%wide.region_7.8_spmd.sunk | while | flops 25725956 | bytes 602461 | solution.py:124
  309.7 2.9 copy.141
  312.6 3.9 all-to-all-done.5
  316.5 12.9 %all-to-all-start.6 = ((bf16[32,1,8,64,128]{4,3,2,1,0:T(8,128)(2,1)}), bf16[32,1,8,64,128]{4,3,2,1,0:T(8,128)(2,1)}, u32[]{:S(2)}, u32[]{:S(2)}) async-start(bf16[32,1,8,64,128]{4,3,2,1,0:T(8,128)(2,1)} %bitcast.178), calls=%async_computation.6 | async-start | bytes 8388608 | tf_op jit(solution)/shard_map/all_to_all | solution.py:134
  330.8 181.9 %all-to-all-done.6 = bf16[32,1,8,64,128]{4,3,2,1,0:T(8,128)(2,1)} async-done(((bf16[32,1,8,64,128]{4,3,2,1,0:T(8,128)(2,1)}), bf16[32,1,8,64,128]{4,3,2,1,0:T(8,128)(2,1)}, u32[]{:S(2)}, u32[]{:S(2)}) %all-to-all-start.6) | async-done | bytes 4194336 | tf_op jit(solution)/shard_map/all_to_all | solution.py:134
  512.7 3.7 gather_fusion.7
  (150 shorter events, 33.7 us)
Async XLA Ops:
  0.6 32.2 %copy-start = (bf16[6,8,64,128]{3,2,1,0:T(8,128)(2,1)S(1)}, bf16[6,8,64,128]{3,2,1,0:T(8,128)(2,1)}, u32[]{:S(2)}) copy-start(bf16[6,8,64,128]{3,2,1,0:T(8,128)(2,1)} %param.26) | copy-start | bytes 2359300
  0.6 19.6 %copy-start.1 = (s32[192]{0:T(256)S(1)}, s32[192]{0:T(256)}, u32[]{:S(2)}) copy-start(s32[192]{0:T(256)} %param.28) | copy-start | bytes 2308
  2.2 14.0 %all-to-all-start.3 = ((bf16[72,16,8]{0,2,1:T(8,128)(2,1)}), bf16[72,16,8]{0,2,1:T(8,128)(2,1)S(1)}, u32[]{:S(2)}, u32[]{:S(2)}) async-start(bf16[72,16,8]{0,2,1:T(8,128)(2,1)} %bitcast.30), calls=%async_computation.3 | async-start | bytes 65536 | tf_op jit(solution)/shard_map/all_to_all | solution.py:67
  16.2 11.7 %all-to-all-start.2 = ((bf16[72,16,128]{2,0,1:T(8,128)(2,1)}), bf16[72,16,128]{2,0,1:T(8,128)(2,1)S(1)}, u32[]{:S(2)}, u32[]{:S(2)}) async-start(bf16[72,16,128]{2,0,1:T(8,128)(2,1)} %bitcast.26), calls=%async_computation.2 | async-start | bytes 589824 | tf_op jit(solution)/shard_map/all_to_all | solution.py:73
  21.8 0.7 copy-start.2
  22.5 1.8 copy-start.7
  27.9 8.0 %copy-start.8 = (bf16[72,16,128]{2,0,1:T(8,128)(2,1)}, bf16[72,16,128]{2,0,1:T(8,128)(2,1)S(1)}, u32[]{:S(2)}) copy-start(bf16[72,16,128]{2,0,1:T(8,128)(2,1)S(1)} %all-to-all-done.2) | copy-start | bytes 884740
  27.9 19.1 %all-to-all-start = ((bf16[72,16,512]{2,0,1:T(8,128)(2,1)}), bf16[72,16,512]{2,0,1:T(8,128)(2,1)S(1)}, u32[]{:S(2)}, u32[]{:S(2)}) async-start(bf16[72,16,512]{2,0,1:T(8,128)(2,1)} %bitcast.142), calls=%async_computation | async-start | bytes 2359296 | tf_op jit(solution)/shard_map/all_to_all | solution.py:66
  40.4 28.1 %copy-start.9 = (bf16[72,512]{1,0:T(8,128)(2,1)S(1)}, bf16[72,512]{1,0:T(8,128)(2,1)}, u32[]{:S(2)}) copy-start(bf16[72,512]{1,0:T(8,128)(2,1)} %param.22) | copy-start | bytes 221188
  40.4 29.4 %copy-start.10 = (s32[32,6]{0,1:T(8,128)S(1)}, s32[32,6]{0,1:T(8,128)}, u32[]{:S(2)}) copy-start(s32[32,6]{0,1:T(8,128)} %param.27) | copy-start | bytes 2308
  40.4 29.6 %copy-start.3 = (s32[192]{0:T(256)S(1)}, s32[192]{0:T(256)}, u32[]{:S(2)}) copy-start(s32[192]{0:T(256)} %param.30) | copy-start | bytes 2308
  40.4 30.3 %copy-start.15 = (f32[8]{0:T(128)S(1)}, f32[8]{0:T(128)}, u32[]{:S(2)}) copy-start(f32[8]{0:T(128)} %param.23) | copy-start | bytes 100
  47.1 1.0 copy-start.4
  48.1 203.6 %all-to-all-start.4 = ((bf16[32,1,8,64,128]{4,3,2,1,0:T(8,128)(2,1)}), bf16[32,1,8,64,128]{4,3,2,1,0:T(8,128)(2,1)}, u32[]{:S(2)}, u32[]{:S(2)}) async-start(bf16[32,1,8,64,128]{4,3,2,1,0:T(8,128)(2,1)} %bitcast_select_fusion), calls=%async_computation.4 | async-start | bytes 8388608 | tf_op jit(solution)/shard_map/all_to_all | solution.py:94
  68.4 2.5 copy-start.14
  70.0 185.6 %copy-start.12 = (s32[6]{0:T(128)}, s32[6]{0:T(128)S(1)}, u32[]{:S(2)}) copy-start(s32[6]{0:T(128)S(1)} %get-tuple-element.246) | copy-start | bytes 76
  251.7 12.3 %all-to-all-start.1 = ((bf16[72,16,128]{2,0,1:T(8,128)(2,1)}), bf16[72,16,128]{2,0,1:T(8,128)(2,1)S(1)}, u32[]{:S(2)}, u32[]{:S(2)}) async-start(bf16[72,16,128]{2,0,1:T(8,128)(2,1)} %bitcast.22), calls=%async_computation.1 | async-start | bytes 589824 | tf_op jit(solution)/shard_map/all_to_all | solution.py:74
  261.1 2.9 copy-start.16
  286.3 0.9 copy-start.5
  292.5 6.7 %copy-start.6 = (bf16[6,8,64,128]{3,2,1,0:T(8,128)(2,1)S(1)}, bf16[6,8,64,128]{3,2,1,0:T(8,128)(2,1)}, u32[]{:S(2)}) copy-start(bf16[6,8,64,128]{3,2,1,0:T(8,128)(2,1)} %custom-call.17) | copy-start | bytes 2359300
  292.5 24.0 %all-to-all-start.5 = ((bf16[16,72,512]{2,1,0:T(8,128)(2,1)}), bf16[16,72,512]{2,1,0:T(8,128)(2,1)S(1)}, u32[]{:S(2)}, u32[]{:S(2)}) async-start(bf16[16,72,512]{2,1,0:T(8,128)(2,1)} %all_to_all.76), calls=%async_computation.5 | async-start | bytes 2359296 | tf_op jit(solution)/shard_map/all_to_all | solution.py:135
  299.3 9.2 %copy-start.13 = (s32[6]{0:T(128)S(1)}, s32[6]{0:T(128)}, u32[]{:S(2)}) copy-start(s32[6]{0:T(128)} %copy-done.12) | copy-start | bytes 76
  316.5 12.9 %copy-start.11 = (pred[32,6]{0,1:T(8,128)(4,1)S(1)}, pred[32,6]{0,1:T(8,128)(4,1)}, u32[]{:S(2)}) copy-start(pred[32,6]{0,1:T(8,128)(4,1)} %get-tuple-element.241) | copy-start | bytes 580
  316.5 196.2 %all-to-all-start.6 = ((bf16[32,1,8,64,128]{4,3,2,1,0:T(8,128)(2,1)}), bf16[32,1,8,64,128]{4,3,2,1,0:T(8,128)(2,1)}, u32[]{:S(2)}, u32[]{:S(2)}) async-start(bf16[32,1,8,64,128]{4,3,2,1,0:T(8,128)(2,1)} %bitcast.178), calls=%async_computation.6 | async-start | bytes 8388608 | tf_op jit(solution)/shard_map/all_to_all | solution.py:134
where the time goes:
time: 523 us; the launch traced here: 516 us
  waiting for transfers between devices  375 us (72%)
  starting transfers between devices  59.3 us (11%)
  local copies, waits for them, and re-layouts  39.2 us (7%)
  matrix products  30.4 us (6%)
  other arithmetic  11.3 us (2%)
    all_to_all x1, waiting for transfers between devices, per_device(): lax.all_to_all(packed, 'req', split_axis=0, concat_axis=0, tiled=True)  182 us
    all_to_all x1, waiting for transfers between devices, per_device(): lax.all_to_all(outgoing, 'req', split_axis=0, concat_axis=0, tiled=True)  177 us
    all_to_all x1, starting transfers between devices, per_device(): lax.all_to_all(outgoing, 'req', split_axis=0, concat_axis=0, tiled=True)  20.4 us
    dot_general x6, matrix products, session_mixed(): jnp.einsum('htu,uhp->thp', weights, values, preferred_element_type=jnp.fl...  14.2 us
    all_to_all x1, starting transfers between devices, per_device(): lax.all_to_all(packed, 'req', split_axis=0, concat_axis=0, tiled=True)  12.9 us
  transfers between devices with their start and end apart: 7, of which 6 were waited for; matrix products, arithmetic and copies ran while one was open for 9% of the time, Pallas kernels for 0%

commit v1 on v0

v1 whole, which is shorter than its diff:
```python
import functools

import jax
import jax.numpy as jnp
from jax import lax
from jax.experimental import pallas as pl
from jax.experimental.pallas import tpu as pltpu
from jax.sharding import PartitionSpec as P

HEADS = 128
HEAD_DIM = 64
STATE = 128
GROUPS = 4
MAXLEN = 192
LANES = 128
VMEM_LIMIT = 48 * 1024 * 1024


def pack_kernel(x_ref, dt_ref, b_ref, c_ref, out_ref):
    width = x_ref.shape[1]
    out_ref[0, :, :width] = x_ref[...]
    out_ref[0, :, width : width + STATE] = b_ref[...]
    out_ref[0, :, width + STATE : width + 2 * STATE] = c_ref[...]
    out_ref[0, :, width + 2 * STATE :] = dt_ref[...]


def pack_tokens(x_in, dt_raw, b_in, c_in, parts):
    rows, columns = x_in.shape
    width = columns // parts
    share = parts // GROUPS
    total = width + 2 * STATE + HEADS
    return pl.pallas_call(
        pack_kernel,
        grid=(parts,),
        in_specs=[
            pl.BlockSpec((rows, width), lambda t: (0, t)),
            pl.BlockSpec((rows, HEADS), lambda t: (0, 0)),
            pl.BlockSpec((rows, STATE), lambda t: (0, t // share)),
            pl.BlockSpec((rows, STATE), lambda t: (0, t // share)),
        ],
        out_specs=pl.BlockSpec((1, rows, total), lambda t: (t, 0, 0)),
        out_shape=jax.ShapeDtypeStruct((parts, rows, total), x_in.dtype),
        compiler_params=pltpu.CompilerParams(vmem_limit_bytes=VMEM_LIMIT),
        name="pack_tokens",
    )(x_in, dt_raw, b_in, c_in)


def cache_row(sessions_ref, owners_ref, slots_ref, slot_count, index):
    session = sessions_ref[index]
    return owners_ref[session] * slot_count + slots_ref[session]


def order_kernel(sessions_ref, owners_ref, slots_ref, in_ref, out_ref, *, slot_count, to_owner):
    def step(index, carry):
        row = cache_row(sessions_ref, owners_ref, slots_ref, slot_count, index)
        if to_owner:
            out_ref[row] = in_ref[index]
        else:
            out_ref[index] = in_ref[row]
        return carry

    lax.fori_loop(0, in_ref.shape[0], step, 0, unroll=8)


def reorder(pieces, sessions, owners, slots, slot_count, to_owner):
    smem = pl.BlockSpec(memory_space=pltpu.SMEM)
    vmem = pl.BlockSpec(memory_space=pltpu.VMEM)
    return pl.pallas_call(
        functools.partial(order_kernel, slot_count=slot_count, to_owner=to_owner),
        in_specs=[smem, smem, smem, vmem],
        out_specs=vmem,
        out_shape=jax.ShapeDtypeStruct(pieces.shape, pieces.dtype),
        compiler_params=pltpu.CompilerParams(vmem_limit_bytes=VMEM_LIMIT),
        name="to_owner_order" if to_owner else "to_group_order",
    )(sessions, owners, slots, pieces)


def session_kernel(
    place_ref,
    sessions_ref,
    lengths_ref,
    packed_ref,
    start_ref,
    a_log_ref,
    bias_ref,
    skip_ref,
    y_ref,
    closing_ref,
    *,
    heads,
    slot_count,
):
    highest = lax.Precision.HIGHEST
    f32 = jnp.float32
    bf16 = jnp.bfloat16
    width = heads * HEAD_DIM
    rows = MAXLEN
    half = LANES
    session = sessions_ref[place_ref[0] * slot_count + pl.program_id(0)]
    length = lengths_ref[session]

    values = packed_ref[:, :width]
    in_proj = packed_ref[:, width : width + STATE]
    out_proj = packed_ref[:, width + STATE : width + 2 * STATE]
    all_steps = packed_ref[:, width + 2 * STATE :]

    lane_from = lax.broadcasted_iota(jnp.int32, (HEADS, LANES), 0)
    lane_to = lax.broadcasted_iota(jnp.int32, (HEADS, LANES), 1)
    chosen = ((lane_from == lane_to + place_ref[1] * heads) & (lane_to < heads)).astype(bf16)
    raw = jnp.dot(all_steps, chosen, preferred_element_type=f32)
    row_index = lax.broadcasted_iota(jnp.int32, (rows, LANES), 0)
    shifted = raw + bias_ref[...]
    soft = jnp.maximum(shifted, 0.0) + jnp.log(1.0 + jnp.exp(-jnp.abs(shifted)))
    step = jnp.where(row_index < length, soft, 0.0)
    rate = -jnp.exp(a_log_ref[...])
    t_index = lax.broadcasted_iota(jnp.int32, (rows, rows), 0)
    u_index = lax.broadcasted_iota(jnp.int32, (rows, rows), 1)
    causal = t_index >= u_index
    cum = jnp.dot(
        causal.astype(f32), step * rate, precision=highest, preferred_element_type=f32
    )
    drop = cum - jnp.log(step)
    last = cum[rows - 1 : rows, :]
    to_end = jnp.exp(last - cum) * step
    grown = jnp.exp(cum)
    drop_rows = drop.T

    affinity = lax.dot_general(
        out_proj, in_proj, (((1,), (1,)), ((), ())), preferred_element_type=f32
    )
    affinity = jnp.where(causal, affinity, 0.0)
    top, low = affinity[:half, :half], affinity[half:, :]

    start = start_ref[...].reshape(width, STATE)
    carried = lax.dot_general(
        out_proj, start, (((1,), (1,)), ((), ())), preferred_element_type=f32
    )
    live = row_index < length
    left = lax.broadcasted_iota(jnp.int32, (rows, LANES), 1) < HEAD_DIM

    def spread(columns, first):
        one = jnp.broadcast_to(columns[:, first : first + 1], (rows, LANES))
        two = jnp.broadcast_to(columns[:, first + 1 : first + 2], (rows, LANES))
        return jnp.where(left, one, two)

    scaled_parts = []
    for first in range(0, heads, 2):
        lanes = slice(first * HEAD_DIM, (first + 2) * HEAD_DIM)
        pair = values[:, lanes]
        mixed = []
        for head in (first, first + 1):
            column = cum[:, head : head + 1]
            line = drop_rows[head : head + 1, :]
            w_top = top * jnp.exp(jnp.minimum(column[:half] - line[:, :half], 80.0))
            w_low = low * jnp.exp(jnp.minimum(column[half:] - line, 80.0))
            mixed.append(
                jnp.concatenate(
                    [
                        jnp.dot(w_top.astype(bf16), pair[:half], preferred_element_type=f32),
                        jnp.dot(w_low.astype(bf16), pair, preferred_element_type=f32),
                    ],
                    axis=0,
                )
            )
        pair_f32 = pair.astype(f32)
        out = (
            jnp.where(left, mixed[0], mixed[1])
            + spread(grown, first) * carried[:, lanes]
            + skip_ref[:, lanes] * pair_f32
        )
        y_ref[:, lanes] = jnp.where(live, out, 0.0).astype(bf16)
        scaled_parts.append((pair_f32 * spread(to_end, first)).astype(bf16))
    scaled = jnp.concatenate(scaled_parts, axis=1)
    added = lax.dot_general(
        scaled, in_proj, (((0,), (0,)), ((), ())), preferred_element_type=f32
    )
    kept = jnp.exp(last)
    for head in range(heads):
        channels = slice(head * HEAD_DIM, (head + 1) * HEAD_DIM)
        closing = kept[:, head : head + 1] * start[channels].astype(f32) + added[channels]
        per = closing_ref.shape[2]
        begin = head * HEAD_DIM // per
        closing_ref[begin : begin + HEAD_DIM // per, 0] = closing.astype(bf16).reshape(
            HEAD_DIM // per, per, STATE
        )


def run_sessions(place, sessions, lengths, packed, start, a_log, dt_bias, d_skip):
    heads = a_log.shape[0]
    pieces, slot_count, per, _ = start.shape
    width = heads * HEAD_DIM
    pad = ((0, 0), (0, LANES - heads))
    a_row = jnp.pad(a_log[None, :], pad)
    bias_row = jnp.pad(dt_bias[None, :], pad)
    skip_row = jnp.repeat(d_skip, HEAD_DIM)[None, :]
    whole = lambda j, *_: (0, 0)
    return pl.pallas_call(
        functools.partial(session_kernel, heads=heads, slot_count=slot_count),
        grid_spec=pltpu.PrefetchScalarGridSpec(
            num_scalar_prefetch=3,
            grid=(slot_count,),
            in_specs=[
                pl.BlockSpec((MAXLEN, packed.shape[1]), lambda j, *_: (j, 0)),
                pl.BlockSpec((pieces, 1, per, STATE), lambda j, *_: (0, j, 0, 0)),
                pl.BlockSpec((1, LANES), whole),
                pl.BlockSpec((1, LANES), whole),
                pl.BlockSpec((1, width), whole),
            ],
            out_specs=[
                pl.BlockSpec((MAXLEN, width), lambda j, *_: (j, 0)),
                pl.BlockSpec((pieces, 1, per, STATE), lambda j, *_: (0, j, 0, 0)),
            ],
        ),
        out_shape=[
            jax.ShapeDtypeStruct((packed.shape[0], width), jnp.bfloat16),
            jax.ShapeDtypeStruct(start.shape, jnp.bfloat16),
        ],
        compiler_params=pltpu.CompilerParams(vmem_limit_bytes=VMEM_LIMIT),
        name="run_sessions",
    )(place, sessions, lengths, packed, start, a_row, bias_row, skip_row)


def per_device(
    x_in,
    dt_raw,
    b_in,
    c_in,
    a_log,
    dt_bias,
    d_skip,
    state_cache,
    group_sessions,
    owners,
    cache_slots,
    lengths,
):
    tensor_size = lax.axis_size("tensor")
    req_size = lax.axis_size("req")
    slot_count, heads = state_cache.shape[:2]
    per = heads * HEAD_DIM // req_size
    place = jnp.stack([lax.axis_index("req"), lax.axis_index("tensor")]).astype(jnp.int32)
    sessions = group_sessions.reshape(-1)

    pieces = state_cache.reshape(slot_count, req_size, per, STATE)
    spread = lax.all_to_all(pieces, "req", split_axis=1, concat_axis=0, tiled=False)
    spread = spread.reshape(req_size * slot_count, per, STATE)
    spread = reorder(spread, sessions, owners, cache_slots, slot_count, False)
    start = lax.all_to_all(
        spread.reshape(req_size, slot_count, per, STATE), "req", split_axis=0, concat_axis=0
    )

    packed = pack_tokens(x_in, dt_raw, b_in, c_in, tensor_size)
    packed = lax.all_to_all(packed, "tensor", split_axis=0, concat_axis=0)
    packed = packed.reshape(tensor_size * x_in.shape[0], packed.shape[2])

    mixed, closing = run_sessions(
        place, sessions, lengths, packed, start, a_log, dt_bias, d_skip
    )

    back = lax.all_to_all(closing, "req", split_axis=0, concat_axis=0)
    back = back.reshape(req_size * slot_count, per, STATE)
    back = reorder(back, sessions, owners, cache_slots, slot_count, True)
    back = lax.all_to_all(
        back.reshape(req_size, slot_count, per, STATE), "req", split_axis=0, concat_axis=0
    )
    new_cache = back.transpose(1, 0, 2, 3).reshape(state_cache.shape)

    shard = mixed.reshape(tensor_size, x_in.shape[0], heads * HEAD_DIM)
    y_out = lax.all_to_all(shard, "tensor", split_axis=0, concat_axis=0)
    y_out = y_out.transpose(1, 0, 2).reshape(x_in.shape)
    return y_out, new_cache


def solution(mesh):
    tokens = P(("req", "tensor"), None)
    states = P("req", "tensor", None, None)
    placed = (tokens,) * 4 + (P("tensor"),) * 3 + (states,) + (P(),) * 4
    return jax.shard_map(
        per_device,
        mesh=mesh,
        in_specs=placed,
        out_specs=(tokens, states),
        check_vma=False,
    )
```

time: 523 us -> 286 us (0.55); the launches traced: 516 us -> 285 us
  waiting for transfers between devices: 375 us -> 174 us
  blocking collectives: 0 us -> 47.8 us
  local copies, waits for them, and re-layouts: 39.2 us -> 6.96 us
  matrix products: 30.4 us -> 0 us
  starting transfers between devices: 59.3 us -> 39.9 us
  Pallas kernels: 0 us -> 15.7 us
  other arithmetic: 11.3 us -> 0.07 us
    all_to_all x7 -> x5, waiting for transfers between devices: 375 us -> 174 us  [the longest x1 44.4 us: per_device(): lax.all_to_all(spread.reshape(req_size, slot_count, per, STATE), 'req', s...]
    all_to_all x0 -> x1, blocking collectives: none -> 47.8 us  [per_device(): back = lax.all_to_all(closing, 'req', split_axis=0, concat_axis=0)]
    dot_general x25 -> x0, matrix products: 30.4 us -> none  [the longest x6 14.2 us: session_mixed(): jnp.einsum('htu,uhp->thp', weights, values, preferred_element_type=jnp.fl...]
    all_to_all x7 -> x5, starting transfers between devices: 59.3 us -> 39.9 us  [the longest x1 16.7 us: per_device(): lax.all_to_all(pieces, 'req', split_axis=1, concat_axis=0, tiled=False)]
    gather x12 -> x0, local copies, waits for them, and re-layouts: 16.5 us -> none  [the longest x1 3.74 us: per_device(): new_cache = flat_back[placement]]
    pallas_call x0 -> x4, Pallas kernels: none -> 15.7 us  [the longest x1 11.5 us: run_sessions(): pl.pallas_call(functools.partial(session_kernel, heads=heads, slot_count=...]
    while x9 -> x0, local copies, waits for them, and re-layouts: 5.98 us -> none  [the longest x3 5.48 us: per_device(): lax.map(lambda pieces: session_mixed(pieces, d_skip), (session_values, se...]
  transfers between devices with their start and end apart: 7 -> 5, of which waited for: 6 -> 5; matrix products, arithmetic and copies ran while one was open for 9% -> 1% of each run, Pallas kernels for 0% -> 1%
where the time goes in v1:
time: 286 us; the launch traced here: 285 us
  waiting for transfers between devices  174 us (61%)
  blocking collectives  47.8 us (17%)
  starting transfers between devices  39.9 us (14%)
  Pallas kernels  15.7 us (5%)
  local copies, waits for them, and re-layouts  6.96 us (2%)
    all_to_all x1, blocking collectives, per_device(): back = lax.all_to_all(closing, 'req', split_axis=0, concat_axis=0)  47.8 us
    all_to_all x1, waiting for transfers between devices, per_device(): lax.all_to_all(spread.reshape(req_size, slot_count, per, STATE), 'req', s...  44.4 us
    all_to_all x1, waiting for transfers between devices, per_device(): lax.all_to_all(back.reshape(req_size, slot_count, per, STATE), 'req', spl...  43.5 us
    all_to_all x1, waiting for transfers between devices, per_device(): lax.all_to_all(pieces, 'req', split_axis=1, concat_axis=0, tiled=False)  42.3 us
    all_to_all x1, waiting for transfers between devices, per_device(): packed = lax.all_to_all(packed, 'tensor', split_axis=0, concat_axis=0)  28.5 us
    all_to_all x1, starting transfers between devices, per_device(): lax.all_to_all(pieces, 'req', split_axis=1, concat_axis=0, tiled=False)  16.7 us
    all_to_all x1, waiting for transfers between devices, per_device(): y_out = lax.all_to_all(shard, 'tensor', split_axis=0, concat_axis=0)  15.1 us
    pallas_call x1, Pallas kernels, run_sessions(): pl.pallas_call(functools.partial(session_kernel, heads=heads, slot_count=...  11.5 us
  transfers between devices with their start and end apart: 5, of which 5 were waited for; matrix products, arithmetic and copies ran while one was open for 1% of the time, Pallas kernels for 1%

profile of v1, /device:TPU:1, one launch (start us, length us, event | category | flops | bytes accessed | tf_op | source)
XLA Modules:
  0.0 285.1 jit_solution(1449639563339270189)
XLA Ops:
  0.6 0.0 copy-start.3
  0.7 2.2 copy.25
  2.9 16.7 %all-to-all-start.1 = ((bf16[1,6,32,16,128]{4,3,1,0,2:T(8,128)(2,1)}), bf16[1,6,32,16,128]{4,3,1,0,2:T(8,128)(2,1)S(1)}, u32[]{:S(2)}, u32[]{:S(2)}) async-start(bf16[1,6,32,16,128]{4,3,1,0,2:T(8,128)(2,1)} %copy.25), calls=%async_computation.1 | async-start | bytes 1572864 | tf_op jit(solution)/shard_map/all_to_all | solution.py:245
  19.7 1.0 pack_tokens.1
  20.7 1.3 copy-done
  22.0 42.3 %all-to-all-done.1 = bf16[1,6,32,16,128]{4,3,1,0,2:T(8,128)(2,1)S(1)} async-done(((bf16[1,6,32,16,128]{4,3,1,0,2:T(8,128)(2,1)}), bf16[1,6,32,16,128]{4,3,1,0,2:T(8,128)(2,1)S(1)}, u32[]{:S(2)}, u32[]{:S(2)}) %all-to-all-start.1) | async-done | bytes 786464 | tf_op jit(solution)/shard_map/all_to_all | solution.py:245
  64.3 6.8 %all-to-all-start = ((bf16[16,72,896]{2,1,0:T(8,128)(2,1)}), bf16[16,72,896]{2,1,0:T(8,128)(2,1)S(1)}, u32[]{:S(2)}, u32[]{:S(2)}) async-start(bf16[16,72,896]{2,1,0:T(8,128)(2,1)} %copy-done), calls=%async_computation | async-start | bytes 4128768 | tf_op jit(solution)/shard_map/all_to_all | solution.py:253
  71.1 0.1 copy.24
  71.2 0.1 reshape.29.sessions_ref
  71.3 0.0 copy-done.7
  71.3 0.0 copy-done.8
  71.3 1.2 to_group_order.1
  72.5 0.0 copy-start.1
  72.6 0.9 copy-done.1
  73.4 28.5 %all-to-all-done = bf16[16,72,896]{2,1,0:T(8,128)(2,1)S(1)} async-done(((bf16[16,72,896]{2,1,0:T(8,128)(2,1)}), bf16[16,72,896]{2,1,0:T(8,128)(2,1)S(1)}, u32[]{:S(2)}, u32[]{:S(2)}) %all-to-all-start) | async-done | bytes 2064416 | tf_op jit(solution)/shard_map/all_to_all | solution.py:253
  102.0 5.2 %all-to-all-start.2 = ((bf16[32,6,16,128]{3,2,1,0:T(8,128)(2,1)}), bf16[32,6,16,128]{3,2,1,0:T(8,128)(2,1)S(1)}, u32[]{:S(2)}, u32[]{:S(2)}) async-start(bf16[32,6,16,128]{3,2,1,0:T(8,128)(2,1)} %bitcast.21), calls=%async_computation.2 | async-start | bytes 1572864 | tf_op jit(solution)/shard_map/all_to_all | solution.py:248
  107.3 0.1 broadcast_in_dim.11
  107.3 0.1 broadcast_in_dim_reshape.7.skip_ref
  107.4 0.1 pad_add_fusion.place_ref
  107.5 44.4 %all-to-all-done.2.start_ref = bf16[32,6,16,128]{3,2,1,0:T(8,128)(2,1)S(1)} async-done(((bf16[32,6,16,128]{3,2,1,0:T(8,128)(2,1)}), bf16[32,6,16,128]{3,2,1,0:T(8,128)(2,1)S(1)}, u32[]{:S(2)}, u32[]{:S(2)}) %all-to-all-start.2) | async-done | bytes 786464 | tf_op jit(solution)/shard_map/all_to_all | solution.py:248
  151.9 0.0 copy-done.9
  151.9 11.5 %run_sessions.1 = (bf16[1152,512]{1,0:T(8,128)(2,1)S(1)}, bf16[32,6,16,128]{3,2,1,0:T(8,128)(2,1)S(1)}) custom-call(s32[2]{0:T(128)S(1)} %pad_add_fusion.place_ref, s32[192]{0:T(256)S(1)} %reshape.29.sessions_ref, s32[192]{0:T(256)S(1)} %copy-done.9, bf16[1152,896]{1,0:T(8,128)(2,1)S(1)} %bitcast.20, bf16[32,6,16,128]{3,2,1,0:T(8,128)(2,1)S(1)} %all-to-all-done.2.start_ref, ...), custom_call_target="tpu_custom_call" | custom-call | tf_op jit(solution)/shard_map/run_sessions/pallas_call | solution.py:197
  163.4 0.0 copy-start.2
  163.4 47.8 %all_to_all.40 = bf16[32,6,16,128]{3,2,1,0:T(8,128)(2,1)S(1)} all-to-all(bf16[32,6,16,128]{3,2,1,0:T(8,128)(2,1)S(1)} %get-tuple-element.5), channel_id=1, replica_groups=mesh['req'=32,'tensor'=16] {'req'}, dimensions={0} | all-to-all | bytes 1572864 | tf_op jit(solution)/shard_map/all_to_all | solution.py:260
  211.2 0.0 copy-done.2
  211.2 3.8 %all-to-all-start.3 = ((bf16[16,72,512]{2,1,0:T(8,128)(2,1)}), bf16[16,72,512]{2,1,0:T(8,128)(2,1)S(1)}, u32[]{:S(2)}, u32[]{:S(2)}) async-start(bf16[16,72,512]{2,1,0:T(8,128)(2,1)} %bitcast.24), calls=%async_computation.3 | async-start | bytes 2359296 | tf_op jit(solution)/shard_map/all_to_all | solution.py:269
  215.0 2.0 to_owner_order.1
  217.0 15.1 %all-to-all-done.3 = bf16[16,72,512]{2,1,0:T(8,128)(2,1)S(1)} async-done(((bf16[16,72,512]{2,1,0:T(8,128)(2,1)}), bf16[16,72,512]{2,1,0:T(8,128)(2,1)S(1)}, u32[]{:S(2)}, u32[]{:S(2)}) %all-to-all-start.3) | async-done | bytes 1179680 | tf_op jit(solution)/shard_map/all_to_all | solution.py:269
  232.1 7.4 %all-to-all-start.5 = ((bf16[32,6,16,128]{3,2,1,0:T(8,128)(2,1)}), bf16[32,6,16,128]{3,2,1,0:T(8,128)(2,1)S(1)}, u32[]{:S(2)}, u32[]{:S(2)}) async-start(bf16[32,6,16,128]{3,2,1,0:T(8,128)(2,1)} %bitcast.13), calls=%async_computation.5 | async-start | bytes 1572864 | tf_op jit(solution)/shard_map/all_to_all | solution.py:263
  239.4 1.1 copy.28
  240.5 43.5 %all-to-all-done.5 = bf16[32,6,16,128]{3,2,1,0:T(8,128)(2,1)S(1)} async-done(((bf16[32,6,16,128]{3,2,1,0:T(8,128)(2,1)}), bf16[32,6,16,128]{3,2,1,0:T(8,128)(2,1)S(1)}, u32[]{:S(2)}, u32[]{:S(2)}) %all-to-all-start.5) | async-done | bytes 786464 | tf_op jit(solution)/shard_map/all_to_all | solution.py:263
  284.1 1.0 copy.27
  (21 shorter events, 0.0 us)
Async XLA Ops:
  0.6 19.0 %copy-start.3 = (bf16[72,8192]{1,0:T(8,128)(2,1)S(1)}, bf16[72,8192]{1,0:T(8,128)(2,1)}, u32[]{:S(2)}) copy-start(bf16[72,8192]{1,0:T(8,128)(2,1)} %x_ref.1) | copy-start | bytes 3538948
  0.6 19.0 %copy-start.4 = (bf16[72,512]{1,0:T(8,128)(2,1)S(1)}, bf16[72,512]{1,0:T(8,128)(2,1)}, u32[]{:S(2)}) copy-start(bf16[72,512]{1,0:T(8,128)(2,1)} %b_ref.1) | copy-start | bytes 221188
  0.7 19.0 %copy-start.5 = (bf16[72,512]{1,0:T(8,128)(2,1)S(1)}, bf16[72,512]{1,0:T(8,128)(2,1)}, u32[]{:S(2)}) copy-start(bf16[72,512]{1,0:T(8,128)(2,1)} %c_ref.1) | copy-start | bytes 221188
  0.7 19.0 %copy-start.6 = (bf16[72,128]{1,0:T(8,128)(2,1)S(1)}, bf16[72,128]{1,0:T(8,128)(2,1)}, u32[]{:S(2)}) copy-start(bf16[72,128]{1,0:T(8,128)(2,1)} %dt_ref.1) | copy-start | bytes 55300
  2.9 61.4 %all-to-all-start.1 = ((bf16[1,6,32,16,128]{4,3,1,0,2:T(8,128)(2,1)}), bf16[1,6,32,16,128]{4,3,1,0,2:T(8,128)(2,1)S(1)}, u32[]{:S(2)}, u32[]{:S(2)}) async-start(bf16[1,6,32,16,128]{4,3,1,0,2:T(8,128)(2,1)} %copy.25), calls=%async_computation.1 | async-start | bytes 1572864 | tf_op jit(solution)/shard_map/all_to_all | solution.py:245
  20.7 1.3 copy-start
  22.0 49.1 %copy-start.10 = (s32[32,6]{0,1:T(8,128)S(1)}, s32[32,6]{0,1:T(8,128)}, u32[]{:S(2)}) copy-start(s32[32,6]{0,1:T(8,128)} %param.20) | copy-start | bytes 2308
  22.0 49.3 %copy-start.7 = (s32[192]{0:T(256)S(1)}, s32[192]{0:T(256)}, u32[]{:S(2)}) copy-start(s32[192]{0:T(256)} %owners_ref.3) | copy-start | bytes 2308
  22.0 49.3 %copy-start.8 = (s32[192]{0:T(256)S(1)}, s32[192]{0:T(256)}, u32[]{:S(2)}) copy-start(s32[192]{0:T(256)} %slots_ref.3) | copy-start | bytes 2308
  64.3 37.6 %all-to-all-start = ((bf16[16,72,896]{2,1,0:T(8,128)(2,1)}), bf16[16,72,896]{2,1,0:T(8,128)(2,1)S(1)}, u32[]{:S(2)}, u32[]{:S(2)}) async-start(bf16[16,72,896]{2,1,0:T(8,128)(2,1)} %copy-done), calls=%async_computation | async-start | bytes 4128768 | tf_op jit(solution)/shard_map/all_to_all | solution.py:253
  72.5 0.9 copy-start.1
  73.4 33.8 %copy-start.12 = (f32[8]{0:T(128)S(1)}, f32[8]{0:T(128)}, u32[]{:S(2)}) copy-start(f32[8]{0:T(128)} %param.16) | copy-start | bytes 100
  73.4 33.8 %copy-start.13 = (f32[8]{0:T(128)S(1)}, f32[8]{0:T(128)}, u32[]{:S(2)}) copy-start(f32[8]{0:T(128)} %param.17) | copy-start | bytes 100
  73.4 33.8 %copy-start.11 = (f32[8]{0:T(128)S(1)}, f32[8]{0:T(128)}, u32[]{:S(2)}) copy-start(f32[8]{0:T(128)} %param.18) | copy-start | bytes 100
  73.4 78.4 %copy-start.9 = (s32[192]{0:T(256)S(1)}, s32[192]{0:T(256)}, u32[]{:S(2)}) copy-start(s32[192]{0:T(256)} %lengths_ref.1) | copy-start | bytes 2308
  102.0 49.9 %all-to-all-start.2 = ((bf16[32,6,16,128]{3,2,1,0:T(8,128)(2,1)}), bf16[32,6,16,128]{3,2,1,0:T(8,128)(2,1)S(1)}, u32[]{:S(2)}, u32[]{:S(2)}) async-start(bf16[32,6,16,128]{3,2,1,0:T(8,128)(2,1)} %bitcast.21), calls=%async_computation.2 | async-start | bytes 1572864 | tf_op jit(solution)/shard_map/all_to_all | solution.py:248
  163.4 47.8 %copy-start.2 = (bf16[1152,512]{1,0:T(8,128)(2,1)}, bf16[1152,512]{1,0:T(8,128)(2,1)S(1)}, u32[]{:S(2)}) copy-start(bf16[1152,512]{1,0:T(8,128)(2,1)S(1)} %get-tuple-element.4) | copy-start | bytes 3538948
  211.2 20.9 %all-to-all-start.3 = ((bf16[16,72,512]{2,1,0:T(8,128)(2,1)}), bf16[16,72,512]{2,1,0:T(8,128)(2,1)S(1)}, u32[]{:S(2)}, u32[]{:S(2)}) async-start(bf16[16,72,512]{2,1,0:T(8,128)(2,1)} %bitcast.24), calls=%async_computation.3 | async-start | bytes 2359296 | tf_op jit(solution)/shard_map/all_to_all | solution.py:269
  232.1 52.0 %all-to-all-start.5 = ((bf16[32,6,16,128]{3,2,1,0:T(8,128)(2,1)}), bf16[32,6,16,128]{3,2,1,0:T(8,128)(2,1)S(1)}, u32[]{:S(2)}, u32[]{:S(2)}) async-start(bf16[32,6,16,128]{3,2,1,0:T(8,128)(2,1)} %bitcast.13), calls=%async_computation.5 | async-start | bytes 1572864 | tf_op jit(solution)/shard_map/all_to_all | solution.py:263

commit v2 on v1

--- a/solution.py
+++ b/solution.py
@@ -16,33 +16,64 @@
 VMEM_LIMIT = 48 * 1024 * 1024
 
 
-def pack_kernel(x_ref, dt_ref, b_ref, c_ref, out_ref):
-    width = x_ref.shape[1]
-    out_ref[0, :, :width] = x_ref[...]
-    out_ref[0, :, width : width + STATE] = b_ref[...]
-    out_ref[0, :, width + STATE : width + 2 * STATE] = c_ref[...]
-    out_ref[0, :, width + 2 * STATE :] = dt_ref[...]
-
-
-def pack_tokens(x_in, dt_raw, b_in, c_in, parts):
-    rows, columns = x_in.shape
-    width = columns // parts
+def pack_kernel(place_ref, x_ref, dt_ref, b_ref, c_ref, *out_refs):
+    parts = len(out_refs)
+    width = x_ref.shape[1] // parts
     share = parts // GROUPS
-    total = width + 2 * STATE + HEADS
+    for shift, out_ref in enumerate(out_refs):
+        target = lax.rem(place_ref[1] + shift, parts)
+        columns = pl.ds(pl.multiple_of(target * width, LANES), width)
+        group = pl.ds(pl.multiple_of(target // share * STATE, LANES), STATE)
+        out_ref[:, :width] = x_ref[:, columns]
+        out_ref[:, width : width + STATE] = b_ref[:, group]
+        out_ref[:, width + STATE : width + 2 * STATE] = c_ref[:, group]
+        out_ref[:, width + 2 * STATE :] = dt_ref[...]
+
+
+def gather_kernel(place_ref, *refs):
+    out_ref = refs[-1]
+    parts = len(refs) - 1
+    for shift in range(parts):
+        out_ref[lax.rem(place_ref[1] + parts - shift, parts)] = refs[shift][...]
+
+
+def split_kernel(place_ref, rows_ref, *out_refs):
+    parts = len(out_refs)
+    for shift, out_ref in enumerate(out_refs):
+        out_ref[...] = rows_ref[lax.rem(place_ref[1] + shift, parts)]
+
+
+def columns_kernel(place_ref, *refs):
+    out_ref = refs[-1]
+    parts = len(refs) - 1
+    width = refs[0].shape[1]
+    for shift in range(parts):
+        source = lax.rem(place_ref[1] + parts - shift, parts)
+        out_ref[:, pl.ds(pl.multiple_of(source * width, LANES), width)] = refs[shift][...]
+
+
+def local_call(kernel, place, arrays, out_shape, name):
+    smem = pl.BlockSpec(memory_space=pltpu.SMEM)
+    vmem = pl.BlockSpec(memory_space=pltpu.VMEM)
+    several = isinstance(out_shape, list)
     return pl.pallas_call(
-        pack_kernel,
-        grid=(parts,),
-        in_specs=[
-            pl.BlockSpec((rows, width), lambda t: (0, t)),
-            pl.BlockSpec((rows, HEADS), lambda t: (0, 0)),
-            pl.BlockSpec((rows, STATE), lambda t: (0, t // share)),
-            pl.BlockSpec((rows, STATE), lambda t: (0, t // share)),
-        ],
-        out_specs=pl.BlockSpec((1, rows, total), lambda t: (t, 0, 0)),
-        out_shape=jax.ShapeDtypeStruct((parts, rows, total), x_in.dtype),
+        kernel,
+        in_specs=[smem] + [vmem] * len(arrays),
+        out_specs=[vmem] * len(out_shape) if several else vmem,
+        out_shape=out_shape,
         compiler_params=pltpu.CompilerParams(vmem_limit_bytes=VMEM_LIMIT),
-        name="pack_tokens",
-    )(x_in, dt_raw, b_in, c_in)
+        name=name,
+    )(place, *arrays)
+
+
+def send_shifted(arrays, axis):
+    parts = len(arrays)
+    moved = [arrays[0]]
+    for shift in range(1, parts):
+        moved.append(
+            lax.ppermute(arrays[shift], axis, [(i, (i + shift) % parts) for i in range(parts)])
+        )
+    return moved
 
 
 def cache_row(sessions_ref, owners_ref, slots_ref, slot_count, index):
@@ -249,9 +280,20 @@
         spread.reshape(req_size, slot_count, per, STATE), "req", split_axis=0, concat_axis=0
     )
 
-    packed = pack_tokens(x_in, dt_raw, b_in, c_in, tensor_size)
-    packed = lax.all_to_all(packed, "tensor", split_axis=0, concat_axis=0)
-    packed = packed.reshape(tensor_size * x_in.shape[0], packed.shape[2])
+    rows = x_in.shape[0]
+    width = heads * HEAD_DIM
+    total = width + 2 * STATE + HEADS
+    piece = jax.ShapeDtypeStruct((rows, total), jnp.bfloat16)
+    sent = local_call(
+        pack_kernel, place, (x_in, dt_raw, b_in, c_in), [piece] * tensor_size, "pack_tokens"
+    )
+    packed = local_call(
+        gather_kernel,
+        place,
+        send_shifted(sent, "tensor"),
+        jax.ShapeDtypeStruct((tensor_size, rows, total), jnp.bfloat16),
+        "gather_tokens",
+    ).reshape(tensor_size * rows, total)
 
     mixed, closing = run_sessions(
         place, sessions, lengths, packed, start, a_log, dt_bias, d_skip
@@ -265,9 +307,20 @@
     )
     new_cache = back.transpose(1, 0, 2, 3).reshape(state_cache.shape)
 
-    shard = mixed.reshape(tensor_size, x_in.shape[0], heads * HEAD_DIM)
-    y_out = lax.all_to_all(shard, "tensor", split_axis=0, concat_axis=0)
-    y_out = y_out.transpose(1, 0, 2).reshape(x_in.shape)
+    sent = local_call(
+        split_kernel,
+        place,
+        (mixed.reshape(tensor_size, rows, width),),
+        [jax.ShapeDtypeStruct((rows, width), jnp.bfloat16)] * tensor_size,
+        "split_rows",
+    )
+    y_out = local_call(
+        columns_kernel,
+        place,
+        send_shifted(sent, "tensor"),
+        jax.ShapeDtypeStruct(x_in.shape, jnp.bfloat16),
+        "join_columns",
+    )
     return y_out, new_cache
 
 

time: 286 us -> 291 us (1.017); the launches traced: 285 us -> 285 us
  waiting for transfers between devices: 174 us -> 47.3 us
  starting transfers between devices: 39.9 us -> 135 us
  blocking collectives: 47.8 us -> 61.7 us
  local copies, waits for them, and re-layouts: 6.96 us -> 20.6 us
  Pallas kernels: 15.7 us -> 19.3 us
    ppermute x0 -> x30, starting transfers between devices: none -> 109 us  [send_shifted(): lax.ppermute(arrays[shift], axis, [(i, (i + shift) % parts) for i in rang...]
    all_to_all x1, waiting for transfers between devices: 44.4 us -> 0.01 us  [per_device(): lax.all_to_all(spread.reshape(req_size, slot_count, per, STATE), 'req', s...]
    all_to_all x2 -> x0, waiting for transfers between devices: 43.6 us -> none  [the longest x1 28.5 us: per_device(): packed = lax.all_to_all(packed, 'tensor', split_axis=0, concat_axis=0)]
    all_to_all x1, waiting for transfers between devices: 43.5 us -> 0.01 us  [per_device(): lax.all_to_all(back.reshape(req_size, slot_count, per, STATE), 'req', spl...]
    unnamed x29 -> x71, local copies, waits for them, and re-layouts: 2.32 us -> 17.2 us
    all_to_all x1, blocking collectives: 47.8 us -> 61.7 us  [per_device(): back = lax.all_to_all(closing, 'req', split_axis=0, concat_axis=0)]
    all_to_all x2 -> x0, starting transfers between devices: 10.5 us -> none  [the longest x1 6.76 us: per_device(): packed = lax.all_to_all(packed, 'tensor', split_axis=0, concat_axis=0)]
    all_to_all x1, starting transfers between devices: 7.37 us -> 4.2 us  [per_device(): lax.all_to_all(back.reshape(req_size, slot_count, per, STATE), 'req', spl...]
  transfers between devices with their start and end apart: 5 -> 33, of which waited for: 5 -> 3; matrix products, arithmetic and copies ran while one was open for 1% -> 0% of each run, Pallas kernels for 1% -> 1%
where the time goes in v2:
time: 291 us; the launch traced here: 285 us
  starting transfers between devices  135 us (46%)
  blocking collectives  61.7 us (21%)
  waiting for transfers between devices  47.3 us (16%)
  local copies, waits for them, and re-layouts  20.6 us (7%)
  Pallas kernels  19.3 us (7%)
    ppermute x30, starting transfers between devices, send_shifted(): lax.ppermute(arrays[shift], axis, [(i, (i + shift) % parts) for i in rang...  109 us
    all_to_all x1, blocking collectives, per_device(): back = lax.all_to_all(closing, 'req', split_axis=0, concat_axis=0)  61.7 us
    all_to_all x1, waiting for transfers between devices, per_device(): lax.all_to_all(pieces, 'req', split_axis=1, concat_axis=0, tiled=False)  44.5 us
    unnamed x71, local copies, waits for them, and re-layouts  17.2 us
    all_to_all x1, starting transfers between devices, per_device(): lax.all_to_all(pieces, 'req', split_axis=1, concat_axis=0, tiled=False)  16.9 us
    pallas_call x1, Pallas kernels, run_sessions(): pl.pallas_call(functools.partial(session_kernel, heads=heads, slot_count=...  11.4 us
  transfers between devices with their start and end apart: 33, of which 3 were waited for; matrix products, arithmetic and copies ran while one was open for 0% of the time, Pallas kernels for 1%

profile of v2, /device:TPU:1, one launch (start us, length us, event | category | flops | bytes accessed | tf_op | source)
XLA Modules:
  0.0 284.9 jit_solution(16510667602755596768)
XLA Ops:
  2.8 16.9 %all-to-all-start = ((bf16[1,6,32,16,128]{4,3,1,0,2:T(8,128)(2,1)}), bf16[1,6,32,16,128]{4,3,1,0,2:T(8,128)(2,1)S(1)}, u32[]{:S(2)}, u32[]{:S(2)}) async-start(bf16[1,6,32,16,128]{4,3,1,0,2:T(8,128)(2,1)} %copy.22), calls=%async_computation | async-start | bytes 1572864 | tf_op jit(solution)/shard_map/all_to_all | solution.py:276
  19.9 44.5 %all-to-all-done = bf16[1,6,32,16,128]{4,3,1,0,2:T(8,128)(2,1)S(1)} async-done(((bf16[1,6,32,16,128]{4,3,1,0,2:T(8,128)(2,1)}), bf16[1,6,32,16,128]{4,3,1,0,2:T(8,128)(2,1)S(1)}, u32[]{:S(2)}, u32[]{:S(2)}) %all-to-all-start) | async-done | bytes 786464 | tf_op jit(solution)/shard_map/all_to_all | solution.py:276
  66.5 4.2 %all-to-all-start.1 = ((bf16[32,6,16,128]{3,2,1,0:T(8,128)(2,1)}), bf16[32,6,16,128]{3,2,1,0:T(8,128)(2,1)S(1)}, u32[]{:S(2)}, u32[]{:S(2)}) async-start(bf16[32,6,16,128]{3,2,1,0:T(8,128)(2,1)} %bitcast.7), calls=%async_computation.1 | async-start | bytes 1572864 | tf_op jit(solution)/shard_map/all_to_all | solution.py:279
  71.7 3.1 %collective-permute-start = (bf16[72,896]{1,0:T(8,128)(2,1)S(1)}, bf16[72,896]{1,0:T(8,128)(2,1)S(1)}, u32[]{:S(2)}, u32[]{:S(2)}) collective-permute-start(bf16[72,896]{1,0:T(8,128)(2,1)S(1)} %get-tuple-element.37), channel_id=1, source_target_pairs={{0,1},{1,2},{2,3},{3,4},{4,5},{5,6},{6,7},{7,8},{8,9},{9,10},{10,1... | collective-permute-start | bytes 387080 | tf_op jit(solution)/shard_map/ppermute | solution.py:74
  74.8 4.4 %collective-permute-start.1 = (bf16[72,896]{1,0:T(8,128)(2,1)S(1)}, bf16[72,896]{1,0:T(8,128)(2,1)S(1)}, u32[]{:S(2)}, u32[]{:S(2)}) collective-permute-start(bf16[72,896]{1,0:T(8,128)(2,1)S(1)} %get-tuple-element.38), channel_id=1, source_target_pairs={{0,2},{1,3},{2,4},{3,5},{4,6},{5,7},{6,8},{7,9},{8,10},{9,11},{10,... | collective-permute-start | bytes 387080 | tf_op jit(solution)/shard_map/ppermute | solution.py:74
  79.1 6.4 %collective-permute-start.10 = (bf16[72,896]{1,0:T(8,128)(2,1)S(1)}, bf16[72,896]{1,0:T(8,128)(2,1)S(1)}, u32[]{:S(2)}, u32[]{:S(2)}) collective-permute-start(bf16[72,896]{1,0:T(8,128)(2,1)S(1)} %get-tuple-element.47), channel_id=1, source_target_pairs={{0,11},{1,12},{2,13},{3,14},{4,15},{5,0},{6,1},{7,2},{8,3},{9,4},{... | collective-permute-start | bytes 387080 | tf_op jit(solution)/shard_map/ppermute | solution.py:74
  85.6 3.0 %collective-permute-start.11 = (bf16[72,896]{1,0:T(8,128)(2,1)S(1)}, bf16[72,896]{1,0:T(8,128)(2,1)S(1)}, u32[]{:S(2)}, u32[]{:S(2)}) collective-permute-start(bf16[72,896]{1,0:T(8,128)(2,1)S(1)} %get-tuple-element.48), channel_id=1, source_target_pairs={{0,12},{1,13},{2,14},{3,15},{4,0},{5,1},{6,2},{7,3},{8,4},{9,5},{1... | collective-permute-start | bytes 387080 | tf_op jit(solution)/shard_map/ppermute | solution.py:74
  90.5 2.5 collective-permute-start.13
  93.0 3.7 %collective-permute-start.14 = (bf16[72,896]{1,0:T(8,128)(2,1)S(1)}, bf16[72,896]{1,0:T(8,128)(2,1)S(1)}, u32[]{:S(2)}, u32[]{:S(2)}) collective-permute-start(bf16[72,896]{1,0:T(8,128)(2,1)S(1)} %get-tuple-element.51), channel_id=1, source_target_pairs={{0,15},{1,0},{2,1},{3,2},{4,3},{5,4},{6,5},{7,6},{8,7},{9,8},{10,9... | collective-permute-start | bytes 387080 | tf_op jit(solution)/shard_map/ppermute | solution.py:74
  96.7 2.8 collective-permute-start.2
  99.5 2.5 collective-permute-start.3
  102.7 3.2 %collective-permute-start.4 = (bf16[72,896]{1,0:T(8,128)(2,1)S(1)}, bf16[72,896]{1,0:T(8,128)(2,1)S(1)}, u32[]{:S(2)}, u32[]{:S(2)}) collective-permute-start(bf16[72,896]{1,0:T(8,128)(2,1)S(1)} %get-tuple-element.41), channel_id=1, source_target_pairs={{0,5},{1,6},{2,7},{3,8},{4,9},{5,10},{6,11},{7,12},{8,13},{9,14},{... | collective-permute-start | bytes 387080 | tf_op jit(solution)/shard_map/ppermute | solution.py:74
  106.6 5.6 %collective-permute-start.5 = (bf16[72,896]{1,0:T(8,128)(2,1)S(1)}, bf16[72,896]{1,0:T(8,128)(2,1)S(1)}, u32[]{:S(2)}, u32[]{:S(2)}) collective-permute-start(bf16[72,896]{1,0:T(8,128)(2,1)S(1)} %get-tuple-element.42), channel_id=1, source_target_pairs={{0,6},{1,7},{2,8},{3,9},{4,10},{5,11},{6,12},{7,13},{8,14},{9,15},... | collective-permute-start | bytes 387080 | tf_op jit(solution)/shard_map/ppermute | solution.py:74
  112.9 3.8 %collective-permute-start.6 = (bf16[72,896]{1,0:T(8,128)(2,1)S(1)}, bf16[72,896]{1,0:T(8,128)(2,1)S(1)}, u32[]{:S(2)}, u32[]{:S(2)}) collective-permute-start(bf16[72,896]{1,0:T(8,128)(2,1)S(1)} %get-tuple-element.43), channel_id=1, source_target_pairs={{0,7},{1,8},{2,9},{3,10},{4,11},{5,12},{6,13},{7,14},{8,15},{9,0},... | collective-permute-start | bytes 387080 | tf_op jit(solution)/shard_map/ppermute | solution.py:74
  117.4 3.9 %collective-permute-start.7 = (bf16[72,896]{1,0:T(8,128)(2,1)S(1)}, bf16[72,896]{1,0:T(8,128)(2,1)S(1)}, u32[]{:S(2)}, u32[]{:S(2)}) collective-permute-start(bf16[72,896]{1,0:T(8,128)(2,1)S(1)} %get-tuple-element.44), channel_id=1, source_target_pairs={{0,8},{1,9},{2,10},{3,11},{4,12},{5,13},{6,14},{7,15},{8,0},{9,1},... | collective-permute-start | bytes 387080 | tf_op jit(solution)/shard_map/ppermute | solution.py:74
  122.0 4.0 %collective-permute-start.8 = (bf16[72,896]{1,0:T(8,128)(2,1)S(1)}, bf16[72,896]{1,0:T(8,128)(2,1)S(1)}, u32[]{:S(2)}, u32[]{:S(2)}) collective-permute-start(bf16[72,896]{1,0:T(8,128)(2,1)S(1)} %get-tuple-element.45), channel_id=1, source_target_pairs={{0,9},{1,10},{2,11},{3,12},{4,13},{5,14},{6,15},{7,0},{8,1},{9,2},... | collective-permute-start | bytes 387080 | tf_op jit(solution)/shard_map/ppermute | solution.py:74
  126.7 4.8 %collective-permute-start.9 = (bf16[72,896]{1,0:T(8,128)(2,1)S(1)}, bf16[72,896]{1,0:T(8,128)(2,1)S(1)}, u32[]{:S(2)}, u32[]{:S(2)}) collective-permute-start(bf16[72,896]{1,0:T(8,128)(2,1)S(1)} %get-tuple-element.46), channel_id=1, source_target_pairs={{0,10},{1,11},{2,12},{3,13},{4,14},{5,15},{6,0},{7,1},{8,2},{9,3},... | collective-permute-start | bytes 387080 | tf_op jit(solution)/shard_map/ppermute | solution.py:74
  146.2 11.4 %run_sessions.1 = (bf16[1152,512]{1,0:T(8,128)(2,1)S(1)}, bf16[32,6,16,128]{3,2,1,0:T(8,128)(2,1)S(1)}) custom-call(s32[2]{0:T(128)S(1)} %pad_add_fusion.place_ref, s32[192]{0:T(256)S(1)} %reshape.26.sessions_ref, s32[192]{0:T(256)S(1)} %copy-done.30, bf16[1152,896]{1,0:T(8,128)(2,1)S(1)} %bitcast.17, bf16[32,6,16,128]{3,2,1,0:T(8,128)(2,1)S(1)} %all-to-all-done.1.start_ref, ...), custom_call_target="tpu_custom_call" | custom-call | tf_op jit(solution)/shard_map/run_sessions/pallas_call | solution.py:228
  157.6 61.7 %all_to_all.30 = bf16[32,6,16,128]{3,2,1,0:T(8,128)(2,1)S(1)} all-to-all(bf16[32,6,16,128]{3,2,1,0:T(8,128)(2,1)S(1)} %get-tuple-element.69), channel_id=1, replica_groups=mesh['req'=32,'tensor'=16] {'req'}, dimensions={0} | all-to-all | bytes 1572864 | tf_op jit(solution)/shard_map/all_to_all | solution.py:302
  221.3 4.2 %all-to-all-start.3 = ((bf16[32,6,16,128]{3,2,1,0:T(8,128)(2,1)}), bf16[32,6,16,128]{3,2,1,0:T(8,128)(2,1)S(1)}, u32[]{:S(2)}, u32[]{:S(2)}) async-start(bf16[32,6,16,128]{3,2,1,0:T(8,128)(2,1)} %bitcast.12), calls=%async_computation.3 | async-start | bytes 1572864 | tf_op jit(solution)/shard_map/all_to_all | solution.py:305
  228.1 5.2 %collective-permute-start.16 = (bf16[72,512]{1,0:T(8,128)(2,1)S(1)}, bf16[72,512]{1,0:T(8,128)(2,1)S(1)}, u32[]{:S(2)}, u32[]{:S(2)}) collective-permute-start(bf16[72,512]{1,0:T(8,128)(2,1)S(1)} %get-tuple-element.55), channel_id=1, source_target_pairs={{0,2},{1,3},{2,4},{3,5},{4,6},{5,7},{6,8},{7,9},{8,10},{9,11},{10,... | collective-permute-start | bytes 221192 | tf_op jit(solution)/shard_map/ppermute | solution.py:74
  233.3 2.8 collective-permute-start.17
  236.1 3.6 %collective-permute-start.18 = (bf16[72,512]{1,0:T(8,128)(2,1)S(1)}, bf16[72,512]{1,0:T(8,128)(2,1)S(1)}, u32[]{:S(2)}, u32[]{:S(2)}) collective-permute-start(bf16[72,512]{1,0:T(8,128)(2,1)S(1)} %get-tuple-element.57), channel_id=1, source_target_pairs={{0,4},{1,5},{2,6},{3,7},{4,8},{5,9},{6,10},{7,11},{8,12},{9,13},{1... | collective-permute-start | bytes 221192 | tf_op jit(solution)/shard_map/ppermute | solution.py:74
  239.7 2.5 collective-permute-start.19
  242.3 3.4 %collective-permute-start.20 = (bf16[72,512]{1,0:T(8,128)(2,1)S(1)}, bf16[72,512]{1,0:T(8,128)(2,1)S(1)}, u32[]{:S(2)}, u32[]{:S(2)}) collective-permute-start(bf16[72,512]{1,0:T(8,128)(2,1)S(1)} %get-tuple-element.59), channel_id=1, source_target_pairs={{0,6},{1,7},{2,8},{3,9},{4,10},{5,11},{6,12},{7,13},{8,14},{9,15},... | collective-permute-start | bytes 221192 | tf_op jit(solution)/shard_map/ppermute | solution.py:74
  245.6 6.6 %collective-permute-start.21 = (bf16[72,512]{1,0:T(8,128)(2,1)S(1)}, bf16[72,512]{1,0:T(8,128)(2,1)S(1)}, u32[]{:S(2)}, u32[]{:S(2)}) collective-permute-start(bf16[72,512]{1,0:T(8,128)(2,1)S(1)} %get-tuple-element.60), channel_id=1, source_target_pairs={{0,7},{1,8},{2,9},{3,10},{4,11},{5,12},{6,13},{7,14},{8,15},{9,0},... | collective-permute-start | bytes 221192 | tf_op jit(solution)/shard_map/ppermute | solution.py:74
  254.4 3.9 %collective-permute-start.23 = (bf16[72,512]{1,0:T(8,128)(2,1)S(1)}, bf16[72,512]{1,0:T(8,128)(2,1)S(1)}, u32[]{:S(2)}, u32[]{:S(2)}) collective-permute-start(bf16[72,512]{1,0:T(8,128)(2,1)S(1)} %get-tuple-element.62), channel_id=1, source_target_pairs={{0,9},{1,10},{2,11},{3,12},{4,13},{5,14},{6,15},{7,0},{8,1},{9,2},... | collective-permute-start | bytes 221192 | tf_op jit(solution)/shard_map/ppermute | solution.py:74
  258.2 5.0 %collective-permute-start.24 = (bf16[72,512]{1,0:T(8,128)(2,1)S(1)}, bf16[72,512]{1,0:T(8,128)(2,1)S(1)}, u32[]{:S(2)}, u32[]{:S(2)}) collective-permute-start(bf16[72,512]{1,0:T(8,128)(2,1)S(1)} %get-tuple-element.63), channel_id=1, source_target_pairs={{0,10},{1,11},{2,12},{3,13},{4,14},{5,15},{6,0},{7,1},{8,2},{9,3},... | collective-permute-start | bytes 221192 | tf_op jit(solution)/shard_map/ppermute | solution.py:74
  263.2 4.3 %collective-permute-start.25 = (bf16[72,512]{1,0:T(8,128)(2,1)S(1)}, bf16[72,512]{1,0:T(8,128)(2,1)S(1)}, u32[]{:S(2)}, u32[]{:S(2)}) collective-permute-start(bf16[72,512]{1,0:T(8,128)(2,1)S(1)} %get-tuple-element.64), channel_id=1, source_target_pairs={{0,11},{1,12},{2,13},{3,14},{4,15},{5,0},{6,1},{7,2},{8,3},{9,4},{... | collective-permute-start | bytes 221192 | tf_op jit(solution)/shard_map/ppermute | solution.py:74
  267.6 3.8 %collective-permute-start.26 = (bf16[72,512]{1,0:T(8,128)(2,1)S(1)}, bf16[72,512]{1,0:T(8,128)(2,1)S(1)}, u32[]{:S(2)}, u32[]{:S(2)}) collective-permute-start(bf16[72,512]{1,0:T(8,128)(2,1)S(1)} %get-tuple-element.65), channel_id=1, source_target_pairs={{0,12},{1,13},{2,14},{3,15},{4,0},{5,1},{6,2},{7,3},{8,4},{9,5},{1... | collective-permute-start | bytes 221192 | tf_op jit(solution)/shard_map/ppermute | solution.py:74
  273.3 2.5 collective-permute-start.28
  275.8 4.2 %collective-permute-start.29 = (bf16[72,512]{1,0:T(8,128)(2,1)S(1)}, bf16[72,512]{1,0:T(8,128)(2,1)S(1)}, u32[]{:S(2)}, u32[]{:S(2)}) collective-permute-start(bf16[72,512]{1,0:T(8,128)(2,1)S(1)} %get-tuple-element.68), channel_id=1, source_target_pairs={{0,15},{1,0},{2,1},{3,2},{4,3},{5,4},{6,5},{7,6},{8,7},{9,8},{10,9... | collective-permute-start | bytes 221192 | tf_op jit(solution)/shard_map/ppermute | solution.py:74
  (121 shorter events, 39.3 us)
Async XLA Ops:
  2.8 61.6 %all-to-all-start = ((bf16[1,6,32,16,128]{4,3,1,0,2:T(8,128)(2,1)}), bf16[1,6,32,16,128]{4,3,1,0,2:T(8,128)(2,1)S(1)}, u32[]{:S(2)}, u32[]{:S(2)}) async-start(bf16[1,6,32,16,128]{4,3,1,0,2:T(8,128)(2,1)} %copy.22), calls=%async_computation | async-start | bytes 1572864 | tf_op jit(solution)/shard_map/all_to_all | solution.py:276
  66.5 79.6 %all-to-all-start.1 = ((bf16[32,6,16,128]{3,2,1,0:T(8,128)(2,1)}), bf16[32,6,16,128]{3,2,1,0:T(8,128)(2,1)S(1)}, u32[]{:S(2)}, u32[]{:S(2)}) async-start(bf16[32,6,16,128]{3,2,1,0:T(8,128)(2,1)} %bitcast.7), calls=%async_computation.1 | async-start | bytes 1572864 | tf_op jit(solution)/shard_map/all_to_all | solution.py:279
  71.7 18.8 %collective-permute-start = (bf16[72,896]{1,0:T(8,128)(2,1)S(1)}, bf16[72,896]{1,0:T(8,128)(2,1)S(1)}, u32[]{:S(2)}, u32[]{:S(2)}) collective-permute-start(bf16[72,896]{1,0:T(8,128)(2,1)S(1)} %get-tuple-element.37), channel_id=1, source_target_pairs={{0,1},{1,2},{2,3},{3,4},{4,5},{5,6},{6,7},{7,8},{8,9},{9,10},{10,1... | collective-permute-start | bytes 387080 | tf_op jit(solution)/shard_map/ppermute | solution.py:74
  74.8 18.2 %collective-permute-start.1 = (bf16[72,896]{1,0:T(8,128)(2,1)S(1)}, bf16[72,896]{1,0:T(8,128)(2,1)S(1)}, u32[]{:S(2)}, u32[]{:S(2)}) collective-permute-start(bf16[72,896]{1,0:T(8,128)(2,1)S(1)} %get-tuple-element.38), channel_id=1, source_target_pairs={{0,2},{1,3},{2,4},{3,5},{4,6},{5,7},{6,8},{7,9},{8,10},{9,11},{10,... | collective-permute-start | bytes 387080 | tf_op jit(solution)/shard_map/ppermute | solution.py:74
  79.1 17.6 %collective-permute-start.10 = (bf16[72,896]{1,0:T(8,128)(2,1)S(1)}, bf16[72,896]{1,0:T(8,128)(2,1)S(1)}, u32[]{:S(2)}, u32[]{:S(2)}) collective-permute-start(bf16[72,896]{1,0:T(8,128)(2,1)S(1)} %get-tuple-element.47), channel_id=1, source_target_pairs={{0,11},{1,12},{2,13},{3,14},{4,15},{5,0},{6,1},{7,2},{8,3},{9,4},{... | collective-permute-start | bytes 387080 | tf_op jit(solution)/shard_map/ppermute | solution.py:74
  85.6 13.9 %collective-permute-start.11 = (bf16[72,896]{1,0:T(8,128)(2,1)S(1)}, bf16[72,896]{1,0:T(8,128)(2,1)S(1)}, u32[]{:S(2)}, u32[]{:S(2)}) collective-permute-start(bf16[72,896]{1,0:T(8,128)(2,1)S(1)} %get-tuple-element.48), channel_id=1, source_target_pairs={{0,12},{1,13},{2,14},{3,15},{4,0},{5,1},{6,2},{7,3},{8,4},{9,5},{1... | collective-permute-start | bytes 387080 | tf_op jit(solution)/shard_map/ppermute | solution.py:74
  88.6 13.5 %collective-permute-start.12 = (bf16[72,896]{1,0:T(8,128)(2,1)S(1)}, bf16[72,896]{1,0:T(8,128)(2,1)S(1)}, u32[]{:S(2)}, u32[]{:S(2)}) collective-permute-start(bf16[72,896]{1,0:T(8,128)(2,1)S(1)} %get-tuple-element.49), channel_id=1, source_target_pairs={{0,13},{1,14},{2,15},{3,0},{4,1},{5,2},{6,3},{7,4},{8,5},{9,6},{10... | collective-permute-start | bytes 387080 | tf_op jit(solution)/shard_map/ppermute | solution.py:74
  90.5 15.4 %collective-permute-start.13 = (bf16[72,896]{1,0:T(8,128)(2,1)S(1)}, bf16[72,896]{1,0:T(8,128)(2,1)S(1)}, u32[]{:S(2)}, u32[]{:S(2)}) collective-permute-start(bf16[72,896]{1,0:T(8,128)(2,1)S(1)} %get-tuple-element.50), channel_id=1, source_target_pairs={{0,14},{1,15},{2,0},{3,1},{4,2},{5,3},{6,4},{7,5},{8,6},{9,7},{10,... | collective-permute-start | bytes 387080 | tf_op jit(solution)/shard_map/ppermute | solution.py:74
  93.0 19.3 %collective-permute-start.14 = (bf16[72,896]{1,0:T(8,128)(2,1)S(1)}, bf16[72,896]{1,0:T(8,128)(2,1)S(1)}, u32[]{:S(2)}, u32[]{:S(2)}) collective-permute-start(bf16[72,896]{1,0:T(8,128)(2,1)S(1)} %get-tuple-element.51), channel_id=1, source_target_pairs={{0,15},{1,0},{2,1},{3,2},{4,3},{5,4},{6,5},{7,6},{8,7},{9,8},{10,9... | collective-permute-start | bytes 387080 | tf_op jit(solution)/shard_map/ppermute | solution.py:74
  96.7 20.0 %collective-permute-start.2 = (bf16[72,896]{1,0:T(8,128)(2,1)S(1)}, bf16[72,896]{1,0:T(8,128)(2,1)S(1)}, u32[]{:S(2)}, u32[]{:S(2)}) collective-permute-start(bf16[72,896]{1,0:T(8,128)(2,1)S(1)} %get-tuple-element.39), channel_id=1, source_target_pairs={{0,3},{1,4},{2,5},{3,6},{4,7},{5,8},{6,9},{7,10},{8,11},{9,12},{10... | collective-permute-start | bytes 387080 | tf_op jit(solution)/shard_map/ppermute | solution.py:74
  99.5 21.8 %collective-permute-start.3 = (bf16[72,896]{1,0:T(8,128)(2,1)S(1)}, bf16[72,896]{1,0:T(8,128)(2,1)S(1)}, u32[]{:S(2)}, u32[]{:S(2)}) collective-permute-start(bf16[72,896]{1,0:T(8,128)(2,1)S(1)} %get-tuple-element.40), channel_id=1, source_target_pairs={{0,4},{1,5},{2,6},{3,7},{4,8},{5,9},{6,10},{7,11},{8,12},{9,13},{1... | collective-permute-start | bytes 387080 | tf_op jit(solution)/shard_map/ppermute | solution.py:74
  102.7 23.3 %collective-permute-start.4 = (bf16[72,896]{1,0:T(8,128)(2,1)S(1)}, bf16[72,896]{1,0:T(8,128)(2,1)S(1)}, u32[]{:S(2)}, u32[]{:S(2)}) collective-permute-start(bf16[72,896]{1,0:T(8,128)(2,1)S(1)} %get-tuple-element.41), channel_id=1, source_target_pairs={{0,5},{1,6},{2,7},{3,8},{4,9},{5,10},{6,11},{7,12},{8,13},{9,14},{... | collective-permute-start | bytes 387080 | tf_op jit(solution)/shard_map/ppermute | solution.py:74
  106.6 25.1 %collective-permute-start.5 = (bf16[72,896]{1,0:T(8,128)(2,1)S(1)}, bf16[72,896]{1,0:T(8,128)(2,1)S(1)}, u32[]{:S(2)}, u32[]{:S(2)}) collective-permute-start(bf16[72,896]{1,0:T(8,128)(2,1)S(1)} %get-tuple-element.42), channel_id=1, source_target_pairs={{0,6},{1,7},{2,8},{3,9},{4,10},{5,11},{6,12},{7,13},{8,14},{9,15},... | collective-permute-start | bytes 387080 | tf_op jit(solution)/shard_map/ppermute | solution.py:74
  112.9 19.4 %collective-permute-start.6 = (bf16[72,896]{1,0:T(8,128)(2,1)S(1)}, bf16[72,896]{1,0:T(8,128)(2,1)S(1)}, u32[]{:S(2)}, u32[]{:S(2)}) collective-permute-start(bf16[72,896]{1,0:T(8,128)(2,1)S(1)} %get-tuple-element.43), channel_id=1, source_target_pairs={{0,7},{1,8},{2,9},{3,10},{4,11},{5,12},{6,13},{7,14},{8,15},{9,0},... | collective-permute-start | bytes 387080 | tf_op jit(solution)/shard_map/ppermute | solution.py:74
  117.4 15.6 %collective-permute-start.7 = (bf16[72,896]{1,0:T(8,128)(2,1)S(1)}, bf16[72,896]{1,0:T(8,128)(2,1)S(1)}, u32[]{:S(2)}, u32[]{:S(2)}) collective-permute-start(bf16[72,896]{1,0:T(8,128)(2,1)S(1)} %get-tuple-element.44), channel_id=1, source_target_pairs={{0,8},{1,9},{2,10},{3,11},{4,12},{5,13},{6,14},{7,15},{8,0},{9,1},... | collective-permute-start | bytes 387080 | tf_op jit(solution)/shard_map/ppermute | solution.py:74
  122.0 11.7 %collective-permute-start.8 = (bf16[72,896]{1,0:T(8,128)(2,1)S(1)}, bf16[72,896]{1,0:T(8,128)(2,1)S(1)}, u32[]{:S(2)}, u32[]{:S(2)}) collective-permute-start(bf16[72,896]{1,0:T(8,128)(2,1)S(1)} %get-tuple-element.45), channel_id=1, source_target_pairs={{0,9},{1,10},{2,11},{3,12},{4,13},{5,14},{6,15},{7,0},{8,1},{9,2},... | collective-permute-start | bytes 387080 | tf_op jit(solution)/shard_map/ppermute | solution.py:74
  126.7 8.2 %collective-permute-start.9 = (bf16[72,896]{1,0:T(8,128)(2,1)S(1)}, bf16[72,896]{1,0:T(8,128)(2,1)S(1)}, u32[]{:S(2)}, u32[]{:S(2)}) collective-permute-start(bf16[72,896]{1,0:T(8,128)(2,1)S(1)} %get-tuple-element.46), channel_id=1, source_target_pairs={{0,10},{1,11},{2,12},{3,13},{4,14},{5,15},{6,0},{7,1},{8,2},{9,3},... | collective-permute-start | bytes 387080 | tf_op jit(solution)/shard_map/ppermute | solution.py:74
  221.3 62.6 %all-to-all-start.3 = ((bf16[32,6,16,128]{3,2,1,0:T(8,128)(2,1)}), bf16[32,6,16,128]{3,2,1,0:T(8,128)(2,1)S(1)}, u32[]{:S(2)}, u32[]{:S(2)}) async-start(bf16[32,6,16,128]{3,2,1,0:T(8,128)(2,1)} %bitcast.12), calls=%async_computation.3 | async-start | bytes 1572864 | tf_op jit(solution)/shard_map/all_to_all | solution.py:305
  226.2 16.1 %collective-permute-start.15 = (bf16[72,512]{1,0:T(8,128)(2,1)S(1)}, bf16[72,512]{1,0:T(8,128)(2,1)S(1)}, u32[]{:S(2)}, u32[]{:S(2)}) collective-permute-start(bf16[72,512]{1,0:T(8,128)(2,1)S(1)} %get-tuple-element.54), channel_id=1, source_target_pairs={{0,1},{1,2},{2,3},{3,4},{4,5},{5,6},{6,7},{7,8},{8,9},{9,10},{10,1... | collective-permute-start | bytes 221192 | tf_op jit(solution)/shard_map/ppermute | solution.py:74
  228.1 17.5 %collective-permute-start.16 = (bf16[72,512]{1,0:T(8,128)(2,1)S(1)}, bf16[72,512]{1,0:T(8,128)(2,1)S(1)}, u32[]{:S(2)}, u32[]{:S(2)}) collective-permute-start(bf16[72,512]{1,0:T(8,128)(2,1)S(1)} %get-tuple-element.55), channel_id=1, source_target_pairs={{0,2},{1,3},{2,4},{3,5},{4,6},{5,7},{6,8},{7,9},{8,10},{9,11},{10,... | collective-permute-start | bytes 221192 | tf_op jit(solution)/shard_map/ppermute | solution.py:74
  233.3 19.0 %collective-permute-start.17 = (bf16[72,512]{1,0:T(8,128)(2,1)S(1)}, bf16[72,512]{1,0:T(8,128)(2,1)S(1)}, u32[]{:S(2)}, u32[]{:S(2)}) collective-permute-start(bf16[72,512]{1,0:T(8,128)(2,1)S(1)} %get-tuple-element.56), channel_id=1, source_target_pairs={{0,3},{1,4},{2,5},{3,6},{4,7},{5,8},{6,9},{7,10},{8,11},{9,12},{10... | collective-permute-start | bytes 221192 | tf_op jit(solution)/shard_map/ppermute | solution.py:74
  236.1 18.3 %collective-permute-start.18 = (bf16[72,512]{1,0:T(8,128)(2,1)S(1)}, bf16[72,512]{1,0:T(8,128)(2,1)S(1)}, u32[]{:S(2)}, u32[]{:S(2)}) collective-permute-start(bf16[72,512]{1,0:T(8,128)(2,1)S(1)} %get-tuple-element.57), channel_id=1, source_target_pairs={{0,4},{1,5},{2,6},{3,7},{4,8},{5,9},{6,10},{7,11},{8,12},{9,13},{1... | collective-permute-start | bytes 221192 | tf_op jit(solution)/shard_map/ppermute | solution.py:74
  239.7 18.5 %collective-permute-start.19 = (bf16[72,512]{1,0:T(8,128)(2,1)S(1)}, bf16[72,512]{1,0:T(8,128)(2,1)S(1)}, u32[]{:S(2)}, u32[]{:S(2)}) collective-permute-start(bf16[72,512]{1,0:T(8,128)(2,1)S(1)} %get-tuple-element.58), channel_id=1, source_target_pairs={{0,5},{1,6},{2,7},{3,8},{4,9},{5,10},{6,11},{7,12},{8,13},{9,14},{... | collective-permute-start | bytes 221192 | tf_op jit(solution)/shard_map/ppermute | solution.py:74
  242.3 21.0 %collective-permute-start.20 = (bf16[72,512]{1,0:T(8,128)(2,1)S(1)}, bf16[72,512]{1,0:T(8,128)(2,1)S(1)}, u32[]{:S(2)}, u32[]{:S(2)}) collective-permute-start(bf16[72,512]{1,0:T(8,128)(2,1)S(1)} %get-tuple-element.59), channel_id=1, source_target_pairs={{0,6},{1,7},{2,8},{3,9},{4,10},{5,11},{6,12},{7,13},{8,14},{9,15},... | collective-permute-start | bytes 221192 | tf_op jit(solution)/shard_map/ppermute | solution.py:74
  245.6 21.9 %collective-permute-start.21 = (bf16[72,512]{1,0:T(8,128)(2,1)S(1)}, bf16[72,512]{1,0:T(8,128)(2,1)S(1)}, u32[]{:S(2)}, u32[]{:S(2)}) collective-permute-start(bf16[72,512]{1,0:T(8,128)(2,1)S(1)} %get-tuple-element.60), channel_id=1, source_target_pairs={{0,7},{1,8},{2,9},{3,10},{4,11},{5,12},{6,13},{7,14},{8,15},{9,0},... | collective-permute-start | bytes 221192 | tf_op jit(solution)/shard_map/ppermute | solution.py:74
  252.3 19.0 %collective-permute-start.22 = (bf16[72,512]{1,0:T(8,128)(2,1)S(1)}, bf16[72,512]{1,0:T(8,128)(2,1)S(1)}, u32[]{:S(2)}, u32[]{:S(2)}) collective-permute-start(bf16[72,512]{1,0:T(8,128)(2,1)S(1)} %get-tuple-element.61), channel_id=1, source_target_pairs={{0,8},{1,9},{2,10},{3,11},{4,12},{5,13},{6,14},{7,15},{8,0},{9,1},... | collective-permute-start | bytes 221192 | tf_op jit(solution)/shard_map/ppermute | solution.py:74
  254.4 18.9 %collective-permute-start.23 = (bf16[72,512]{1,0:T(8,128)(2,1)S(1)}, bf16[72,512]{1,0:T(8,128)(2,1)S(1)}, u32[]{:S(2)}, u32[]{:S(2)}) collective-permute-start(bf16[72,512]{1,0:T(8,128)(2,1)S(1)} %get-tuple-element.62), channel_id=1, source_target_pairs={{0,9},{1,10},{2,11},{3,12},{4,13},{5,14},{6,15},{7,0},{8,1},{9,2},... | collective-permute-start | bytes 221192 | tf_op jit(solution)/shard_map/ppermute | solution.py:74
  258.2 17.5 %collective-permute-start.24 = (bf16[72,512]{1,0:T(8,128)(2,1)S(1)}, bf16[72,512]{1,0:T(8,128)(2,1)S(1)}, u32[]{:S(2)}, u32[]{:S(2)}) collective-permute-start(bf16[72,512]{1,0:T(8,128)(2,1)S(1)} %get-tuple-element.63), channel_id=1, source_target_pairs={{0,10},{1,11},{2,12},{3,13},{4,14},{5,15},{6,0},{7,1},{8,2},{9,3},... | collective-permute-start | bytes 221192 | tf_op jit(solution)/shard_map/ppermute | solution.py:74
  263.2 16.7 %collective-permute-start.25 = (bf16[72,512]{1,0:T(8,128)(2,1)S(1)}, bf16[72,512]{1,0:T(8,128)(2,1)S(1)}, u32[]{:S(2)}, u32[]{:S(2)}) collective-permute-start(bf16[72,512]{1,0:T(8,128)(2,1)S(1)} %get-tuple-element.64), channel_id=1, source_target_pairs={{0,11},{1,12},{2,13},{3,14},{4,15},{5,0},{6,1},{7,2},{8,3},{9,4},{... | collective-permute-start | bytes 221192 | tf_op jit(solution)/shard_map/ppermute | solution.py:74
  267.6 12.4 %collective-permute-start.26 = (bf16[72,512]{1,0:T(8,128)(2,1)S(1)}, bf16[72,512]{1,0:T(8,128)(2,1)S(1)}, u32[]{:S(2)}, u32[]{:S(2)}) collective-permute-start(bf16[72,512]{1,0:T(8,128)(2,1)S(1)} %get-tuple-element.65), channel_id=1, source_target_pairs={{0,12},{1,13},{2,14},{3,15},{4,0},{5,1},{6,2},{7,3},{8,4},{9,5},{1... | collective-permute-start | bytes 221192 | tf_op jit(solution)/shard_map/ppermute | solution.py:74
  271.3 8.7 %collective-permute-start.27 = (bf16[72,512]{1,0:T(8,128)(2,1)S(1)}, bf16[72,512]{1,0:T(8,128)(2,1)S(1)}, u32[]{:S(2)}, u32[]{:S(2)}) collective-permute-start(bf16[72,512]{1,0:T(8,128)(2,1)S(1)} %get-tuple-element.66), channel_id=1, source_target_pairs={{0,13},{1,14},{2,15},{3,0},{4,1},{5,2},{6,3},{7,4},{8,5},{9,6},{10... | collective-permute-start | bytes 221192 | tf_op jit(solution)/shard_map/ppermute | solution.py:74
  273.3 6.7 %collective-permute-start.28 = (bf16[72,512]{1,0:T(8,128)(2,1)S(1)}, bf16[72,512]{1,0:T(8,128)(2,1)S(1)}, u32[]{:S(2)}, u32[]{:S(2)}) collective-permute-start(bf16[72,512]{1,0:T(8,128)(2,1)S(1)} %get-tuple-element.67), channel_id=1, source_target_pairs={{0,14},{1,15},{2,0},{3,1},{4,2},{5,3},{6,4},{7,5},{8,6},{9,7},{10,... | collective-permute-start | bytes 221192 | tf_op jit(solution)/shard_map/ppermute | solution.py:74
  (36 other events, 447.1 us)

commit v3 on v2

v3 whole, which is shorter than its diff:
```python
import functools

import jax
import jax.numpy as jnp
from jax import lax
from jax.experimental import pallas as pl
from jax.experimental.pallas import tpu as pltpu
from jax.sharding import PartitionSpec as P

HEADS = 128
HEAD_DIM = 64
STATE = 128
GROUPS = 4
MAXLEN = 192
LANES = 128
VMEM_LIMIT = 48 * 1024 * 1024


def pack_kernel(place_ref, x_ref, dt_ref, b_ref, c_ref, proj_ref, *out_refs):
    parts = len(out_refs)
    width = x_ref.shape[1] // parts
    group = place_ref[2]
    for shift, out_ref in enumerate(out_refs):
        target = lax.rem(group + shift, parts)
        out_ref[...] = x_ref[:, pl.ds(pl.multiple_of(target * width, LANES), width)]
    wide = b_ref.shape[1]
    proj_ref[:, :wide] = b_ref[...]
    proj_ref[:, wide : 2 * wide] = c_ref[...]
    proj_ref[:, 2 * wide :] = dt_ref[...]


def turn_in_kernel(place_ref, *refs):
    half = len(refs) // 2
    width = refs[0].shape[1] // half
    for shift in range(half):
        target = lax.rem(place_ref[3] + shift, half)
        columns = pl.ds(pl.multiple_of(target * width, LANES), width)
        for row in range(half):
            refs[half + shift][row] = refs[row][:, columns]


def gather_kernel(place_ref, *refs):
    out_ref = refs[-1]
    parts = len(refs) - 1
    for across in range(parts):
        x_from = lax.rem(place_ref[3] + parts - across, parts)
        for down in range(parts):
            y_from = lax.rem(place_ref[2] + parts - down, parts)
            out_ref[y_from * parts + x_from] = refs[across][down]


def split_kernel(place_ref, rows_ref, *out_refs):
    parts = len(out_refs)
    for across, out_ref in enumerate(out_refs):
        x_to = lax.rem(place_ref[3] + across, parts)
        for down in range(parts):
            y_to = lax.rem(place_ref[2] + down, parts)
            out_ref[down] = rows_ref[y_to * parts + x_to]


def turn_out_kernel(place_ref, *refs):
    half = len(refs) // 2
    width = refs[0].shape[2]
    for across in range(half):
        x_from = lax.rem(place_ref[3] + half - across, half)
        columns = pl.ds(pl.multiple_of(x_from * width, LANES), width)
        for down in range(half):
            refs[half + down][:, columns] = refs[across][down]


def columns_kernel(place_ref, *refs):
    out_ref = refs[-1]
    parts = len(refs) - 1
    width = refs[0].shape[1]
    for shift in range(parts):
        source = lax.rem(place_ref[2] + parts - shift, parts)
        out_ref[:, pl.ds(pl.multiple_of(source * width, LANES), width)] = refs[shift][...]


def local_call(kernel, place, arrays, out_shape, name):
    smem = pl.BlockSpec(memory_space=pltpu.SMEM)
    vmem = pl.BlockSpec(memory_space=pltpu.VMEM)
    several = isinstance(out_shape, list)
    return pl.pallas_call(
        kernel,
        in_specs=[smem] + [vmem] * len(arrays),
        out_specs=[vmem] * len(out_shape) if several else vmem,
        out_shape=out_shape,
        compiler_params=pltpu.CompilerParams(vmem_limit_bytes=VMEM_LIMIT),
        name=name,
    )(place, *arrays)


def send_along(arrays, count, along_y):
    moved = [arrays[0]]
    for shift in range(1, count):
        if along_y:
            pairs = [
                (i, (i // count + shift) % count * count + i % count) for i in range(count * count)
            ]
        else:
            pairs = [
                (i, i // count * count + (i % count + shift) % count) for i in range(count * count)
            ]
        moved.append(lax.ppermute(arrays[shift], "tensor", pairs))
    return moved


def cache_row(sessions_ref, owners_ref, slots_ref, slot_count, index):
    session = sessions_ref[index]
    return owners_ref[session] * slot_count + slots_ref[session]


def outgoing_kernel(sessions_ref, owners_ref, slots_ref, state_ref, delta_ref, out_ref):
    slot_count = delta_ref.shape[1]

    def step(group, carry):
        for slot in range(slot_count):
            row = cache_row(
                sessions_ref, owners_ref, slots_ref, slot_count, group * slot_count + slot
            )
            out_ref[group, slot] = state_ref[row]
            out_ref[group, slot_count + slot] = delta_ref[group, slot]
        return carry

    lax.fori_loop(0, delta_ref.shape[0], step, 0)


def closing_kernel(
    place_ref, sessions_ref, owners_ref, slots_ref, kept_ref, state_ref, arrived_ref, out_ref, *, heads
):
    groups, slots_twice, per, _ = arrived_ref.shape
    slot_count = slots_twice // 2
    head = place_ref[0] * per // HEAD_DIM

    def step(group, carry):
        for slot in range(slot_count):
            index = group * slot_count + slot
            row = cache_row(sessions_ref, owners_ref, slots_ref, slot_count, index)
            kept = kept_ref[index * heads + head]
            added = arrived_ref[group, slot_count + slot].astype(jnp.float32)
            closing = kept * state_ref[row].astype(jnp.float32) + added
            out_ref[row] = closing.astype(out_ref.dtype)
        return carry

    lax.fori_loop(0, groups, step, 0)


def token_steps(place_ref, steps_ref, bias_ref, a_log_ref, length, heads):
    f32 = jnp.float32
    lane_from = lax.broadcasted_iota(jnp.int32, (HEADS, LANES), 0)
    lane_to = lax.broadcasted_iota(jnp.int32, (HEADS, LANES), 1)
    chosen = (lane_from == lane_to + place_ref[1] * heads) & (lane_to < heads)
    raw = jnp.dot(steps_ref[...], chosen.astype(jnp.bfloat16), preferred_element_type=f32)
    row_index = lax.broadcasted_iota(jnp.int32, (MAXLEN, LANES), 0)
    shifted = raw + bias_ref[...]
    soft = jnp.maximum(shifted, 0.0) + jnp.log(1.0 + jnp.exp(-jnp.abs(shifted)))
    live = row_index < length
    step = jnp.where(live, soft, 0.0)
    t_index = lax.broadcasted_iota(jnp.int32, (MAXLEN, MAXLEN), 0)
    u_index = lax.broadcasted_iota(jnp.int32, (MAXLEN, MAXLEN), 1)
    causal = t_index >= u_index
    cum = jnp.dot(
        causal.astype(f32),
        step * -jnp.exp(a_log_ref[...]),
        precision=lax.Precision.HIGHEST,
        preferred_element_type=f32,
    )
    return step, cum, live, causal


def spread(columns, first, left):
    one = jnp.broadcast_to(columns[:, first : first + 1], left.shape)
    two = jnp.broadcast_to(columns[:, first + 1 : first + 2], left.shape)
    return jnp.where(left, one, two)


def left_half():
    return lax.broadcasted_iota(jnp.int32, (MAXLEN, LANES), 1) < HEAD_DIM


def delta_kernel(
    place_ref, sessions_ref, lengths_ref, x_ref, b_ref, steps_ref, a_log_ref, bias_ref,
    delta_ref, kept_ref, *, heads, slot_count
):
    length = lengths_ref[sessions_ref[place_ref[0] * slot_count + pl.program_id(0)]]
    step, cum, _, _ = token_steps(place_ref, steps_ref, bias_ref, a_log_ref, length, heads)
    last = cum[MAXLEN - 1 : MAXLEN, :]
    to_end = jnp.exp(last - cum) * step
    kept_ref[0] = jnp.broadcast_to(jnp.exp(last), kept_ref.shape[1:])
    left = left_half()
    in_proj = b_ref[...]
    per = delta_ref.shape[2]
    for first in range(0, heads, 2):
        lanes = slice(first * HEAD_DIM, (first + 2) * HEAD_DIM)
        scaled = x_ref[:, lanes].astype(jnp.float32) * spread(to_end, first, left)
        added = lax.dot_general(
            scaled.astype(jnp.bfloat16),
            in_proj,
            (((0,), (0,)), ((), ())),
            preferred_element_type=jnp.float32,
        )
        begin, count = first * HEAD_DIM // per, 2 * HEAD_DIM // per
        delta_ref[begin : begin + count, 0] = added.astype(jnp.bfloat16).reshape(
            count, per, STATE
        )


def local_kernel(
    place_ref, sessions_ref, lengths_ref, x_ref, b_ref, c_ref, steps_ref, a_log_ref, bias_ref,
    skip_ref, local_ref, grown_ref, *, heads, slot_count
):
    f32 = jnp.float32
    bf16 = jnp.bfloat16
    half = LANES
    length = lengths_ref[sessions_ref[place_ref[0] * slot_count + pl.program_id(0)]]
    step, cum, live, causal = token_steps(
        place_ref, steps_ref, bias_ref, a_log_ref, length, heads
    )
    drop_rows = (cum - jnp.log(step)).T
    grown_ref[...] = jnp.where(live, jnp.exp(cum), 0.0)
    affinity = lax.dot_general(
        c_ref[...], b_ref[...], (((1,), (1,)), ((), ())), preferred_element_type=f32
    )
    affinity = jnp.where(causal, affinity, 0.0)
    top, low = affinity[:half, :half], affinity[half:, :]
    left = left_half()
    for first in range(0, heads, 2):
        lanes = slice(first * HEAD_DIM, (first + 2) * HEAD_DIM)
        pair = x_ref[:, lanes]
        mixed = []
        for head in (first, first + 1):
            column = cum[:, head : head + 1]
            line = drop_rows[head : head + 1, :]
            w_top = top * jnp.exp(jnp.minimum(column[:half] - line[:, :half], 80.0))
            w_low = low * jnp.exp(jnp.minimum(column[half:] - line, 80.0))
            mixed.append(
                jnp.concatenate(
                    [
                        jnp.dot(w_top.astype(bf16), pair[:half], preferred_element_type=f32),
                        jnp.dot(w_low.astype(bf16), pair, preferred_element_type=f32),
                    ],
                    axis=0,
                )
            )
        out = jnp.where(left, mixed[0], mixed[1]) + skip_ref[:, lanes] * pair.astype(f32)
        local_ref[:, lanes] = jnp.where(live, out, 0.0)


def carry_kernel(place_ref, c_ref, start_ref, local_ref, grown_ref, y_ref, *, heads):
    width = heads * HEAD_DIM
    start = start_ref[...].reshape(width, STATE)
    carried = lax.dot_general(
        c_ref[...], start, (((1,), (1,)), ((), ())), preferred_element_type=jnp.float32
    )
    grown = grown_ref[...]
    left = left_half()
    for first in range(0, heads, 2):
        lanes = slice(first * HEAD_DIM, (first + 2) * HEAD_DIM)
        out = local_ref[:, lanes] + spread(grown, first, left) * carried[:, lanes]
        y_ref[:, lanes] = out.astype(jnp.bfloat16)


def session_call(kernel, scalars, slot_count, operands, outputs, flops, name):
    return pl.pallas_call(
        kernel,
        grid_spec=pltpu.PrefetchScalarGridSpec(
            num_scalar_prefetch=len(scalars),
            grid=(slot_count,),
            in_specs=[pl.BlockSpec(block, index) for _, block, index in operands],
            out_specs=[pl.BlockSpec(block, index) for _, block, index in outputs],
        ),
        out_shape=[shape for shape, _, _ in outputs],
        compiler_params=pltpu.CompilerParams(vmem_limit_bytes=VMEM_LIMIT),
        cost_estimate=pl.CostEstimate(
            flops=flops, bytes_accessed=8 * 1024 * 1024, transcendentals=0
        ),
        name=name,
    )(*scalars, *(array for array, _, _ in operands))


def per_device(
    x_in,
    dt_raw,
    b_in,
    c_in,
    a_log,
    dt_bias,
    d_skip,
    state_cache,
    group_sessions,
    owners,
    cache_slots,
    lengths,
):
    tensor_size = lax.axis_size("tensor")
    req_size = lax.axis_size("req")
    slot_count, heads = state_cache.shape[:2]
    per = heads * HEAD_DIM // req_size
    side = tensor_size // GROUPS
    rows = x_in.shape[0]
    width = heads * HEAD_DIM
    bf16 = jnp.bfloat16
    f32 = jnp.float32
    shape = jax.ShapeDtypeStruct
    req_index = lax.axis_index("req")
    tensor_index = lax.axis_index("tensor")
    place = jnp.stack(
        [req_index, tensor_index, tensor_index // side, tensor_index % side]
    ).astype(jnp.int32)
    sessions = group_sessions.reshape(-1)
    smem = pl.BlockSpec(memory_space=pltpu.SMEM)
    vmem = pl.BlockSpec(memory_space=pltpu.VMEM)
    params = pltpu.CompilerParams(vmem_limit_bytes=VMEM_LIMIT)

    pieces = state_cache.reshape(slot_count, req_size, per, STATE)
    held = lax.all_to_all(pieces, "req", split_axis=1, concat_axis=0, tiled=False)
    held = held.reshape(req_size * slot_count, per, STATE)

    proj, *sent = local_call(
        pack_kernel,
        place,
        (x_in, dt_raw, b_in, c_in),
        [shape((rows, 2 * GROUPS * STATE + HEADS), bf16)]
        + [shape((rows, side * width), bf16)] * GROUPS,
        "pack_tokens",
    )
    proj = lax.all_gather(proj, "tensor", axis=0, tiled=True)
    sent = local_call(
        turn_in_kernel,
        place,
        send_along(sent, side, True),
        [shape((GROUPS, rows, width), bf16)] * side,
        "turn_in",
    )
    tokens = local_call(
        gather_kernel,
        place,
        send_along(sent, side, False),
        shape((tensor_size, rows, width), bf16),
        "gather_tokens",
    ).reshape(tensor_size * rows, width)

    pad = ((0, 0), (0, LANES - heads))
    a_row = jnp.pad(a_log[None, :], pad)
    bias_row = jnp.pad(dt_bias[None, :], pad)
    skip_row = jnp.repeat(d_skip, HEAD_DIM)[None, :]
    one_row = lambda j, *_: (0, 0)
    by_session = lambda j, *_: (j, 0)
    x_op = (tokens, (MAXLEN, width), by_session)
    b_op = (proj, (MAXLEN, STATE), lambda j, place, *_: (j, place[2]))
    c_op = (proj, (MAXLEN, STATE), lambda j, place, *_: (j, GROUPS + place[2]))
    steps_op = (proj, (MAXLEN, HEADS), lambda j, *_: (j, 2 * GROUPS))
    a_op = (a_row, (1, LANES), one_row)
    bias_op = (bias_row, (1, LANES), one_row)
    skip_op = (skip_row, (1, width), one_row)
    scalars = (place, sessions, lengths)
    sizes = dict(heads=heads, slot_count=slot_count)
    piece_block = (req_size, 1, per, STATE)
    by_slot = lambda j, *_: (0, j, 0, 0)
    total_rows = tensor_size * rows

    delta, kept = session_call(
        functools.partial(delta_kernel, **sizes),
        scalars,
        slot_count,
        [x_op, b_op, steps_op, a_op, bias_op],
        [
            (shape((req_size, slot_count, per, STATE), bf16), piece_block, by_slot),
            (shape((slot_count, 8, LANES), f32), (1, 8, LANES), lambda j, *_: (j, 0, 0)),
        ],
        4_000_000_000,
        "delta_states",
    )
    kept = lax.all_gather(kept[:, 0, :heads], "req", axis=0, tiled=True).reshape(-1)

    outgoing = pl.pallas_call(
        outgoing_kernel,
        in_specs=[smem, smem, smem, vmem, vmem],
        out_specs=vmem,
        out_shape=shape((req_size, 2 * slot_count, per, STATE), bf16),
        compiler_params=params,
        name="starts_and_deltas",
    )(sessions, owners, cache_slots, held, delta)
    arrived = lax.all_to_all(outgoing, "req", split_axis=0, concat_axis=0)

    local, grown = session_call(
        functools.partial(local_kernel, **sizes),
        scalars,
        slot_count,
        [x_op, b_op, c_op, steps_op, a_op, bias_op, skip_op],
        [
            (shape((total_rows, width), f32), (MAXLEN, width), by_session),
            (shape((total_rows, LANES), f32), (MAXLEN, LANES), by_session),
        ],
        10_000_000_000,
        "local_part",
    )

    closing = pl.pallas_call(
        functools.partial(closing_kernel, heads=heads),
        in_specs=[smem] * 5 + [vmem] * 2,
        out_specs=vmem,
        out_shape=shape(held.shape, bf16),
        compiler_params=params,
        name="closing_states",
    )(place, sessions, owners, cache_slots, kept, held, arrived)
    closing, arrived = lax.optimization_barrier((closing, arrived))
    back = lax.all_to_all(
        closing.reshape(req_size, slot_count, per, STATE), "req", split_axis=0, concat_axis=0
    )
    new_cache = back.transpose(1, 0, 2, 3).reshape(state_cache.shape)

    (mixed,) = session_call(
        functools.partial(carry_kernel, heads=heads),
        (place,),
        slot_count,
        [
            c_op,
            (arrived, piece_block, by_slot),
            (local, (MAXLEN, width), by_session),
            (grown, (MAXLEN, LANES), by_session),
        ],
        [(shape((total_rows, width), bf16), (MAXLEN, width), by_session)],
        3_000_000_000,
        "carried_part",
    )
    sent = local_call(
        split_kernel,
        place,
        (mixed.reshape(tensor_size, rows, width),),
        [shape((GROUPS, rows, width), bf16)] * side,
        "split_rows",
    )
    sent = local_call(
        turn_out_kernel,
        place,
        send_along(sent, side, False),
        [shape((rows, side * width), bf16)] * GROUPS,
        "turn_out",
    )
    y_out = local_call(
        columns_kernel,
        place,
        send_along(sent, side, True),
        shape(x_in.shape, bf16),
        "join_columns",
    )
    return y_out, new_cache


def solution(mesh):
    tokens = P(("req", "tensor"), None)
    states = P("req", "tensor", None, None)
    placed = (tokens,) * 4 + (P("tensor"),) * 3 + (states,) + (P(),) * 4
    return jax.shard_map(
        per_device,
        mesh=mesh,
        in_specs=placed,
        out_specs=(tokens, states),
        check_vma=False,
    )
```

time: 291 us -> 296 us (1.017)
  starting transfers between devices: 135 us -> 81.7 us
  blocking collectives: 61.7 us -> 96.6 us
  between operations: 1.32 us -> 14.4 us
  Pallas kernels: 19.3 us -> 31.3 us
  local copies, waits for them, and re-layouts: 20.6 us -> 13.3 us
  waiting for transfers between devices: 47.3 us -> 52.5 us
    all_gather x0 -> x1, blocking collectives: none -> 96.6 us  [per_device(): lax.all_gather(kept[:, 0, :heads], 'req', axis=0, tiled=True).reshape(-1)]
    ppermute x30 -> x12, starting transfers between devices: 109 us -> 41.8 us  [send_along(): moved.append(lax.ppermute(arrays[shift], 'tensor', pairs))]
    all_to_all x1 -> x0, blocking collectives: 61.7 us -> none  [per_device(): back = lax.all_to_all(closing, 'req', split_axis=0, concat_axis=0)]
    all_to_all x1, waiting for transfers between devices: 44.5 us -> 0.01 us  [per_device(): lax.all_to_all(pieces, 'req', split_axis=1, concat_axis=0, tiled=False)]
    ppermute x30 -> x12, waiting for transfers between devices: 2.88 us -> 45.7 us  [send_along(): moved.append(lax.ppermute(arrays[shift], 'tensor', pairs))]
    all_to_all x2, starting transfers between devices: 8.41 us -> 23 us  [the longest x1 12.8 us: per_device(): arrived = lax.all_to_all(outgoing, 'req', split_axis=0, concat_axis=0)]
    unnamed x71 -> x43, local copies, waits for them, and re-layouts: 17.2 us -> 7.6 us
    pallas_call x3 -> x5, Pallas kernels: 15.5 us -> 25.1 us  [the longest x3 20.2 us: session_call(): pl.pallas_call(kernel, grid_spec=pltpu.PrefetchScalarGridSpec(num_scalar_...]
  transfers between devices with their start and end apart: 33 -> 16, of which waited for: 3 -> 12; matrix products, arithmetic and copies ran while one was open for 0% -> 2% of each run, Pallas kernels for 1% -> 9%
where the time goes in v3:
time: 296 us; the launch traced here: 292 us
  blocking collectives  96.6 us (33%)
  starting transfers between devices  81.7 us (28%)
  waiting for transfers between devices  52.5 us (18%)
  Pallas kernels  31.3 us (11%)
  between operations  14.4 us (5%)
  local copies, waits for them, and re-layouts  13.3 us (4%)
    all_gather x1, blocking collectives, per_device(): lax.all_gather(kept[:, 0, :heads], 'req', axis=0, tiled=True).reshape(-1)  96.6 us
    ppermute x12, waiting for transfers between devices, send_along(): moved.append(lax.ppermute(arrays[shift], 'tensor', pairs))  45.7 us
    ppermute x12, starting transfers between devices, send_along(): moved.append(lax.ppermute(arrays[shift], 'tensor', pairs))  41.8 us
    pallas_call x3, Pallas kernels, session_call(): pl.pallas_call(kernel, grid_spec=pltpu.PrefetchScalarGridSpec(num_scalar_...  20.2 us
    all_to_all x1, starting transfers between devices, per_device(): lax.all_to_all(pieces, 'req', split_axis=1, concat_axis=0, tiled=False)  16.9 us
    all_to_all x1, starting transfers between devices, per_device(): arrived = lax.all_to_all(outgoing, 'req', split_axis=0, concat_axis=0)  12.8 us
    all_to_all x1, starting transfers between devices, per_device(): lax.all_to_all(closing.reshape(req_size, slot_count, per, STATE), 'req',...  10.2 us
    unnamed x43, local copies, waits for them, and re-layouts  7.6 us
  transfers between devices with their start and end apart: 16, of which 12 were waited for; matrix products, arithmetic and copies ran while one was open for 2% of the time, Pallas kernels for 9%

profile of v3, /device:TPU:1, one launch (start us, length us, event | category | flops | bytes accessed | tf_op | source)
XLA Modules:
  0.0 292.2 jit_solution(13301566906664981969)
XLA Ops:
  13.4 16.9 %all-to-all-start = ((bf16[1,6,32,16,128]{4,3,1,0,2:T(8,128)(2,1)}), bf16[1,6,32,16,128]{4,3,1,0,2:T(8,128)(2,1)S(1)}, u32[]{:S(2)}, u32[]{:S(2)}) async-start(bf16[1,6,32,16,128]{4,3,1,0,2:T(8,128)(2,1)} %copy.22), calls=%async_computation | async-start | bytes 1572864 | tf_op jit(solution)/shard_map/all_to_all | solution.py:317
  30.3 3.2 %collective-permute-start = (bf16[72,2048]{1,0:T(8,128)(2,1)S(1)}, bf16[72,2048]{1,0:T(8,128)(2,1)S(1)}, u32[]{:S(2)}, u32[]{:S(2)}) collective-permute-start(bf16[72,2048]{1,0:T(8,128)(2,1)S(1)} %get-tuple-element.27), channel_id=1, source_target_pairs={{0,4},{1,5},{2,6},{3,7},{4,8},{5,9},{6,10},{7,11},{8,12},{9,13},{1... | collective-permute-start | bytes 884744 | tf_op jit(solution)/shard_map/ppermute | solution.py:105
  33.5 4.5 %collective-permute-start.1 = (bf16[72,2048]{1,0:T(8,128)(2,1)S(1)}, bf16[72,2048]{1,0:T(8,128)(2,1)S(1)}, u32[]{:S(2)}, u32[]{:S(2)}) collective-permute-start(bf16[72,2048]{1,0:T(8,128)(2,1)S(1)} %get-tuple-element.28), channel_id=1, source_target_pairs={{0,8},{1,9},{2,10},{3,11},{4,12},{5,13},{6,14},{7,15},{8,0},{9,1},... | collective-permute-start | bytes 884744 | tf_op jit(solution)/shard_map/ppermute | solution.py:105
  38.1 3.0 %collective-permute-start.2 = (bf16[72,2048]{1,0:T(8,128)(2,1)S(1)}, bf16[72,2048]{1,0:T(8,128)(2,1)S(1)}, u32[]{:S(2)}, u32[]{:S(2)}) collective-permute-start(bf16[72,2048]{1,0:T(8,128)(2,1)S(1)} %get-tuple-element.29), channel_id=1, source_target_pairs={{0,12},{1,13},{2,14},{3,15},{4,0},{5,1},{6,2},{7,3},{8,4},{9,5},{1... | collective-permute-start | bytes 884744 | tf_op jit(solution)/shard_map/ppermute | solution.py:105
  41.1 1.8 collective-permute-done.refs_1_
  42.8 9.2 %collective-permute-done.1.refs_2_ = bf16[72,2048]{1,0:T(8,128)(2,1)S(1)} collective-permute-done((bf16[72,2048]{1,0:T(8,128)(2,1)S(1)}, bf16[72,2048]{1,0:T(8,128)(2,1)S(1)}, u32[]{:S(2)}, u32[]{:S(2)}) %collective-permute-start.1) | collective-permute-done | bytes 294944 | tf_op jit(solution)/shard_map/ppermute | solution.py:105
  55.0 3.1 %collective-permute-start.3 = (bf16[4,72,512]{2,1,0:T(8,128)(2,1)}, bf16[4,72,512]{2,1,0:T(8,128)(2,1)S(1)}, u32[]{:S(2)}, u32[]{:S(2)}) collective-permute-start(bf16[4,72,512]{2,1,0:T(8,128)(2,1)} %get-tuple-element.31), channel_id=1, source_target_pairs={{0,1},{1,2},{2,3},{3,0},{4,5},{5,6},{6,7},{7,4},{8,9},{9,10},{10,1... | collective-permute-start | bytes 884744 | tf_op jit(solution)/shard_map/ppermute | solution.py:105
  58.1 4.3 %collective-permute-start.4 = (bf16[4,72,512]{2,1,0:T(8,128)(2,1)}, bf16[4,72,512]{2,1,0:T(8,128)(2,1)S(1)}, u32[]{:S(2)}, u32[]{:S(2)}) collective-permute-start(bf16[4,72,512]{2,1,0:T(8,128)(2,1)} %get-tuple-element.32), channel_id=1, source_target_pairs={{0,2},{1,3},{2,0},{3,1},{4,6},{5,7},{6,4},{7,5},{8,10},{9,11},{10,... | collective-permute-start | bytes 884744 | tf_op jit(solution)/shard_map/ppermute | solution.py:105
  62.4 3.1 %collective-permute-start.5 = (bf16[4,72,512]{2,1,0:T(8,128)(2,1)S(1)}, bf16[4,72,512]{2,1,0:T(8,128)(2,1)S(1)}, u32[]{:S(2)}, u32[]{:S(2)}) collective-permute-start(bf16[4,72,512]{2,1,0:T(8,128)(2,1)S(1)} %get-tuple-element.33), channel_id=1, source_target_pairs={{0,3},{1,0},{2,1},{3,2},{4,7},{5,4},{6,5},{7,6},{8,11},{9,8},{10,9... | collective-permute-start | bytes 884744 | tf_op jit(solution)/shard_map/ppermute | solution.py:105
  66.2 8.7 %collective-permute-done.4.refs_2_ = bf16[4,72,512]{2,1,0:T(8,128)(2,1)S(1)} collective-permute-done((bf16[4,72,512]{2,1,0:T(8,128)(2,1)}, bf16[4,72,512]{2,1,0:T(8,128)(2,1)S(1)}, u32[]{:S(2)}, u32[]{:S(2)}) %collective-permute-start.4) | collective-permute-done | bytes 294944 | tf_op jit(solution)/shard_map/ppermute | solution.py:105
  74.9 5.6 %collective-permute-done.5.refs_3_ = bf16[4,72,512]{2,1,0:T(8,128)(2,1)S(1)} collective-permute-done((bf16[4,72,512]{2,1,0:T(8,128)(2,1)S(1)}, bf16[4,72,512]{2,1,0:T(8,128)(2,1)S(1)}, u32[]{:S(2)}, u32[]{:S(2)}) %collective-permute-start.5) | collective-permute-done | bytes 294944 | tf_op jit(solution)/shard_map/ppermute | solution.py:105
  81.2 6.8 %all-gather.3.cloned.1.call-done.b_ref.steps_ref.c_ref = bf16[1152,1152]{1,0:T(8,128)(2,1)} async-done(((bf16[72,1152]{1,0:T(8,128)(2,1)}), bf16[1152,1152]{1,0:T(8,128)(2,1)}) %all-gather.3.cloned.1.call-update) | async-done | bytes 2654224 | tf_op jit(solution)/shard_map/all_gather | solution.py:328
  87.9 1.7 copy-done.9
  89.7 7.6 %delta_states.1 = (bf16[32,6,16,128]{3,2,1,0:T(8,128)(2,1)S(1)}, f32[6,8,128]{2,1,0:T(8,128)S(1)}) custom-call(s32[4]{0:T(128)S(1)} %pad_add_fusion.place_ref, s32[192]{0:T(256)S(1)} %reshape.23.sessions_ref, s32[192]{0:T(256)S(1)} %copy-done.10, bf16[1152,512]{1,0:T(8,128)(2,1)S(1)} %bitcast.19, bf16[1152,1152]{1,0:T(8,128)(2,1)S(1)} %copy-done.9, ...), custom_call_target="tpu_custom_call" | custom-call | flops 4000000000 | bytes 8388608 | tf_op jit(solution)/shard_map/delta_states/pallas_call | solution.py:265
  98.0 2.3 starts_and_deltas.1
  100.3 12.8 %all-to-all-start.1 = ((bf16[32,12,16,128]{3,2,1,0:T(8,128)(2,1)}), bf16[32,12,16,128]{3,2,1,0:T(8,128)(2,1)S(1)}, u32[]{:S(2)}, u32[]{:S(2)}) async-start(bf16[32,12,16,128]{3,2,1,0:T(8,128)(2,1)} %starts_and_deltas.1), calls=%async_computation.1 | async-start | bytes 3145728 | tf_op jit(solution)/shard_map/all_to_all | solution.py:385
  113.9 96.6 %all-gather = f32[192,1,8]{2,1,0:T(1,128)} all-gather(f32[6,1,8]{2,1,0:T(1,128)S(1)} %slice.3), channel_id=2, replica_groups=mesh['req'=32,'tensor'=16] {'req'}, dimensions={0}, use_global_device_ids=true | all-gather | bytes 6336 | tf_op jit(solution)/shard_map/all_gather | solution.py:375
  211.0 2.4 reduce.3
  215.8 2.5 closing_states.1
  218.3 10.2 %all-to-all-start.2 = ((bf16[32,6,16,128]{3,2,1,0:T(8,128)(2,1)}), bf16[32,6,16,128]{3,2,1,0:T(8,128)(2,1)}, u32[]{:S(2)}, u32[]{:S(2)}) async-start(bf16[32,6,16,128]{3,2,1,0:T(8,128)(2,1)} %bitcast.14), calls=%async_computation.2 | async-start | bytes 1572864 | tf_op jit(solution)/shard_map/all_to_all | solution.py:409
  228.7 8.4 %local_part.1 = (f32[1152,512]{1,0:T(8,128)S(1)}, f32[1152,128]{1,0:T(8,128)S(1)}) custom-call(s32[4]{0:T(128)S(1)} %pad_add_fusion.place_ref, s32[192]{0:T(256)S(1)} %reshape.23.sessions_ref, s32[192]{0:T(256)S(1)} %copy-done.11, bf16[1152,512]{1,0:T(8,128)(2,1)S(1)} %bitcast.20, bf16[1152,1152]{1,0:T(8,128)(2,1)} %all-gather.3.cloned.1.call-done.b_ref.steps_ref.c_ref, ...), custom_call_target="tpu_custom_call" | custom-call | flops 10000000000 | bytes 8388608 | tf_op jit(solution)/shard_map/local_part/pallas_call | solution.py:265
  237.0 4.3 %carried_part.1 = bf16[1152,512]{1,0:T(8,128)(2,1)S(1)} custom-call(s32[4]{0:T(128)S(1)} %pad_add_fusion.place_ref, bf16[1152,1152]{1,0:T(8,128)(2,1)} %all-gather.3.cloned.1.call-done.b_ref.steps_ref.c_ref, bf16[32,12,16,128]{3,2,1,0:T(8,128)(2,1)S(1)} %all-to-all-done.1.arrived_ref.start_ref, f32[1152,512]{1,0:T(8,128)S(1)} %get-tuple-element.37.local_ref, ...), custom_call_target="tpu_custom_call" | custom-call | flops 3000000000 | bytes 8388608 | tf_op jit(solution)/shard_map/carried_part/pallas_call | solution.py:265
  241.9 3.8 %collective-permute-start.6 = (bf16[4,72,512]{2,1,0:T(8,128)(2,1)S(1)}, bf16[4,72,512]{2,1,0:T(8,128)(2,1)S(1)}, u32[]{:S(2)}, u32[]{:S(2)}) collective-permute-start(bf16[4,72,512]{2,1,0:T(8,128)(2,1)S(1)} %get-tuple-element.40), channel_id=1, source_target_pairs={{0,1},{1,2},{2,3},{3,0},{4,5},{5,6},{6,7},{7,4},{8,9},{9,10},{10,1... | collective-permute-start | bytes 884744 | tf_op jit(solution)/shard_map/ppermute | solution.py:105
  245.7 3.4 %collective-permute-start.7 = (bf16[4,72,512]{2,1,0:T(8,128)(2,1)S(1)}, bf16[4,72,512]{2,1,0:T(8,128)(2,1)S(1)}, u32[]{:S(2)}, u32[]{:S(2)}) collective-permute-start(bf16[4,72,512]{2,1,0:T(8,128)(2,1)S(1)} %get-tuple-element.41), channel_id=1, source_target_pairs={{0,2},{1,3},{2,0},{3,1},{4,6},{5,7},{6,4},{7,5},{8,10},{9,11},{10,... | collective-permute-start | bytes 884744 | tf_op jit(solution)/shard_map/ppermute | solution.py:105
  249.1 2.9 collective-permute-start.8
  253.5 7.0 %collective-permute-done.7.refs_2_ = bf16[4,72,512]{2,1,0:T(8,128)(2,1)S(1)} collective-permute-done((bf16[4,72,512]{2,1,0:T(8,128)(2,1)S(1)}, bf16[4,72,512]{2,1,0:T(8,128)(2,1)S(1)}, u32[]{:S(2)}, u32[]{:S(2)}) %collective-permute-start.7) | collective-permute-done | bytes 294944 | tf_op jit(solution)/shard_map/ppermute | solution.py:105
  262.6 4.2 %collective-permute-start.9 = (bf16[72,2048]{1,0:T(8,128)(2,1)S(1)}, bf16[72,2048]{1,0:T(8,128)(2,1)S(1)}, u32[]{:S(2)}, u32[]{:S(2)}) collective-permute-start(bf16[72,2048]{1,0:T(8,128)(2,1)S(1)} %get-tuple-element.44), channel_id=1, source_target_pairs={{0,4},{1,5},{2,6},{3,7},{4,8},{5,9},{6,10},{7,11},{8,12},{9,13},{1... | collective-permute-start | bytes 884744 | tf_op jit(solution)/shard_map/ppermute | solution.py:105
  266.8 3.5 %collective-permute-start.10 = (bf16[72,2048]{1,0:T(8,128)(2,1)S(1)}, bf16[72,2048]{1,0:T(8,128)(2,1)S(1)}, u32[]{:S(2)}, u32[]{:S(2)}) collective-permute-start(bf16[72,2048]{1,0:T(8,128)(2,1)S(1)} %get-tuple-element.45), channel_id=1, source_target_pairs={{0,8},{1,9},{2,10},{3,11},{4,12},{5,13},{6,14},{7,15},{8,0},{9,1},... | collective-permute-start | bytes 884744 | tf_op jit(solution)/shard_map/ppermute | solution.py:105
  270.4 2.8 collective-permute-start.11
  273.2 7.2 %collective-permute-done.10.refs_2_ = bf16[72,2048]{1,0:T(8,128)(2,1)S(1)} collective-permute-done((bf16[72,2048]{1,0:T(8,128)(2,1)S(1)}, bf16[72,2048]{1,0:T(8,128)(2,1)S(1)}, u32[]{:S(2)}, u32[]{:S(2)}) %collective-permute-start.10) | collective-permute-done | bytes 294944 | tf_op jit(solution)/shard_map/ppermute | solution.py:105
  281.6 1.6 join_columns.1
  283.2 2.1 copy.23
  (68 shorter events, 20.4 us)
Async XLA Ops:
  7.2 80.8 %all-gather.3.cloned.1.call-start = ((), (), s32[]{:S(2)}) async-start(), calls=%async_computation.3 | async-start | bytes 2820096 | tf_op jit(solution)/shard_map/all_gather | solution.py:328
  7.3 1.3 copy-start
  8.6 0.9 copy-start.1
  11.1 1.3 copy-start.16
  13.4 52.1 %copy-start.19 = (f32[8]{0:T(128)S(1)}, f32[8]{0:T(128)}, u32[]{:S(2)}) copy-start(f32[8]{0:T(128)} %param.16) | copy-start | bytes 100
  13.4 52.1 %copy-start.20 = (f32[8]{0:T(128)S(1)}, f32[8]{0:T(128)}, u32[]{:S(2)}) copy-start(f32[8]{0:T(128)} %param.17) | copy-start | bytes 100
  13.4 52.1 %copy-start.17 = (s32[32,6]{0,1:T(8,128)S(1)}, s32[32,6]{0,1:T(8,128)}, u32[]{:S(2)}) copy-start(s32[32,6]{0,1:T(8,128)} %param.20) | copy-start | bytes 2308
  13.4 84.5 %all-to-all-start = ((bf16[1,6,32,16,128]{4,3,1,0,2:T(8,128)(2,1)}), bf16[1,6,32,16,128]{4,3,1,0,2:T(8,128)(2,1)S(1)}, u32[]{:S(2)}, u32[]{:S(2)}) async-start(bf16[1,6,32,16,128]{4,3,1,0,2:T(8,128)(2,1)} %copy.22), calls=%async_computation | async-start | bytes 1572864 | tf_op jit(solution)/shard_map/all_to_all | solution.py:317
  30.3 12.5 %collective-permute-start = (bf16[72,2048]{1,0:T(8,128)(2,1)S(1)}, bf16[72,2048]{1,0:T(8,128)(2,1)S(1)}, u32[]{:S(2)}, u32[]{:S(2)}) collective-permute-start(bf16[72,2048]{1,0:T(8,128)(2,1)S(1)} %get-tuple-element.27), channel_id=1, source_target_pairs={{0,4},{1,5},{2,6},{3,7},{4,8},{5,9},{6,10},{7,11},{8,12},{9,13},{1... | collective-permute-start | bytes 884744 | tf_op jit(solution)/shard_map/ppermute | solution.py:105
  33.5 18.5 %collective-permute-start.1 = (bf16[72,2048]{1,0:T(8,128)(2,1)S(1)}, bf16[72,2048]{1,0:T(8,128)(2,1)S(1)}, u32[]{:S(2)}, u32[]{:S(2)}) collective-permute-start(bf16[72,2048]{1,0:T(8,128)(2,1)S(1)} %get-tuple-element.28), channel_id=1, source_target_pairs={{0,8},{1,9},{2,10},{3,11},{4,12},{5,13},{6,14},{7,15},{8,0},{9,1},... | collective-permute-start | bytes 884744 | tf_op jit(solution)/shard_map/ppermute | solution.py:105
  38.1 15.5 %collective-permute-start.2 = (bf16[72,2048]{1,0:T(8,128)(2,1)S(1)}, bf16[72,2048]{1,0:T(8,128)(2,1)S(1)}, u32[]{:S(2)}, u32[]{:S(2)}) collective-permute-start(bf16[72,2048]{1,0:T(8,128)(2,1)S(1)} %get-tuple-element.29), channel_id=1, source_target_pairs={{0,12},{1,13},{2,14},{3,15},{4,0},{5,1},{6,2},{7,3},{8,4},{9,5},{1... | collective-permute-start | bytes 884744 | tf_op jit(solution)/shard_map/ppermute | solution.py:105
  53.6 34.4 %copy-start.10 = (s32[192]{0:T(256)S(1)}, s32[192]{0:T(256)}, u32[]{:S(2)}) copy-start(s32[192]{0:T(256)} %lengths_ref.3) | copy-start | bytes 2308
  55.0 11.2 %collective-permute-start.3 = (bf16[4,72,512]{2,1,0:T(8,128)(2,1)}, bf16[4,72,512]{2,1,0:T(8,128)(2,1)S(1)}, u32[]{:S(2)}, u32[]{:S(2)}) collective-permute-start(bf16[4,72,512]{2,1,0:T(8,128)(2,1)} %get-tuple-element.31), channel_id=1, source_target_pairs={{0,1},{1,2},{2,3},{3,0},{4,5},{5,6},{6,7},{7,4},{8,9},{9,10},{10,1... | collective-permute-start | bytes 884744 | tf_op jit(solution)/shard_map/ppermute | solution.py:105
  58.1 16.8 %collective-permute-start.4 = (bf16[4,72,512]{2,1,0:T(8,128)(2,1)}, bf16[4,72,512]{2,1,0:T(8,128)(2,1)S(1)}, u32[]{:S(2)}, u32[]{:S(2)}) collective-permute-start(bf16[4,72,512]{2,1,0:T(8,128)(2,1)} %get-tuple-element.32), channel_id=1, source_target_pairs={{0,2},{1,3},{2,0},{3,1},{4,6},{5,7},{6,4},{7,5},{8,10},{9,11},{10,... | collective-permute-start | bytes 884744 | tf_op jit(solution)/shard_map/ppermute | solution.py:105
  62.4 18.1 %collective-permute-start.5 = (bf16[4,72,512]{2,1,0:T(8,128)(2,1)S(1)}, bf16[4,72,512]{2,1,0:T(8,128)(2,1)S(1)}, u32[]{:S(2)}, u32[]{:S(2)}) collective-permute-start(bf16[4,72,512]{2,1,0:T(8,128)(2,1)S(1)} %get-tuple-element.33), channel_id=1, source_target_pairs={{0,3},{1,0},{2,1},{3,2},{4,7},{5,4},{6,5},{7,6},{8,11},{9,8},{10,9... | collective-permute-start | bytes 884744 | tf_op jit(solution)/shard_map/ppermute | solution.py:105
  65.5 31.8 %copy-start.12 = (f32[1,128]{1,0:T(1,128)}, f32[1,128]{1,0:T(1,128)S(1)}, u32[]{:S(2)}) copy-start(f32[1,128]{1,0:T(1,128)S(1)} %pad.7.a_log_ref) | copy-start | bytes 1540
  65.6 31.7 %copy-start.14 = (f32[1,128]{1,0:T(1,128)}, f32[1,128]{1,0:T(1,128)S(1)}, u32[]{:S(2)}) copy-start(f32[1,128]{1,0:T(1,128)S(1)} %pad.8.bias_ref) | copy-start | bytes 1540
  87.9 1.8 copy-start.9
  89.7 8.3 %copy-start.4 = (s32[192]{0:T(256)S(1)}, s32[192]{0:T(256)}, u32[]{:S(2)}) copy-start(s32[192]{0:T(256)} %owners_ref.3) | copy-start | bytes 2308
  89.7 8.3 %copy-start.6 = (s32[192]{0:T(256)S(1)}, s32[192]{0:T(256)}, u32[]{:S(2)}) copy-start(s32[192]{0:T(256)} %slots_ref.3) | copy-start | bytes 2308
  100.3 114.1 %all-to-all-start.1 = ((bf16[32,12,16,128]{3,2,1,0:T(8,128)(2,1)}), bf16[32,12,16,128]{3,2,1,0:T(8,128)(2,1)S(1)}, u32[]{:S(2)}, u32[]{:S(2)}) async-start(bf16[32,12,16,128]{3,2,1,0:T(8,128)(2,1)} %starts_and_deltas.1), calls=%async_computation.1 | async-start | bytes 3145728 | tf_op jit(solution)/shard_map/all_to_all | solution.py:385
  218.3 10.2 %copy-start.18 = (f32[8]{0:T(128)S(1)}, f32[8]{0:T(128)}, u32[]{:S(2)}) copy-start(f32[8]{0:T(128)} %param.18) | copy-start | bytes 100
  218.3 10.4 %copy-start.11 = (s32[192]{0:T(256)S(1)}, s32[192]{0:T(256)}, u32[]{:S(2)}) copy-start(s32[192]{0:T(256)} %lengths_ref.3) | copy-start | bytes 2308
  218.3 10.4 %copy-start.13 = (f32[1,128]{1,0:T(1,128)S(1)}, f32[1,128]{1,0:T(1,128)}, u32[]{:S(2)}) copy-start(f32[1,128]{1,0:T(1,128)} %copy-done.12) | copy-start | bytes 1540
  218.3 10.4 %copy-start.15 = (f32[1,128]{1,0:T(1,128)S(1)}, f32[1,128]{1,0:T(1,128)}, u32[]{:S(2)}) copy-start(f32[1,128]{1,0:T(1,128)} %copy-done.14) | copy-start | bytes 1540
  218.3 65.0 %all-to-all-start.2 = ((bf16[32,6,16,128]{3,2,1,0:T(8,128)(2,1)}), bf16[32,6,16,128]{3,2,1,0:T(8,128)(2,1)}, u32[]{:S(2)}, u32[]{:S(2)}) async-start(bf16[32,6,16,128]{3,2,1,0:T(8,128)(2,1)} %bitcast.14), calls=%async_computation.2 | async-start | bytes 1572864 | tf_op jit(solution)/shard_map/all_to_all | solution.py:409
  241.9 11.5 %collective-permute-start.6 = (bf16[4,72,512]{2,1,0:T(8,128)(2,1)S(1)}, bf16[4,72,512]{2,1,0:T(8,128)(2,1)S(1)}, u32[]{:S(2)}, u32[]{:S(2)}) collective-permute-start(bf16[4,72,512]{2,1,0:T(8,128)(2,1)S(1)} %get-tuple-element.40), channel_id=1, source_target_pairs={{0,1},{1,2},{2,3},{3,0},{4,5},{5,6},{6,7},{7,4},{8,9},{9,10},{10,1... | collective-permute-start | bytes 884744 | tf_op jit(solution)/shard_map/ppermute | solution.py:105
  245.7 14.7 %collective-permute-start.7 = (bf16[4,72,512]{2,1,0:T(8,128)(2,1)S(1)}, bf16[4,72,512]{2,1,0:T(8,128)(2,1)S(1)}, u32[]{:S(2)}, u32[]{:S(2)}) collective-permute-start(bf16[4,72,512]{2,1,0:T(8,128)(2,1)S(1)} %get-tuple-element.41), channel_id=1, source_target_pairs={{0,2},{1,3},{2,0},{3,1},{4,6},{5,7},{6,4},{7,5},{8,10},{9,11},{10,... | collective-permute-start | bytes 884744 | tf_op jit(solution)/shard_map/ppermute | solution.py:105
  249.1 12.9 %collective-permute-start.8 = (bf16[4,72,512]{2,1,0:T(8,128)(2,1)S(1)}, bf16[4,72,512]{2,1,0:T(8,128)(2,1)S(1)}, u32[]{:S(2)}, u32[]{:S(2)}) collective-permute-start(bf16[4,72,512]{2,1,0:T(8,128)(2,1)S(1)} %get-tuple-element.42), channel_id=1, source_target_pairs={{0,3},{1,0},{2,1},{3,2},{4,7},{5,4},{6,5},{7,6},{8,11},{9,8},{10,9... | collective-permute-start | bytes 884744 | tf_op jit(solution)/shard_map/ppermute | solution.py:105
  262.6 10.6 %collective-permute-start.9 = (bf16[72,2048]{1,0:T(8,128)(2,1)S(1)}, bf16[72,2048]{1,0:T(8,128)(2,1)S(1)}, u32[]{:S(2)}, u32[]{:S(2)}) collective-permute-start(bf16[72,2048]{1,0:T(8,128)(2,1)S(1)} %get-tuple-element.44), channel_id=1, source_target_pairs={{0,4},{1,5},{2,6},{3,7},{4,8},{5,9},{6,10},{7,11},{8,12},{9,13},{1... | collective-permute-start | bytes 884744 | tf_op jit(solution)/shard_map/ppermute | solution.py:105
  266.8 13.6 %collective-permute-start.10 = (bf16[72,2048]{1,0:T(8,128)(2,1)S(1)}, bf16[72,2048]{1,0:T(8,128)(2,1)S(1)}, u32[]{:S(2)}, u32[]{:S(2)}) collective-permute-start(bf16[72,2048]{1,0:T(8,128)(2,1)S(1)} %get-tuple-element.45), channel_id=1, source_target_pairs={{0,8},{1,9},{2,10},{3,11},{4,12},{5,13},{6,14},{7,15},{8,0},{9,1},... | collective-permute-start | bytes 884744 | tf_op jit(solution)/shard_map/ppermute | solution.py:105
  270.4 11.3 %collective-permute-start.11 = (bf16[72,2048]{1,0:T(8,128)(2,1)S(1)}, bf16[72,2048]{1,0:T(8,128)(2,1)S(1)}, u32[]{:S(2)}, u32[]{:S(2)}) collective-permute-start(bf16[72,2048]{1,0:T(8,128)(2,1)S(1)} %get-tuple-element.46), channel_id=1, source_target_pairs={{0,12},{1,13},{2,14},{3,15},{4,0},{5,1},{6,2},{7,3},{8,4},{9,5},{1... | collective-permute-start | bytes 884744 | tf_op jit(solution)/shard_map/ppermute | solution.py:105
  (5 other events, 3.6 us)
Sparse Core Ops, SparseCore 0:
  12.5 75.3 all-gather.2

commit v4 on v3

--- a/solution.py
+++ b/solution.py
@@ -111,39 +111,29 @@
     return owners_ref[session] * slot_count + slots_ref[session]
 
 
-def outgoing_kernel(sessions_ref, owners_ref, slots_ref, state_ref, delta_ref, out_ref):
-    slot_count = delta_ref.shape[1]
-
-    def step(group, carry):
-        for slot in range(slot_count):
-            row = cache_row(
-                sessions_ref, owners_ref, slots_ref, slot_count, group * slot_count + slot
-            )
-            out_ref[group, slot] = state_ref[row]
-            out_ref[group, slot_count + slot] = delta_ref[group, slot]
+def order_kernel(sessions_ref, owners_ref, slots_ref, in_ref, out_ref, *, slot_count, to_owner):
+    def step(index, carry):
+        row = cache_row(sessions_ref, owners_ref, slots_ref, slot_count, index)
+        if to_owner:
+            out_ref[row] = in_ref[index]
+        else:
+            out_ref[index] = in_ref[row]
         return carry
 
-    lax.fori_loop(0, delta_ref.shape[0], step, 0)
-
-
-def closing_kernel(
-    place_ref, sessions_ref, owners_ref, slots_ref, kept_ref, state_ref, arrived_ref, out_ref, *, heads
-):
-    groups, slots_twice, per, _ = arrived_ref.shape
-    slot_count = slots_twice // 2
-    head = place_ref[0] * per // HEAD_DIM
-
-    def step(group, carry):
-        for slot in range(slot_count):
-            index = group * slot_count + slot
-            row = cache_row(sessions_ref, owners_ref, slots_ref, slot_count, index)
-            kept = kept_ref[index * heads + head]
-            added = arrived_ref[group, slot_count + slot].astype(jnp.float32)
-            closing = kept * state_ref[row].astype(jnp.float32) + added
-            out_ref[row] = closing.astype(out_ref.dtype)
-        return carry
-
-    lax.fori_loop(0, groups, step, 0)
+    lax.fori_loop(0, in_ref.shape[0], step, 0, unroll=8)
+
+
+def reorder(pieces, sessions, owners, slots, slot_count, to_owner):
+    smem = pl.BlockSpec(memory_space=pltpu.SMEM)
+    vmem = pl.BlockSpec(memory_space=pltpu.VMEM)
+    return pl.pallas_call(
+        functools.partial(order_kernel, slot_count=slot_count, to_owner=to_owner),
+        in_specs=[smem, smem, smem, vmem],
+        out_specs=vmem,
+        out_shape=jax.ShapeDtypeStruct(pieces.shape, pieces.dtype),
+        compiler_params=pltpu.CompilerParams(vmem_limit_bytes=VMEM_LIMIT),
+        name="to_owner_order" if to_owner else "to_group_order",
+    )(sessions, owners, slots, pieces)
 
 
 def token_steps(place_ref, steps_ref, bias_ref, a_log_ref, length, heads):
@@ -179,36 +169,9 @@
     return lax.broadcasted_iota(jnp.int32, (MAXLEN, LANES), 1) < HEAD_DIM
 
 
-def delta_kernel(
-    place_ref, sessions_ref, lengths_ref, x_ref, b_ref, steps_ref, a_log_ref, bias_ref,
-    delta_ref, kept_ref, *, heads, slot_count
-):
-    length = lengths_ref[sessions_ref[place_ref[0] * slot_count + pl.program_id(0)]]
-    step, cum, _, _ = token_steps(place_ref, steps_ref, bias_ref, a_log_ref, length, heads)
-    last = cum[MAXLEN - 1 : MAXLEN, :]
-    to_end = jnp.exp(last - cum) * step
-    kept_ref[0] = jnp.broadcast_to(jnp.exp(last), kept_ref.shape[1:])
-    left = left_half()
-    in_proj = b_ref[...]
-    per = delta_ref.shape[2]
-    for first in range(0, heads, 2):
-        lanes = slice(first * HEAD_DIM, (first + 2) * HEAD_DIM)
-        scaled = x_ref[:, lanes].astype(jnp.float32) * spread(to_end, first, left)
-        added = lax.dot_general(
-            scaled.astype(jnp.bfloat16),
-            in_proj,
-            (((0,), (0,)), ((), ())),
-            preferred_element_type=jnp.float32,
-        )
-        begin, count = first * HEAD_DIM // per, 2 * HEAD_DIM // per
-        delta_ref[begin : begin + count, 0] = added.astype(jnp.bfloat16).reshape(
-            count, per, STATE
-        )
-
-
-def local_kernel(
+def tokens_kernel(
     place_ref, sessions_ref, lengths_ref, x_ref, b_ref, c_ref, steps_ref, a_log_ref, bias_ref,
-    skip_ref, local_ref, grown_ref, *, heads, slot_count
+    skip_ref, local_ref, grown_ref, delta_ref, kept_ref, *, heads, slot_count
 ):
     f32 = jnp.float32
     bf16 = jnp.bfloat16
@@ -217,17 +180,23 @@
     step, cum, live, causal = token_steps(
         place_ref, steps_ref, bias_ref, a_log_ref, length, heads
     )
+    last = cum[MAXLEN - 1 : MAXLEN, :]
+    to_end = jnp.exp(last - cum) * step
+    kept_ref[0] = jnp.broadcast_to(jnp.exp(last), kept_ref.shape[1:])
     drop_rows = (cum - jnp.log(step)).T
     grown_ref[...] = jnp.where(live, jnp.exp(cum), 0.0)
+    in_proj = b_ref[...]
     affinity = lax.dot_general(
-        c_ref[...], b_ref[...], (((1,), (1,)), ((), ())), preferred_element_type=f32
+        c_ref[...], in_proj, (((1,), (1,)), ((), ())), preferred_element_type=f32
     )
     affinity = jnp.where(causal, affinity, 0.0)
     top, low = affinity[:half, :half], affinity[half:, :]
     left = left_half()
+    per = delta_ref.shape[2]
     for first in range(0, heads, 2):
         lanes = slice(first * HEAD_DIM, (first + 2) * HEAD_DIM)
         pair = x_ref[:, lanes]
+        pair_f32 = pair.astype(f32)
         mixed = []
         for head in (first, first + 1):
             column = cum[:, head : head + 1]
@@ -243,8 +212,24 @@
                     axis=0,
                 )
             )
-        out = jnp.where(left, mixed[0], mixed[1]) + skip_ref[:, lanes] * pair.astype(f32)
+        out = jnp.where(left, mixed[0], mixed[1]) + skip_ref[:, lanes] * pair_f32
         local_ref[:, lanes] = jnp.where(live, out, 0.0)
+        scaled = (pair_f32 * spread(to_end, first, left)).astype(bf16)
+        added = lax.dot_general(
+            scaled, in_proj, (((0,), (0,)), ((), ())), preferred_element_type=f32
+        )
+        begin, count = first * HEAD_DIM // per, 2 * HEAD_DIM // per
+        delta_ref[begin : begin + count, 0] = added.reshape(count, per, STATE)
+
+
+def closing_kernel(start_ref, delta_ref, kept_ref, closing_ref, *, heads):
+    per = start_ref.shape[2]
+    count = HEAD_DIM // per
+    for head in range(heads):
+        rows = slice(head * count, (head + 1) * count)
+        kept = kept_ref[0, :1, head : head + 1].reshape(1, 1, 1)
+        closing = kept * start_ref[rows, 0].astype(jnp.float32) + delta_ref[rows, 0]
+        closing_ref[rows, 0] = closing.astype(jnp.bfloat16)
 
 
 def carry_kernel(place_ref, c_ref, start_ref, local_ref, grown_ref, y_ref, *, heads):
@@ -309,13 +294,11 @@
         [req_index, tensor_index, tensor_index // side, tensor_index % side]
     ).astype(jnp.int32)
     sessions = group_sessions.reshape(-1)
-    smem = pl.BlockSpec(memory_space=pltpu.SMEM)
-    vmem = pl.BlockSpec(memory_space=pltpu.VMEM)
-    params = pltpu.CompilerParams(vmem_limit_bytes=VMEM_LIMIT)
 
     pieces = state_cache.reshape(slot_count, req_size, per, STATE)
     held = lax.all_to_all(pieces, "req", split_axis=1, concat_axis=0, tiled=False)
     held = held.reshape(req_size * slot_count, per, STATE)
+    held = reorder(held, sessions, owners, cache_slots, slot_count, False)
 
     proj, *sent = local_call(
         pack_kernel,
@@ -332,6 +315,10 @@
         send_along(sent, side, True),
         [shape((GROUPS, rows, width), bf16)] * side,
         "turn_in",
+    )
+    held, *sent = lax.optimization_barrier((held, *sent))
+    start = lax.all_to_all(
+        held.reshape(req_size, slot_count, per, STATE), "req", split_axis=0, concat_axis=0
     )
     tokens = local_call(
         gather_kernel,
@@ -360,56 +347,36 @@
     by_slot = lambda j, *_: (0, j, 0, 0)
     total_rows = tensor_size * rows
 
-    delta, kept = session_call(
-        functools.partial(delta_kernel, **sizes),
-        scalars,
-        slot_count,
-        [x_op, b_op, steps_op, a_op, bias_op],
-        [
-            (shape((req_size, slot_count, per, STATE), bf16), piece_block, by_slot),
-            (shape((slot_count, 8, LANES), f32), (1, 8, LANES), lambda j, *_: (j, 0, 0)),
-        ],
-        4_000_000_000,
-        "delta_states",
-    )
-    kept = lax.all_gather(kept[:, 0, :heads], "req", axis=0, tiled=True).reshape(-1)
-
-    outgoing = pl.pallas_call(
-        outgoing_kernel,
-        in_specs=[smem, smem, smem, vmem, vmem],
-        out_specs=vmem,
-        out_shape=shape((req_size, 2 * slot_count, per, STATE), bf16),
-        compiler_params=params,
-        name="starts_and_deltas",
-    )(sessions, owners, cache_slots, held, delta)
-    arrived = lax.all_to_all(outgoing, "req", split_axis=0, concat_axis=0)
-
-    local, grown = session_call(
-        functools.partial(local_kernel, **sizes),
+    state_shape = (req_size, slot_count, per, STATE)
+    kept_block = ((1, 8, LANES), lambda j, *_: (j, 0, 0))
+    local, grown, delta, kept = session_call(
+        functools.partial(tokens_kernel, **sizes),
         scalars,
         slot_count,
         [x_op, b_op, c_op, steps_op, a_op, bias_op, skip_op],
         [
             (shape((total_rows, width), f32), (MAXLEN, width), by_session),
             (shape((total_rows, LANES), f32), (MAXLEN, LANES), by_session),
+            (shape(state_shape, f32), piece_block, by_slot),
+            (shape((slot_count, 8, LANES), f32), *kept_block),
         ],
         10_000_000_000,
-        "local_part",
-    )
-
-    closing = pl.pallas_call(
+        "tokens_part",
+    )
+
+    (closing,) = session_call(
         functools.partial(closing_kernel, heads=heads),
-        in_specs=[smem] * 5 + [vmem] * 2,
-        out_specs=vmem,
-        out_shape=shape(held.shape, bf16),
-        compiler_params=params,
-        name="closing_states",
-    )(place, sessions, owners, cache_slots, kept, held, arrived)
-    closing, arrived = lax.optimization_barrier((closing, arrived))
-    back = lax.all_to_all(
-        closing.reshape(req_size, slot_count, per, STATE), "req", split_axis=0, concat_axis=0
-    )
-    new_cache = back.transpose(1, 0, 2, 3).reshape(state_cache.shape)
+        (),
+        slot_count,
+        [(start, piece_block, by_slot), (delta, piece_block, by_slot), (kept, *kept_block)],
+        [(shape(state_shape, bf16), piece_block, by_slot)],
+        1_000_000_000,
+        "closing_states",
+    )
+    closing, start = lax.optimization_barrier((closing, start))
+    back = lax.all_to_all(closing, "req", split_axis=0, concat_axis=0)
+    back = back.reshape(req_size * slot_count, per, STATE)
+    back = reorder(back, sessions, owners, cache_slots, slot_count, True)
 
     (mixed,) = session_call(
         functools.partial(carry_kernel, heads=heads),
@@ -417,7 +384,7 @@
         slot_count,
         [
             c_op,
-            (arrived, piece_block, by_slot),
+            (start, piece_block, by_slot),
             (local, (MAXLEN, width), by_session),
             (grown, (MAXLEN, LANES), by_session),
         ],
@@ -439,6 +406,11 @@
         [shape((rows, side * width), bf16)] * GROUPS,
         "turn_out",
     )
+    back, *sent = lax.optimization_barrier((back, *sent))
+    back = lax.all_to_all(
+        back.reshape(req_size, slot_count, per, STATE), "req", split_axis=0, concat_axis=0
+    )
+    new_cache = back.transpose(1, 0, 2, 3).reshape(state_cache.shape)
     y_out = local_call(
         columns_kernel,
         place,

time: 296 us -> 239 us (0.81)
  blocking collectives: 96.6 us -> 0 us
  waiting for transfers between devices: 52.5 us -> 110 us
  starting transfers between devices: 81.7 us -> 75.8 us
  local copies, waits for them, and re-layouts: 13.3 us -> 9.28 us
  Pallas kernels: 31.3 us -> 28.2 us
    all_gather x1 -> x0, blocking collectives: 96.6 us -> none  [per_device(): lax.all_gather(kept[:, 0, :heads], 'req', axis=0, tiled=True).reshape(-1)]
    all_to_all x2 -> x3, waiting for transfers between devices: 0.01 us -> 44.9 us  [the longest x1 23.1 us: per_device(): lax.all_to_all(back.reshape(req_size, slot_count, per, STATE), 'req', spl...]
    all_to_all x1, waiting for transfers between devices: 0.01 us -> 21.6 us  [per_device(): lax.all_to_all(pieces, 'req', split_axis=1, concat_axis=0, tiled=False)]
    all_gather x1, waiting for transfers between devices: 6.78 us -> 0.02 us  [per_device(): proj = lax.all_gather(proj, 'tensor', axis=0, tiled=True)]
    all_to_all x2 -> x3, starting transfers between devices: 23 us -> 17.1 us  [the longest x1 8.82 us: per_device(): back = lax.all_to_all(closing, 'req', split_axis=0, concat_axis=0)]
    unnamed x43 -> x31, local copies, waits for them, and re-layouts: 7.6 us -> 5.85 us
  transfers between devices with their start and end apart: 16 -> 17, of which waited for: 12 -> 15; matrix products, arithmetic and copies ran while one was open for 2% -> 0% of each run, Pallas kernels for 9% -> 10%
where the time goes in v4:
time: 239 us; the launch traced here: 238 us
  waiting for transfers between devices  110 us (46%)
  starting transfers between devices  75.8 us (32%)
  Pallas kernels  28.2 us (12%)
  between operations  14.4 us (6%)
  local copies, waits for them, and re-layouts  9.28 us (4%)
    ppermute x12, waiting for transfers between devices, send_along(): moved.append(lax.ppermute(arrays[shift], 'tensor', pairs))  43.8 us
    ppermute x12, starting transfers between devices, send_along(): moved.append(lax.ppermute(arrays[shift], 'tensor', pairs))  41.8 us
    all_to_all x1, waiting for transfers between devices, per_device(): lax.all_to_all(back.reshape(req_size, slot_count, per, STATE), 'req', spl...  23.1 us
    all_to_all x1, waiting for transfers between devices, per_device(): lax.all_to_all(pieces, 'req', split_axis=1, concat_axis=0, tiled=False)  21.6 us
    pallas_call x3, Pallas kernels, session_call(): pl.pallas_call(kernel, grid_spec=pltpu.PrefetchScalarGridSpec(num_scalar_...  17.8 us
    all_to_all x1, waiting for transfers between devices, per_device(): back = lax.all_to_all(closing, 'req', split_axis=0, concat_axis=0)  17.5 us
    all_to_all x1, starting transfers between devices, per_device(): lax.all_to_all(pieces, 'req', split_axis=1, concat_axis=0, tiled=False)  16.9 us
    all_to_all x1, starting transfers between devices, per_device(): back = lax.all_to_all(closing, 'req', split_axis=0, concat_axis=0)  8.82 us
  transfers between devices with their start and end apart: 17, of which 15 were waited for; matrix products, arithmetic and copies ran while one was open for 0% of the time, Pallas kernels for 10%

profile of v4, /device:TPU:1, one launch (start us, length us, event | category | flops | bytes accessed | tf_op | source)
XLA Modules:
  0.0 237.9 jit_solution(3054043852327670083)
XLA Ops:
  7.2 2.1 copy.22
  9.3 16.9 %all-to-all-start = ((bf16[1,6,32,16,128]{4,3,1,0,2:T(8,128)(2,1)}), bf16[1,6,32,16,128]{4,3,1,0,2:T(8,128)(2,1)S(1)}, u32[]{:S(2)}, u32[]{:S(2)}) async-start(bf16[1,6,32,16,128]{4,3,1,0,2:T(8,128)(2,1)} %copy.22), calls=%async_computation | async-start | bytes 1572864 | tf_op jit(solution)/shard_map/all_to_all | solution.py:299
  27.7 3.2 %collective-permute-start = (bf16[72,2048]{1,0:T(8,128)(2,1)S(1)}, bf16[72,2048]{1,0:T(8,128)(2,1)S(1)}, u32[]{:S(2)}, u32[]{:S(2)}) collective-permute-start(bf16[72,2048]{1,0:T(8,128)(2,1)S(1)} %get-tuple-element.36), channel_id=1, source_target_pairs={{0,4},{1,5},{2,6},{3,7},{4,8},{5,9},{6,10},{7,11},{8,12},{9,13},{1... | collective-permute-start | bytes 884744 | tf_op jit(solution)/shard_map/ppermute | solution.py:105
  31.0 4.5 %collective-permute-start.1 = (bf16[72,2048]{1,0:T(8,128)(2,1)S(1)}, bf16[72,2048]{1,0:T(8,128)(2,1)S(1)}, u32[]{:S(2)}, u32[]{:S(2)}) collective-permute-start(bf16[72,2048]{1,0:T(8,128)(2,1)S(1)} %get-tuple-element.37), channel_id=1, source_target_pairs={{0,8},{1,9},{2,10},{3,11},{4,12},{5,13},{6,14},{7,15},{8,0},{9,1},... | collective-permute-start | bytes 884744 | tf_op jit(solution)/shard_map/ppermute | solution.py:105
  35.5 3.0 %collective-permute-start.2 = (bf16[72,2048]{1,0:T(8,128)(2,1)S(1)}, bf16[72,2048]{1,0:T(8,128)(2,1)S(1)}, u32[]{:S(2)}, u32[]{:S(2)}) collective-permute-start(bf16[72,2048]{1,0:T(8,128)(2,1)S(1)} %get-tuple-element.38), channel_id=1, source_target_pairs={{0,12},{1,13},{2,14},{3,15},{4,0},{5,1},{6,2},{7,3},{8,4},{9,5},{1... | collective-permute-start | bytes 884744 | tf_op jit(solution)/shard_map/ppermute | solution.py:105
  39.4 7.4 %collective-permute-done.1.refs_2_ = bf16[72,2048]{1,0:T(8,128)(2,1)S(1)} collective-permute-done((bf16[72,2048]{1,0:T(8,128)(2,1)S(1)}, bf16[72,2048]{1,0:T(8,128)(2,1)S(1)}, u32[]{:S(2)}, u32[]{:S(2)}) %collective-permute-start.1) | collective-permute-done | bytes 294944 | tf_op jit(solution)/shard_map/ppermute | solution.py:105
  49.3 21.6 %all-to-all-done = bf16[1,6,32,16,128]{4,3,1,0,2:T(8,128)(2,1)S(1)} async-done(((bf16[1,6,32,16,128]{4,3,1,0,2:T(8,128)(2,1)}), bf16[1,6,32,16,128]{4,3,1,0,2:T(8,128)(2,1)S(1)}, u32[]{:S(2)}, u32[]{:S(2)}) %all-to-all-start) | async-done | bytes 786464 | tf_op jit(solution)/shard_map/all_to_all | solution.py:299
  70.9 2.1 to_group_order.1
  73.0 4.2 %all-to-all-start.1 = ((bf16[32,6,16,128]{3,2,1,0:T(8,128)(2,1)}), bf16[32,6,16,128]{3,2,1,0:T(8,128)(2,1)S(1)}, u32[]{:S(2)}, u32[]{:S(2)}) async-start(bf16[32,6,16,128]{3,2,1,0:T(8,128)(2,1)} %bitcast.8), calls=%async_computation.1 | async-start | bytes 1572864 | tf_op jit(solution)/shard_map/all_to_all | solution.py:320
  77.2 3.1 %collective-permute-start.3 = (bf16[4,72,512]{2,1,0:T(8,128)(2,1)}, bf16[4,72,512]{2,1,0:T(8,128)(2,1)S(1)}, u32[]{:S(2)}, u32[]{:S(2)}) collective-permute-start(bf16[4,72,512]{2,1,0:T(8,128)(2,1)} %get-tuple-element.45), channel_id=1, source_target_pairs={{0,1},{1,2},{2,3},{3,0},{4,5},{5,6},{6,7},{7,4},{8,9},{9,10},{10,1... | collective-permute-start | bytes 884744 | tf_op jit(solution)/shard_map/ppermute | solution.py:105
  80.3 4.4 %collective-permute-start.4 = (bf16[4,72,512]{2,1,0:T(8,128)(2,1)}, bf16[4,72,512]{2,1,0:T(8,128)(2,1)S(1)}, u32[]{:S(2)}, u32[]{:S(2)}) collective-permute-start(bf16[4,72,512]{2,1,0:T(8,128)(2,1)} %get-tuple-element.46), channel_id=1, source_target_pairs={{0,2},{1,3},{2,0},{3,1},{4,6},{5,7},{6,4},{7,5},{8,10},{9,11},{10,... | collective-permute-start | bytes 884744 | tf_op jit(solution)/shard_map/ppermute | solution.py:105
  84.7 3.1 %collective-permute-start.5 = (bf16[4,72,512]{2,1,0:T(8,128)(2,1)S(1)}, bf16[4,72,512]{2,1,0:T(8,128)(2,1)S(1)}, u32[]{:S(2)}, u32[]{:S(2)}) collective-permute-start(bf16[4,72,512]{2,1,0:T(8,128)(2,1)S(1)} %get-tuple-element.47), channel_id=1, source_target_pairs={{0,3},{1,0},{2,1},{3,2},{4,7},{5,4},{6,5},{7,6},{8,11},{9,8},{10,9... | collective-permute-start | bytes 884744 | tf_op jit(solution)/shard_map/ppermute | solution.py:105
  88.0 5.6 %collective-permute-done.3.refs_1_ = bf16[4,72,512]{2,1,0:T(8,128)(2,1)S(1)} collective-permute-done((bf16[4,72,512]{2,1,0:T(8,128)(2,1)}, bf16[4,72,512]{2,1,0:T(8,128)(2,1)S(1)}, u32[]{:S(2)}, u32[]{:S(2)}) %collective-permute-start.3) | collective-permute-done | bytes 294944 | tf_op jit(solution)/shard_map/ppermute | solution.py:105
  93.6 9.7 %collective-permute-done.4.refs_2_ = bf16[4,72,512]{2,1,0:T(8,128)(2,1)S(1)} collective-permute-done((bf16[4,72,512]{2,1,0:T(8,128)(2,1)}, bf16[4,72,512]{2,1,0:T(8,128)(2,1)S(1)}, u32[]{:S(2)}, u32[]{:S(2)}) %collective-permute-start.4) | collective-permute-done | bytes 294944 | tf_op jit(solution)/shard_map/ppermute | solution.py:105
  104.0 10.9 %tokens_part.1 = (f32[1152,512]{1,0:T(8,128)S(1)}, f32[1152,128]{1,0:T(8,128)S(1)}, f32[32,6,16,128]{3,2,1,0:T(8,128)S(1)}, f32[6,8,128]{2,1,0:T(8,128)S(1)}) custom-call(s32[4]{0:T(128)S(1)} %pad_add_fusion.place_ref, s32[192]{0:T(256)S(1)} %reshape.26.sessions_ref, s32[192]{0:T(256)S(1)} %copy-done.6, bf16[1152,512]{1,0:T(8,128)(2,1)S(1)} %bitcast.21, ...), custom_call_target="tpu_custom_call" | custom-call | flops 10000000000 | bytes 8388608 | tf_op jit(solution)/shard_map/tokens_part/pallas_call | solution.py:250
  117.6 4.3 %all-to-all-done.1.start_ref = bf16[32,6,16,128]{3,2,1,0:T(8,128)(2,1)S(1)} async-done(((bf16[32,6,16,128]{3,2,1,0:T(8,128)(2,1)}), bf16[32,6,16,128]{3,2,1,0:T(8,128)(2,1)S(1)}, u32[]{:S(2)}, u32[]{:S(2)}) %all-to-all-start.1) | async-done | bytes 786464 | tf_op jit(solution)/shard_map/all_to_all | solution.py:320
  123.3 2.7 %closing_states.1 = bf16[32,6,16,128]{3,2,1,0:T(8,128)(2,1)} custom-call(bf16[32,6,16,128]{3,2,1,0:T(8,128)(2,1)S(1)} %all-to-all-done.1.start_ref, f32[32,6,16,128]{3,2,1,0:T(8,128)S(1)} %copy-done.8, f32[6,8,128]{2,1,0:T(8,128)S(1)} %get-tuple-element.50.kept_ref), custom_call_target="tpu_custom_call" | custom-call | flops 1000000000 | bytes 8388608 | tf_op jit(solution)/shard_map/closing_states/pallas_call | solution.py:250
  125.9 8.8 %all-to-all-start.2 = ((bf16[32,6,16,128]{3,2,1,0:T(8,128)(2,1)}), bf16[32,6,16,128]{3,2,1,0:T(8,128)(2,1)S(1)}, u32[]{:S(2)}, u32[]{:S(2)}) async-start(bf16[32,6,16,128]{3,2,1,0:T(8,128)(2,1)} %closing_states.1), calls=%async_computation.2 | async-start | bytes 1572864 | tf_op jit(solution)/shard_map/all_to_all | solution.py:377
  136.4 4.2 %carried_part.1 = bf16[1152,512]{1,0:T(8,128)(2,1)S(1)} custom-call(s32[4]{0:T(128)S(1)} %pad_add_fusion.place_ref, bf16[1152,1152]{1,0:T(8,128)(2,1)} %all-gather.2.cloned.1.call-done.b_ref.c_ref.steps_ref, bf16[32,6,16,128]{3,2,1,0:T(8,128)(2,1)S(1)} %all-to-all-done.1.start_ref, f32[1152,512]{1,0:T(8,128)S(1)} %copy-done.10, ...), custom_call_target="tpu_custom_call" | custom-call | flops 3000000000 | bytes 8388608 | tf_op jit(solution)/shard_map/carried_part/pallas_call | solution.py:250
  141.3 3.1 %collective-permute-start.6 = (bf16[4,72,512]{2,1,0:T(8,128)(2,1)S(1)}, bf16[4,72,512]{2,1,0:T(8,128)(2,1)S(1)}, u32[]{:S(2)}, u32[]{:S(2)}) collective-permute-start(bf16[4,72,512]{2,1,0:T(8,128)(2,1)S(1)} %get-tuple-element.56), channel_id=1, source_target_pairs={{0,1},{1,2},{2,3},{3,0},{4,5},{5,6},{6,7},{7,4},{8,9},{9,10},{10,1... | collective-permute-start | bytes 884744 | tf_op jit(solution)/shard_map/ppermute | solution.py:105
  144.4 3.7 %collective-permute-start.7 = (bf16[4,72,512]{2,1,0:T(8,128)(2,1)S(1)}, bf16[4,72,512]{2,1,0:T(8,128)(2,1)S(1)}, u32[]{:S(2)}, u32[]{:S(2)}) collective-permute-start(bf16[4,72,512]{2,1,0:T(8,128)(2,1)S(1)} %get-tuple-element.57), channel_id=1, source_target_pairs={{0,2},{1,3},{2,0},{3,1},{4,6},{5,7},{6,4},{7,5},{8,10},{9,11},{10,... | collective-permute-start | bytes 884744 | tf_op jit(solution)/shard_map/ppermute | solution.py:105
  148.1 3.4 %collective-permute-start.8 = (bf16[4,72,512]{2,1,0:T(8,128)(2,1)S(1)}, bf16[4,72,512]{2,1,0:T(8,128)(2,1)S(1)}, u32[]{:S(2)}, u32[]{:S(2)}) collective-permute-start(bf16[4,72,512]{2,1,0:T(8,128)(2,1)S(1)} %get-tuple-element.58), channel_id=1, source_target_pairs={{0,3},{1,0},{2,1},{3,2},{4,7},{5,4},{6,5},{7,6},{8,11},{9,8},{10,9... | collective-permute-start | bytes 884744 | tf_op jit(solution)/shard_map/ppermute | solution.py:105
  152.8 6.6 %collective-permute-done.7.refs_2_ = bf16[4,72,512]{2,1,0:T(8,128)(2,1)S(1)} collective-permute-done((bf16[4,72,512]{2,1,0:T(8,128)(2,1)S(1)}, bf16[4,72,512]{2,1,0:T(8,128)(2,1)S(1)}, u32[]{:S(2)}, u32[]{:S(2)}) %collective-permute-start.7) | collective-permute-done | bytes 294944 | tf_op jit(solution)/shard_map/ppermute | solution.py:105
  159.3 2.0 collective-permute-done.8.refs_3_
  161.9 17.5 %all-to-all-done.2 = bf16[32,6,16,128]{3,2,1,0:T(8,128)(2,1)S(1)} async-done(((bf16[32,6,16,128]{3,2,1,0:T(8,128)(2,1)}), bf16[32,6,16,128]{3,2,1,0:T(8,128)(2,1)S(1)}, u32[]{:S(2)}, u32[]{:S(2)}) %all-to-all-start.2) | async-done | bytes 786464 | tf_op jit(solution)/shard_map/all_to_all | solution.py:377
  179.4 2.0 to_owner_order.1
  181.4 4.1 %all-to-all-start.3 = ((bf16[32,6,16,128]{3,2,1,0:T(8,128)(2,1)}), bf16[32,6,16,128]{3,2,1,0:T(8,128)(2,1)S(1)}, u32[]{:S(2)}, u32[]{:S(2)}) async-start(bf16[32,6,16,128]{3,2,1,0:T(8,128)(2,1)} %bitcast.14), calls=%async_computation.3 | async-start | bytes 1572864 | tf_op jit(solution)/shard_map/all_to_all | solution.py:410
  185.5 3.0 %collective-permute-start.9 = (bf16[72,2048]{1,0:T(8,128)(2,1)S(1)}, bf16[72,2048]{1,0:T(8,128)(2,1)S(1)}, u32[]{:S(2)}, u32[]{:S(2)}) collective-permute-start(bf16[72,2048]{1,0:T(8,128)(2,1)S(1)} %get-tuple-element.64), channel_id=1, source_target_pairs={{0,4},{1,5},{2,6},{3,7},{4,8},{5,9},{6,10},{7,11},{8,12},{9,13},{1... | collective-permute-start | bytes 884744 | tf_op jit(solution)/shard_map/ppermute | solution.py:105
  188.4 4.3 %collective-permute-start.10 = (bf16[72,2048]{1,0:T(8,128)(2,1)S(1)}, bf16[72,2048]{1,0:T(8,128)(2,1)S(1)}, u32[]{:S(2)}, u32[]{:S(2)}) collective-permute-start(bf16[72,2048]{1,0:T(8,128)(2,1)S(1)} %get-tuple-element.65), channel_id=1, source_target_pairs={{0,8},{1,9},{2,10},{3,11},{4,12},{5,13},{6,14},{7,15},{8,0},{9,1},... | collective-permute-start | bytes 884744 | tf_op jit(solution)/shard_map/ppermute | solution.py:105
  192.8 3.1 %collective-permute-start.11 = (bf16[72,2048]{1,0:T(8,128)(2,1)S(1)}, bf16[72,2048]{1,0:T(8,128)(2,1)S(1)}, u32[]{:S(2)}, u32[]{:S(2)}) collective-permute-start(bf16[72,2048]{1,0:T(8,128)(2,1)S(1)} %get-tuple-element.66), channel_id=1, source_target_pairs={{0,12},{1,13},{2,14},{3,15},{4,0},{5,1},{6,2},{7,3},{8,4},{9,5},{1... | collective-permute-start | bytes 884744 | tf_op jit(solution)/shard_map/ppermute | solution.py:105
  196.8 7.1 %collective-permute-done.10.refs_2_ = bf16[72,2048]{1,0:T(8,128)(2,1)S(1)} collective-permute-done((bf16[72,2048]{1,0:T(8,128)(2,1)S(1)}, bf16[72,2048]{1,0:T(8,128)(2,1)S(1)}, u32[]{:S(2)}, u32[]{:S(2)}) %collective-permute-start.10) | collective-permute-done | bytes 294944 | tf_op jit(solution)/shard_map/ppermute | solution.py:105
  207.0 23.1 %all-to-all-done.3 = bf16[32,6,16,128]{3,2,1,0:T(8,128)(2,1)S(1)} async-done(((bf16[32,6,16,128]{3,2,1,0:T(8,128)(2,1)}), bf16[32,6,16,128]{3,2,1,0:T(8,128)(2,1)S(1)}, u32[]{:S(2)}, u32[]{:S(2)}) %all-to-all-start.3) | async-done | bytes 786464 | tf_op jit(solution)/shard_map/all_to_all | solution.py:410
  (53 shorter events, 18.9 us)
Async XLA Ops:
  9.3 17.1 %copy-start = (bf16[72,8192]{1,0:T(8,128)(2,1)S(1)}, bf16[72,8192]{1,0:T(8,128)(2,1)}, u32[]{:S(2)}) copy-start(bf16[72,8192]{1,0:T(8,128)(2,1)} %x_ref.1) | copy-start | bytes 3538948
  9.3 17.1 %copy-start.1 = (bf16[72,512]{1,0:T(8,128)(2,1)S(1)}, bf16[72,512]{1,0:T(8,128)(2,1)}, u32[]{:S(2)}) copy-start(bf16[72,512]{1,0:T(8,128)(2,1)} %b_ref.1) | copy-start | bytes 221188
  9.3 17.1 %copy-start.2 = (bf16[72,512]{1,0:T(8,128)(2,1)S(1)}, bf16[72,512]{1,0:T(8,128)(2,1)}, u32[]{:S(2)}) copy-start(bf16[72,512]{1,0:T(8,128)(2,1)} %c_ref.1) | copy-start | bytes 221188
  9.3 17.1 %copy-start.3 = (bf16[72,128]{1,0:T(8,128)(2,1)S(1)}, bf16[72,128]{1,0:T(8,128)(2,1)}, u32[]{:S(2)}) copy-start(bf16[72,128]{1,0:T(8,128)(2,1)} %dt_ref.1) | copy-start | bytes 55300
  9.3 61.6 %all-to-all-start = ((bf16[1,6,32,16,128]{4,3,1,0,2:T(8,128)(2,1)}), bf16[1,6,32,16,128]{4,3,1,0,2:T(8,128)(2,1)S(1)}, u32[]{:S(2)}, u32[]{:S(2)}) async-start(bf16[1,6,32,16,128]{4,3,1,0,2:T(8,128)(2,1)} %copy.22), calls=%async_computation | async-start | bytes 1572864 | tf_op jit(solution)/shard_map/all_to_all | solution.py:299
  26.2 12.3 %copy-start.11 = (s32[32,6]{0,1:T(8,128)S(1)}, s32[32,6]{0,1:T(8,128)}, u32[]{:S(2)}) copy-start(s32[32,6]{0,1:T(8,128)} %param.20) | copy-start | bytes 2308
  26.2 77.7 %all-gather.2.cloned.1.call-start = ((), (), s32[]{:S(2)}) async-start(), calls=%async_computation.4 | async-start | bytes 2820096 | tf_op jit(solution)/shard_map/all_gather | solution.py:311
  26.4 44.5 %copy-start.4 = (s32[192]{0:T(256)S(1)}, s32[192]{0:T(256)}, u32[]{:S(2)}) copy-start(s32[192]{0:T(256)} %owners_ref.3) | copy-start | bytes 2308
  26.4 44.5 %copy-start.5 = (s32[192]{0:T(256)S(1)}, s32[192]{0:T(256)}, u32[]{:S(2)}) copy-start(s32[192]{0:T(256)} %slots_ref.3) | copy-start | bytes 2308
  27.7 11.6 %collective-permute-start = (bf16[72,2048]{1,0:T(8,128)(2,1)S(1)}, bf16[72,2048]{1,0:T(8,128)(2,1)S(1)}, u32[]{:S(2)}, u32[]{:S(2)}) collective-permute-start(bf16[72,2048]{1,0:T(8,128)(2,1)S(1)} %get-tuple-element.36), channel_id=1, source_target_pairs={{0,4},{1,5},{2,6},{3,7},{4,8},{5,9},{6,10},{7,11},{8,12},{9,13},{1... | collective-permute-start | bytes 884744 | tf_op jit(solution)/shard_map/ppermute | solution.py:105
  31.0 15.8 %collective-permute-start.1 = (bf16[72,2048]{1,0:T(8,128)(2,1)S(1)}, bf16[72,2048]{1,0:T(8,128)(2,1)S(1)}, u32[]{:S(2)}, u32[]{:S(2)}) collective-permute-start(bf16[72,2048]{1,0:T(8,128)(2,1)S(1)} %get-tuple-element.37), channel_id=1, source_target_pairs={{0,8},{1,9},{2,10},{3,11},{4,12},{5,13},{6,14},{7,15},{8,0},{9,1},... | collective-permute-start | bytes 884744 | tf_op jit(solution)/shard_map/ppermute | solution.py:105
  35.5 12.4 %collective-permute-start.2 = (bf16[72,2048]{1,0:T(8,128)(2,1)S(1)}, bf16[72,2048]{1,0:T(8,128)(2,1)S(1)}, u32[]{:S(2)}, u32[]{:S(2)}) collective-permute-start(bf16[72,2048]{1,0:T(8,128)(2,1)S(1)} %get-tuple-element.38), channel_id=1, source_target_pairs={{0,12},{1,13},{2,14},{3,15},{4,0},{5,1},{6,2},{7,3},{8,4},{9,5},{1... | collective-permute-start | bytes 884744 | tf_op jit(solution)/shard_map/ppermute | solution.py:105
  73.0 14.8 %copy-start.13 = (f32[8]{0:T(128)S(1)}, f32[8]{0:T(128)}, u32[]{:S(2)}) copy-start(f32[8]{0:T(128)} %param.16) | copy-start | bytes 100
  73.0 14.8 %copy-start.14 = (f32[8]{0:T(128)S(1)}, f32[8]{0:T(128)}, u32[]{:S(2)}) copy-start(f32[8]{0:T(128)} %param.17) | copy-start | bytes 100
  73.0 14.8 %copy-start.12 = (f32[8]{0:T(128)S(1)}, f32[8]{0:T(128)}, u32[]{:S(2)}) copy-start(f32[8]{0:T(128)} %param.18) | copy-start | bytes 100
  73.0 48.8 %all-to-all-start.1 = ((bf16[32,6,16,128]{3,2,1,0:T(8,128)(2,1)}), bf16[32,6,16,128]{3,2,1,0:T(8,128)(2,1)S(1)}, u32[]{:S(2)}, u32[]{:S(2)}) async-start(bf16[32,6,16,128]{3,2,1,0:T(8,128)(2,1)} %bitcast.8), calls=%async_computation.1 | async-start | bytes 1572864 | tf_op jit(solution)/shard_map/all_to_all | solution.py:320
  77.2 16.4 %collective-permute-start.3 = (bf16[4,72,512]{2,1,0:T(8,128)(2,1)}, bf16[4,72,512]{2,1,0:T(8,128)(2,1)S(1)}, u32[]{:S(2)}, u32[]{:S(2)}) collective-permute-start(bf16[4,72,512]{2,1,0:T(8,128)(2,1)} %get-tuple-element.45), channel_id=1, source_target_pairs={{0,1},{1,2},{2,3},{3,0},{4,5},{5,6},{6,7},{7,4},{8,9},{9,10},{10,1... | collective-permute-start | bytes 884744 | tf_op jit(solution)/shard_map/ppermute | solution.py:105
  80.3 23.0 %collective-permute-start.4 = (bf16[4,72,512]{2,1,0:T(8,128)(2,1)}, bf16[4,72,512]{2,1,0:T(8,128)(2,1)S(1)}, u32[]{:S(2)}, u32[]{:S(2)}) collective-permute-start(bf16[4,72,512]{2,1,0:T(8,128)(2,1)} %get-tuple-element.46), channel_id=1, source_target_pairs={{0,2},{1,3},{2,0},{3,1},{4,6},{5,7},{6,4},{7,5},{8,10},{9,11},{10,... | collective-permute-start | bytes 884744 | tf_op jit(solution)/shard_map/ppermute | solution.py:105
  84.7 18.6 %collective-permute-start.5 = (bf16[4,72,512]{2,1,0:T(8,128)(2,1)S(1)}, bf16[4,72,512]{2,1,0:T(8,128)(2,1)S(1)}, u32[]{:S(2)}, u32[]{:S(2)}) collective-permute-start(bf16[4,72,512]{2,1,0:T(8,128)(2,1)S(1)} %get-tuple-element.47), channel_id=1, source_target_pairs={{0,3},{1,0},{2,1},{3,2},{4,7},{5,4},{6,5},{7,6},{8,11},{9,8},{10,9... | collective-permute-start | bytes 884744 | tf_op jit(solution)/shard_map/ppermute | solution.py:105
  88.0 16.0 %copy-start.6 = (s32[192]{0:T(256)S(1)}, s32[192]{0:T(256)}, u32[]{:S(2)}) copy-start(s32[192]{0:T(256)} %lengths_ref.1) | copy-start | bytes 2308
  114.9 1.2 copy-start.7
  116.1 1.5 copy-start.9
  121.8 1.4 copy-start.8
  125.9 53.5 %all-to-all-start.2 = ((bf16[32,6,16,128]{3,2,1,0:T(8,128)(2,1)}), bf16[32,6,16,128]{3,2,1,0:T(8,128)(2,1)S(1)}, u32[]{:S(2)}, u32[]{:S(2)}) async-start(bf16[32,6,16,128]{3,2,1,0:T(8,128)(2,1)} %closing_states.1), calls=%async_computation.2 | async-start | bytes 1572864 | tf_op jit(solution)/shard_map/all_to_all | solution.py:377
  134.7 1.7 copy-start.10
  141.3 11.5 %collective-permute-start.6 = (bf16[4,72,512]{2,1,0:T(8,128)(2,1)S(1)}, bf16[4,72,512]{2,1,0:T(8,128)(2,1)S(1)}, u32[]{:S(2)}, u32[]{:S(2)}) collective-permute-start(bf16[4,72,512]{2,1,0:T(8,128)(2,1)S(1)} %get-tuple-element.56), channel_id=1, source_target_pairs={{0,1},{1,2},{2,3},{3,0},{4,5},{5,6},{6,7},{7,4},{8,9},{9,10},{10,1... | collective-permute-start | bytes 884744 | tf_op jit(solution)/shard_map/ppermute | solution.py:105
  144.4 14.9 %collective-permute-start.7 = (bf16[4,72,512]{2,1,0:T(8,128)(2,1)S(1)}, bf16[4,72,512]{2,1,0:T(8,128)(2,1)S(1)}, u32[]{:S(2)}, u32[]{:S(2)}) collective-permute-start(bf16[4,72,512]{2,1,0:T(8,128)(2,1)S(1)} %get-tuple-element.57), channel_id=1, source_target_pairs={{0,2},{1,3},{2,0},{3,1},{4,6},{5,7},{6,4},{7,5},{8,10},{9,11},{10,... | collective-permute-start | bytes 884744 | tf_op jit(solution)/shard_map/ppermute | solution.py:105
  148.1 13.2 %collective-permute-start.8 = (bf16[4,72,512]{2,1,0:T(8,128)(2,1)S(1)}, bf16[4,72,512]{2,1,0:T(8,128)(2,1)S(1)}, u32[]{:S(2)}, u32[]{:S(2)}) collective-permute-start(bf16[4,72,512]{2,1,0:T(8,128)(2,1)S(1)} %get-tuple-element.58), channel_id=1, source_target_pairs={{0,3},{1,0},{2,1},{3,2},{4,7},{5,4},{6,5},{7,6},{8,11},{9,8},{10,9... | collective-permute-start | bytes 884744 | tf_op jit(solution)/shard_map/ppermute | solution.py:105
  181.4 48.7 %all-to-all-start.3 = ((bf16[32,6,16,128]{3,2,1,0:T(8,128)(2,1)}), bf16[32,6,16,128]{3,2,1,0:T(8,128)(2,1)S(1)}, u32[]{:S(2)}, u32[]{:S(2)}) async-start(bf16[32,6,16,128]{3,2,1,0:T(8,128)(2,1)} %bitcast.14), calls=%async_computation.3 | async-start | bytes 1572864 | tf_op jit(solution)/shard_map/all_to_all | solution.py:410
  185.5 11.3 %collective-permute-start.9 = (bf16[72,2048]{1,0:T(8,128)(2,1)S(1)}, bf16[72,2048]{1,0:T(8,128)(2,1)S(1)}, u32[]{:S(2)}, u32[]{:S(2)}) collective-permute-start(bf16[72,2048]{1,0:T(8,128)(2,1)S(1)} %get-tuple-element.64), channel_id=1, source_target_pairs={{0,4},{1,5},{2,6},{3,7},{4,8},{5,9},{6,10},{7,11},{8,12},{9,13},{1... | collective-permute-start | bytes 884744 | tf_op jit(solution)/shard_map/ppermute | solution.py:105
  188.4 15.5 %collective-permute-start.10 = (bf16[72,2048]{1,0:T(8,128)(2,1)S(1)}, bf16[72,2048]{1,0:T(8,128)(2,1)S(1)}, u32[]{:S(2)}, u32[]{:S(2)}) collective-permute-start(bf16[72,2048]{1,0:T(8,128)(2,1)S(1)} %get-tuple-element.65), channel_id=1, source_target_pairs={{0,8},{1,9},{2,10},{3,11},{4,12},{5,13},{6,14},{7,15},{8,0},{9,1},... | collective-permute-start | bytes 884744 | tf_op jit(solution)/shard_map/ppermute | solution.py:105
  192.8 12.5 %collective-permute-start.11 = (bf16[72,2048]{1,0:T(8,128)(2,1)S(1)}, bf16[72,2048]{1,0:T(8,128)(2,1)S(1)}, u32[]{:S(2)}, u32[]{:S(2)}) collective-permute-start(bf16[72,2048]{1,0:T(8,128)(2,1)S(1)} %get-tuple-element.66), channel_id=1, source_target_pairs={{0,12},{1,13},{2,14},{3,15},{4,0},{5,1},{6,2},{7,3},{8,4},{9,5},{1... | collective-permute-start | bytes 884744 | tf_op jit(solution)/shard_map/ppermute | solution.py:105
Sparse Core Ops, SparseCore 0:
  30.1 67.7 all-gather.1

commit v5 on v4

--- a/solution.py
+++ b/solution.py
@@ -16,27 +16,28 @@
 VMEM_LIMIT = 48 * 1024 * 1024
 
 
-def pack_kernel(place_ref, x_ref, dt_ref, b_ref, c_ref, proj_ref, *out_refs):
+def pack_kernel(place_ref, x_ref, dt_ref, b_ref, c_ref, *out_refs):
     parts = len(out_refs)
     width = x_ref.shape[1] // parts
-    group = place_ref[2]
     for shift, out_ref in enumerate(out_refs):
-        target = lax.rem(group + shift, parts)
-        out_ref[...] = x_ref[:, pl.ds(pl.multiple_of(target * width, LANES), width)]
-    wide = b_ref.shape[1]
-    proj_ref[:, :wide] = b_ref[...]
-    proj_ref[:, wide : 2 * wide] = c_ref[...]
-    proj_ref[:, 2 * wide :] = dt_ref[...]
+        target = lax.rem(place_ref[2] + shift, parts)
+        group = pl.ds(pl.multiple_of(target * STATE, LANES), STATE)
+        out_ref[:, :width] = x_ref[:, pl.ds(pl.multiple_of(target * width, LANES), width)]
+        out_ref[:, width : width + STATE] = b_ref[:, group]
+        out_ref[:, width + STATE : width + 2 * STATE] = c_ref[:, group]
+        out_ref[:, width + 2 * STATE :] = dt_ref[...]
 
 
 def turn_in_kernel(place_ref, *refs):
     half = len(refs) // 2
-    width = refs[0].shape[1] // half
+    extra = 2 * STATE + HEADS
+    width = (refs[0].shape[1] - extra) // half
     for shift in range(half):
         target = lax.rem(place_ref[3] + shift, half)
         columns = pl.ds(pl.multiple_of(target * width, LANES), width)
         for row in range(half):
-            refs[half + shift][row] = refs[row][:, columns]
+            refs[half + shift][row, :, :width] = refs[row][:, columns]
+            refs[half + shift][row, :, width:] = refs[row][:, half * width :]
 
 
 def gather_kernel(place_ref, *refs):
@@ -92,8 +93,8 @@
 
 
 def send_along(arrays, count, along_y):
-    moved = [arrays[0]]
-    for shift in range(1, count):
+    moved = list(arrays)
+    for shift in sorted(range(1, count), key=lambda d: -min(d, count - d)):
         if along_y:
             pairs = [
                 (i, (i // count + shift) % count * count + i % count) for i in range(count * count)
@@ -102,38 +103,79 @@
             pairs = [
                 (i, i // count * count + (i % count + shift) % count) for i in range(count * count)
             ]
-        moved.append(lax.ppermute(arrays[shift], "tensor", pairs))
+        moved[shift] = lax.ppermute(arrays[shift], "tensor", pairs)
     return moved
 
 
-def cache_row(sessions_ref, owners_ref, slots_ref, slot_count, index):
-    session = sessions_ref[index]
-    return owners_ref[session] * slot_count + slots_ref[session]
-
-
-def order_kernel(sessions_ref, owners_ref, slots_ref, in_ref, out_ref, *, slot_count, to_owner):
+def member_at(spot, count):
+    chips = count // 2
+    return lax.rem(lax.rem(spot, chips) * 5, chips) * 2 + spot // chips
+
+
+def spot_of(member, count):
+    chips = count // 2
+    return lax.rem(member, 2) * chips + lax.rem(member // 2 * 13, chips)
+
+
+def members(count):
+    chips = count // 2
+    return [spot % chips * 5 % chips * 2 + spot // chips for spot in range(count)]
+
+
+def rows_kernel(sessions_ref, owners_ref, slots_ref, rows_ref, *, slot_count):
+    count = rows_ref.shape[0] // slot_count
+
+    def step(spot, carry):
+        group = member_at(spot, count)
+        for slot in range(slot_count):
+            session = sessions_ref[group * slot_count + slot]
+            owner = spot_of(owners_ref[session], count)
+            rows_ref[spot * slot_count + slot] = owner * slot_count + slots_ref[session]
+        return carry
+
+    lax.fori_loop(0, count, step, 0)
+
+
+def cache_rows(sessions, owners, slots, slot_count):
+    smem = pl.BlockSpec(memory_space=pltpu.SMEM)
+    return pl.pallas_call(
+        functools.partial(rows_kernel, slot_count=slot_count),
+        in_specs=[smem] * 3,
+        out_specs=smem,
+        out_shape=jax.ShapeDtypeStruct(sessions.shape, jnp.int32),
+        name="cache_rows",
+    )(sessions, owners, slots)
+
+
+def order_kernel(rows_ref, in_ref, out_ref, *, to_owner):
     def step(index, carry):
-        row = cache_row(sessions_ref, owners_ref, slots_ref, slot_count, index)
+        row = rows_ref[index]
         if to_owner:
             out_ref[row] = in_ref[index]
         else:
             out_ref[index] = in_ref[row]
         return carry
 
-    lax.fori_loop(0, in_ref.shape[0], step, 0, unroll=8)
-
-
-def reorder(pieces, sessions, owners, slots, slot_count, to_owner):
+    lax.fori_loop(0, in_ref.shape[0], step, 0, unroll=16)
+
+
+def reorder(pieces, rows, to_owner):
     smem = pl.BlockSpec(memory_space=pltpu.SMEM)
     vmem = pl.BlockSpec(memory_space=pltpu.VMEM)
     return pl.pallas_call(
-        functools.partial(order_kernel, slot_count=slot_count, to_owner=to_owner),
-        in_specs=[smem, smem, smem, vmem],
+        functools.partial(order_kernel, to_owner=to_owner),
+        in_specs=[smem, vmem],
         out_specs=vmem,
         out_shape=jax.ShapeDtypeStruct(pieces.shape, pieces.dtype),
         compiler_params=pltpu.CompilerParams(vmem_limit_bytes=VMEM_LIMIT),
         name="to_owner_order" if to_owner else "to_group_order",
-    )(sessions, owners, slots, pieces)
+    )(rows, pieces)
+
+
+def exchange(states, axis_size, split_axis=0):
+    return lax.all_to_all(
+        states, "req", split_axis=split_axis, concat_axis=0, axis_index_groups=[members(axis_size)]
+    )
 
 
 def token_steps(place_ref, steps_ref, bias_ref, a_log_ref, length, heads):
@@ -295,38 +337,37 @@
     ).astype(jnp.int32)
     sessions = group_sessions.reshape(-1)
 
+    state_shape = (req_size, slot_count, per, STATE)
+    table = cache_rows(sessions, owners, cache_slots, slot_count)
     pieces = state_cache.reshape(slot_count, req_size, per, STATE)
-    held = lax.all_to_all(pieces, "req", split_axis=1, concat_axis=0, tiled=False)
-    held = held.reshape(req_size * slot_count, per, STATE)
-    held = reorder(held, sessions, owners, cache_slots, slot_count, False)
-
-    proj, *sent = local_call(
+    held = exchange(pieces, req_size, 1).reshape(req_size * slot_count, per, STATE)
+    held = reorder(held, table, False)
+
+    extra = 2 * STATE + HEADS
+    sent = local_call(
         pack_kernel,
         place,
         (x_in, dt_raw, b_in, c_in),
-        [shape((rows, 2 * GROUPS * STATE + HEADS), bf16)]
-        + [shape((rows, side * width), bf16)] * GROUPS,
+        [shape((rows, side * width + extra), bf16)] * GROUPS,
         "pack_tokens",
     )
-    proj = lax.all_gather(proj, "tensor", axis=0, tiled=True)
     sent = local_call(
         turn_in_kernel,
         place,
         send_along(sent, side, True),
-        [shape((GROUPS, rows, width), bf16)] * side,
+        [shape((GROUPS, rows, width + extra), bf16)] * side,
         "turn_in",
     )
-    held, *sent = lax.optimization_barrier((held, *sent))
-    start = lax.all_to_all(
-        held.reshape(req_size, slot_count, per, STATE), "req", split_axis=0, concat_axis=0
-    )
-    tokens = local_call(
+    sent = send_along(sent, side, False)
+    held, sent[side // 2] = lax.optimization_barrier((held, sent[side // 2]))
+    start = exchange(held.reshape(state_shape), req_size)
+    packed = local_call(
         gather_kernel,
         place,
-        send_along(sent, side, False),
-        shape((tensor_size, rows, width), bf16),
+        sent,
+        shape((tensor_size, rows, width + extra), bf16),
         "gather_tokens",
-    ).reshape(tensor_size * rows, width)
+    ).reshape(tensor_size * rows, width + extra)
 
     pad = ((0, 0), (0, LANES - heads))
     a_row = jnp.pad(a_log[None, :], pad)
@@ -334,10 +375,10 @@
     skip_row = jnp.repeat(d_skip, HEAD_DIM)[None, :]
     one_row = lambda j, *_: (0, 0)
     by_session = lambda j, *_: (j, 0)
-    x_op = (tokens, (MAXLEN, width), by_session)
-    b_op = (proj, (MAXLEN, STATE), lambda j, place, *_: (j, place[2]))
-    c_op = (proj, (MAXLEN, STATE), lambda j, place, *_: (j, GROUPS + place[2]))
-    steps_op = (proj, (MAXLEN, HEADS), lambda j, *_: (j, 2 * GROUPS))
+    x_op = (packed, (MAXLEN, width), by_session)
+    b_op = (packed, (MAXLEN, STATE), lambda j, *_: (j, width // STATE))
+    c_op = (packed, (MAXLEN, STATE), lambda j, *_: (j, width // STATE + 1))
+    steps_op = (packed, (MAXLEN, HEADS), lambda j, *_: (j, width // STATE + 2))
     a_op = (a_row, (1, LANES), one_row)
     bias_op = (bias_row, (1, LANES), one_row)
     skip_op = (skip_row, (1, width), one_row)
@@ -347,7 +388,6 @@
     by_slot = lambda j, *_: (0, j, 0, 0)
     total_rows = tensor_size * rows
 
-    state_shape = (req_size, slot_count, per, STATE)
     kept_block = ((1, 8, LANES), lambda j, *_: (j, 0, 0))
     local, grown, delta, kept = session_call(
         functools.partial(tokens_kernel, **sizes),
@@ -374,9 +414,8 @@
         "closing_states",
     )
     closing, start = lax.optimization_barrier((closing, start))
-    back = lax.all_to_all(closing, "req", split_axis=0, concat_axis=0)
-    back = back.reshape(req_size * slot_count, per, STATE)
-    back = reorder(back, sessions, owners, cache_slots, slot_count, True)
+    back = exchange(closing, req_size).reshape(req_size * slot_count, per, STATE)
+    back = reorder(back, table, True)
 
     (mixed,) = session_call(
         functools.partial(carry_kernel, heads=heads),
@@ -407,9 +446,7 @@
         "turn_out",
     )
     back, *sent = lax.optimization_barrier((back, *sent))
-    back = lax.all_to_all(
-        back.reshape(req_size, slot_count, per, STATE), "req", split_axis=0, concat_axis=0
-    )
+    back = exchange(back.reshape(state_shape), req_size)
     new_cache = back.transpose(1, 0, 2, 3).reshape(state_cache.shape)
     y_out = local_call(
         columns_kernel,

time: 239 us -> 223 us (0.933)
  between operations: 14.4 us -> 1.01 us
  waiting for transfers between devices: 110 us -> 98.9 us
  local copies, waits for them, and re-layouts: 9.28 us -> 16.4 us
    all_to_all x4, waiting for transfers between devices: 66.4 us -> 56.7 us  [exchange(): lax.all_to_all(states, 'req', split_axis=split_axis, concat_axis=0, axis_...]
    unnamed x31 -> x51, local copies, waits for them, and re-layouts: 5.85 us -> 12.3 us
    pallas_call x2 -> x3, Pallas kernels: 4.09 us -> 6.76 us  [the longest x2 3.38 us: reorder(): pl.pallas_call(functools.partial(order_kernel, to_owner=to_owner), in_spe...]
  transfers between devices with their start and end apart: 17 -> 16, of which waited for: 15 -> 15; matrix products, arithmetic and copies ran while one was open for 0% -> 0% of each run, Pallas kernels for 10% -> 12%
where the time goes in v5:
time: 223 us; the launch traced here: 221 us
  waiting for transfers between devices  98.9 us (44%)
  starting transfers between devices  75.1 us (34%)
  Pallas kernels  29.5 us (13%)
  local copies, waits for them, and re-layouts  16.4 us (7%)
    all_to_all x4, waiting for transfers between devices, exchange(): lax.all_to_all(states, 'req', split_axis=split_axis, concat_axis=0, axis_...  56.7 us
    ppermute x12, starting transfers between devices, send_along(): moved[shift] = lax.ppermute(arrays[shift], 'tensor', pairs)  43.3 us
    ppermute x12, waiting for transfers between devices, send_along(): moved[shift] = lax.ppermute(arrays[shift], 'tensor', pairs)  42.2 us
    all_to_all x4, starting transfers between devices, exchange(): lax.all_to_all(states, 'req', split_axis=split_axis, concat_axis=0, axis_...  31.8 us
    pallas_call x3, Pallas kernels, session_call(): pl.pallas_call(kernel, grid_spec=pltpu.PrefetchScalarGridSpec(num_scalar_...  17 us
    unnamed x51, local copies, waits for them, and re-layouts  12.3 us
    pallas_call x6, Pallas kernels, local_call(): pl.pallas_call(kernel, in_specs=[smem] + [vmem] * len(arrays), out_specs=...  5.73 us
  transfers between devices with their start and end apart: 16, of which 15 were waited for; matrix products, arithmetic and copies ran while one was open for 0% of the time, Pallas kernels for 12%

profile of v5, /device:TPU:1, one launch (start us, length us, event | category | flops | bytes accessed | tf_op | source)
XLA Modules:
  0.0 220.9 jit_solution(15266426669467431456)
XLA Ops:
  0.7 2.2 %copy.22 = bf16[1,6,32,16,128]{4,3,1,0,2:T(8,128)(2,1)} copy(bf16[1,6,32,16,128]{4,3,2,1,0:T(8,128)(2,1)} %bitcast.28) | data formatting | bytes 1572864 | tf_op jit(solution)/shard_map/broadcast_in_dim;reshape | solution.py:176
  2.9 16.8 %all-to-all-start = ((bf16[1,6,32,16,128]{4,3,1,0,2:T(8,128)(2,1)}), bf16[1,6,32,16,128]{4,3,1,0,2:T(8,128)(2,1)S(1)}, u32[]{:S(2)}, u32[]{:S(2)}) async-start(bf16[1,6,32,16,128]{4,3,1,0,2:T(8,128)(2,1)} %copy.22), calls=%async_computation | async-start | bytes 1572864 | tf_op jit(solution)/shard_map/all_to_all | solution.py:176
  20.5 3.2 %collective-permute-start = (bf16[72,2432]{1,0:T(8,128)(2,1)S(1)}, bf16[72,2432]{1,0:T(8,128)(2,1)S(1)}, u32[]{:S(2)}, u32[]{:S(2)}) collective-permute-start(bf16[72,2432]{1,0:T(8,128)(2,1)S(1)} %get-tuple-element.32), channel_id=1, source_target_pairs={{0,4},{1,5},{2,6},{3,7},{4,8},{5,9},{6,10},{7,11},{8,12},{9,13},{1... | collective-permute-start | bytes 1050632 | tf_op jit(solution)/shard_map/ppermute | solution.py:106
  23.7 4.5 %collective-permute-start.1 = (bf16[72,2432]{1,0:T(8,128)(2,1)S(1)}, bf16[72,2432]{1,0:T(8,128)(2,1)S(1)}, u32[]{:S(2)}, u32[]{:S(2)}) collective-permute-start(bf16[72,2432]{1,0:T(8,128)(2,1)S(1)} %get-tuple-element.33), channel_id=1, source_target_pairs={{0,8},{1,9},{2,10},{3,11},{4,12},{5,13},{6,14},{7,15},{8,0},{9,1},... | collective-permute-start | bytes 1050632 | tf_op jit(solution)/shard_map/ppermute | solution.py:106
  28.2 3.0 %collective-permute-start.2 = (bf16[72,2432]{1,0:T(8,128)(2,1)S(1)}, bf16[72,2432]{1,0:T(8,128)(2,1)S(1)}, u32[]{:S(2)}, u32[]{:S(2)}) collective-permute-start(bf16[72,2432]{1,0:T(8,128)(2,1)S(1)} %get-tuple-element.34), channel_id=1, source_target_pairs={{0,12},{1,13},{2,14},{3,15},{4,0},{5,1},{6,2},{7,3},{8,4},{9,5},{1... | collective-permute-start | bytes 1050632 | tf_op jit(solution)/shard_map/ppermute | solution.py:106
  31.2 2.1 collective-permute-done.refs_1_
  33.3 8.6 %collective-permute-done.1.refs_2_ = bf16[72,2432]{1,0:T(8,128)(2,1)S(1)} collective-permute-done((bf16[72,2432]{1,0:T(8,128)(2,1)S(1)}, bf16[72,2432]{1,0:T(8,128)(2,1)S(1)}, u32[]{:S(2)}, u32[]{:S(2)}) %collective-permute-start.1) | collective-permute-done | bytes 350240 | tf_op jit(solution)/shard_map/ppermute | solution.py:106
  44.5 4.6 %collective-permute-start.3 = (bf16[4,72,896]{2,1,0:T(8,128)(2,1)S(1)}, bf16[4,72,896]{2,1,0:T(8,128)(2,1)S(1)}, u32[]{:S(2)}, u32[]{:S(2)}) collective-permute-start(bf16[4,72,896]{2,1,0:T(8,128)(2,1)S(1)} %get-tuple-element.35), channel_id=1, source_target_pairs={{0,2},{1,3},{2,0},{3,1},{4,6},{5,7},{6,4},{7,5},{8,10},{9,11},{10,... | collective-permute-start | bytes 1548296 | tf_op jit(solution)/shard_map/ppermute | solution.py:106
  49.9 3.4 %cache_rows.1.rows_ref = s32[192]{0:T(256)} custom-call(s32[192]{0:T(256)} %reshape.26.sessions_ref, s32[192]{0:T(256)} %owners_ref.1, s32[192]{0:T(256)} %slots_ref.1), custom_call_target="tpu_custom_call" | custom-call | tf_op jit(solution)/shard_map/cache_rows/pallas_call | solution.py:141
  53.3 10.8 %all-to-all-done = bf16[1,6,32,16,128]{4,3,1,0,2:T(8,128)(2,1)S(1)} async-done(((bf16[1,6,32,16,128]{4,3,1,0,2:T(8,128)(2,1)}), bf16[1,6,32,16,128]{4,3,1,0,2:T(8,128)(2,1)S(1)}, u32[]{:S(2)}, u32[]{:S(2)}) %all-to-all-start) | async-done | bytes 786464 | tf_op jit(solution)/shard_map/all_to_all | solution.py:176
  64.9 1.7 to_group_order.1
  66.5 7.2 %all-to-all-start.1 = ((bf16[32,6,16,128]{3,2,1,0:T(8,128)(2,1)}), bf16[32,6,16,128]{3,2,1,0:T(8,128)(2,1)S(1)}, u32[]{:S(2)}, u32[]{:S(2)}) async-start(bf16[32,6,16,128]{3,2,1,0:T(8,128)(2,1)} %bitcast.8), calls=%async_computation.1 | async-start | bytes 1572864 | tf_op jit(solution)/shard_map/all_to_all | solution.py:176
  73.7 3.1 %collective-permute-start.4 = (bf16[4,72,896]{2,1,0:T(8,128)(2,1)}, bf16[4,72,896]{2,1,0:T(8,128)(2,1)S(1)}, u32[]{:S(2)}, u32[]{:S(2)}) collective-permute-start(bf16[4,72,896]{2,1,0:T(8,128)(2,1)} %get-tuple-element.38), channel_id=1, source_target_pairs={{0,1},{1,2},{2,3},{3,0},{4,5},{5,6},{6,7},{7,4},{8,9},{9,10},{10,1... | collective-permute-start | bytes 1548296 | tf_op jit(solution)/shard_map/ppermute | solution.py:106
  76.9 3.4 %collective-permute-start.5 = (bf16[4,72,896]{2,1,0:T(8,128)(2,1)S(1)}, bf16[4,72,896]{2,1,0:T(8,128)(2,1)S(1)}, u32[]{:S(2)}, u32[]{:S(2)}) collective-permute-start(bf16[4,72,896]{2,1,0:T(8,128)(2,1)S(1)} %get-tuple-element.40), channel_id=1, source_target_pairs={{0,3},{1,0},{2,1},{3,2},{4,7},{5,4},{6,5},{7,6},{8,11},{9,8},{10,9... | collective-permute-start | bytes 1548296 | tf_op jit(solution)/shard_map/ppermute | solution.py:106
  80.5 9.7 %collective-permute-done.4.refs_1_ = bf16[4,72,896]{2,1,0:T(8,128)(2,1)S(1)} collective-permute-done((bf16[4,72,896]{2,1,0:T(8,128)(2,1)}, bf16[4,72,896]{2,1,0:T(8,128)(2,1)S(1)}, u32[]{:S(2)}, u32[]{:S(2)}) %collective-permute-start.4) | collective-permute-done | bytes 516128 | tf_op jit(solution)/shard_map/ppermute | solution.py:106
  96.2 11.0 %tokens_part.1 = (f32[1152,512]{1,0:T(8,128)}, f32[1152,128]{1,0:T(8,128)S(1)}, f32[32,6,16,128]{3,2,1,0:T(8,128)S(1)}, f32[6,8,128]{2,1,0:T(8,128)S(1)}) custom-call(s32[4]{0:T(128)S(1)} %pad_add_fusion.place_ref, s32[192]{0:T(256)S(1)} %copy-done.15, s32[192]{0:T(256)S(1)} %copy-done.16, bf16[1152,896]{1,0:T(8,128)(2,1)S(1)} %bitcast.21, ...), custom_call_target="tpu_custom_call" | custom-call | flops 10000000000 | bytes 8388608 | tf_op jit(solution)/shard_map/tokens_part/pallas_call | solution.py:292
  109.2 9.1 %all-to-all-done.1.start_ref = bf16[32,6,16,128]{3,2,1,0:T(8,128)(2,1)S(1)} async-done(((bf16[32,6,16,128]{3,2,1,0:T(8,128)(2,1)}), bf16[32,6,16,128]{3,2,1,0:T(8,128)(2,1)S(1)}, u32[]{:S(2)}, u32[]{:S(2)}) %all-to-all-start.1) | async-done | bytes 786464 | tf_op jit(solution)/shard_map/all_to_all | solution.py:176
  118.2 1.7 copy-done.18
  121.9 4.1 %all-to-all-start.2 = ((bf16[32,6,16,128]{3,2,1,0:T(8,128)(2,1)}), bf16[32,6,16,128]{3,2,1,0:T(8,128)(2,1)S(1)}, u32[]{:S(2)}, u32[]{:S(2)}) async-start(bf16[32,6,16,128]{3,2,1,0:T(8,128)(2,1)} %copy-done.3), calls=%async_computation.2 | async-start | bytes 1572864 | tf_op jit(solution)/shard_map/all_to_all | solution.py:176
  128.3 4.9 %carried_part.1 = bf16[1152,512]{1,0:T(8,128)(2,1)S(1)} custom-call(s32[4]{0:T(128)S(1)} %pad_add_fusion.place_ref, bf16[1152,896]{1,0:T(8,128)(2,1)S(1)} %bitcast.25, bf16[32,6,16,128]{3,2,1,0:T(8,128)(2,1)S(1)} %copy-done.2, f32[1152,512]{1,0:T(8,128)} %get-tuple-element.45.local_ref, f32[1152,128]{1,0:T(8,128)S(1)} %copy-done.20), custom_call_target="tpu_custom_call" | custom-call | flops 3000000000 | bytes 8388608 | tf_op jit(solution)/shard_map/carried_part/pallas_call | solution.py:292
  133.9 3.1 %collective-permute-start.6 = (bf16[4,72,512]{2,1,0:T(8,128)(2,1)S(1)}, bf16[4,72,512]{2,1,0:T(8,128)(2,1)S(1)}, u32[]{:S(2)}, u32[]{:S(2)}) collective-permute-start(bf16[4,72,512]{2,1,0:T(8,128)(2,1)S(1)} %get-tuple-element.48), channel_id=1, source_target_pairs={{0,1},{1,2},{2,3},{3,0},{4,5},{5,6},{6,7},{7,4},{8,9},{9,10},{10,1... | collective-permute-start | bytes 884744 | tf_op jit(solution)/shard_map/ppermute | solution.py:106
  137.0 4.6 %collective-permute-start.7 = (bf16[4,72,512]{2,1,0:T(8,128)(2,1)S(1)}, bf16[4,72,512]{2,1,0:T(8,128)(2,1)S(1)}, u32[]{:S(2)}, u32[]{:S(2)}) collective-permute-start(bf16[4,72,512]{2,1,0:T(8,128)(2,1)S(1)} %get-tuple-element.49), channel_id=1, source_target_pairs={{0,2},{1,3},{2,0},{3,1},{4,6},{5,7},{6,4},{7,5},{8,10},{9,11},{10,... | collective-permute-start | bytes 884744 | tf_op jit(solution)/shard_map/ppermute | solution.py:106
  141.5 2.6 %collective-permute-start.8 = (bf16[4,72,512]{2,1,0:T(8,128)(2,1)S(1)}, bf16[4,72,512]{2,1,0:T(8,128)(2,1)S(1)}, u32[]{:S(2)}, u32[]{:S(2)}) collective-permute-start(bf16[4,72,512]{2,1,0:T(8,128)(2,1)S(1)} %get-tuple-element.50), channel_id=1, source_target_pairs={{0,3},{1,0},{2,1},{3,2},{4,7},{5,4},{6,5},{7,6},{8,11},{9,8},{10,9... | collective-permute-start | bytes 884744 | tf_op jit(solution)/shard_map/ppermute | solution.py:106
  145.4 7.5 %collective-permute-done.7.refs_2_ = bf16[4,72,512]{2,1,0:T(8,128)(2,1)S(1)} collective-permute-done((bf16[4,72,512]{2,1,0:T(8,128)(2,1)S(1)}, bf16[4,72,512]{2,1,0:T(8,128)(2,1)S(1)}, u32[]{:S(2)}, u32[]{:S(2)}) %collective-permute-start.7) | collective-permute-done | bytes 294944 | tf_op jit(solution)/shard_map/ppermute | solution.py:106
  154.5 16.0 %all-to-all-done.2 = bf16[32,6,16,128]{3,2,1,0:T(8,128)(2,1)S(1)} async-done(((bf16[32,6,16,128]{3,2,1,0:T(8,128)(2,1)}), bf16[32,6,16,128]{3,2,1,0:T(8,128)(2,1)S(1)}, u32[]{:S(2)}, u32[]{:S(2)}) %all-to-all-start.2) | async-done | bytes 786464 | tf_op jit(solution)/shard_map/all_to_all | solution.py:176
  170.6 1.7 to_owner_order.1
  172.3 3.7 %all-to-all-start.3 = ((bf16[32,6,16,128]{3,2,1,0:T(8,128)(2,1)}), bf16[32,6,16,128]{3,2,1,0:T(8,128)(2,1)S(1)}, u32[]{:S(2)}, u32[]{:S(2)}) async-start(bf16[32,6,16,128]{3,2,1,0:T(8,128)(2,1)} %bitcast.14), calls=%async_computation.3 | async-start | bytes 1572864 | tf_op jit(solution)/shard_map/all_to_all | solution.py:176
  176.0 5.0 %collective-permute-start.9 = (bf16[72,2048]{1,0:T(8,128)(2,1)S(1)}, bf16[72,2048]{1,0:T(8,128)(2,1)S(1)}, u32[]{:S(2)}, u32[]{:S(2)}) collective-permute-start(bf16[72,2048]{1,0:T(8,128)(2,1)S(1)} %get-tuple-element.56), channel_id=1, source_target_pairs={{0,4},{1,5},{2,6},{3,7},{4,8},{5,9},{6,10},{7,11},{8,12},{9,13},{1... | collective-permute-start | bytes 884744 | tf_op jit(solution)/shard_map/ppermute | solution.py:106
  181.0 3.2 %collective-permute-start.10 = (bf16[72,2048]{1,0:T(8,128)(2,1)S(1)}, bf16[72,2048]{1,0:T(8,128)(2,1)S(1)}, u32[]{:S(2)}, u32[]{:S(2)}) collective-permute-start(bf16[72,2048]{1,0:T(8,128)(2,1)S(1)} %get-tuple-element.57), channel_id=1, source_target_pairs={{0,8},{1,9},{2,10},{3,11},{4,12},{5,13},{6,14},{7,15},{8,0},{9,1},... | collective-permute-start | bytes 884744 | tf_op jit(solution)/shard_map/ppermute | solution.py:106
  184.3 3.0 %collective-permute-start.11 = (bf16[72,2048]{1,0:T(8,128)(2,1)S(1)}, bf16[72,2048]{1,0:T(8,128)(2,1)S(1)}, u32[]{:S(2)}, u32[]{:S(2)}) collective-permute-start(bf16[72,2048]{1,0:T(8,128)(2,1)S(1)} %get-tuple-element.58), channel_id=1, source_target_pairs={{0,12},{1,13},{2,14},{3,15},{4,0},{5,1},{6,2},{7,3},{8,4},{9,5},{1... | collective-permute-start | bytes 884744 | tf_op jit(solution)/shard_map/ppermute | solution.py:106
  188.5 7.7 %collective-permute-done.10.refs_2_ = bf16[72,2048]{1,0:T(8,128)(2,1)S(1)} collective-permute-done((bf16[72,2048]{1,0:T(8,128)(2,1)S(1)}, bf16[72,2048]{1,0:T(8,128)(2,1)S(1)}, u32[]{:S(2)}, u32[]{:S(2)}) %collective-permute-start.10) | collective-permute-done | bytes 294944 | tf_op jit(solution)/shard_map/ppermute | solution.py:106
  199.2 20.7 %all-to-all-done.3 = bf16[32,6,16,128]{3,2,1,0:T(8,128)(2,1)S(1)} async-done(((bf16[32,6,16,128]{3,2,1,0:T(8,128)(2,1)}), bf16[32,6,16,128]{3,2,1,0:T(8,128)(2,1)S(1)}, u32[]{:S(2)}, u32[]{:S(2)}) %all-to-all-start.3) | async-done | bytes 786464 | tf_op jit(solution)/shard_map/all_to_all | solution.py:176
  (71 shorter events, 26.0 us)
Async XLA Ops:
  0.6 19.2 %copy-start = (bf16[72,8192]{1,0:T(8,128)(2,1)S(1)}, bf16[72,8192]{1,0:T(8,128)(2,1)}, u32[]{:S(2)}) copy-start(bf16[72,8192]{1,0:T(8,128)(2,1)} %x_ref.1) | copy-start | bytes 3538948
  0.6 19.2 %copy-start.10 = (bf16[72,512]{1,0:T(8,128)(2,1)S(1)}, bf16[72,512]{1,0:T(8,128)(2,1)}, u32[]{:S(2)}) copy-start(bf16[72,512]{1,0:T(8,128)(2,1)} %b_ref.1) | copy-start | bytes 221188
  0.7 19.1 %copy-start.11 = (bf16[72,512]{1,0:T(8,128)(2,1)S(1)}, bf16[72,512]{1,0:T(8,128)(2,1)}, u32[]{:S(2)}) copy-start(bf16[72,512]{1,0:T(8,128)(2,1)} %c_ref.1) | copy-start | bytes 221188
  0.7 19.1 %copy-start.12 = (bf16[72,128]{1,0:T(8,128)(2,1)S(1)}, bf16[72,128]{1,0:T(8,128)(2,1)}, u32[]{:S(2)}) copy-start(bf16[72,128]{1,0:T(8,128)(2,1)} %dt_ref.1) | copy-start | bytes 55300
  2.9 61.3 %all-to-all-start = ((bf16[1,6,32,16,128]{4,3,1,0,2:T(8,128)(2,1)}), bf16[1,6,32,16,128]{4,3,1,0,2:T(8,128)(2,1)S(1)}, u32[]{:S(2)}, u32[]{:S(2)}) async-start(bf16[1,6,32,16,128]{4,3,1,0,2:T(8,128)(2,1)} %copy.22), calls=%async_computation | async-start | bytes 1572864 | tf_op jit(solution)/shard_map/all_to_all | solution.py:176
  19.7 29.5 %copy-start.21 = (s32[32,6]{0,1:T(8,128)S(1)}, s32[32,6]{0,1:T(8,128)}, u32[]{:S(2)}) copy-start(s32[32,6]{0,1:T(8,128)} %param.20) | copy-start | bytes 2308
  20.5 12.8 %collective-permute-start = (bf16[72,2432]{1,0:T(8,128)(2,1)S(1)}, bf16[72,2432]{1,0:T(8,128)(2,1)S(1)}, u32[]{:S(2)}, u32[]{:S(2)}) collective-permute-start(bf16[72,2432]{1,0:T(8,128)(2,1)S(1)} %get-tuple-element.32), channel_id=1, source_target_pairs={{0,4},{1,5},{2,6},{3,7},{4,8},{5,9},{6,10},{7,11},{8,12},{9,13},{1... | collective-permute-start | bytes 1050632 | tf_op jit(solution)/shard_map/ppermute | solution.py:106
  23.7 18.2 %collective-permute-start.1 = (bf16[72,2432]{1,0:T(8,128)(2,1)S(1)}, bf16[72,2432]{1,0:T(8,128)(2,1)S(1)}, u32[]{:S(2)}, u32[]{:S(2)}) collective-permute-start(bf16[72,2432]{1,0:T(8,128)(2,1)S(1)} %get-tuple-element.33), channel_id=1, source_target_pairs={{0,8},{1,9},{2,10},{3,11},{4,12},{5,13},{6,14},{7,15},{8,0},{9,1},... | collective-permute-start | bytes 1050632 | tf_op jit(solution)/shard_map/ppermute | solution.py:106
  28.2 14.8 %collective-permute-start.2 = (bf16[72,2432]{1,0:T(8,128)(2,1)S(1)}, bf16[72,2432]{1,0:T(8,128)(2,1)S(1)}, u32[]{:S(2)}, u32[]{:S(2)}) collective-permute-start(bf16[72,2432]{1,0:T(8,128)(2,1)S(1)} %get-tuple-element.34), channel_id=1, source_target_pairs={{0,12},{1,13},{2,14},{3,15},{4,0},{5,1},{6,2},{7,3},{8,4},{9,5},{1... | collective-permute-start | bytes 1050632 | tf_op jit(solution)/shard_map/ppermute | solution.py:106
  44.5 22.0 %collective-permute-start.3 = (bf16[4,72,896]{2,1,0:T(8,128)(2,1)S(1)}, bf16[4,72,896]{2,1,0:T(8,128)(2,1)S(1)}, u32[]{:S(2)}, u32[]{:S(2)}) collective-permute-start(bf16[4,72,896]{2,1,0:T(8,128)(2,1)S(1)} %get-tuple-element.35), channel_id=1, source_target_pairs={{0,2},{1,3},{2,0},{3,1},{4,6},{5,7},{6,4},{7,5},{8,10},{9,11},{10,... | collective-permute-start | bytes 1548296 | tf_op jit(solution)/shard_map/ppermute | solution.py:106
  64.8 15.4 %copy-start.23 = (f32[8]{0:T(128)S(1)}, f32[8]{0:T(128)}, u32[]{:S(2)}) copy-start(f32[8]{0:T(128)} %param.16) | copy-start | bytes 100
  64.9 15.4 %copy-start.24 = (f32[8]{0:T(128)S(1)}, f32[8]{0:T(128)}, u32[]{:S(2)}) copy-start(f32[8]{0:T(128)} %param.17) | copy-start | bytes 100
  64.9 15.4 %copy-start.22 = (f32[8]{0:T(128)S(1)}, f32[8]{0:T(128)}, u32[]{:S(2)}) copy-start(f32[8]{0:T(128)} %param.18) | copy-start | bytes 100
  66.5 25.0 %copy-start.4 = (bf16[4,72,896]{2,1,0:T(8,128)(2,1)}, bf16[4,72,896]{2,1,0:T(8,128)(2,1)S(1)}, u32[]{:S(2)}) copy-start(bf16[4,72,896]{2,1,0:T(8,128)(2,1)S(1)} %collective-permute-done.3.refs_2_) | copy-start | bytes 1548292
  66.5 51.7 %all-to-all-start.1 = ((bf16[32,6,16,128]{3,2,1,0:T(8,128)(2,1)}), bf16[32,6,16,128]{3,2,1,0:T(8,128)(2,1)S(1)}, u32[]{:S(2)}, u32[]{:S(2)}) async-start(bf16[32,6,16,128]{3,2,1,0:T(8,128)(2,1)} %bitcast.8), calls=%async_computation.1 | async-start | bytes 1572864 | tf_op jit(solution)/shard_map/all_to_all | solution.py:176
  73.7 16.4 %collective-permute-start.4 = (bf16[4,72,896]{2,1,0:T(8,128)(2,1)}, bf16[4,72,896]{2,1,0:T(8,128)(2,1)S(1)}, u32[]{:S(2)}, u32[]{:S(2)}) collective-permute-start(bf16[4,72,896]{2,1,0:T(8,128)(2,1)} %get-tuple-element.38), channel_id=1, source_target_pairs={{0,1},{1,2},{2,3},{3,0},{4,5},{5,6},{6,7},{7,4},{8,9},{9,10},{10,1... | collective-permute-start | bytes 1548296 | tf_op jit(solution)/shard_map/ppermute | solution.py:106
  76.9 14.7 %collective-permute-start.5 = (bf16[4,72,896]{2,1,0:T(8,128)(2,1)S(1)}, bf16[4,72,896]{2,1,0:T(8,128)(2,1)S(1)}, u32[]{:S(2)}, u32[]{:S(2)}) collective-permute-start(bf16[4,72,896]{2,1,0:T(8,128)(2,1)S(1)} %get-tuple-element.40), channel_id=1, source_target_pairs={{0,3},{1,0},{2,1},{3,2},{4,7},{5,4},{6,5},{7,6},{8,11},{9,8},{10,9... | collective-permute-start | bytes 1548296 | tf_op jit(solution)/shard_map/ppermute | solution.py:106
  93.4 1.0 copy-start.7
  107.2 1.1 copy-start.17
  118.2 2.8 %copy-start.1 = (bf16[32,6,16,128]{3,2,1,0:T(8,128)(2,1)}, bf16[32,6,16,128]{3,2,1,0:T(8,128)(2,1)S(1)}, u32[]{:S(2)}) copy-start(bf16[32,6,16,128]{3,2,1,0:T(8,128)(2,1)S(1)} %all-to-all-done.1.start_ref) | copy-start | bytes 2359300
  118.2 1.7 copy-start.18
  121.9 48.6 %all-to-all-start.2 = ((bf16[32,6,16,128]{3,2,1,0:T(8,128)(2,1)}), bf16[32,6,16,128]{3,2,1,0:T(8,128)(2,1)S(1)}, u32[]{:S(2)}, u32[]{:S(2)}) async-start(bf16[32,6,16,128]{3,2,1,0:T(8,128)(2,1)} %copy-done.3), calls=%async_computation.2 | async-start | bytes 1572864 | tf_op jit(solution)/shard_map/all_to_all | solution.py:176
  126.1 1.1 copy-start.2
  127.2 1.1 copy-start.20
  133.2 37.4 %copy-start.14 = (s32[192]{0:T(256)S(1)}, s32[192]{0:T(256)}, u32[]{:S(2)}) copy-start(s32[192]{0:T(256)} %cache_rows.1.rows_ref) | copy-start | bytes 2308
  133.9 11.5 %collective-permute-start.6 = (bf16[4,72,512]{2,1,0:T(8,128)(2,1)S(1)}, bf16[4,72,512]{2,1,0:T(8,128)(2,1)S(1)}, u32[]{:S(2)}, u32[]{:S(2)}) collective-permute-start(bf16[4,72,512]{2,1,0:T(8,128)(2,1)S(1)} %get-tuple-element.48), channel_id=1, source_target_pairs={{0,1},{1,2},{2,3},{3,0},{4,5},{5,6},{6,7},{7,4},{8,9},{9,10},{10,1... | collective-permute-start | bytes 884744 | tf_op jit(solution)/shard_map/ppermute | solution.py:106
  137.0 15.9 %collective-permute-start.7 = (bf16[4,72,512]{2,1,0:T(8,128)(2,1)S(1)}, bf16[4,72,512]{2,1,0:T(8,128)(2,1)S(1)}, u32[]{:S(2)}, u32[]{:S(2)}) collective-permute-start(bf16[4,72,512]{2,1,0:T(8,128)(2,1)S(1)} %get-tuple-element.49), channel_id=1, source_target_pairs={{0,2},{1,3},{2,0},{3,1},{4,6},{5,7},{6,4},{7,5},{8,10},{9,11},{10,... | collective-permute-start | bytes 884744 | tf_op jit(solution)/shard_map/ppermute | solution.py:106
  141.5 12.4 %collective-permute-start.8 = (bf16[4,72,512]{2,1,0:T(8,128)(2,1)S(1)}, bf16[4,72,512]{2,1,0:T(8,128)(2,1)S(1)}, u32[]{:S(2)}, u32[]{:S(2)}) collective-permute-start(bf16[4,72,512]{2,1,0:T(8,128)(2,1)S(1)} %get-tuple-element.50), channel_id=1, source_target_pairs={{0,3},{1,0},{2,1},{3,2},{4,7},{5,4},{6,5},{7,6},{8,11},{9,8},{10,9... | collective-permute-start | bytes 884744 | tf_op jit(solution)/shard_map/ppermute | solution.py:106
  172.3 47.6 %all-to-all-start.3 = ((bf16[32,6,16,128]{3,2,1,0:T(8,128)(2,1)}), bf16[32,6,16,128]{3,2,1,0:T(8,128)(2,1)S(1)}, u32[]{:S(2)}, u32[]{:S(2)}) async-start(bf16[32,6,16,128]{3,2,1,0:T(8,128)(2,1)} %bitcast.14), calls=%async_computation.3 | async-start | bytes 1572864 | tf_op jit(solution)/shard_map/all_to_all | solution.py:176
  176.0 12.5 %collective-permute-start.9 = (bf16[72,2048]{1,0:T(8,128)(2,1)S(1)}, bf16[72,2048]{1,0:T(8,128)(2,1)S(1)}, u32[]{:S(2)}, u32[]{:S(2)}) collective-permute-start(bf16[72,2048]{1,0:T(8,128)(2,1)S(1)} %get-tuple-element.56), channel_id=1, source_target_pairs={{0,4},{1,5},{2,6},{3,7},{4,8},{5,9},{6,10},{7,11},{8,12},{9,13},{1... | collective-permute-start | bytes 884744 | tf_op jit(solution)/shard_map/ppermute | solution.py:106
  181.0 15.2 %collective-permute-start.10 = (bf16[72,2048]{1,0:T(8,128)(2,1)S(1)}, bf16[72,2048]{1,0:T(8,128)(2,1)S(1)}, u32[]{:S(2)}, u32[]{:S(2)}) collective-permute-start(bf16[72,2048]{1,0:T(8,128)(2,1)S(1)} %get-tuple-element.57), channel_id=1, source_target_pairs={{0,8},{1,9},{2,10},{3,11},{4,12},{5,13},{6,14},{7,15},{8,0},{9,1},... | collective-permute-start | bytes 884744 | tf_op jit(solution)/shard_map/ppermute | solution.py:106
  184.3 13.3 %collective-permute-start.11 = (bf16[72,2048]{1,0:T(8,128)(2,1)S(1)}, bf16[72,2048]{1,0:T(8,128)(2,1)S(1)}, u32[]{:S(2)}, u32[]{:S(2)}) collective-permute-start(bf16[72,2048]{1,0:T(8,128)(2,1)S(1)} %get-tuple-element.58), channel_id=1, source_target_pairs={{0,12},{1,13},{2,14},{3,15},{4,0},{5,1},{6,2},{7,3},{8,4},{9,5},{1... | collective-permute-start | bytes 884744 | tf_op jit(solution)/shard_map/ppermute | solution.py:106
  (9 other events, 7.5 us)

commit v6 on v5

--- a/solution.py
+++ b/solution.py
@@ -13,41 +13,31 @@
 GROUPS = 4
 MAXLEN = 192
 LANES = 128
-VMEM_LIMIT = 48 * 1024 * 1024
+VMEM_LIMIT = 20 * 1024 * 1024
 
 
 def pack_kernel(place_ref, x_ref, dt_ref, b_ref, c_ref, *out_refs):
     parts = len(out_refs)
+    side = parts // GROUPS
     width = x_ref.shape[1] // parts
     for shift, out_ref in enumerate(out_refs):
-        target = lax.rem(place_ref[2] + shift, parts)
-        group = pl.ds(pl.multiple_of(target * STATE, LANES), STATE)
-        out_ref[:, :width] = x_ref[:, pl.ds(pl.multiple_of(target * width, LANES), width)]
+        y_to = lax.rem(place_ref[2] + shift // side, GROUPS)
+        x_to = lax.rem(place_ref[3] + shift % side, side)
+        columns = pl.ds(pl.multiple_of((y_to * side + x_to) * width, LANES), width)
+        group = pl.ds(pl.multiple_of(y_to * STATE, LANES), STATE)
+        out_ref[:, :width] = x_ref[:, columns]
         out_ref[:, width : width + STATE] = b_ref[:, group]
         out_ref[:, width + STATE : width + 2 * STATE] = c_ref[:, group]
         out_ref[:, width + 2 * STATE :] = dt_ref[...]
 
 
-def turn_in_kernel(place_ref, *refs):
-    half = len(refs) // 2
-    extra = 2 * STATE + HEADS
-    width = (refs[0].shape[1] - extra) // half
-    for shift in range(half):
-        target = lax.rem(place_ref[3] + shift, half)
-        columns = pl.ds(pl.multiple_of(target * width, LANES), width)
-        for row in range(half):
-            refs[half + shift][row, :, :width] = refs[row][:, columns]
-            refs[half + shift][row, :, width:] = refs[row][:, half * width :]
-
-
 def gather_kernel(place_ref, *refs):
     out_ref = refs[-1]
-    parts = len(refs) - 1
-    for across in range(parts):
-        x_from = lax.rem(place_ref[3] + parts - across, parts)
-        for down in range(parts):
-            y_from = lax.rem(place_ref[2] + parts - down, parts)
-            out_ref[y_from * parts + x_from] = refs[across][down]
+    side = (len(refs) - 1) // GROUPS
+    for shift in range(len(refs) - 1):
+        y_from = lax.rem(place_ref[2] + GROUPS - shift // side, GROUPS)
+        x_from = lax.rem(place_ref[3] + side - shift % side, side)
+        out_ref[y_from * side + x_from] = refs[shift][...]
 
 
 def split_kernel(place_ref, rows_ref, *out_refs):
@@ -92,34 +82,34 @@
     )(place, *arrays)
 
 
+def moved_by(count, down, across):
+    return [
+        (i, (i // count + down) % count * count + (i % count + across) % count)
+        for i in range(count * count)
+    ]
+
+
 def send_along(arrays, count, along_y):
     moved = list(arrays)
     for shift in sorted(range(1, count), key=lambda d: -min(d, count - d)):
-        if along_y:
-            pairs = [
-                (i, (i // count + shift) % count * count + i % count) for i in range(count * count)
-            ]
-        else:
-            pairs = [
-                (i, i // count * count + (i % count + shift) % count) for i in range(count * count)
-            ]
+        pairs = moved_by(count, shift, 0) if along_y else moved_by(count, 0, shift)
         moved[shift] = lax.ppermute(arrays[shift], "tensor", pairs)
     return moved
 
 
 def member_at(spot, count):
     chips = count // 2
-    return lax.rem(lax.rem(spot, chips) * 5, chips) * 2 + spot // chips
+    return lax.rem(lax.rem(spot, chips) * 7, chips) * 2 + spot // chips
 
 
 def spot_of(member, count):
     chips = count // 2
-    return lax.rem(member, 2) * chips + lax.rem(member // 2 * 13, chips)
+    return lax.rem(member, 2) * chips + lax.rem(member // 2 * 7, chips)
 
 
 def members(count):
     chips = count // 2
-    return [spot % chips * 5 % chips * 2 + spot // chips for spot in range(count)]
+    return [spot % chips * 7 % chips * 2 + spot // chips for spot in range(count)]
 
 
 def rows_kernel(sessions_ref, owners_ref, slots_ref, rows_ref, *, slot_count):
@@ -211,34 +201,71 @@
     return lax.broadcasted_iota(jnp.int32, (MAXLEN, LANES), 1) < HEAD_DIM
 
 
-def tokens_kernel(
-    place_ref, sessions_ref, lengths_ref, x_ref, b_ref, c_ref, steps_ref, a_log_ref, bias_ref,
-    skip_ref, local_ref, grown_ref, delta_ref, kept_ref, *, heads, slot_count
+def delta_kernel(
+    place_ref, sessions_ref, lengths_ref, x_ref, b_ref, steps_ref, a_log_ref, bias_ref,
+    delta_ref, kept_ref, *, heads, slot_count
+):
+    length = lengths_ref[sessions_ref[place_ref[0] * slot_count + pl.program_id(0)]]
+    step, cum, _, _ = token_steps(place_ref, steps_ref, bias_ref, a_log_ref, length, heads)
+    last = cum[MAXLEN - 1 : MAXLEN, :]
+    to_end = jnp.exp(last - cum) * step
+    kept_ref[0] = jnp.broadcast_to(jnp.exp(last), kept_ref.shape[1:])
+    left = left_half()
+    in_proj = b_ref[...]
+    per = delta_ref.shape[2]
+    for first in range(0, heads, 2):
+        lanes = slice(first * HEAD_DIM, (first + 2) * HEAD_DIM)
+        scaled = x_ref[:, lanes].astype(jnp.float32) * spread(to_end, first, left)
+        added = lax.dot_general(
+            scaled.astype(jnp.bfloat16),
+            in_proj,
+            (((0,), (0,)), ((), ())),
+            preferred_element_type=jnp.float32,
+        )
+        begin, count = first * HEAD_DIM // per, 2 * HEAD_DIM // per
+        delta_ref[begin : begin + count, 0] = added.reshape(count, per, STATE)
+
+
+def closing_kernel(start_ref, delta_ref, kept_ref, closing_ref, *, heads):
+    per = start_ref.shape[2]
+    count = HEAD_DIM // per
+    for head in range(heads):
+        rows = slice(head * count, (head + 1) * count)
+        kept = kept_ref[0, :1, head : head + 1].reshape(1, 1, 1)
+        closing = kept * start_ref[rows, 0].astype(jnp.float32) + delta_ref[rows, 0]
+        closing_ref[rows, 0] = closing.astype(jnp.bfloat16)
+
+
+def outputs_kernel(
+    place_ref, sessions_ref, lengths_ref, x_ref, b_ref, c_ref, steps_ref, start_ref, a_log_ref,
+    bias_ref, skip_ref, y_ref, *, heads, slot_count
 ):
     f32 = jnp.float32
     bf16 = jnp.bfloat16
     half = LANES
+    width = heads * HEAD_DIM
     length = lengths_ref[sessions_ref[place_ref[0] * slot_count + pl.program_id(0)]]
     step, cum, live, causal = token_steps(
         place_ref, steps_ref, bias_ref, a_log_ref, length, heads
     )
-    last = cum[MAXLEN - 1 : MAXLEN, :]
-    to_end = jnp.exp(last - cum) * step
-    kept_ref[0] = jnp.broadcast_to(jnp.exp(last), kept_ref.shape[1:])
     drop_rows = (cum - jnp.log(step)).T
-    grown_ref[...] = jnp.where(live, jnp.exp(cum), 0.0)
-    in_proj = b_ref[...]
+    grown = jnp.exp(cum)
+    out_proj = c_ref[...]
     affinity = lax.dot_general(
-        c_ref[...], in_proj, (((1,), (1,)), ((), ())), preferred_element_type=f32
+        out_proj, b_ref[...], (((1,), (1,)), ((), ())), preferred_element_type=f32
     )
     affinity = jnp.where(causal, affinity, 0.0)
     top, low = affinity[:half, :half], affinity[half:, :]
+    carried = lax.dot_general(
+        out_proj,
+        start_ref[...].reshape(width, STATE),
+        (((1,), (1,)), ((), ())),
+        preferred_element_type=f32,
+    )
     left = left_half()
-    per = delta_ref.shape[2]
     for first in range(0, heads, 2):
         lanes = slice(first * HEAD_DIM, (first + 2) * HEAD_DIM)
         pair = x_ref[:, lanes]
-        pair_f32 = pair.astype(f32)
         mixed = []
         for head in (first, first + 1):
             column = cum[:, head : head + 1]
@@ -254,38 +281,12 @@
                     axis=0,
                 )
             )
-        out = jnp.where(left, mixed[0], mixed[1]) + skip_ref[:, lanes] * pair_f32
-        local_ref[:, lanes] = jnp.where(live, out, 0.0)
-        scaled = (pair_f32 * spread(to_end, first, left)).astype(bf16)
-        added = lax.dot_general(
-            scaled, in_proj, (((0,), (0,)), ((), ())), preferred_element_type=f32
+        out = (
+            jnp.where(left, mixed[0], mixed[1])
+            + spread(grown, first, left) * carried[:, lanes]
+            + skip_ref[:, lanes] * pair.astype(f32)
         )
-        begin, count = first * HEAD_DIM // per, 2 * HEAD_DIM // per
-        delta_ref[begin : begin + count, 0] = added.reshape(count, per, STATE)
-
-
-def closing_kernel(start_ref, delta_ref, kept_ref, closing_ref, *, heads):
-    per = start_ref.shape[2]
-    count = HEAD_DIM // per
-    for head in range(heads):
-        rows = slice(head * count, (head + 1) * count)
-        kept = kept_ref[0, :1, head : head + 1].reshape(1, 1, 1)
-        closing = kept * start_ref[rows, 0].astype(jnp.float32) + delta_ref[rows, 0]
-        closing_ref[rows, 0] = closing.astype(jnp.bfloat16)
-
-
-def carry_kernel(place_ref, c_ref, start_ref, local_ref, grown_ref, y_ref, *, heads):
-    width = heads * HEAD_DIM
-    start = start_ref[...].reshape(width, STATE)
-    carried = lax.dot_general(
-        c_ref[...], start, (((1,), (1,)), ((), ())), preferred_element_type=jnp.float32
-    )
-    grown = grown_ref[...]
-    left = left_half()
-    for first in range(0, heads, 2):
-        lanes = slice(first * HEAD_DIM, (first + 2) * HEAD_DIM)
-        out = local_ref[:, lanes] + spread(grown, first, left) * carried[:, lanes]
-        y_ref[:, lanes] = out.astype(jnp.bfloat16)
+        y_ref[:, lanes] = jnp.where(live, out, 0.0).astype(bf16)
 
 
 def session_call(kernel, scalars, slot_count, operands, outputs, flops, name):
@@ -344,22 +345,16 @@
     held = reorder(held, table, False)
 
     extra = 2 * STATE + HEADS
+    piece = shape((rows, width + extra), bf16)
     sent = local_call(
-        pack_kernel,
-        place,
-        (x_in, dt_raw, b_in, c_in),
-        [shape((rows, side * width + extra), bf16)] * GROUPS,
-        "pack_tokens",
-    )
-    sent = local_call(
-        turn_in_kernel,
-        place,
-        send_along(sent, side, True),
-        [shape((GROUPS, rows, width + extra), bf16)] * side,
-        "turn_in",
-    )
-    sent = send_along(sent, side, False)
-    held, sent[side // 2] = lax.optimization_barrier((held, sent[side // 2]))
+        pack_kernel, place, (x_in, dt_raw, b_in, c_in), [piece] * tensor_size, "pack_tokens"
+    )
+    sent = list(sent)
+    for shift in range(1, tensor_size):
+        pairs = moved_by(side, shift // side, shift % side)
+        sent[shift] = lax.ppermute(sent[shift], "tensor", pairs)
+    early = tensor_size // 2 + 1
+    held, *sent[:early] = lax.optimization_barrier((held, *sent[:early]))
     start = exchange(held.reshape(state_shape), req_size)
     packed = local_call(
         gather_kernel,
@@ -389,19 +384,17 @@
     total_rows = tensor_size * rows
 
     kept_block = ((1, 8, LANES), lambda j, *_: (j, 0, 0))
-    local, grown, delta, kept = session_call(
-        functools.partial(tokens_kernel, **sizes),
+    delta, kept = session_call(
+        functools.partial(delta_kernel, **sizes),
         scalars,
         slot_count,
-        [x_op, b_op, c_op, steps_op, a_op, bias_op, skip_op],
+        [x_op, b_op, steps_op, a_op, bias_op],
         [
-            (shape((total_rows, width), f32), (MAXLEN, width), by_session),
-            (shape((total_rows, LANES), f32), (MAXLEN, LANES), by_session),
             (shape(state_shape, f32), piece_block, by_slot),
             (shape((slot_count, 8, LANES), f32), *kept_block),
         ],
-        10_000_000_000,
-        "tokens_part",
+        4_000_000_000,
+        "delta_states",
     )
 
     (closing,) = session_call(
@@ -417,19 +410,15 @@
     back = exchange(closing, req_size).reshape(req_size * slot_count, per, STATE)
     back = reorder(back, table, True)
 
+    start_op = (start, piece_block, by_slot)
     (mixed,) = session_call(
-        functools.partial(carry_kernel, heads=heads),
-        (place,),
+        functools.partial(outputs_kernel, **sizes),
+        scalars,
         slot_count,
-        [
-            c_op,
-            (start, piece_block, by_slot),
-            (local, (MAXLEN, width), by_session),
-            (grown, (MAXLEN, LANES), by_session),
-        ],
+        [x_op, b_op, c_op, steps_op, start_op, a_op, bias_op, skip_op],
         [(shape((total_rows, width), bf16), (MAXLEN, width), by_session)],
-        3_000_000_000,
-        "carried_part",
+        10_000_000_000,
+        "session_outputs",
     )
     sent = local_call(
         split_kernel,

time: 223 us -> 228 us (1.022)
  starting transfers between devices: 75.1 us -> 121 us
  waiting for transfers between devices: 98.9 us -> 57.3 us
    ppermute x0 -> x15, starting transfers between devices: none -> 54.1 us  [per_device(): sent[shift] = lax.ppermute(sent[shift], 'tensor', pairs)]
    all_to_all x4, waiting for transfers between devices: 56.7 us -> 30.5 us  [exchange(): lax.all_to_all(states, 'req', split_axis=split_axis, concat_axis=0, axis_...]
    ppermute x12 -> x6, starting transfers between devices: 43.3 us -> 18.2 us  [send_along(): moved[shift] = lax.ppermute(arrays[shift], 'tensor', pairs)]
    ppermute x12 -> x6, waiting for transfers between devices: 42.2 us -> 21.8 us  [send_along(): moved[shift] = lax.ppermute(arrays[shift], 'tensor', pairs)]
    all_to_all x4, starting transfers between devices: 31.8 us -> 49 us  [exchange(): lax.all_to_all(states, 'req', split_axis=split_axis, concat_axis=0, axis_...]
    ppermute x0 -> x15, waiting for transfers between devices: none -> 5.04 us  [per_device(): sent[shift] = lax.ppermute(sent[shift], 'tensor', pairs)]
    unnamed x51 -> x59, local copies, waits for them, and re-layouts: 12.3 us -> 10.6 us
    pallas_call x6 -> x5, Pallas kernels: 5.73 us -> 5.1 us  [local_call(): pl.pallas_call(kernel, in_specs=[smem] + [vmem] * len(arrays), out_specs=...]
  transfers between devices with their start and end apart: 16 -> 25, of which waited for: 15 -> 11; matrix products, arithmetic and copies ran while one was open for 0% -> 0% of each run, Pallas kernels for 12% -> 12%
where the time goes in v6:
time: 228 us; the launch traced here: 224 us
  starting transfers between devices  121 us (53%)
  waiting for transfers between devices  57.3 us (25%)
  Pallas kernels  29.4 us (13%)
  local copies, waits for them, and re-layouts  14.6 us (6%)
    ppermute x15, starting transfers between devices, per_device(): sent[shift] = lax.ppermute(sent[shift], 'tensor', pairs)  54.1 us
    all_to_all x4, starting transfers between devices, exchange(): lax.all_to_all(states, 'req', split_axis=split_axis, concat_axis=0, axis_...  49 us
    all_to_all x4, waiting for transfers between devices, exchange(): lax.all_to_all(states, 'req', split_axis=split_axis, concat_axis=0, axis_...  30.5 us
    ppermute x6, waiting for transfers between devices, send_along(): moved[shift] = lax.ppermute(arrays[shift], 'tensor', pairs)  21.8 us
    ppermute x6, starting transfers between devices, send_along(): moved[shift] = lax.ppermute(arrays[shift], 'tensor', pairs)  18.2 us
    pallas_call x3, Pallas kernels, session_call(): pl.pallas_call(kernel, grid_spec=pltpu.PrefetchScalarGridSpec(num_scalar_...  17.6 us
    unnamed x59, local copies, waits for them, and re-layouts  10.6 us
    pallas_call x5, Pallas kernels, local_call(): pl.pallas_call(kernel, in_specs=[smem] + [vmem] * len(arrays), out_specs=...  5.1 us
  transfers between devices with their start and end apart: 25, of which 11 were waited for; matrix products, arithmetic and copies ran while one was open for 0% of the time, Pallas kernels for 12%

profile of v6, /device:TPU:1, one launch (start us, length us, event | category | flops | bytes accessed | tf_op | source)
XLA Modules:
  0.0 224.0 jit_solution(10732575310208914875)
XLA Ops:
  2.8 16.9 %all-to-all-start = ((bf16[1,6,32,16,128]{4,3,1,0,2:T(8,128)(2,1)}), bf16[1,6,32,16,128]{4,3,1,0,2:T(8,128)(2,1)S(1)}, u32[]{:S(2)}, u32[]{:S(2)}) async-start(bf16[1,6,32,16,128]{4,3,1,0,2:T(8,128)(2,1)} %copy.22), calls=%async_computation | async-start | bytes 1572864 | tf_op jit(solution)/shard_map/all_to_all | solution.py:166
  22.6 3.1 %collective-permute-start = (bf16[72,896]{1,0:T(8,128)(2,1)S(1)}, bf16[72,896]{1,0:T(8,128)(2,1)S(1)}, u32[]{:S(2)}, u32[]{:S(2)}) collective-permute-start(bf16[72,896]{1,0:T(8,128)(2,1)S(1)} %get-tuple-element.46), channel_id=1, source_target_pairs={{0,1},{1,2},{2,3},{3,0},{4,5},{5,6},{6,7},{7,4},{8,9},{9,10},{10,1... | collective-permute-start | bytes 387080 | tf_op jit(solution)/shard_map/ppermute | solution.py:355
  25.8 4.4 %collective-permute-start.1 = (bf16[72,896]{1,0:T(8,128)(2,1)S(1)}, bf16[72,896]{1,0:T(8,128)(2,1)S(1)}, u32[]{:S(2)}, u32[]{:S(2)}) collective-permute-start(bf16[72,896]{1,0:T(8,128)(2,1)S(1)} %get-tuple-element.47), channel_id=1, source_target_pairs={{0,2},{1,3},{2,0},{3,1},{4,6},{5,7},{6,4},{7,5},{8,10},{9,11},{10,... | collective-permute-start | bytes 387080 | tf_op jit(solution)/shard_map/ppermute | solution.py:355
  30.1 3.1 %collective-permute-start.2 = (bf16[72,896]{1,0:T(8,128)(2,1)S(1)}, bf16[72,896]{1,0:T(8,128)(2,1)S(1)}, u32[]{:S(2)}, u32[]{:S(2)}) collective-permute-start(bf16[72,896]{1,0:T(8,128)(2,1)S(1)} %get-tuple-element.48), channel_id=1, source_target_pairs={{0,3},{1,0},{2,1},{3,2},{4,7},{5,4},{6,5},{7,6},{8,11},{9,8},{10,9... | collective-permute-start | bytes 387080 | tf_op jit(solution)/shard_map/ppermute | solution.py:355
  33.2 3.2 %collective-permute-start.3 = (bf16[72,896]{1,0:T(8,128)(2,1)}, bf16[72,896]{1,0:T(8,128)(2,1)S(1)}, u32[]{:S(2)}, u32[]{:S(2)}) collective-permute-start(bf16[72,896]{1,0:T(8,128)(2,1)} %get-tuple-element.49), channel_id=1, source_target_pairs={{0,4},{1,5},{2,6},{3,7},{4,8},{5,9},{6,10},{7,11},{8,12},{9,13},{1... | collective-permute-start | bytes 387080 | tf_op jit(solution)/shard_map/ppermute | solution.py:355
  36.4 3.2 %collective-permute-start.4 = (bf16[72,896]{1,0:T(8,128)(2,1)}, bf16[72,896]{1,0:T(8,128)(2,1)S(1)}, u32[]{:S(2)}, u32[]{:S(2)}) collective-permute-start(bf16[72,896]{1,0:T(8,128)(2,1)} %get-tuple-element.50), channel_id=1, source_target_pairs={{0,5},{1,6},{2,7},{3,4},{4,9},{5,10},{6,11},{7,8},{8,13},{9,14},{1... | collective-permute-start | bytes 387080 | tf_op jit(solution)/shard_map/ppermute | solution.py:355
  39.7 3.5 %collective-permute-start.5 = (bf16[72,896]{1,0:T(8,128)(2,1)}, bf16[72,896]{1,0:T(8,128)(2,1)S(1)}, u32[]{:S(2)}, u32[]{:S(2)}) collective-permute-start(bf16[72,896]{1,0:T(8,128)(2,1)} %get-tuple-element.51), channel_id=1, source_target_pairs={{0,6},{1,7},{2,4},{3,5},{4,10},{5,11},{6,8},{7,9},{8,14},{9,15},{1... | collective-permute-start | bytes 387080 | tf_op jit(solution)/shard_map/ppermute | solution.py:355
  43.2 3.4 %collective-permute-start.6 = (bf16[72,896]{1,0:T(8,128)(2,1)}, bf16[72,896]{1,0:T(8,128)(2,1)S(1)}, u32[]{:S(2)}, u32[]{:S(2)}) collective-permute-start(bf16[72,896]{1,0:T(8,128)(2,1)} %get-tuple-element.52), channel_id=1, source_target_pairs={{0,7},{1,4},{2,5},{3,6},{4,11},{5,8},{6,9},{7,10},{8,15},{9,12},{1... | collective-permute-start | bytes 387080 | tf_op jit(solution)/shard_map/ppermute | solution.py:355
  46.6 4.1 %collective-permute-start.7 = (bf16[72,896]{1,0:T(8,128)(2,1)}, bf16[72,896]{1,0:T(8,128)(2,1)S(1)}, u32[]{:S(2)}, u32[]{:S(2)}) collective-permute-start(bf16[72,896]{1,0:T(8,128)(2,1)} %get-tuple-element.53), channel_id=1, source_target_pairs={{0,8},{1,9},{2,10},{3,11},{4,12},{5,13},{6,14},{7,15},{8,0},{9,1},... | collective-permute-start | bytes 387080 | tf_op jit(solution)/shard_map/ppermute | solution.py:355
  51.5 3.4 %cache_rows.1.rows_ref = s32[192]{0:T(256)} custom-call(s32[192]{0:T(256)} %reshape.26.sessions_ref, s32[192]{0:T(256)} %owners_ref.1, s32[192]{0:T(256)} %slots_ref.1), custom_call_target="tpu_custom_call" | custom-call | tf_op jit(solution)/shard_map/cache_rows/pallas_call | solution.py:131
  54.9 4.4 %all-to-all-done = bf16[1,6,32,16,128]{4,3,1,0,2:T(8,128)(2,1)S(1)} async-done(((bf16[1,6,32,16,128]{4,3,1,0,2:T(8,128)(2,1)}), bf16[1,6,32,16,128]{4,3,1,0,2:T(8,128)(2,1)S(1)}, u32[]{:S(2)}, u32[]{:S(2)}) %all-to-all-start) | async-done | bytes 786464 | tf_op jit(solution)/shard_map/all_to_all | solution.py:166
  61.7 10.2 %all-to-all-start.1 = ((bf16[32,6,16,128]{3,2,1,0:T(8,128)(2,1)}), bf16[32,6,16,128]{3,2,1,0:T(8,128)(2,1)S(1)}, u32[]{:S(2)}, u32[]{:S(2)}) async-start(bf16[32,6,16,128]{3,2,1,0:T(8,128)(2,1)} %bitcast.8), calls=%async_computation.1 | async-start | bytes 1572864 | tf_op jit(solution)/shard_map/all_to_all | solution.py:166
  71.9 3.7 %collective-permute-start.8 = (bf16[72,896]{1,0:T(8,128)(2,1)S(1)}, bf16[72,896]{1,0:T(8,128)(2,1)S(1)}, u32[]{:S(2)}, u32[]{:S(2)}) collective-permute-start(bf16[72,896]{1,0:T(8,128)(2,1)S(1)} %copy-done.21), channel_id=1, source_target_pairs={{0,9},{1,10},{2,11},{3,8},{4,13},{5,14},{6,15},{7,12},{8,1},{9,2},... | collective-permute-start | bytes 387080 | tf_op jit(solution)/shard_map/ppermute | solution.py:355
  75.6 5.0 %collective-permute-start.9 = (bf16[72,896]{1,0:T(8,128)(2,1)S(1)}, bf16[72,896]{1,0:T(8,128)(2,1)S(1)}, u32[]{:S(2)}, u32[]{:S(2)}) collective-permute-start(bf16[72,896]{1,0:T(8,128)(2,1)S(1)} %copy-done.19), channel_id=1, source_target_pairs={{0,10},{1,11},{2,8},{3,9},{4,14},{5,15},{6,12},{7,13},{8,2},{9,3},... | collective-permute-start | bytes 387080 | tf_op jit(solution)/shard_map/ppermute | solution.py:355
  80.6 4.8 %collective-permute-start.10 = (bf16[72,896]{1,0:T(8,128)(2,1)S(1)}, bf16[72,896]{1,0:T(8,128)(2,1)S(1)}, u32[]{:S(2)}, u32[]{:S(2)}) collective-permute-start(bf16[72,896]{1,0:T(8,128)(2,1)S(1)} %get-tuple-element.66), channel_id=1, source_target_pairs={{0,11},{1,8},{2,9},{3,10},{4,15},{5,12},{6,13},{7,14},{8,3},{9,0},... | collective-permute-start | bytes 387080 | tf_op jit(solution)/shard_map/ppermute | solution.py:355
  85.5 3.8 %collective-permute-start.11 = (bf16[72,896]{1,0:T(8,128)(2,1)S(1)}, bf16[72,896]{1,0:T(8,128)(2,1)S(1)}, u32[]{:S(2)}, u32[]{:S(2)}) collective-permute-start(bf16[72,896]{1,0:T(8,128)(2,1)S(1)} %get-tuple-element.67), channel_id=1, source_target_pairs={{0,12},{1,13},{2,14},{3,15},{4,0},{5,1},{6,2},{7,3},{8,4},{9,5},{1... | collective-permute-start | bytes 387080 | tf_op jit(solution)/shard_map/ppermute | solution.py:355
  91.3 2.7 %collective-permute-start.13 = (bf16[72,896]{1,0:T(8,128)(2,1)S(1)}, bf16[72,896]{1,0:T(8,128)(2,1)S(1)}, u32[]{:S(2)}, u32[]{:S(2)}) collective-permute-start(bf16[72,896]{1,0:T(8,128)(2,1)S(1)} %get-tuple-element.69), channel_id=1, source_target_pairs={{0,14},{1,15},{2,12},{3,13},{4,2},{5,3},{6,0},{7,1},{8,6},{9,7},{1... | collective-permute-start | bytes 387080 | tf_op jit(solution)/shard_map/ppermute | solution.py:355
  94.0 4.2 %collective-permute-start.14 = (bf16[72,896]{1,0:T(8,128)(2,1)S(1)}, bf16[72,896]{1,0:T(8,128)(2,1)S(1)}, u32[]{:S(2)}, u32[]{:S(2)}) collective-permute-start(bf16[72,896]{1,0:T(8,128)(2,1)S(1)} %get-tuple-element.70), channel_id=1, source_target_pairs={{0,15},{1,12},{2,13},{3,14},{4,3},{5,0},{6,1},{7,2},{8,7},{9,4},{1... | collective-permute-start | bytes 387080 | tf_op jit(solution)/shard_map/ppermute | solution.py:355
  99.5 3.8 %collective-permute-done.14.refs_15_ = bf16[72,896]{1,0:T(8,128)(2,1)S(1)} collective-permute-done((bf16[72,896]{1,0:T(8,128)(2,1)S(1)}, bf16[72,896]{1,0:T(8,128)(2,1)S(1)}, u32[]{:S(2)}, u32[]{:S(2)}) %collective-permute-start.14) | collective-permute-done | bytes 129056 | tf_op jit(solution)/shard_map/ppermute | solution.py:355
  107.6 7.6 %delta_states.1 = (f32[32,6,16,128]{3,2,1,0:T(8,128)S(1)}, f32[6,8,128]{2,1,0:T(8,128)S(1)}) custom-call(s32[4]{0:T(128)S(1)} %pad_add_fusion.place_ref, s32[192]{0:T(256)S(1)} %copy-done.17, s32[192]{0:T(256)S(1)} %copy-done.22, bf16[1152,896]{1,0:T(8,128)(2,1)S(1)} %bitcast.21, bf16[1152,896]{1,0:T(8,128)(2,1)S(1)} %bitcast.22, ...), custom_call_target="tpu_custom_call" | custom-call | flops 4000000000 | bytes 8388608 | tf_op jit(solution)/shard_map/delta_states/pallas_call | solution.py:293
  120.2 14.0 %all-to-all-start.2 = ((bf16[32,6,16,128]{3,2,1,0:T(8,128)(2,1)}), bf16[32,6,16,128]{3,2,1,0:T(8,128)(2,1)S(1)}, u32[]{:S(2)}, u32[]{:S(2)}) async-start(bf16[32,6,16,128]{3,2,1,0:T(8,128)(2,1)} %copy-done.3), calls=%async_computation.2 | async-start | bytes 1572864 | tf_op jit(solution)/shard_map/all_to_all | solution.py:166
  135.4 8.8 %session_outputs.1 = bf16[1152,512]{1,0:T(8,128)(2,1)S(1)} custom-call(s32[4]{0:T(128)S(1)} %pad_add_fusion.place_ref, s32[192]{0:T(256)S(1)} %copy-done.17, s32[192]{0:T(256)S(1)} %copy-done.22, bf16[1152,896]{1,0:T(8,128)(2,1)S(1)} %bitcast.24, bf16[1152,896]{1,0:T(8,128)(2,1)S(1)} %bitcast.25, bf16[1152,896]{1,0:T(8,128)(2,1)S(1)} %bitcast.26, ...), custom_call_target="tpu_custom_call" | custom-call | flops 10000000000 | bytes 8388608 | tf_op jit(solution)/shard_map/session_outputs/pallas_call | solution.py:293
  144.9 2.9 %collective-permute-start.15 = (bf16[4,72,512]{2,1,0:T(8,128)(2,1)S(1)}, bf16[4,72,512]{2,1,0:T(8,128)(2,1)S(1)}, u32[]{:S(2)}, u32[]{:S(2)}) collective-permute-start(bf16[4,72,512]{2,1,0:T(8,128)(2,1)S(1)} %get-tuple-element.76), channel_id=1, source_target_pairs={{0,1},{1,2},{2,3},{3,0},{4,5},{5,6},{6,7},{7,4},{8,9},{9,10},{10,1... | collective-permute-start | bytes 884744 | tf_op jit(solution)/shard_map/ppermute | solution.py:96
  147.8 4.1 %collective-permute-start.16 = (bf16[4,72,512]{2,1,0:T(8,128)(2,1)S(1)}, bf16[4,72,512]{2,1,0:T(8,128)(2,1)S(1)}, u32[]{:S(2)}, u32[]{:S(2)}) collective-permute-start(bf16[4,72,512]{2,1,0:T(8,128)(2,1)S(1)} %get-tuple-element.77), channel_id=1, source_target_pairs={{0,2},{1,3},{2,0},{3,1},{4,6},{5,7},{6,4},{7,5},{8,10},{9,11},{10,... | collective-permute-start | bytes 884744 | tf_op jit(solution)/shard_map/ppermute | solution.py:96
  156.4 6.9 %collective-permute-done.16.refs_2_ = bf16[4,72,512]{2,1,0:T(8,128)(2,1)S(1)} collective-permute-done((bf16[4,72,512]{2,1,0:T(8,128)(2,1)S(1)}, bf16[4,72,512]{2,1,0:T(8,128)(2,1)S(1)}, u32[]{:S(2)}, u32[]{:S(2)}) %collective-permute-start.16) | collective-permute-done | bytes 294944 | tf_op jit(solution)/shard_map/ppermute | solution.py:96
  165.6 8.1 %all-to-all-done.2 = bf16[32,6,16,128]{3,2,1,0:T(8,128)(2,1)S(1)} async-done(((bf16[32,6,16,128]{3,2,1,0:T(8,128)(2,1)}), bf16[32,6,16,128]{3,2,1,0:T(8,128)(2,1)S(1)}, u32[]{:S(2)}, u32[]{:S(2)}) %all-to-all-start.2) | async-done | bytes 786464 | tf_op jit(solution)/shard_map/all_to_all | solution.py:166
  175.4 8.0 %all-to-all-start.3 = ((bf16[32,6,16,128]{3,2,1,0:T(8,128)(2,1)}), bf16[32,6,16,128]{3,2,1,0:T(8,128)(2,1)S(1)}, u32[]{:S(2)}, u32[]{:S(2)}) async-start(bf16[32,6,16,128]{3,2,1,0:T(8,128)(2,1)} %bitcast.14), calls=%async_computation.3 | async-start | bytes 1572864 | tf_op jit(solution)/shard_map/all_to_all | solution.py:166
  183.4 2.8 %collective-permute-start.18 = (bf16[72,2048]{1,0:T(8,128)(2,1)S(1)}, bf16[72,2048]{1,0:T(8,128)(2,1)S(1)}, u32[]{:S(2)}, u32[]{:S(2)}) collective-permute-start(bf16[72,2048]{1,0:T(8,128)(2,1)S(1)} %get-tuple-element.84), channel_id=1, source_target_pairs={{0,4},{1,5},{2,6},{3,7},{4,8},{5,9},{6,10},{7,11},{8,12},{9,13},{1... | collective-permute-start | bytes 884744 | tf_op jit(solution)/shard_map/ppermute | solution.py:96
  186.2 3.8 %collective-permute-start.19 = (bf16[72,2048]{1,0:T(8,128)(2,1)S(1)}, bf16[72,2048]{1,0:T(8,128)(2,1)S(1)}, u32[]{:S(2)}, u32[]{:S(2)}) collective-permute-start(bf16[72,2048]{1,0:T(8,128)(2,1)S(1)} %get-tuple-element.85), channel_id=1, source_target_pairs={{0,8},{1,9},{2,10},{3,11},{4,12},{5,13},{6,14},{7,15},{8,0},{9,1},... | collective-permute-start | bytes 884744 | tf_op jit(solution)/shard_map/ppermute | solution.py:96
  192.4 2.4 %collective-permute-done.18.refs_1_ = bf16[72,2048]{1,0:T(8,128)(2,1)S(1)} collective-permute-done((bf16[72,2048]{1,0:T(8,128)(2,1)S(1)}, bf16[72,2048]{1,0:T(8,128)(2,1)S(1)}, u32[]{:S(2)}, u32[]{:S(2)}) %collective-permute-start.18) | collective-permute-done | bytes 294944 | tf_op jit(solution)/shard_map/ppermute | solution.py:96
  194.9 6.5 %collective-permute-done.19.refs_2_ = bf16[72,2048]{1,0:T(8,128)(2,1)S(1)} collective-permute-done((bf16[72,2048]{1,0:T(8,128)(2,1)S(1)}, bf16[72,2048]{1,0:T(8,128)(2,1)S(1)}, u32[]{:S(2)}, u32[]{:S(2)}) %collective-permute-start.19) | collective-permute-done | bytes 294944 | tf_op jit(solution)/shard_map/ppermute | solution.py:96
  205.0 17.9 %all-to-all-done.3 = bf16[32,6,16,128]{3,2,1,0:T(8,128)(2,1)S(1)} async-done(((bf16[32,6,16,128]{3,2,1,0:T(8,128)(2,1)}), bf16[32,6,16,128]{3,2,1,0:T(8,128)(2,1)S(1)}, u32[]{:S(2)}, u32[]{:S(2)}) %all-to-all-start.3) | async-done | bytes 786464 | tf_op jit(solution)/shard_map/all_to_all | solution.py:166
  (96 shorter events, 38.0 us)
Async XLA Ops:
  2.8 47.9 %copy-start.25 = (s32[32,6]{0,1:T(8,128)S(1)}, s32[32,6]{0,1:T(8,128)}, u32[]{:S(2)}) copy-start(s32[32,6]{0,1:T(8,128)} %param.20) | copy-start | bytes 2308
  2.8 56.5 %all-to-all-start = ((bf16[1,6,32,16,128]{4,3,1,0,2:T(8,128)(2,1)}), bf16[1,6,32,16,128]{4,3,1,0,2:T(8,128)(2,1)S(1)}, u32[]{:S(2)}, u32[]{:S(2)}) async-start(bf16[1,6,32,16,128]{4,3,1,0,2:T(8,128)(2,1)} %copy.22), calls=%async_computation | async-start | bytes 1572864 | tf_op jit(solution)/shard_map/all_to_all | solution.py:166
  22.6 17.0 %collective-permute-start = (bf16[72,896]{1,0:T(8,128)(2,1)S(1)}, bf16[72,896]{1,0:T(8,128)(2,1)S(1)}, u32[]{:S(2)}, u32[]{:S(2)}) collective-permute-start(bf16[72,896]{1,0:T(8,128)(2,1)S(1)} %get-tuple-element.46), channel_id=1, source_target_pairs={{0,1},{1,2},{2,3},{3,0},{4,5},{5,6},{6,7},{7,4},{8,9},{9,10},{10,1... | collective-permute-start | bytes 387080 | tf_op jit(solution)/shard_map/ppermute | solution.py:355
  25.8 17.4 %collective-permute-start.1 = (bf16[72,896]{1,0:T(8,128)(2,1)S(1)}, bf16[72,896]{1,0:T(8,128)(2,1)S(1)}, u32[]{:S(2)}, u32[]{:S(2)}) collective-permute-start(bf16[72,896]{1,0:T(8,128)(2,1)S(1)} %get-tuple-element.47), channel_id=1, source_target_pairs={{0,2},{1,3},{2,0},{3,1},{4,6},{5,7},{6,4},{7,5},{8,10},{9,11},{10,... | collective-permute-start | bytes 387080 | tf_op jit(solution)/shard_map/ppermute | solution.py:355
  30.1 16.5 %collective-permute-start.2 = (bf16[72,896]{1,0:T(8,128)(2,1)S(1)}, bf16[72,896]{1,0:T(8,128)(2,1)S(1)}, u32[]{:S(2)}, u32[]{:S(2)}) collective-permute-start(bf16[72,896]{1,0:T(8,128)(2,1)S(1)} %get-tuple-element.48), channel_id=1, source_target_pairs={{0,3},{1,0},{2,1},{3,2},{4,7},{5,4},{6,5},{7,6},{8,11},{9,8},{10,9... | collective-permute-start | bytes 387080 | tf_op jit(solution)/shard_map/ppermute | solution.py:355
  33.2 28.5 %collective-permute-start.3 = (bf16[72,896]{1,0:T(8,128)(2,1)}, bf16[72,896]{1,0:T(8,128)(2,1)S(1)}, u32[]{:S(2)}, u32[]{:S(2)}) collective-permute-start(bf16[72,896]{1,0:T(8,128)(2,1)} %get-tuple-element.49), channel_id=1, source_target_pairs={{0,4},{1,5},{2,6},{3,7},{4,8},{5,9},{6,10},{7,11},{8,12},{9,13},{1... | collective-permute-start | bytes 387080 | tf_op jit(solution)/shard_map/ppermute | solution.py:355
  36.4 25.3 %collective-permute-start.4 = (bf16[72,896]{1,0:T(8,128)(2,1)}, bf16[72,896]{1,0:T(8,128)(2,1)S(1)}, u32[]{:S(2)}, u32[]{:S(2)}) collective-permute-start(bf16[72,896]{1,0:T(8,128)(2,1)} %get-tuple-element.50), channel_id=1, source_target_pairs={{0,5},{1,6},{2,7},{3,4},{4,9},{5,10},{6,11},{7,8},{8,13},{9,14},{1... | collective-permute-start | bytes 387080 | tf_op jit(solution)/shard_map/ppermute | solution.py:355
  39.7 22.0 %collective-permute-start.5 = (bf16[72,896]{1,0:T(8,128)(2,1)}, bf16[72,896]{1,0:T(8,128)(2,1)S(1)}, u32[]{:S(2)}, u32[]{:S(2)}) collective-permute-start(bf16[72,896]{1,0:T(8,128)(2,1)} %get-tuple-element.51), channel_id=1, source_target_pairs={{0,6},{1,7},{2,4},{3,5},{4,10},{5,11},{6,8},{7,9},{8,14},{9,15},{1... | collective-permute-start | bytes 387080 | tf_op jit(solution)/shard_map/ppermute | solution.py:355
  43.2 18.5 %collective-permute-start.6 = (bf16[72,896]{1,0:T(8,128)(2,1)}, bf16[72,896]{1,0:T(8,128)(2,1)S(1)}, u32[]{:S(2)}, u32[]{:S(2)}) collective-permute-start(bf16[72,896]{1,0:T(8,128)(2,1)} %get-tuple-element.52), channel_id=1, source_target_pairs={{0,7},{1,4},{2,5},{3,6},{4,11},{5,8},{6,9},{7,10},{8,15},{9,12},{1... | collective-permute-start | bytes 387080 | tf_op jit(solution)/shard_map/ppermute | solution.py:355
  46.6 15.1 %collective-permute-start.7 = (bf16[72,896]{1,0:T(8,128)(2,1)}, bf16[72,896]{1,0:T(8,128)(2,1)S(1)}, u32[]{:S(2)}, u32[]{:S(2)}) collective-permute-start(bf16[72,896]{1,0:T(8,128)(2,1)} %get-tuple-element.53), channel_id=1, source_target_pairs={{0,8},{1,9},{2,10},{3,11},{4,12},{5,13},{6,14},{7,15},{8,0},{9,1},... | collective-permute-start | bytes 387080 | tf_op jit(solution)/shard_map/ppermute | solution.py:355
  61.6 36.5 %copy-start.27 = (f32[8]{0:T(128)S(1)}, f32[8]{0:T(128)}, u32[]{:S(2)}) copy-start(f32[8]{0:T(128)} %param.16) | copy-start | bytes 100
  61.6 36.5 %copy-start.28 = (f32[8]{0:T(128)S(1)}, f32[8]{0:T(128)}, u32[]{:S(2)}) copy-start(f32[8]{0:T(128)} %param.17) | copy-start | bytes 100
  61.7 37.8 %copy-start.4 = (bf16[72,896]{1,0:T(8,128)(2,1)}, bf16[72,896]{1,0:T(8,128)(2,1)S(1)}, u32[]{:S(2)}) copy-start(bf16[72,896]{1,0:T(8,128)(2,1)S(1)} %collective-permute-done.4.refs_5_) | copy-start | bytes 387076
  61.7 37.8 %copy-start.6 = (bf16[72,896]{1,0:T(8,128)(2,1)}, bf16[72,896]{1,0:T(8,128)(2,1)S(1)}, u32[]{:S(2)}) copy-start(bf16[72,896]{1,0:T(8,128)(2,1)S(1)} %collective-permute-done.5.refs_6_) | copy-start | bytes 387076
  61.7 37.8 %copy-start.8 = (bf16[72,896]{1,0:T(8,128)(2,1)}, bf16[72,896]{1,0:T(8,128)(2,1)S(1)}, u32[]{:S(2)}) copy-start(bf16[72,896]{1,0:T(8,128)(2,1)S(1)} %collective-permute-done.6.refs_7_) | copy-start | bytes 387076
  61.7 37.7 %copy-start.10 = (bf16[72,896]{1,0:T(8,128)(2,1)}, bf16[72,896]{1,0:T(8,128)(2,1)S(1)}, u32[]{:S(2)}) copy-start(bf16[72,896]{1,0:T(8,128)(2,1)S(1)} %collective-permute-done.7.refs_8_) | copy-start | bytes 387076
  61.7 54.7 %all-to-all-start.1 = ((bf16[32,6,16,128]{3,2,1,0:T(8,128)(2,1)}), bf16[32,6,16,128]{3,2,1,0:T(8,128)(2,1)S(1)}, u32[]{:S(2)}, u32[]{:S(2)}) async-start(bf16[32,6,16,128]{3,2,1,0:T(8,128)(2,1)} %bitcast.8), calls=%async_computation.1 | async-start | bytes 1572864 | tf_op jit(solution)/shard_map/all_to_all | solution.py:166
  71.9 19.3 %collective-permute-start.8 = (bf16[72,896]{1,0:T(8,128)(2,1)S(1)}, bf16[72,896]{1,0:T(8,128)(2,1)S(1)}, u32[]{:S(2)}, u32[]{:S(2)}) collective-permute-start(bf16[72,896]{1,0:T(8,128)(2,1)S(1)} %copy-done.21), channel_id=1, source_target_pairs={{0,9},{1,10},{2,11},{3,8},{4,13},{5,14},{6,15},{7,12},{8,1},{9,2},... | collective-permute-start | bytes 387080 | tf_op jit(solution)/shard_map/ppermute | solution.py:355
  75.6 18.3 %collective-permute-start.9 = (bf16[72,896]{1,0:T(8,128)(2,1)S(1)}, bf16[72,896]{1,0:T(8,128)(2,1)S(1)}, u32[]{:S(2)}, u32[]{:S(2)}) collective-permute-start(bf16[72,896]{1,0:T(8,128)(2,1)S(1)} %copy-done.19), channel_id=1, source_target_pairs={{0,10},{1,11},{2,8},{3,9},{4,14},{5,15},{6,12},{7,13},{8,2},{9,3},... | collective-permute-start | bytes 387080 | tf_op jit(solution)/shard_map/ppermute | solution.py:355
  80.6 17.6 %collective-permute-start.10 = (bf16[72,896]{1,0:T(8,128)(2,1)S(1)}, bf16[72,896]{1,0:T(8,128)(2,1)S(1)}, u32[]{:S(2)}, u32[]{:S(2)}) collective-permute-start(bf16[72,896]{1,0:T(8,128)(2,1)S(1)} %get-tuple-element.66), channel_id=1, source_target_pairs={{0,11},{1,8},{2,9},{3,10},{4,15},{5,12},{6,13},{7,14},{8,3},{9,0},... | collective-permute-start | bytes 387080 | tf_op jit(solution)/shard_map/ppermute | solution.py:355
  85.5 12.8 %collective-permute-start.11 = (bf16[72,896]{1,0:T(8,128)(2,1)S(1)}, bf16[72,896]{1,0:T(8,128)(2,1)S(1)}, u32[]{:S(2)}, u32[]{:S(2)}) collective-permute-start(bf16[72,896]{1,0:T(8,128)(2,1)S(1)} %get-tuple-element.67), channel_id=1, source_target_pairs={{0,12},{1,13},{2,14},{3,15},{4,0},{5,1},{6,2},{7,3},{8,4},{9,5},{1... | collective-permute-start | bytes 387080 | tf_op jit(solution)/shard_map/ppermute | solution.py:355
  89.3 8.9 %collective-permute-start.12 = (bf16[72,896]{1,0:T(8,128)(2,1)S(1)}, bf16[72,896]{1,0:T(8,128)(2,1)S(1)}, u32[]{:S(2)}, u32[]{:S(2)}) collective-permute-start(bf16[72,896]{1,0:T(8,128)(2,1)S(1)} %get-tuple-element.68), channel_id=1, source_target_pairs={{0,13},{1,14},{2,15},{3,12},{4,1},{5,2},{6,3},{7,0},{8,5},{9,6},{1... | collective-permute-start | bytes 387080 | tf_op jit(solution)/shard_map/ppermute | solution.py:355
  91.3 8.2 %collective-permute-start.13 = (bf16[72,896]{1,0:T(8,128)(2,1)S(1)}, bf16[72,896]{1,0:T(8,128)(2,1)S(1)}, u32[]{:S(2)}, u32[]{:S(2)}) collective-permute-start(bf16[72,896]{1,0:T(8,128)(2,1)S(1)} %get-tuple-element.69), channel_id=1, source_target_pairs={{0,14},{1,15},{2,12},{3,13},{4,2},{5,3},{6,0},{7,1},{8,6},{9,7},{1... | collective-permute-start | bytes 387080 | tf_op jit(solution)/shard_map/ppermute | solution.py:355
  94.0 9.3 %collective-permute-start.14 = (bf16[72,896]{1,0:T(8,128)(2,1)S(1)}, bf16[72,896]{1,0:T(8,128)(2,1)S(1)}, u32[]{:S(2)}, u32[]{:S(2)}) collective-permute-start(bf16[72,896]{1,0:T(8,128)(2,1)S(1)} %get-tuple-element.70), channel_id=1, source_target_pairs={{0,15},{1,12},{2,13},{3,14},{4,3},{5,0},{6,1},{7,2},{8,7},{9,4},{1... | collective-permute-start | bytes 387080 | tf_op jit(solution)/shard_map/ppermute | solution.py:355
  120.2 53.5 %all-to-all-start.2 = ((bf16[32,6,16,128]{3,2,1,0:T(8,128)(2,1)}), bf16[32,6,16,128]{3,2,1,0:T(8,128)(2,1)S(1)}, u32[]{:S(2)}, u32[]{:S(2)}) async-start(bf16[32,6,16,128]{3,2,1,0:T(8,128)(2,1)} %copy-done.3), calls=%async_computation.2 | async-start | bytes 1572864 | tf_op jit(solution)/shard_map/all_to_all | solution.py:166
  144.9 11.5 %collective-permute-start.15 = (bf16[4,72,512]{2,1,0:T(8,128)(2,1)S(1)}, bf16[4,72,512]{2,1,0:T(8,128)(2,1)S(1)}, u32[]{:S(2)}, u32[]{:S(2)}) collective-permute-start(bf16[4,72,512]{2,1,0:T(8,128)(2,1)S(1)} %get-tuple-element.76), channel_id=1, source_target_pairs={{0,1},{1,2},{2,3},{3,0},{4,5},{5,6},{6,7},{7,4},{8,9},{9,10},{10,1... | collective-permute-start | bytes 884744 | tf_op jit(solution)/shard_map/ppermute | solution.py:96
  147.8 15.4 %collective-permute-start.16 = (bf16[4,72,512]{2,1,0:T(8,128)(2,1)S(1)}, bf16[4,72,512]{2,1,0:T(8,128)(2,1)S(1)}, u32[]{:S(2)}, u32[]{:S(2)}) collective-permute-start(bf16[4,72,512]{2,1,0:T(8,128)(2,1)S(1)} %get-tuple-element.77), channel_id=1, source_target_pairs={{0,2},{1,3},{2,0},{3,1},{4,6},{5,7},{6,4},{7,5},{8,10},{9,11},{10,... | collective-permute-start | bytes 884744 | tf_op jit(solution)/shard_map/ppermute | solution.py:96
  152.0 13.0 %collective-permute-start.17 = (bf16[4,72,512]{2,1,0:T(8,128)(2,1)S(1)}, bf16[4,72,512]{2,1,0:T(8,128)(2,1)S(1)}, u32[]{:S(2)}, u32[]{:S(2)}) collective-permute-start(bf16[4,72,512]{2,1,0:T(8,128)(2,1)S(1)} %get-tuple-element.78), channel_id=1, source_target_pairs={{0,3},{1,0},{2,1},{3,2},{4,7},{5,4},{6,5},{7,6},{8,11},{9,8},{10,9... | collective-permute-start | bytes 884744 | tf_op jit(solution)/shard_map/ppermute | solution.py:96
  175.4 47.6 %all-to-all-start.3 = ((bf16[32,6,16,128]{3,2,1,0:T(8,128)(2,1)}), bf16[32,6,16,128]{3,2,1,0:T(8,128)(2,1)S(1)}, u32[]{:S(2)}, u32[]{:S(2)}) async-start(bf16[32,6,16,128]{3,2,1,0:T(8,128)(2,1)} %bitcast.14), calls=%async_computation.3 | async-start | bytes 1572864 | tf_op jit(solution)/shard_map/all_to_all | solution.py:166
  183.4 11.5 %collective-permute-start.18 = (bf16[72,2048]{1,0:T(8,128)(2,1)S(1)}, bf16[72,2048]{1,0:T(8,128)(2,1)S(1)}, u32[]{:S(2)}, u32[]{:S(2)}) collective-permute-start(bf16[72,2048]{1,0:T(8,128)(2,1)S(1)} %get-tuple-element.84), channel_id=1, source_target_pairs={{0,4},{1,5},{2,6},{3,7},{4,8},{5,9},{6,10},{7,11},{8,12},{9,13},{1... | collective-permute-start | bytes 884744 | tf_op jit(solution)/shard_map/ppermute | solution.py:96
  186.2 15.1 %collective-permute-start.19 = (bf16[72,2048]{1,0:T(8,128)(2,1)S(1)}, bf16[72,2048]{1,0:T(8,128)(2,1)S(1)}, u32[]{:S(2)}, u32[]{:S(2)}) collective-permute-start(bf16[72,2048]{1,0:T(8,128)(2,1)S(1)} %get-tuple-element.85), channel_id=1, source_target_pairs={{0,8},{1,9},{2,10},{3,11},{4,12},{5,13},{6,14},{7,15},{8,0},{9,1},... | collective-permute-start | bytes 884744 | tf_op jit(solution)/shard_map/ppermute | solution.py:96
  190.1 13.3 %collective-permute-start.20 = (bf16[72,2048]{1,0:T(8,128)(2,1)S(1)}, bf16[72,2048]{1,0:T(8,128)(2,1)S(1)}, u32[]{:S(2)}, u32[]{:S(2)}) collective-permute-start(bf16[72,2048]{1,0:T(8,128)(2,1)S(1)} %get-tuple-element.86), channel_id=1, source_target_pairs={{0,12},{1,13},{2,14},{3,15},{4,0},{5,1},{6,2},{7,3},{8,4},{9,5},{1... | collective-permute-start | bytes 884744 | tf_op jit(solution)/shard_map/ppermute | solution.py:96
  (22 other events, 167.9 us)

commit v7 on v6

--- a/solution.py
+++ b/solution.py
@@ -18,26 +18,36 @@
 
 def pack_kernel(place_ref, x_ref, dt_ref, b_ref, c_ref, *out_refs):
     parts = len(out_refs)
-    side = parts // GROUPS
     width = x_ref.shape[1] // parts
     for shift, out_ref in enumerate(out_refs):
-        y_to = lax.rem(place_ref[2] + shift // side, GROUPS)
-        x_to = lax.rem(place_ref[3] + shift % side, side)
-        columns = pl.ds(pl.multiple_of((y_to * side + x_to) * width, LANES), width)
-        group = pl.ds(pl.multiple_of(y_to * STATE, LANES), STATE)
-        out_ref[:, :width] = x_ref[:, columns]
+        target = lax.rem(place_ref[2] + shift, parts)
+        group = pl.ds(pl.multiple_of(target * STATE, LANES), STATE)
+        out_ref[:, :width] = x_ref[:, pl.ds(pl.multiple_of(target * width, LANES), width)]
         out_ref[:, width : width + STATE] = b_ref[:, group]
         out_ref[:, width + STATE : width + 2 * STATE] = c_ref[:, group]
         out_ref[:, width + 2 * STATE :] = dt_ref[...]
 
 
+def turn_in_kernel(place_ref, *refs):
+    half = len(refs) // 2
+    extra = 2 * STATE + HEADS
+    width = (refs[0].shape[1] - extra) // half
+    for shift in range(half):
+        target = lax.rem(place_ref[3] + shift, half)
+        columns = pl.ds(pl.multiple_of(target * width, LANES), width)
+        for row in range(half):
+            refs[half + shift][row, :, :width] = refs[row][:, columns]
+            refs[half + shift][row, :, width:] = refs[row][:, half * width :]
+
+
 def gather_kernel(place_ref, *refs):
     out_ref = refs[-1]
-    side = (len(refs) - 1) // GROUPS
-    for shift in range(len(refs) - 1):
-        y_from = lax.rem(place_ref[2] + GROUPS - shift // side, GROUPS)
-        x_from = lax.rem(place_ref[3] + side - shift % side, side)
-        out_ref[y_from * side + x_from] = refs[shift][...]
+    parts = len(refs) - 1
+    for across in range(parts):
+        x_from = lax.rem(place_ref[3] + parts - across, parts)
+        for down in range(parts):
+            y_from = lax.rem(place_ref[2] + parts - down, parts)
+            out_ref[y_from * parts + x_from] = refs[across][down]
 
 
 def split_kernel(place_ref, rows_ref, *out_refs):
@@ -99,17 +109,17 @@
 
 def member_at(spot, count):
     chips = count // 2
-    return lax.rem(lax.rem(spot, chips) * 7, chips) * 2 + spot // chips
+    return lax.rem(lax.rem(spot, chips) * 3, chips) * 2 + spot // chips
 
 
 def spot_of(member, count):
     chips = count // 2
-    return lax.rem(member, 2) * chips + lax.rem(member // 2 * 7, chips)
+    return lax.rem(member, 2) * chips + lax.rem(member // 2 * 11, chips)
 
 
 def members(count):
     chips = count // 2
-    return [spot % chips * 7 % chips * 2 + spot // chips for spot in range(count)]
+    return [spot % chips * 3 % chips * 2 + spot // chips for spot in range(count)]
 
 
 def rows_kernel(sessions_ref, owners_ref, slots_ref, rows_ref, *, slot_count):
@@ -345,16 +355,22 @@
     held = reorder(held, table, False)
 
     extra = 2 * STATE + HEADS
-    piece = shape((rows, width + extra), bf16)
     sent = local_call(
-        pack_kernel, place, (x_in, dt_raw, b_in, c_in), [piece] * tensor_size, "pack_tokens"
-    )
-    sent = list(sent)
-    for shift in range(1, tensor_size):
-        pairs = moved_by(side, shift // side, shift % side)
-        sent[shift] = lax.ppermute(sent[shift], "tensor", pairs)
-    early = tensor_size // 2 + 1
-    held, *sent[:early] = lax.optimization_barrier((held, *sent[:early]))
+        pack_kernel,
+        place,
+        (x_in, dt_raw, b_in, c_in),
+        [shape((rows, side * width + extra), bf16)] * GROUPS,
+        "pack_tokens",
+    )
+    sent = local_call(
+        turn_in_kernel,
+        place,
+        send_along(sent, side, True),
+        [shape((GROUPS, rows, width + extra), bf16)] * side,
+        "turn_in",
+    )
+    sent = send_along(sent, side, False)
+    held, sent[1] = lax.optimization_barrier((held, sent[1]))
     start = exchange(held.reshape(state_shape), req_size)
     packed = local_call(
         gather_kernel,
@@ -390,7 +406,7 @@
         slot_count,
         [x_op, b_op, steps_op, a_op, bias_op],
         [
-            (shape(state_shape, f32), piece_block, by_slot),
+            (pltpu.HBM(state_shape, f32), piece_block, by_slot),
             (shape((slot_count, 8, LANES), f32), *kept_block),
         ],
         4_000_000_000,
@@ -402,7 +418,7 @@
         (),
         slot_count,
         [(start, piece_block, by_slot), (delta, piece_block, by_slot), (kept, *kept_block)],
-        [(shape(state_shape, bf16), piece_block, by_slot)],
+        [(pltpu.HBM(state_shape, bf16), piece_block, by_slot)],
         1_000_000_000,
         "closing_states",
     )

time: 228 us -> 221 us (0.969)
  starting transfers between devices: 121 us -> 80.4 us
  waiting for transfers between devices: 57.3 us -> 97 us
  local copies, waits for them, and re-layouts: 14.6 us -> 8.63 us
    ppermute x15 -> x0, starting transfers between devices: 54.1 us -> none  [per_device(): sent[shift] = lax.ppermute(sent[shift], 'tensor', pairs)]
    ppermute x6 -> x12, waiting for transfers between devices: 21.8 us -> 52.2 us  [send_along(): moved[shift] = lax.ppermute(arrays[shift], 'tensor', pairs)]
    ppermute x6 -> x12, starting transfers between devices: 18.2 us -> 40.8 us  [send_along(): moved[shift] = lax.ppermute(arrays[shift], 'tensor', pairs)]
    all_to_all x4, waiting for transfers between devices: 30.5 us -> 44.9 us  [exchange(): lax.all_to_all(states, 'req', split_axis=split_axis, concat_axis=0, axis_...]
    all_to_all x4, starting transfers between devices: 49 us -> 39.6 us  [exchange(): lax.all_to_all(states, 'req', split_axis=split_axis, concat_axis=0, axis_...]
    unnamed x59 -> x35, local copies, waits for them, and re-layouts: 10.6 us -> 4.66 us
    ppermute x15 -> x0, waiting for transfers between devices: 5.04 us -> none  [per_device(): sent[shift] = lax.ppermute(sent[shift], 'tensor', pairs)]
    pallas_call x5 -> x6, Pallas kernels: 5.1 us -> 4.94 us  [local_call(): pl.pallas_call(kernel, in_specs=[smem] + [vmem] * len(arrays), out_specs=...]
  transfers between devices with their start and end apart: 25 -> 16, of which waited for: 11 -> 15; matrix products, arithmetic and copies ran while one was open for 0% -> 0% of each run, Pallas kernels for 12% -> 12%
where the time goes in v7:
time: 221 us; the launch traced here: 219 us
  waiting for transfers between devices  97 us (44%)
  starting transfers between devices  80.4 us (36%)
  Pallas kernels  31.5 us (14%)
  local copies, waits for them, and re-layouts  8.63 us (4%)
    ppermute x12, waiting for transfers between devices, send_along(): moved[shift] = lax.ppermute(arrays[shift], 'tensor', pairs)  52.2 us
    all_to_all x4, waiting for transfers between devices, exchange(): lax.all_to_all(states, 'req', split_axis=split_axis, concat_axis=0, axis_...  44.9 us
    ppermute x12, starting transfers between devices, send_along(): moved[shift] = lax.ppermute(arrays[shift], 'tensor', pairs)  40.8 us
    all_to_all x4, starting transfers between devices, exchange(): lax.all_to_all(states, 'req', split_axis=split_axis, concat_axis=0, axis_...  39.6 us
    pallas_call x3, Pallas kernels, session_call(): pl.pallas_call(kernel, grid_spec=pltpu.PrefetchScalarGridSpec(num_scalar_...  19.8 us
    pallas_call x6, Pallas kernels, local_call(): pl.pallas_call(kernel, in_specs=[smem] + [vmem] * len(arrays), out_specs=...  4.94 us
    unnamed x35, local copies, waits for them, and re-layouts  4.66 us
  transfers between devices with their start and end apart: 16, of which 15 were waited for; matrix products, arithmetic and copies ran while one was open for 0% of the time, Pallas kernels for 12%

profile of v7, /device:TPU:1, one launch (start us, length us, event | category | flops | bytes accessed | tf_op | source)
XLA Modules:
  0.0 218.6 jit_solution(3339686877051188089)
XLA Ops:
  0.6 2.1 copy.22
  2.8 16.9 %all-to-all-start = ((bf16[1,6,32,16,128]{4,3,1,0,2:T(8,128)(2,1)}), bf16[1,6,32,16,128]{4,3,1,0,2:T(8,128)(2,1)S(1)}, u32[]{:S(2)}, u32[]{:S(2)}) async-start(bf16[1,6,32,16,128]{4,3,1,0,2:T(8,128)(2,1)} %copy.22), calls=%async_computation | async-start | bytes 1572864 | tf_op jit(solution)/shard_map/all_to_all | solution.py:176
  20.5 3.2 %collective-permute-start = (bf16[72,2432]{1,0:T(8,128)(2,1)S(1)}, bf16[72,2432]{1,0:T(8,128)(2,1)S(1)}, u32[]{:S(2)}, u32[]{:S(2)}) collective-permute-start(bf16[72,2432]{1,0:T(8,128)(2,1)S(1)} %get-tuple-element.30), channel_id=1, source_target_pairs={{0,4},{1,5},{2,6},{3,7},{4,8},{5,9},{6,10},{7,11},{8,12},{9,13},{1... | collective-permute-start | bytes 1050632 | tf_op jit(solution)/shard_map/ppermute | solution.py:106
  23.7 4.5 %collective-permute-start.1 = (bf16[72,2432]{1,0:T(8,128)(2,1)S(1)}, bf16[72,2432]{1,0:T(8,128)(2,1)S(1)}, u32[]{:S(2)}, u32[]{:S(2)}) collective-permute-start(bf16[72,2432]{1,0:T(8,128)(2,1)S(1)} %get-tuple-element.31), channel_id=1, source_target_pairs={{0,8},{1,9},{2,10},{3,11},{4,12},{5,13},{6,14},{7,15},{8,0},{9,1},... | collective-permute-start | bytes 1050632 | tf_op jit(solution)/shard_map/ppermute | solution.py:106
  28.2 3.0 %collective-permute-start.2 = (bf16[72,2432]{1,0:T(8,128)(2,1)S(1)}, bf16[72,2432]{1,0:T(8,128)(2,1)S(1)}, u32[]{:S(2)}, u32[]{:S(2)}) collective-permute-start(bf16[72,2432]{1,0:T(8,128)(2,1)S(1)} %get-tuple-element.32), channel_id=1, source_target_pairs={{0,12},{1,13},{2,14},{3,15},{4,0},{5,1},{6,2},{7,3},{8,4},{9,5},{1... | collective-permute-start | bytes 1050632 | tf_op jit(solution)/shard_map/ppermute | solution.py:106
  31.2 2.1 collective-permute-done.refs_1_
  33.3 8.6 %collective-permute-done.1.refs_2_ = bf16[72,2432]{1,0:T(8,128)(2,1)S(1)} collective-permute-done((bf16[72,2432]{1,0:T(8,128)(2,1)S(1)}, bf16[72,2432]{1,0:T(8,128)(2,1)S(1)}, u32[]{:S(2)}, u32[]{:S(2)}) %collective-permute-start.1) | collective-permute-done | bytes 350240 | tf_op jit(solution)/shard_map/ppermute | solution.py:106
  43.7 3.1 %collective-permute-start.3 = (bf16[4,72,896]{2,1,0:T(8,128)(2,1)S(1)}, bf16[4,72,896]{2,1,0:T(8,128)(2,1)S(1)}, u32[]{:S(2)}, u32[]{:S(2)}) collective-permute-start(bf16[4,72,896]{2,1,0:T(8,128)(2,1)S(1)} %get-tuple-element.33), channel_id=1, source_target_pairs={{0,1},{1,2},{2,3},{3,0},{4,5},{5,6},{6,7},{7,4},{8,9},{9,10},{10,1... | collective-permute-start | bytes 1548296 | tf_op jit(solution)/shard_map/ppermute | solution.py:106
  47.6 3.4 %cache_rows.1.rows_ref = s32[192]{0:T(256)} custom-call(s32[192]{0:T(256)} %reshape.26.sessions_ref, s32[192]{0:T(256)} %owners_ref.1, s32[192]{0:T(256)} %slots_ref.1), custom_call_target="tpu_custom_call" | custom-call | tf_op jit(solution)/shard_map/cache_rows/pallas_call | solution.py:141
  51.0 10.4 %all-to-all-done = bf16[1,6,32,16,128]{4,3,1,0,2:T(8,128)(2,1)S(1)} async-done(((bf16[1,6,32,16,128]{4,3,1,0,2:T(8,128)(2,1)}), bf16[1,6,32,16,128]{4,3,1,0,2:T(8,128)(2,1)S(1)}, u32[]{:S(2)}, u32[]{:S(2)}) %all-to-all-start) | async-done | bytes 786464 | tf_op jit(solution)/shard_map/all_to_all | solution.py:176
  63.8 8.9 %all-to-all-start.1 = ((bf16[32,6,16,128]{3,2,1,0:T(8,128)(2,1)}), bf16[32,6,16,128]{3,2,1,0:T(8,128)(2,1)S(1)}, u32[]{:S(2)}, u32[]{:S(2)}) async-start(bf16[32,6,16,128]{3,2,1,0:T(8,128)(2,1)} %bitcast.8), calls=%async_computation.1 | async-start | bytes 1572864 | tf_op jit(solution)/shard_map/all_to_all | solution.py:176
  72.7 3.4 %collective-permute-start.4 = (bf16[4,72,896]{2,1,0:T(8,128)(2,1)S(1)}, bf16[4,72,896]{2,1,0:T(8,128)(2,1)S(1)}, u32[]{:S(2)}, u32[]{:S(2)}) collective-permute-start(bf16[4,72,896]{2,1,0:T(8,128)(2,1)S(1)} %get-tuple-element.37), channel_id=1, source_target_pairs={{0,2},{1,3},{2,0},{3,1},{4,6},{5,7},{6,4},{7,5},{8,10},{9,11},{10,... | collective-permute-start | bytes 1548296 | tf_op jit(solution)/shard_map/ppermute | solution.py:106
  76.1 2.8 %collective-permute-start.5 = (bf16[4,72,896]{2,1,0:T(8,128)(2,1)S(1)}, bf16[4,72,896]{2,1,0:T(8,128)(2,1)S(1)}, u32[]{:S(2)}, u32[]{:S(2)}) collective-permute-start(bf16[4,72,896]{2,1,0:T(8,128)(2,1)S(1)} %get-tuple-element.38), channel_id=1, source_target_pairs={{0,3},{1,0},{2,1},{3,2},{4,7},{5,4},{6,5},{7,6},{8,11},{9,8},{10,9... | collective-permute-start | bytes 1548296 | tf_op jit(solution)/shard_map/ppermute | solution.py:106
  79.0 10.2 %collective-permute-done.4.refs_2_ = bf16[4,72,896]{2,1,0:T(8,128)(2,1)S(1)} collective-permute-done((bf16[4,72,896]{2,1,0:T(8,128)(2,1)S(1)}, bf16[4,72,896]{2,1,0:T(8,128)(2,1)S(1)}, u32[]{:S(2)}, u32[]{:S(2)}) %collective-permute-start.4) | collective-permute-done | bytes 516128 | tf_op jit(solution)/shard_map/ppermute | solution.py:106
  89.2 10.0 %collective-permute-done.5.refs_3_ = bf16[4,72,896]{2,1,0:T(8,128)(2,1)S(1)} collective-permute-done((bf16[4,72,896]{2,1,0:T(8,128)(2,1)S(1)}, bf16[4,72,896]{2,1,0:T(8,128)(2,1)S(1)}, u32[]{:S(2)}, u32[]{:S(2)}) %collective-permute-start.5) | collective-permute-done | bytes 516128 | tf_op jit(solution)/shard_map/ppermute | solution.py:106
  101.0 8.3 %delta_states.1 = (f32[32,6,16,128]{3,2,1,0:T(8,128)}, f32[6,8,128]{2,1,0:T(8,128)S(1)}) custom-call(s32[4]{0:T(128)S(1)} %pad_add_fusion.place_ref, s32[192]{0:T(256)S(1)} %copy-done.10, s32[192]{0:T(256)S(1)} %copy-done.11, bf16[1152,896]{1,0:T(8,128)(2,1)S(1)} %bitcast.21, bf16[1152,896]{1,0:T(8,128)(2,1)S(1)} %bitcast.22, ...), custom_call_target="tpu_custom_call" | custom-call | flops 4000000000 | bytes 8388608 | tf_op jit(solution)/shard_map/delta_states/pallas_call | solution.py:303
  109.3 5.1 %all-to-all-done.1.start_ref = bf16[32,6,16,128]{3,2,1,0:T(8,128)(2,1)S(1)} async-done(((bf16[32,6,16,128]{3,2,1,0:T(8,128)(2,1)}), bf16[32,6,16,128]{3,2,1,0:T(8,128)(2,1)S(1)}, u32[]{:S(2)}, u32[]{:S(2)}) %all-to-all-start.1) | async-done | bytes 786464 | tf_op jit(solution)/shard_map/all_to_all | solution.py:176
  116.1 2.7 %closing_states.1 = bf16[32,6,16,128]{3,2,1,0:T(8,128)(2,1)} custom-call(bf16[32,6,16,128]{3,2,1,0:T(8,128)(2,1)S(1)} %all-to-all-done.1.start_ref, f32[32,6,16,128]{3,2,1,0:T(8,128)S(1)} %copy-done.12, f32[6,8,128]{2,1,0:T(8,128)S(1)} %get-tuple-element.40.kept_ref), custom_call_target="tpu_custom_call" | custom-call | flops 1000000000 | bytes 8388608 | tf_op jit(solution)/shard_map/closing_states/pallas_call | solution.py:303
  118.8 7.9 %all-to-all-start.2 = ((bf16[32,6,16,128]{3,2,1,0:T(8,128)(2,1)}), bf16[32,6,16,128]{3,2,1,0:T(8,128)(2,1)S(1)}, u32[]{:S(2)}, u32[]{:S(2)}) async-start(bf16[32,6,16,128]{3,2,1,0:T(8,128)(2,1)} %closing_states.1), calls=%async_computation.2 | async-start | bytes 1572864 | tf_op jit(solution)/shard_map/all_to_all | solution.py:176
  128.0 8.8 %session_outputs.1 = bf16[1152,512]{1,0:T(8,128)(2,1)S(1)} custom-call(s32[4]{0:T(128)S(1)} %pad_add_fusion.place_ref, s32[192]{0:T(256)S(1)} %copy-done.10, s32[192]{0:T(256)S(1)} %copy-done.11, bf16[1152,896]{1,0:T(8,128)(2,1)S(1)} %bitcast.24, bf16[1152,896]{1,0:T(8,128)(2,1)S(1)} %bitcast.25, bf16[1152,896]{1,0:T(8,128)(2,1)S(1)} %bitcast.26, ...), custom_call_target="tpu_custom_call" | custom-call | flops 10000000000 | bytes 8388608 | tf_op jit(solution)/shard_map/session_outputs/pallas_call | solution.py:303
  137.5 3.0 %collective-permute-start.6 = (bf16[4,72,512]{2,1,0:T(8,128)(2,1)S(1)}, bf16[4,72,512]{2,1,0:T(8,128)(2,1)S(1)}, u32[]{:S(2)}, u32[]{:S(2)}) collective-permute-start(bf16[4,72,512]{2,1,0:T(8,128)(2,1)S(1)} %get-tuple-element.44), channel_id=1, source_target_pairs={{0,1},{1,2},{2,3},{3,0},{4,5},{5,6},{6,7},{7,4},{8,9},{9,10},{10,1... | collective-permute-start | bytes 884744 | tf_op jit(solution)/shard_map/ppermute | solution.py:106
  140.5 4.4 %collective-permute-start.7 = (bf16[4,72,512]{2,1,0:T(8,128)(2,1)S(1)}, bf16[4,72,512]{2,1,0:T(8,128)(2,1)S(1)}, u32[]{:S(2)}, u32[]{:S(2)}) collective-permute-start(bf16[4,72,512]{2,1,0:T(8,128)(2,1)S(1)} %get-tuple-element.45), channel_id=1, source_target_pairs={{0,2},{1,3},{2,0},{3,1},{4,6},{5,7},{6,4},{7,5},{8,10},{9,11},{10,... | collective-permute-start | bytes 884744 | tf_op jit(solution)/shard_map/ppermute | solution.py:106
  144.8 2.2 collective-permute-start.8
  147.0 1.9 collective-permute-done.6.refs_1_
  149.0 7.2 %collective-permute-done.7.refs_2_ = bf16[4,72,512]{2,1,0:T(8,128)(2,1)S(1)} collective-permute-done((bf16[4,72,512]{2,1,0:T(8,128)(2,1)S(1)}, bf16[4,72,512]{2,1,0:T(8,128)(2,1)S(1)}, u32[]{:S(2)}, u32[]{:S(2)}) %collective-permute-start.7) | collective-permute-done | bytes 294944 | tf_op jit(solution)/shard_map/ppermute | solution.py:106
  158.1 10.3 %all-to-all-done.2 = bf16[32,6,16,128]{3,2,1,0:T(8,128)(2,1)S(1)} async-done(((bf16[32,6,16,128]{3,2,1,0:T(8,128)(2,1)}), bf16[32,6,16,128]{3,2,1,0:T(8,128)(2,1)S(1)}, u32[]{:S(2)}, u32[]{:S(2)}) %all-to-all-start.2) | async-done | bytes 786464 | tf_op jit(solution)/shard_map/all_to_all | solution.py:176
  170.1 5.8 %all-to-all-start.3 = ((bf16[32,6,16,128]{3,2,1,0:T(8,128)(2,1)}), bf16[32,6,16,128]{3,2,1,0:T(8,128)(2,1)S(1)}, u32[]{:S(2)}, u32[]{:S(2)}) async-start(bf16[32,6,16,128]{3,2,1,0:T(8,128)(2,1)} %bitcast.14), calls=%async_computation.3 | async-start | bytes 1572864 | tf_op jit(solution)/shard_map/all_to_all | solution.py:176
  175.9 5.0 %collective-permute-start.9 = (bf16[72,2048]{1,0:T(8,128)(2,1)S(1)}, bf16[72,2048]{1,0:T(8,128)(2,1)S(1)}, u32[]{:S(2)}, u32[]{:S(2)}) collective-permute-start(bf16[72,2048]{1,0:T(8,128)(2,1)S(1)} %get-tuple-element.52), channel_id=1, source_target_pairs={{0,4},{1,5},{2,6},{3,7},{4,8},{5,9},{6,10},{7,11},{8,12},{9,13},{1... | collective-permute-start | bytes 884744 | tf_op jit(solution)/shard_map/ppermute | solution.py:106
  181.0 3.2 %collective-permute-start.10 = (bf16[72,2048]{1,0:T(8,128)(2,1)S(1)}, bf16[72,2048]{1,0:T(8,128)(2,1)S(1)}, u32[]{:S(2)}, u32[]{:S(2)}) collective-permute-start(bf16[72,2048]{1,0:T(8,128)(2,1)S(1)} %get-tuple-element.53), channel_id=1, source_target_pairs={{0,8},{1,9},{2,10},{3,11},{4,12},{5,13},{6,14},{7,15},{8,0},{9,1},... | collective-permute-start | bytes 884744 | tf_op jit(solution)/shard_map/ppermute | solution.py:106
  184.2 3.0 %collective-permute-start.11 = (bf16[72,2048]{1,0:T(8,128)(2,1)S(1)}, bf16[72,2048]{1,0:T(8,128)(2,1)S(1)}, u32[]{:S(2)}, u32[]{:S(2)}) collective-permute-start(bf16[72,2048]{1,0:T(8,128)(2,1)S(1)} %get-tuple-element.54), channel_id=1, source_target_pairs={{0,12},{1,13},{2,14},{3,15},{4,0},{5,1},{6,2},{7,3},{8,4},{9,5},{1... | collective-permute-start | bytes 884744 | tf_op jit(solution)/shard_map/ppermute | solution.py:106
  188.3 7.2 %collective-permute-done.10.refs_2_ = bf16[72,2048]{1,0:T(8,128)(2,1)S(1)} collective-permute-done((bf16[72,2048]{1,0:T(8,128)(2,1)S(1)}, bf16[72,2048]{1,0:T(8,128)(2,1)S(1)}, u32[]{:S(2)}, u32[]{:S(2)}) %collective-permute-start.10) | collective-permute-done | bytes 294944 | tf_op jit(solution)/shard_map/ppermute | solution.py:106
  198.5 19.1 %all-to-all-done.3 = bf16[32,6,16,128]{3,2,1,0:T(8,128)(2,1)S(1)} async-done(((bf16[32,6,16,128]{3,2,1,0:T(8,128)(2,1)}), bf16[32,6,16,128]{3,2,1,0:T(8,128)(2,1)S(1)}, u32[]{:S(2)}, u32[]{:S(2)}) %all-to-all-start.3) | async-done | bytes 786464 | tf_op jit(solution)/shard_map/all_to_all | solution.py:176
  (55 shorter events, 19.9 us)
Async XLA Ops:
  2.8 17.0 %copy-start = (bf16[72,8192]{1,0:T(8,128)(2,1)S(1)}, bf16[72,8192]{1,0:T(8,128)(2,1)}, u32[]{:S(2)}) copy-start(bf16[72,8192]{1,0:T(8,128)(2,1)} %x_ref.1) | copy-start | bytes 3538948
  2.8 17.0 %copy-start.5 = (bf16[72,512]{1,0:T(8,128)(2,1)S(1)}, bf16[72,512]{1,0:T(8,128)(2,1)}, u32[]{:S(2)}) copy-start(bf16[72,512]{1,0:T(8,128)(2,1)} %b_ref.1) | copy-start | bytes 221188
  2.8 17.0 %copy-start.6 = (bf16[72,512]{1,0:T(8,128)(2,1)S(1)}, bf16[72,512]{1,0:T(8,128)(2,1)}, u32[]{:S(2)}) copy-start(bf16[72,512]{1,0:T(8,128)(2,1)} %c_ref.1) | copy-start | bytes 221188
  2.8 17.0 %copy-start.7 = (bf16[72,128]{1,0:T(8,128)(2,1)S(1)}, bf16[72,128]{1,0:T(8,128)(2,1)}, u32[]{:S(2)}) copy-start(bf16[72,128]{1,0:T(8,128)(2,1)} %dt_ref.1) | copy-start | bytes 55300
  2.8 58.6 %all-to-all-start = ((bf16[1,6,32,16,128]{4,3,1,0,2:T(8,128)(2,1)}), bf16[1,6,32,16,128]{4,3,1,0,2:T(8,128)(2,1)S(1)}, u32[]{:S(2)}, u32[]{:S(2)}) async-start(bf16[1,6,32,16,128]{4,3,1,0,2:T(8,128)(2,1)} %copy.22), calls=%async_computation | async-start | bytes 1572864 | tf_op jit(solution)/shard_map/all_to_all | solution.py:176
  19.8 27.1 %copy-start.13 = (s32[32,6]{0,1:T(8,128)S(1)}, s32[32,6]{0,1:T(8,128)}, u32[]{:S(2)}) copy-start(s32[32,6]{0,1:T(8,128)} %param.20) | copy-start | bytes 2308
  20.5 12.8 %collective-permute-start = (bf16[72,2432]{1,0:T(8,128)(2,1)S(1)}, bf16[72,2432]{1,0:T(8,128)(2,1)S(1)}, u32[]{:S(2)}, u32[]{:S(2)}) collective-permute-start(bf16[72,2432]{1,0:T(8,128)(2,1)S(1)} %get-tuple-element.30), channel_id=1, source_target_pairs={{0,4},{1,5},{2,6},{3,7},{4,8},{5,9},{6,10},{7,11},{8,12},{9,13},{1... | collective-permute-start | bytes 1050632 | tf_op jit(solution)/shard_map/ppermute | solution.py:106
  23.7 18.2 %collective-permute-start.1 = (bf16[72,2432]{1,0:T(8,128)(2,1)S(1)}, bf16[72,2432]{1,0:T(8,128)(2,1)S(1)}, u32[]{:S(2)}, u32[]{:S(2)}) collective-permute-start(bf16[72,2432]{1,0:T(8,128)(2,1)S(1)} %get-tuple-element.31), channel_id=1, source_target_pairs={{0,8},{1,9},{2,10},{3,11},{4,12},{5,13},{6,14},{7,15},{8,0},{9,1},... | collective-permute-start | bytes 1050632 | tf_op jit(solution)/shard_map/ppermute | solution.py:106
  28.2 14.8 %collective-permute-start.2 = (bf16[72,2432]{1,0:T(8,128)(2,1)S(1)}, bf16[72,2432]{1,0:T(8,128)(2,1)S(1)}, u32[]{:S(2)}, u32[]{:S(2)}) collective-permute-start(bf16[72,2432]{1,0:T(8,128)(2,1)S(1)} %get-tuple-element.32), channel_id=1, source_target_pairs={{0,12},{1,13},{2,14},{3,15},{4,0},{5,1},{6,2},{7,3},{8,4},{9,5},{1... | collective-permute-start | bytes 1050632 | tf_op jit(solution)/shard_map/ppermute | solution.py:106
  43.7 20.0 %collective-permute-start.3 = (bf16[4,72,896]{2,1,0:T(8,128)(2,1)S(1)}, bf16[4,72,896]{2,1,0:T(8,128)(2,1)S(1)}, u32[]{:S(2)}, u32[]{:S(2)}) collective-permute-start(bf16[4,72,896]{2,1,0:T(8,128)(2,1)S(1)} %get-tuple-element.33), channel_id=1, source_target_pairs={{0,1},{1,2},{2,3},{3,0},{4,5},{5,6},{6,7},{7,4},{8,9},{9,10},{10,1... | collective-permute-start | bytes 1548296 | tf_op jit(solution)/shard_map/ppermute | solution.py:106
  63.7 15.2 %copy-start.15 = (f32[8]{0:T(128)S(1)}, f32[8]{0:T(128)}, u32[]{:S(2)}) copy-start(f32[8]{0:T(128)} %param.16) | copy-start | bytes 100
  63.7 15.2 %copy-start.16 = (f32[8]{0:T(128)S(1)}, f32[8]{0:T(128)}, u32[]{:S(2)}) copy-start(f32[8]{0:T(128)} %param.17) | copy-start | bytes 100
  63.8 35.4 %copy-start.3 = (bf16[4,72,896]{2,1,0:T(8,128)(2,1)}, bf16[4,72,896]{2,1,0:T(8,128)(2,1)S(1)}, u32[]{:S(2)}) copy-start(bf16[4,72,896]{2,1,0:T(8,128)(2,1)S(1)} %collective-permute-done.3.refs_1_) | copy-start | bytes 1548292
  63.8 50.6 %all-to-all-start.1 = ((bf16[32,6,16,128]{3,2,1,0:T(8,128)(2,1)}), bf16[32,6,16,128]{3,2,1,0:T(8,128)(2,1)S(1)}, u32[]{:S(2)}, u32[]{:S(2)}) async-start(bf16[32,6,16,128]{3,2,1,0:T(8,128)(2,1)} %bitcast.8), calls=%async_computation.1 | async-start | bytes 1572864 | tf_op jit(solution)/shard_map/all_to_all | solution.py:176
  72.7 16.5 %collective-permute-start.4 = (bf16[4,72,896]{2,1,0:T(8,128)(2,1)S(1)}, bf16[4,72,896]{2,1,0:T(8,128)(2,1)S(1)}, u32[]{:S(2)}, u32[]{:S(2)}) collective-permute-start(bf16[4,72,896]{2,1,0:T(8,128)(2,1)S(1)} %get-tuple-element.37), channel_id=1, source_target_pairs={{0,2},{1,3},{2,0},{3,1},{4,6},{5,7},{6,4},{7,5},{8,10},{9,11},{10,... | collective-permute-start | bytes 1548296 | tf_op jit(solution)/shard_map/ppermute | solution.py:106
  76.1 23.0 %collective-permute-start.5 = (bf16[4,72,896]{2,1,0:T(8,128)(2,1)S(1)}, bf16[4,72,896]{2,1,0:T(8,128)(2,1)S(1)}, u32[]{:S(2)}, u32[]{:S(2)}) collective-permute-start(bf16[4,72,896]{2,1,0:T(8,128)(2,1)S(1)} %get-tuple-element.38), channel_id=1, source_target_pairs={{0,3},{1,0},{2,1},{3,2},{4,7},{5,4},{6,5},{7,6},{8,11},{9,8},{10,9... | collective-permute-start | bytes 1548296 | tf_op jit(solution)/shard_map/ppermute | solution.py:106
  99.2 1.0 copy-start.4
  100.2 0.7 copy-start.10
  100.2 0.7 copy-start.11
  114.4 4.4 %copy-start.1 = (bf16[32,6,16,128]{3,2,1,0:T(8,128)(2,1)}, bf16[32,6,16,128]{3,2,1,0:T(8,128)(2,1)S(1)}, u32[]{:S(2)}) copy-start(bf16[32,6,16,128]{3,2,1,0:T(8,128)(2,1)S(1)} %all-to-all-done.1.start_ref) | copy-start | bytes 2359300
  114.4 1.7 copy-start.12
  118.8 7.9 %copy-start.14 = (f32[8]{0:T(128)S(1)}, f32[8]{0:T(128)}, u32[]{:S(2)}) copy-start(f32[8]{0:T(128)} %param.18) | copy-start | bytes 100
  118.8 49.6 %all-to-all-start.2 = ((bf16[32,6,16,128]{3,2,1,0:T(8,128)(2,1)}), bf16[32,6,16,128]{3,2,1,0:T(8,128)(2,1)S(1)}, u32[]{:S(2)}, u32[]{:S(2)}) async-start(bf16[32,6,16,128]{3,2,1,0:T(8,128)(2,1)} %closing_states.1), calls=%async_computation.2 | async-start | bytes 1572864 | tf_op jit(solution)/shard_map/all_to_all | solution.py:176
  126.8 1.1 copy-start.2
  136.8 31.6 %copy-start.9 = (s32[192]{0:T(256)S(1)}, s32[192]{0:T(256)}, u32[]{:S(2)}) copy-start(s32[192]{0:T(256)} %cache_rows.1.rows_ref) | copy-start | bytes 2308
  137.5 11.5 %collective-permute-start.6 = (bf16[4,72,512]{2,1,0:T(8,128)(2,1)S(1)}, bf16[4,72,512]{2,1,0:T(8,128)(2,1)S(1)}, u32[]{:S(2)}, u32[]{:S(2)}) collective-permute-start(bf16[4,72,512]{2,1,0:T(8,128)(2,1)S(1)} %get-tuple-element.44), channel_id=1, source_target_pairs={{0,1},{1,2},{2,3},{3,0},{4,5},{5,6},{6,7},{7,4},{8,9},{9,10},{10,1... | collective-permute-start | bytes 884744 | tf_op jit(solution)/shard_map/ppermute | solution.py:106
  140.5 15.7 %collective-permute-start.7 = (bf16[4,72,512]{2,1,0:T(8,128)(2,1)S(1)}, bf16[4,72,512]{2,1,0:T(8,128)(2,1)S(1)}, u32[]{:S(2)}, u32[]{:S(2)}) collective-permute-start(bf16[4,72,512]{2,1,0:T(8,128)(2,1)S(1)} %get-tuple-element.45), channel_id=1, source_target_pairs={{0,2},{1,3},{2,0},{3,1},{4,6},{5,7},{6,4},{7,5},{8,10},{9,11},{10,... | collective-permute-start | bytes 884744 | tf_op jit(solution)/shard_map/ppermute | solution.py:106
  144.8 12.7 %collective-permute-start.8 = (bf16[4,72,512]{2,1,0:T(8,128)(2,1)S(1)}, bf16[4,72,512]{2,1,0:T(8,128)(2,1)S(1)}, u32[]{:S(2)}, u32[]{:S(2)}) collective-permute-start(bf16[4,72,512]{2,1,0:T(8,128)(2,1)S(1)} %get-tuple-element.46), channel_id=1, source_target_pairs={{0,3},{1,0},{2,1},{3,2},{4,7},{5,4},{6,5},{7,6},{8,11},{9,8},{10,9... | collective-permute-start | bytes 884744 | tf_op jit(solution)/shard_map/ppermute | solution.py:106
  170.1 47.5 %all-to-all-start.3 = ((bf16[32,6,16,128]{3,2,1,0:T(8,128)(2,1)}), bf16[32,6,16,128]{3,2,1,0:T(8,128)(2,1)S(1)}, u32[]{:S(2)}, u32[]{:S(2)}) async-start(bf16[32,6,16,128]{3,2,1,0:T(8,128)(2,1)} %bitcast.14), calls=%async_computation.3 | async-start | bytes 1572864 | tf_op jit(solution)/shard_map/all_to_all | solution.py:176
  175.9 12.4 %collective-permute-start.9 = (bf16[72,2048]{1,0:T(8,128)(2,1)S(1)}, bf16[72,2048]{1,0:T(8,128)(2,1)S(1)}, u32[]{:S(2)}, u32[]{:S(2)}) collective-permute-start(bf16[72,2048]{1,0:T(8,128)(2,1)S(1)} %get-tuple-element.52), channel_id=1, source_target_pairs={{0,4},{1,5},{2,6},{3,7},{4,8},{5,9},{6,10},{7,11},{8,12},{9,13},{1... | collective-permute-start | bytes 884744 | tf_op jit(solution)/shard_map/ppermute | solution.py:106
  181.0 14.5 %collective-permute-start.10 = (bf16[72,2048]{1,0:T(8,128)(2,1)S(1)}, bf16[72,2048]{1,0:T(8,128)(2,1)S(1)}, u32[]{:S(2)}, u32[]{:S(2)}) collective-permute-start(bf16[72,2048]{1,0:T(8,128)(2,1)S(1)} %get-tuple-element.53), channel_id=1, source_target_pairs={{0,8},{1,9},{2,10},{3,11},{4,12},{5,13},{6,14},{7,15},{8,0},{9,1},... | collective-permute-start | bytes 884744 | tf_op jit(solution)/shard_map/ppermute | solution.py:106
  184.2 12.7 %collective-permute-start.11 = (bf16[72,2048]{1,0:T(8,128)(2,1)S(1)}, bf16[72,2048]{1,0:T(8,128)(2,1)S(1)}, u32[]{:S(2)}, u32[]{:S(2)}) collective-permute-start(bf16[72,2048]{1,0:T(8,128)(2,1)S(1)} %get-tuple-element.54), channel_id=1, source_target_pairs={{0,12},{1,13},{2,14},{3,15},{4,0},{5,1},{6,2},{7,3},{8,4},{9,5},{1... | collective-permute-start | bytes 884744 | tf_op jit(solution)/shard_map/ppermute | solution.py:106
  (1 other events, 0.7 us)

commit v8 on v7

--- a/solution.py
+++ b/solution.py
@@ -28,6 +28,10 @@
         out_ref[:, width + 2 * STATE :] = dt_ref[...]
 
 
+def long_first(count):
+    return sorted(range(count), key=lambda d: (d != 0, -min(d, count - d)))
+
+
 def turn_in_kernel(place_ref, *refs):
     half = len(refs) // 2
     extra = 2 * STATE + HEADS
@@ -35,9 +39,9 @@
     for shift in range(half):
         target = lax.rem(place_ref[3] + shift, half)
         columns = pl.ds(pl.multiple_of(target * width, LANES), width)
-        for row in range(half):
-            refs[half + shift][row, :, :width] = refs[row][:, columns]
-            refs[half + shift][row, :, width:] = refs[row][:, half * width :]
+        for place, row in enumerate(long_first(half)):
+            refs[half + shift][row, :, :width] = refs[place][:, columns]
+            refs[half + shift][row, :, width:] = refs[place][:, half * width :]
 
 
 def gather_kernel(place_ref, *refs):
@@ -101,7 +105,7 @@
 
 def send_along(arrays, count, along_y):
     moved = list(arrays)
-    for shift in sorted(range(1, count), key=lambda d: -min(d, count - d)):
+    for shift in long_first(count)[1:]:
         pairs = moved_by(count, shift, 0) if along_y else moved_by(count, 0, shift)
         moved[shift] = lax.ppermute(arrays[shift], "tensor", pairs)
     return moved
@@ -109,17 +113,19 @@
 
 def member_at(spot, count):
     chips = count // 2
-    return lax.rem(lax.rem(spot, chips) * 3, chips) * 2 + spot // chips
+    core = lax.rem(spot, 2)
+    return lax.rem(spot // 2 * 7 + core * (chips // 2), chips) * 2 + core
 
 
 def spot_of(member, count):
     chips = count // 2
-    return lax.rem(member, 2) * chips + lax.rem(member // 2 * 11, chips)
+    core = lax.rem(member, 2)
+    return lax.rem((member // 2 + core * (chips // 2)) * 7, chips) * 2 + core
 
 
 def members(count):
     chips = count // 2
-    return [spot % chips * 3 % chips * 2 + spot // chips for spot in range(count)]
+    return [(spot // 2 * 7 + spot % 2 * (chips // 2)) % chips * 2 + spot % 2 for spot in range(count)]
 
 
 def rows_kernel(sessions_ref, owners_ref, slots_ref, rows_ref, *, slot_count):
@@ -178,27 +184,43 @@
     )
 
 
-def token_steps(place_ref, steps_ref, bias_ref, a_log_ref, length, heads):
+def steps_kernel(
+    place_ref, sessions_ref, lengths_ref, raw_ref, bias_ref, a_log_ref, step_ref, cum_ref, *, heads
+):
     f32 = jnp.float32
+    slot_count = step_ref.shape[0]
     lane_from = lax.broadcasted_iota(jnp.int32, (HEADS, LANES), 0)
     lane_to = lax.broadcasted_iota(jnp.int32, (HEADS, LANES), 1)
-    chosen = (lane_from == lane_to + place_ref[1] * heads) & (lane_to < heads)
-    raw = jnp.dot(steps_ref[...], chosen.astype(jnp.bfloat16), preferred_element_type=f32)
     row_index = lax.broadcasted_iota(jnp.int32, (MAXLEN, LANES), 0)
+    lane_index = lax.broadcasted_iota(jnp.int32, (MAXLEN, LANES), 1)
+    raw = jnp.zeros((MAXLEN, LANES), f32)
+    length = jnp.zeros((MAXLEN, LANES), jnp.int32)
+    for slot in range(slot_count):
+        head = lane_to - slot * heads
+        chosen = (lane_from == head + place_ref[1] * heads) & (head >= 0) & (head < heads)
+        raw += jnp.dot(
+            raw_ref[slot * MAXLEN : (slot + 1) * MAXLEN, :],
+            chosen.astype(jnp.bfloat16),
+            preferred_element_type=f32,
+        )
+        session = sessions_ref[place_ref[0] * slot_count + slot]
+        mine = (lane_index >= slot * heads) & (lane_index < (slot + 1) * heads)
+        length = jnp.where(mine, lengths_ref[session], length)
     shifted = raw + bias_ref[...]
     soft = jnp.maximum(shifted, 0.0) + jnp.log(1.0 + jnp.exp(-jnp.abs(shifted)))
-    live = row_index < length
-    step = jnp.where(live, soft, 0.0)
+    step = jnp.where(row_index < length, soft, 0.0)
     t_index = lax.broadcasted_iota(jnp.int32, (MAXLEN, MAXLEN), 0)
     u_index = lax.broadcasted_iota(jnp.int32, (MAXLEN, MAXLEN), 1)
-    causal = t_index >= u_index
     cum = jnp.dot(
-        causal.astype(f32),
+        (t_index >= u_index).astype(f32),
         step * -jnp.exp(a_log_ref[...]),
         precision=lax.Precision.HIGHEST,
         preferred_element_type=f32,
     )
-    return step, cum, live, causal
+    for slot in range(slot_count):
+        back = (LANES - slot * heads) % LANES
+        step_ref[slot] = pltpu.roll(step, back, 1) if back else step
+        cum_ref[slot] = pltpu.roll(cum, back, 1) if back else cum
 
 
 def spread(columns, first, left):
@@ -212,11 +234,9 @@
 
 
 def delta_kernel(
-    place_ref, sessions_ref, lengths_ref, x_ref, b_ref, steps_ref, a_log_ref, bias_ref,
-    delta_ref, kept_ref, *, heads, slot_count
+    x_ref, b_ref, step_ref, cum_ref, delta_ref, kept_ref, *, heads
 ):
-    length = lengths_ref[sessions_ref[place_ref[0] * slot_count + pl.program_id(0)]]
-    step, cum, _, _ = token_steps(place_ref, steps_ref, bias_ref, a_log_ref, length, heads)
+    step, cum = step_ref[0], cum_ref[0]
     last = cum[MAXLEN - 1 : MAXLEN, :]
     to_end = jnp.exp(last - cum) * step
     kept_ref[0] = jnp.broadcast_to(jnp.exp(last), kept_ref.shape[1:])
@@ -247,17 +267,19 @@
 
 
 def outputs_kernel(
-    place_ref, sessions_ref, lengths_ref, x_ref, b_ref, c_ref, steps_ref, start_ref, a_log_ref,
-    bias_ref, skip_ref, y_ref, *, heads, slot_count
+    place_ref, sessions_ref, lengths_ref, x_ref, b_ref, c_ref, step_ref, cum_ref, start_ref,
+    skip_ref, y_ref, *, heads, slot_count
 ):
     f32 = jnp.float32
     bf16 = jnp.bfloat16
     half = LANES
     width = heads * HEAD_DIM
     length = lengths_ref[sessions_ref[place_ref[0] * slot_count + pl.program_id(0)]]
-    step, cum, live, causal = token_steps(
-        place_ref, steps_ref, bias_ref, a_log_ref, length, heads
-    )
+    step, cum = step_ref[0], cum_ref[0]
+    live = lax.broadcasted_iota(jnp.int32, (MAXLEN, LANES), 0) < length
+    t_index = lax.broadcasted_iota(jnp.int32, (MAXLEN, MAXLEN), 0)
+    u_index = lax.broadcasted_iota(jnp.int32, (MAXLEN, MAXLEN), 1)
+    causal = t_index >= u_index
     drop_rows = (cum - jnp.log(step)).T
     grown = jnp.exp(cum)
     out_proj = c_ref[...]
@@ -365,7 +387,7 @@
     sent = local_call(
         turn_in_kernel,
         place,
-        send_along(sent, side, True),
+        [send_along(sent, side, True)[shift] for shift in long_first(side)],
         [shape((GROUPS, rows, width + extra), bf16)] * side,
         "turn_in",
     )
@@ -380,18 +402,15 @@
         "gather_tokens",
     ).reshape(tensor_size * rows, width + extra)
 
-    pad = ((0, 0), (0, LANES - heads))
-    a_row = jnp.pad(a_log[None, :], pad)
-    bias_row = jnp.pad(dt_bias[None, :], pad)
+    pad = ((0, 0), (0, LANES - slot_count * heads))
+    a_row = jnp.pad(jnp.tile(a_log, slot_count)[None, :], pad)
+    bias_row = jnp.pad(jnp.tile(dt_bias, slot_count)[None, :], pad)
     skip_row = jnp.repeat(d_skip, HEAD_DIM)[None, :]
     one_row = lambda j, *_: (0, 0)
     by_session = lambda j, *_: (j, 0)
     x_op = (packed, (MAXLEN, width), by_session)
     b_op = (packed, (MAXLEN, STATE), lambda j, *_: (j, width // STATE))
     c_op = (packed, (MAXLEN, STATE), lambda j, *_: (j, width // STATE + 1))
-    steps_op = (packed, (MAXLEN, HEADS), lambda j, *_: (j, width // STATE + 2))
-    a_op = (a_row, (1, LANES), one_row)
-    bias_op = (bias_row, (1, LANES), one_row)
     skip_op = (skip_row, (1, width), one_row)
     scalars = (place, sessions, lengths)
     sizes = dict(heads=heads, slot_count=slot_count)
@@ -400,11 +419,30 @@
     total_rows = tensor_size * rows
 
     kept_block = ((1, 8, LANES), lambda j, *_: (j, 0, 0))
+    step, cum = pl.pallas_call(
+        functools.partial(steps_kernel, heads=heads),
+        grid_spec=pltpu.PrefetchScalarGridSpec(
+            num_scalar_prefetch=len(scalars),
+            grid=(1,),
+            in_specs=[
+                pl.BlockSpec((total_rows, HEADS), lambda j, *_: (0, width // HEADS + 2)),
+                pl.BlockSpec((1, LANES), one_row),
+                pl.BlockSpec((1, LANES), one_row),
+            ],
+            out_specs=[pl.BlockSpec((slot_count, MAXLEN, LANES), lambda j, *_: (0, 0, 0))] * 2,
+        ),
+        out_shape=[shape((slot_count, MAXLEN, LANES), f32)] * 2,
+        compiler_params=pltpu.CompilerParams(vmem_limit_bytes=VMEM_LIMIT),
+        name="steps",
+    )(*scalars, packed, bias_row, a_row)
+    step_block = ((1, MAXLEN, LANES), lambda j, *_: (j, 0, 0))
+    step_op, cum_op = (step, *step_block), (cum, *step_block)
+
     delta, kept = session_call(
-        functools.partial(delta_kernel, **sizes),
-        scalars,
+        functools.partial(delta_kernel, heads=heads),
+        (),
         slot_count,
-        [x_op, b_op, steps_op, a_op, bias_op],
+        [x_op, b_op, step_op, cum_op],
         [
             (pltpu.HBM(state_shape, f32), piece_block, by_slot),
             (shape((slot_count, 8, LANES), f32), *kept_block),
@@ -413,11 +451,12 @@
         "delta_states",
     )
 
+    delta_held = pltpu.with_memory_space_constraint(delta, pltpu.HBM)
     (closing,) = session_call(
         functools.partial(closing_kernel, heads=heads),
         (),
         slot_count,
-        [(start, piece_block, by_slot), (delta, piece_block, by_slot), (kept, *kept_block)],
+        [(start, piece_block, by_slot), (delta_held, piece_block, by_slot), (kept, *kept_block)],
         [(pltpu.HBM(state_shape, bf16), piece_block, by_slot)],
         1_000_000_000,
         "closing_states",
@@ -431,7 +470,7 @@
         functools.partial(outputs_kernel, **sizes),
         scalars,
         slot_count,
-        [x_op, b_op, c_op, steps_op, start_op, a_op, bias_op, skip_op],
+        [x_op, b_op, c_op, step_op, cum_op, start_op, skip_op],
         [(shape((total_rows, width), bf16), (MAXLEN, width), by_session)],
         10_000_000_000,
         "session_outputs",

time: 221 us -> 224 us (1.014)
  local copies, waits for them, and re-layouts: 8.63 us -> 14.5 us
  waiting for transfers between devices: 97 us -> 93.1 us
  starting transfers between devices: 80.4 us -> 83.2 us
  Pallas kernels: 31.5 us -> 28.9 us
    unnamed x35 -> x49, local copies, waits for them, and re-layouts: 4.66 us -> 10.4 us
    pallas_call x3, Pallas kernels: 19.8 us -> 14.8 us  [session_call(): pl.pallas_call(kernel, grid_spec=pltpu.PrefetchScalarGridSpec(num_scalar_...]
    ppermute x12, waiting for transfers between devices: 52.2 us -> 48.9 us  [send_along(): moved[shift] = lax.ppermute(arrays[shift], 'tensor', pairs)]
    all_to_all x4, starting transfers between devices: 39.6 us -> 42.3 us  [exchange(): lax.all_to_all(states, 'req', split_axis=split_axis, concat_axis=0, axis_...]
  transfers between devices with their start and end apart: 16 -> 16, of which waited for: 15 -> 14; matrix products, arithmetic and copies ran while one was open for 0% -> 1% of each run, Pallas kernels for 12% -> 10%
where the time goes in v8:
time: 224 us; the launch traced here: 221 us
  waiting for transfers between devices  93.1 us (42%)
  starting transfers between devices  83.2 us (37%)
  Pallas kernels  28.9 us (13%)
  local copies, waits for them, and re-layouts  14.5 us (6%)
    ppermute x12, waiting for transfers between devices, send_along(): moved[shift] = lax.ppermute(arrays[shift], 'tensor', pairs)  48.9 us
    all_to_all x4, waiting for transfers between devices, exchange(): lax.all_to_all(states, 'req', split_axis=split_axis, concat_axis=0, axis_...  44.2 us
    all_to_all x4, starting transfers between devices, exchange(): lax.all_to_all(states, 'req', split_axis=split_axis, concat_axis=0, axis_...  42.3 us
    ppermute x12, starting transfers between devices, send_along(): moved[shift] = lax.ppermute(arrays[shift], 'tensor', pairs)  40.9 us
    pallas_call x3, Pallas kernels, session_call(): pl.pallas_call(kernel, grid_spec=pltpu.PrefetchScalarGridSpec(num_scalar_...  14.8 us
    unnamed x49, local copies, waits for them, and re-layouts  10.4 us
    pallas_call x6, Pallas kernels, local_call(): pl.pallas_call(kernel, in_specs=[smem] + [vmem] * len(arrays), out_specs=...  5.73 us
  transfers between devices with their start and end apart: 16, of which 14 were waited for; matrix products, arithmetic and copies ran while one was open for 1% of the time, Pallas kernels for 10%

profile of v8, /device:TPU:1, one launch (start us, length us, event | category | flops | bytes accessed | tf_op | source)
XLA Modules:
  0.0 220.8 jit_solution(12670744152745328503)
XLA Ops:
  0.6 2.1 copy.22
  2.8 16.9 %all-to-all-start = ((bf16[1,6,32,16,128]{4,3,1,0,2:T(8,128)(2,1)}), bf16[1,6,32,16,128]{4,3,1,0,2:T(8,128)(2,1)S(1)}, u32[]{:S(2)}, u32[]{:S(2)}) async-start(bf16[1,6,32,16,128]{4,3,1,0,2:T(8,128)(2,1)} %copy.22), calls=%async_computation | async-start | bytes 1572864 | tf_op jit(solution)/shard_map/all_to_all | solution.py:182
  20.5 4.8 %collective-permute-start = (bf16[72,2432]{1,0:T(8,128)(2,1)S(1)}, bf16[72,2432]{1,0:T(8,128)(2,1)S(1)}, u32[]{:S(2)}, u32[]{:S(2)}) collective-permute-start(bf16[72,2432]{1,0:T(8,128)(2,1)S(1)} %get-tuple-element.32), channel_id=1, source_target_pairs={{0,8},{1,9},{2,10},{3,11},{4,12},{5,13},{6,14},{7,15},{8,0},{9,1},... | collective-permute-start | bytes 1050632 | tf_op jit(solution)/shard_map/ppermute | solution.py:110
  25.3 2.3 %collective-permute-start.1 = (bf16[72,2432]{1,0:T(8,128)(2,1)S(1)}, bf16[72,2432]{1,0:T(8,128)(2,1)S(1)}, u32[]{:S(2)}, u32[]{:S(2)}) collective-permute-start(bf16[72,2432]{1,0:T(8,128)(2,1)S(1)} %get-tuple-element.33), channel_id=1, source_target_pairs={{0,4},{1,5},{2,6},{3,7},{4,8},{5,9},{6,10},{7,11},{8,12},{9,13},{1... | collective-permute-start | bytes 1050632 | tf_op jit(solution)/shard_map/ppermute | solution.py:110
  27.6 4.2 %collective-permute-start.2 = (bf16[72,2432]{1,0:T(8,128)(2,1)S(1)}, bf16[72,2432]{1,0:T(8,128)(2,1)S(1)}, u32[]{:S(2)}, u32[]{:S(2)}) collective-permute-start(bf16[72,2432]{1,0:T(8,128)(2,1)S(1)} %get-tuple-element.34), channel_id=1, source_target_pairs={{0,12},{1,13},{2,14},{3,15},{4,0},{5,1},{6,2},{7,3},{8,4},{9,5},{1... | collective-permute-start | bytes 1050632 | tf_op jit(solution)/shard_map/ppermute | solution.py:110
  33.5 8.0 %collective-permute-done.1.refs_2_ = bf16[72,2432]{1,0:T(8,128)(2,1)S(1)} collective-permute-done((bf16[72,2432]{1,0:T(8,128)(2,1)S(1)}, bf16[72,2432]{1,0:T(8,128)(2,1)S(1)}, u32[]{:S(2)}, u32[]{:S(2)}) %collective-permute-start.1) | collective-permute-done | bytes 350240 | tf_op jit(solution)/shard_map/ppermute | solution.py:110
  43.0 3.1 %collective-permute-start.3 = (bf16[4,72,896]{2,1,0:T(8,128)(2,1)S(1)}, bf16[4,72,896]{2,1,0:T(8,128)(2,1)S(1)}, u32[]{:S(2)}, u32[]{:S(2)}) collective-permute-start(bf16[4,72,896]{2,1,0:T(8,128)(2,1)S(1)} %get-tuple-element.35), channel_id=1, source_target_pairs={{0,1},{1,2},{2,3},{3,0},{4,5},{5,6},{6,7},{7,4},{8,9},{9,10},{10,1... | collective-permute-start | bytes 1548296 | tf_op jit(solution)/shard_map/ppermute | solution.py:110
  46.9 3.6 %cache_rows.1.rows_ref = s32[192]{0:T(256)} custom-call(s32[192]{0:T(256)} %reshape.28.sessions_ref, s32[192]{0:T(256)} %owners_ref.1, s32[192]{0:T(256)} %slots_ref.1), custom_call_target="tpu_custom_call" | custom-call | tf_op jit(solution)/shard_map/cache_rows/pallas_call | solution.py:147
  50.5 10.8 %all-to-all-done = bf16[1,6,32,16,128]{4,3,1,0,2:T(8,128)(2,1)S(1)} async-done(((bf16[1,6,32,16,128]{4,3,1,0,2:T(8,128)(2,1)}), bf16[1,6,32,16,128]{4,3,1,0,2:T(8,128)(2,1)S(1)}, u32[]{:S(2)}, u32[]{:S(2)}) %all-to-all-start) | async-done | bytes 786464 | tf_op jit(solution)/shard_map/all_to_all | solution.py:182
  63.7 8.3 %all-to-all-start.1 = ((bf16[32,6,16,128]{3,2,1,0:T(8,128)(2,1)}), bf16[32,6,16,128]{3,2,1,0:T(8,128)(2,1)S(1)}, u32[]{:S(2)}, u32[]{:S(2)}) async-start(bf16[32,6,16,128]{3,2,1,0:T(8,128)(2,1)} %bitcast.8), calls=%async_computation.1 | async-start | bytes 1572864 | tf_op jit(solution)/shard_map/all_to_all | solution.py:182
  72.0 3.4 %collective-permute-start.4 = (bf16[4,72,896]{2,1,0:T(8,128)(2,1)}, bf16[4,72,896]{2,1,0:T(8,128)(2,1)S(1)}, u32[]{:S(2)}, u32[]{:S(2)}) collective-permute-start(bf16[4,72,896]{2,1,0:T(8,128)(2,1)} %get-tuple-element.39), channel_id=1, source_target_pairs={{0,2},{1,3},{2,0},{3,1},{4,6},{5,7},{6,4},{7,5},{8,10},{9,11},{10,... | collective-permute-start | bytes 1548296 | tf_op jit(solution)/shard_map/ppermute | solution.py:110
  75.5 2.8 %collective-permute-start.5 = (bf16[4,72,896]{2,1,0:T(8,128)(2,1)S(1)}, bf16[4,72,896]{2,1,0:T(8,128)(2,1)S(1)}, u32[]{:S(2)}, u32[]{:S(2)}) collective-permute-start(bf16[4,72,896]{2,1,0:T(8,128)(2,1)S(1)} %get-tuple-element.40), channel_id=1, source_target_pairs={{0,3},{1,0},{2,1},{3,2},{4,7},{5,4},{6,5},{7,6},{8,11},{9,8},{10,9... | collective-permute-start | bytes 1548296 | tf_op jit(solution)/shard_map/ppermute | solution.py:110
  78.5 10.3 %collective-permute-done.4.refs_2_ = bf16[4,72,896]{2,1,0:T(8,128)(2,1)S(1)} collective-permute-done((bf16[4,72,896]{2,1,0:T(8,128)(2,1)}, bf16[4,72,896]{2,1,0:T(8,128)(2,1)S(1)}, u32[]{:S(2)}, u32[]{:S(2)}) %collective-permute-start.4) | collective-permute-done | bytes 516128 | tf_op jit(solution)/shard_map/ppermute | solution.py:110
  89.6 9.2 %collective-permute-done.5.refs_3_ = bf16[4,72,896]{2,1,0:T(8,128)(2,1)S(1)} collective-permute-done((bf16[4,72,896]{2,1,0:T(8,128)(2,1)S(1)}, bf16[4,72,896]{2,1,0:T(8,128)(2,1)S(1)}, u32[]{:S(2)}, u32[]{:S(2)}) %collective-permute-start.5) | collective-permute-done | bytes 516128 | tf_op jit(solution)/shard_map/ppermute | solution.py:110
  104.8 4.8 %delta_states.1 = (f32[32,6,16,128]{3,2,1,0:T(8,128)}, f32[6,8,128]{2,1,0:T(8,128)S(1)}) custom-call(bf16[1152,896]{1,0:T(8,128)(2,1)S(1)} %bitcast.18, bf16[1152,896]{1,0:T(8,128)(2,1)S(1)} %bitcast.19, f32[6,192,128]{2,1,0:T(8,128)S(1)} %get-tuple-element.41.step_ref, f32[6,192,128]{2,1,0:T(8,128)S(1)} %get-tuple-element.42.cum_ref), custom_call_target="tpu_custom_call" | custom-call | flops 4000000000 | bytes 8388608 | tf_op jit(solution)/shard_map/delta_states/pallas_call | solution.py:325
  111.3 2.5 %all-to-all-done.1.start_ref = bf16[32,6,16,128]{3,2,1,0:T(8,128)(2,1)S(1)} async-done(((bf16[32,6,16,128]{3,2,1,0:T(8,128)(2,1)}), bf16[32,6,16,128]{3,2,1,0:T(8,128)(2,1)S(1)}, u32[]{:S(2)}, u32[]{:S(2)}) %all-to-all-start.1) | async-done | bytes 786464 | tf_op jit(solution)/shard_map/all_to_all | solution.py:182
  113.7 4.9 %closing_states.1 = bf16[32,6,16,128]{3,2,1,0:T(8,128)(2,1)} custom-call(bf16[32,6,16,128]{3,2,1,0:T(8,128)(2,1)S(1)} %all-to-all-done.1.start_ref, f32[32,6,16,128]{3,2,1,0:T(8,128)} %get-tuple-element.43.delta_ref, f32[6,8,128]{2,1,0:T(8,128)S(1)} %get-tuple-element.44.kept_ref), custom_call_target="tpu_custom_call" | custom-call | flops 1000000000 | bytes 8388608 | tf_op jit(solution)/shard_map/closing_states/pallas_call | solution.py:325
  118.6 10.5 %all-to-all-start.2 = ((bf16[32,6,16,128]{3,2,1,0:T(8,128)(2,1)}), bf16[32,6,16,128]{3,2,1,0:T(8,128)(2,1)S(1)}, u32[]{:S(2)}, u32[]{:S(2)}) async-start(bf16[32,6,16,128]{3,2,1,0:T(8,128)(2,1)} %closing_states.1), calls=%async_computation.2 | async-start | bytes 1572864 | tf_op jit(solution)/shard_map/all_to_all | solution.py:182
  132.5 5.1 %session_outputs.1 = bf16[1152,512]{1,0:T(8,128)(2,1)S(1)} custom-call(s32[4]{0:T(128)S(1)} %pad_add_fusion.place_ref, s32[192]{0:T(256)S(1)} %copy-done.12, s32[192]{0:T(256)S(1)} %copy-done.15, bf16[1152,896]{1,0:T(8,128)(2,1)S(1)} %bitcast.20, bf16[1152,896]{1,0:T(8,128)(2,1)S(1)} %bitcast.21, bf16[1152,896]{1,0:T(8,128)(2,1)S(1)} %bitcast.22, ...), custom_call_target="tpu_custom_call" | custom-call | flops 10000000000 | bytes 8388608 | tf_op jit(solution)/shard_map/session_outputs/pallas_call | solution.py:325
  138.3 3.0 %collective-permute-start.6 = (bf16[4,72,512]{2,1,0:T(8,128)(2,1)S(1)}, bf16[4,72,512]{2,1,0:T(8,128)(2,1)S(1)}, u32[]{:S(2)}, u32[]{:S(2)}) collective-permute-start(bf16[4,72,512]{2,1,0:T(8,128)(2,1)S(1)} %get-tuple-element.48), channel_id=1, source_target_pairs={{0,1},{1,2},{2,3},{3,0},{4,5},{5,6},{6,7},{7,4},{8,9},{9,10},{10,1... | collective-permute-start | bytes 884744 | tf_op jit(solution)/shard_map/ppermute | solution.py:110
  141.3 4.4 %collective-permute-start.7 = (bf16[4,72,512]{2,1,0:T(8,128)(2,1)S(1)}, bf16[4,72,512]{2,1,0:T(8,128)(2,1)S(1)}, u32[]{:S(2)}, u32[]{:S(2)}) collective-permute-start(bf16[4,72,512]{2,1,0:T(8,128)(2,1)S(1)} %get-tuple-element.49), channel_id=1, source_target_pairs={{0,2},{1,3},{2,0},{3,1},{4,6},{5,7},{6,4},{7,5},{8,10},{9,11},{10,... | collective-permute-start | bytes 884744 | tf_op jit(solution)/shard_map/ppermute | solution.py:110
  145.6 2.2 collective-permute-start.8
  147.8 1.9 collective-permute-done.6.refs_1_
  149.8 7.2 %collective-permute-done.7.refs_2_ = bf16[4,72,512]{2,1,0:T(8,128)(2,1)S(1)} collective-permute-done((bf16[4,72,512]{2,1,0:T(8,128)(2,1)S(1)}, bf16[4,72,512]{2,1,0:T(8,128)(2,1)S(1)}, u32[]{:S(2)}, u32[]{:S(2)}) %collective-permute-start.7) | collective-permute-done | bytes 294944 | tf_op jit(solution)/shard_map/ppermute | solution.py:110
  158.9 11.9 %all-to-all-done.2 = bf16[32,6,16,128]{3,2,1,0:T(8,128)(2,1)S(1)} async-done(((bf16[32,6,16,128]{3,2,1,0:T(8,128)(2,1)}), bf16[32,6,16,128]{3,2,1,0:T(8,128)(2,1)S(1)}, u32[]{:S(2)}, u32[]{:S(2)}) %all-to-all-start.2) | async-done | bytes 786464 | tf_op jit(solution)/shard_map/all_to_all | solution.py:182
  170.8 1.7 to_owner_order.1
  172.5 6.6 %all-to-all-start.3 = ((bf16[32,6,16,128]{3,2,1,0:T(8,128)(2,1)}), bf16[32,6,16,128]{3,2,1,0:T(8,128)(2,1)S(1)}, u32[]{:S(2)}, u32[]{:S(2)}) async-start(bf16[32,6,16,128]{3,2,1,0:T(8,128)(2,1)} %bitcast.12), calls=%async_computation.3 | async-start | bytes 1572864 | tf_op jit(solution)/shard_map/all_to_all | solution.py:182
  179.1 3.2 %collective-permute-start.9 = (bf16[72,2048]{1,0:T(8,128)(2,1)S(1)}, bf16[72,2048]{1,0:T(8,128)(2,1)S(1)}, u32[]{:S(2)}, u32[]{:S(2)}) collective-permute-start(bf16[72,2048]{1,0:T(8,128)(2,1)S(1)} %get-tuple-element.56), channel_id=1, source_target_pairs={{0,4},{1,5},{2,6},{3,7},{4,8},{5,9},{6,10},{7,11},{8,12},{9,13},{1... | collective-permute-start | bytes 884744 | tf_op jit(solution)/shard_map/ppermute | solution.py:110
  182.3 4.1 %collective-permute-start.10 = (bf16[72,2048]{1,0:T(8,128)(2,1)S(1)}, bf16[72,2048]{1,0:T(8,128)(2,1)S(1)}, u32[]{:S(2)}, u32[]{:S(2)}) collective-permute-start(bf16[72,2048]{1,0:T(8,128)(2,1)S(1)} %get-tuple-element.57), channel_id=1, source_target_pairs={{0,8},{1,9},{2,10},{3,11},{4,12},{5,13},{6,14},{7,15},{8,0},{9,1},... | collective-permute-start | bytes 884744 | tf_op jit(solution)/shard_map/ppermute | solution.py:110
  186.4 3.5 %collective-permute-start.11 = (bf16[72,2048]{1,0:T(8,128)(2,1)S(1)}, bf16[72,2048]{1,0:T(8,128)(2,1)S(1)}, u32[]{:S(2)}, u32[]{:S(2)}) collective-permute-start(bf16[72,2048]{1,0:T(8,128)(2,1)S(1)} %get-tuple-element.58), channel_id=1, source_target_pairs={{0,12},{1,13},{2,14},{3,15},{4,0},{5,1},{6,2},{7,3},{8,4},{9,5},{1... | collective-permute-start | bytes 884744 | tf_op jit(solution)/shard_map/ppermute | solution.py:110
  190.6 7.1 %collective-permute-done.10.refs_2_ = bf16[72,2048]{1,0:T(8,128)(2,1)S(1)} collective-permute-done((bf16[72,2048]{1,0:T(8,128)(2,1)S(1)}, bf16[72,2048]{1,0:T(8,128)(2,1)S(1)}, u32[]{:S(2)}, u32[]{:S(2)}) %collective-permute-start.10) | collective-permute-done | bytes 294944 | tf_op jit(solution)/shard_map/ppermute | solution.py:110
  200.7 19.0 %all-to-all-done.3 = bf16[32,6,16,128]{3,2,1,0:T(8,128)(2,1)S(1)} async-done(((bf16[32,6,16,128]{3,2,1,0:T(8,128)(2,1)}), bf16[32,6,16,128]{3,2,1,0:T(8,128)(2,1)S(1)}, u32[]{:S(2)}, u32[]{:S(2)}) %all-to-all-start.3) | async-done | bytes 786464 | tf_op jit(solution)/shard_map/all_to_all | solution.py:182
  (74 shorter events, 26.4 us)
Async XLA Ops:
  2.8 17.0 %copy-start = (bf16[72,8192]{1,0:T(8,128)(2,1)S(1)}, bf16[72,8192]{1,0:T(8,128)(2,1)}, u32[]{:S(2)}) copy-start(bf16[72,8192]{1,0:T(8,128)(2,1)} %x_ref.1) | copy-start | bytes 3538948
  2.8 17.0 %copy-start.9 = (bf16[72,512]{1,0:T(8,128)(2,1)S(1)}, bf16[72,512]{1,0:T(8,128)(2,1)}, u32[]{:S(2)}) copy-start(bf16[72,512]{1,0:T(8,128)(2,1)} %b_ref.1) | copy-start | bytes 221188
  2.8 17.0 %copy-start.10 = (bf16[72,512]{1,0:T(8,128)(2,1)S(1)}, bf16[72,512]{1,0:T(8,128)(2,1)}, u32[]{:S(2)}) copy-start(bf16[72,512]{1,0:T(8,128)(2,1)} %c_ref.1) | copy-start | bytes 221188
  2.8 17.0 %copy-start.11 = (bf16[72,128]{1,0:T(8,128)(2,1)S(1)}, bf16[72,128]{1,0:T(8,128)(2,1)}, u32[]{:S(2)}) copy-start(bf16[72,128]{1,0:T(8,128)(2,1)} %dt_ref.1) | copy-start | bytes 55300
  2.8 58.6 %all-to-all-start = ((bf16[1,6,32,16,128]{4,3,1,0,2:T(8,128)(2,1)}), bf16[1,6,32,16,128]{4,3,1,0,2:T(8,128)(2,1)S(1)}, u32[]{:S(2)}, u32[]{:S(2)}) async-start(bf16[1,6,32,16,128]{4,3,1,0,2:T(8,128)(2,1)} %copy.22), calls=%async_computation | async-start | bytes 1572864 | tf_op jit(solution)/shard_map/all_to_all | solution.py:182
  19.8 26.3 %copy-start.20 = (s32[32,6]{0,1:T(8,128)S(1)}, s32[32,6]{0,1:T(8,128)}, u32[]{:S(2)}) copy-start(s32[32,6]{0,1:T(8,128)} %param.20) | copy-start | bytes 2308
  20.5 13.0 %collective-permute-start = (bf16[72,2432]{1,0:T(8,128)(2,1)S(1)}, bf16[72,2432]{1,0:T(8,128)(2,1)S(1)}, u32[]{:S(2)}, u32[]{:S(2)}) collective-permute-start(bf16[72,2432]{1,0:T(8,128)(2,1)S(1)} %get-tuple-element.32), channel_id=1, source_target_pairs={{0,8},{1,9},{2,10},{3,11},{4,12},{5,13},{6,14},{7,15},{8,0},{9,1},... | collective-permute-start | bytes 1050632 | tf_op jit(solution)/shard_map/ppermute | solution.py:110
  25.3 16.2 %collective-permute-start.1 = (bf16[72,2432]{1,0:T(8,128)(2,1)S(1)}, bf16[72,2432]{1,0:T(8,128)(2,1)S(1)}, u32[]{:S(2)}, u32[]{:S(2)}) collective-permute-start(bf16[72,2432]{1,0:T(8,128)(2,1)S(1)} %get-tuple-element.33), channel_id=1, source_target_pairs={{0,4},{1,5},{2,6},{3,7},{4,8},{5,9},{6,10},{7,11},{8,12},{9,13},{1... | collective-permute-start | bytes 1050632 | tf_op jit(solution)/shard_map/ppermute | solution.py:110
  27.6 13.9 %collective-permute-start.2 = (bf16[72,2432]{1,0:T(8,128)(2,1)S(1)}, bf16[72,2432]{1,0:T(8,128)(2,1)S(1)}, u32[]{:S(2)}, u32[]{:S(2)}) collective-permute-start(bf16[72,2432]{1,0:T(8,128)(2,1)S(1)} %get-tuple-element.34), channel_id=1, source_target_pairs={{0,12},{1,13},{2,14},{3,15},{4,0},{5,1},{6,2},{7,3},{8,4},{9,5},{1... | collective-permute-start | bytes 1050632 | tf_op jit(solution)/shard_map/ppermute | solution.py:110
  43.0 20.7 %collective-permute-start.3 = (bf16[4,72,896]{2,1,0:T(8,128)(2,1)S(1)}, bf16[4,72,896]{2,1,0:T(8,128)(2,1)S(1)}, u32[]{:S(2)}, u32[]{:S(2)}) collective-permute-start(bf16[4,72,896]{2,1,0:T(8,128)(2,1)S(1)} %get-tuple-element.35), channel_id=1, source_target_pairs={{0,1},{1,2},{2,3},{3,0},{4,5},{5,6},{6,7},{7,4},{8,9},{9,10},{10,1... | collective-permute-start | bytes 1548296 | tf_op jit(solution)/shard_map/ppermute | solution.py:110
  63.7 14.6 %copy-start.21 = (f32[8]{0:T(128)S(1)}, f32[8]{0:T(128)}, u32[]{:S(2)}) copy-start(f32[8]{0:T(128)} %param.17) | copy-start | bytes 100
  63.7 14.7 %copy-start.22 = (f32[8]{0:T(128)S(1)}, f32[8]{0:T(128)}, u32[]{:S(2)}) copy-start(f32[8]{0:T(128)} %param.16) | copy-start | bytes 100
  63.7 35.1 %copy-start.3 = (bf16[4,72,896]{2,1,0:T(8,128)(2,1)}, bf16[4,72,896]{2,1,0:T(8,128)(2,1)S(1)}, u32[]{:S(2)}) copy-start(bf16[4,72,896]{2,1,0:T(8,128)(2,1)S(1)} %collective-permute-done.3.refs_1_) | copy-start | bytes 1548292
  63.7 50.0 %all-to-all-start.1 = ((bf16[32,6,16,128]{3,2,1,0:T(8,128)(2,1)}), bf16[32,6,16,128]{3,2,1,0:T(8,128)(2,1)S(1)}, u32[]{:S(2)}, u32[]{:S(2)}) async-start(bf16[32,6,16,128]{3,2,1,0:T(8,128)(2,1)} %bitcast.8), calls=%async_computation.1 | async-start | bytes 1572864 | tf_op jit(solution)/shard_map/all_to_all | solution.py:182
  72.0 16.7 %collective-permute-start.4 = (bf16[4,72,896]{2,1,0:T(8,128)(2,1)}, bf16[4,72,896]{2,1,0:T(8,128)(2,1)S(1)}, u32[]{:S(2)}, u32[]{:S(2)}) collective-permute-start(bf16[4,72,896]{2,1,0:T(8,128)(2,1)} %get-tuple-element.39), channel_id=1, source_target_pairs={{0,2},{1,3},{2,0},{3,1},{4,6},{5,7},{6,4},{7,5},{8,10},{9,11},{10,... | collective-permute-start | bytes 1548296 | tf_op jit(solution)/shard_map/ppermute | solution.py:110
  75.5 23.3 %collective-permute-start.5 = (bf16[4,72,896]{2,1,0:T(8,128)(2,1)S(1)}, bf16[4,72,896]{2,1,0:T(8,128)(2,1)S(1)}, u32[]{:S(2)}, u32[]{:S(2)}) collective-permute-start(bf16[4,72,896]{2,1,0:T(8,128)(2,1)S(1)} %get-tuple-element.40), channel_id=1, source_target_pairs={{0,3},{1,0},{2,1},{3,2},{4,7},{5,4},{6,5},{7,6},{8,11},{9,8},{10,9... | collective-permute-start | bytes 1548296 | tf_op jit(solution)/shard_map/ppermute | solution.py:110
  99.6 1.0 copy-start.4
  100.6 1.0 copy-start.6
  113.7 4.9 %copy-start.1 = (bf16[32,6,16,128]{3,2,1,0:T(8,128)(2,1)}, bf16[32,6,16,128]{3,2,1,0:T(8,128)(2,1)S(1)}, u32[]{:S(2)}) copy-start(bf16[32,6,16,128]{3,2,1,0:T(8,128)(2,1)S(1)} %all-to-all-done.1.start_ref) | copy-start | bytes 2359300
  118.6 10.5 %copy-start.23 = (f32[8]{0:T(128)S(1)}, f32[8]{0:T(128)}, u32[]{:S(2)}) copy-start(f32[8]{0:T(128)} %param.18) | copy-start | bytes 100
  118.6 52.2 %all-to-all-start.2 = ((bf16[32,6,16,128]{3,2,1,0:T(8,128)(2,1)}), bf16[32,6,16,128]{3,2,1,0:T(8,128)(2,1)S(1)}, u32[]{:S(2)}, u32[]{:S(2)}) async-start(bf16[32,6,16,128]{3,2,1,0:T(8,128)(2,1)} %closing_states.1), calls=%async_computation.2 | async-start | bytes 1572864 | tf_op jit(solution)/shard_map/all_to_all | solution.py:182
  129.3 1.1 copy-start.2
  130.4 1.1 copy-start.17
  131.5 1.1 copy-start.19
  137.6 33.2 %copy-start.14 = (s32[192]{0:T(256)S(1)}, s32[192]{0:T(256)}, u32[]{:S(2)}) copy-start(s32[192]{0:T(256)} %cache_rows.1.rows_ref) | copy-start | bytes 2308
  138.3 11.5 %collective-permute-start.6 = (bf16[4,72,512]{2,1,0:T(8,128)(2,1)S(1)}, bf16[4,72,512]{2,1,0:T(8,128)(2,1)S(1)}, u32[]{:S(2)}, u32[]{:S(2)}) collective-permute-start(bf16[4,72,512]{2,1,0:T(8,128)(2,1)S(1)} %get-tuple-element.48), channel_id=1, source_target_pairs={{0,1},{1,2},{2,3},{3,0},{4,5},{5,6},{6,7},{7,4},{8,9},{9,10},{10,1... | collective-permute-start | bytes 884744 | tf_op jit(solution)/shard_map/ppermute | solution.py:110
  141.3 15.7 %collective-permute-start.7 = (bf16[4,72,512]{2,1,0:T(8,128)(2,1)S(1)}, bf16[4,72,512]{2,1,0:T(8,128)(2,1)S(1)}, u32[]{:S(2)}, u32[]{:S(2)}) collective-permute-start(bf16[4,72,512]{2,1,0:T(8,128)(2,1)S(1)} %get-tuple-element.49), channel_id=1, source_target_pairs={{0,2},{1,3},{2,0},{3,1},{4,6},{5,7},{6,4},{7,5},{8,10},{9,11},{10,... | collective-permute-start | bytes 884744 | tf_op jit(solution)/shard_map/ppermute | solution.py:110
  145.6 12.7 %collective-permute-start.8 = (bf16[4,72,512]{2,1,0:T(8,128)(2,1)S(1)}, bf16[4,72,512]{2,1,0:T(8,128)(2,1)S(1)}, u32[]{:S(2)}, u32[]{:S(2)}) collective-permute-start(bf16[4,72,512]{2,1,0:T(8,128)(2,1)S(1)} %get-tuple-element.50), channel_id=1, source_target_pairs={{0,3},{1,0},{2,1},{3,2},{4,7},{5,4},{6,5},{7,6},{8,11},{9,8},{10,9... | collective-permute-start | bytes 884744 | tf_op jit(solution)/shard_map/ppermute | solution.py:110
  172.5 47.3 %all-to-all-start.3 = ((bf16[32,6,16,128]{3,2,1,0:T(8,128)(2,1)}), bf16[32,6,16,128]{3,2,1,0:T(8,128)(2,1)S(1)}, u32[]{:S(2)}, u32[]{:S(2)}) async-start(bf16[32,6,16,128]{3,2,1,0:T(8,128)(2,1)} %bitcast.12), calls=%async_computation.3 | async-start | bytes 1572864 | tf_op jit(solution)/shard_map/all_to_all | solution.py:182
  179.1 11.5 %collective-permute-start.9 = (bf16[72,2048]{1,0:T(8,128)(2,1)S(1)}, bf16[72,2048]{1,0:T(8,128)(2,1)S(1)}, u32[]{:S(2)}, u32[]{:S(2)}) collective-permute-start(bf16[72,2048]{1,0:T(8,128)(2,1)S(1)} %get-tuple-element.56), channel_id=1, source_target_pairs={{0,4},{1,5},{2,6},{3,7},{4,8},{5,9},{6,10},{7,11},{8,12},{9,13},{1... | collective-permute-start | bytes 884744 | tf_op jit(solution)/shard_map/ppermute | solution.py:110
  182.3 15.4 %collective-permute-start.10 = (bf16[72,2048]{1,0:T(8,128)(2,1)S(1)}, bf16[72,2048]{1,0:T(8,128)(2,1)S(1)}, u32[]{:S(2)}, u32[]{:S(2)}) collective-permute-start(bf16[72,2048]{1,0:T(8,128)(2,1)S(1)} %get-tuple-element.57), channel_id=1, source_target_pairs={{0,8},{1,9},{2,10},{3,11},{4,12},{5,13},{6,14},{7,15},{8,0},{9,1},... | collective-permute-start | bytes 884744 | tf_op jit(solution)/shard_map/ppermute | solution.py:110
  186.4 12.7 %collective-permute-start.11 = (bf16[72,2048]{1,0:T(8,128)(2,1)S(1)}, bf16[72,2048]{1,0:T(8,128)(2,1)S(1)}, u32[]{:S(2)}, u32[]{:S(2)}) collective-permute-start(bf16[72,2048]{1,0:T(8,128)(2,1)S(1)} %get-tuple-element.58), channel_id=1, source_target_pairs={{0,12},{1,13},{2,14},{3,15},{4,0},{5,1},{6,2},{7,3},{8,4},{9,5},{1... | collective-permute-start | bytes 884744 | tf_op jit(solution)/shard_map/ppermute | solution.py:110
  (8 other events, 6.3 us)

commit v9 on v8

--- a/solution.py
+++ b/solution.py
@@ -113,19 +113,17 @@
 
 def member_at(spot, count):
     chips = count // 2
-    core = lax.rem(spot, 2)
-    return lax.rem(spot // 2 * 7 + core * (chips // 2), chips) * 2 + core
+    return lax.rem(lax.rem(spot, chips) * 3, chips) * 2 + spot // chips
 
 
 def spot_of(member, count):
     chips = count // 2
-    core = lax.rem(member, 2)
-    return lax.rem((member // 2 + core * (chips // 2)) * 7, chips) * 2 + core
+    return lax.rem(member, 2) * chips + lax.rem(member // 2 * 11, chips)
 
 
 def members(count):
     chips = count // 2
-    return [(spot // 2 * 7 + spot % 2 * (chips // 2)) % chips * 2 + spot % 2 for spot in range(count)]
+    return [spot % chips * 3 % chips * 2 + spot // chips for spot in range(count)]
 
 
 def rows_kernel(sessions_ref, owners_ref, slots_ref, rows_ref, *, slot_count):
@@ -392,7 +390,7 @@
         "turn_in",
     )
     sent = send_along(sent, side, False)
-    held, sent[1] = lax.optimization_barrier((held, sent[1]))
+    held, sent[side // 2] = lax.optimization_barrier((held, sent[side // 2]))
     start = exchange(held.reshape(state_shape), req_size)
     packed = local_call(
         gather_kernel,
@@ -451,12 +449,11 @@
         "delta_states",
     )
 
-    delta_held = pltpu.with_memory_space_constraint(delta, pltpu.HBM)
     (closing,) = session_call(
         functools.partial(closing_kernel, heads=heads),
         (),
         slot_count,
-        [(start, piece_block, by_slot), (delta_held, piece_block, by_slot), (kept, *kept_block)],
+        [(start, piece_block, by_slot), (delta, piece_block, by_slot), (kept, *kept_block)],
         [(pltpu.HBM(state_shape, bf16), piece_block, by_slot)],
         1_000_000_000,
         "closing_states",

time: 224 us -> 218 us (0.973)
  Pallas kernels: 28.9 us -> 26.4 us
    ppermute x12, waiting for transfers between devices: 48.9 us -> 38.7 us  [send_along(): moved[shift] = lax.ppermute(arrays[shift], 'tensor', pairs)]
    all_to_all x4, waiting for transfers between devices: 44.2 us -> 53 us  [exchange(): lax.all_to_all(states, 'req', split_axis=split_axis, concat_axis=0, axis_...]
    all_to_all x4, starting transfers between devices: 42.3 us -> 37.3 us  [exchange(): lax.all_to_all(states, 'req', split_axis=split_axis, concat_axis=0, axis_...]
    ppermute x12, starting transfers between devices: 40.9 us -> 43.7 us  [send_along(): moved[shift] = lax.ppermute(arrays[shift], 'tensor', pairs)]
    pallas_call x3, Pallas kernels: 14.8 us -> 12.6 us  [session_call(): pl.pallas_call(kernel, grid_spec=pltpu.PrefetchScalarGridSpec(num_scalar_...]
    unnamed x49 -> x51, local copies, waits for them, and re-layouts: 10.4 us -> 12.1 us
where the time goes in v9:
time: 218 us; the launch traced here: 216 us
  waiting for transfers between devices  91.6 us (42%)
  starting transfers between devices  81 us (37%)
  Pallas kernels  26.4 us (12%)
  local copies, waits for them, and re-layouts  16.3 us (7%)
    all_to_all x4, waiting for transfers between devices, exchange(): lax.all_to_all(states, 'req', split_axis=split_axis, concat_axis=0, axis_...  53 us
    ppermute x12, starting transfers between devices, send_along(): moved[shift] = lax.ppermute(arrays[shift], 'tensor', pairs)  43.7 us
    ppermute x12, waiting for transfers between devices, send_along(): moved[shift] = lax.ppermute(arrays[shift], 'tensor', pairs)  38.7 us
    all_to_all x4, starting transfers between devices, exchange(): lax.all_to_all(states, 'req', split_axis=split_axis, concat_axis=0, axis_...  37.3 us
    pallas_call x3, Pallas kernels, session_call(): pl.pallas_call(kernel, grid_spec=pltpu.PrefetchScalarGridSpec(num_scalar_...  12.6 us
    unnamed x51, local copies, waits for them, and re-layouts  12.1 us
    pallas_call x6, Pallas kernels, local_call(): pl.pallas_call(kernel, in_specs=[smem] + [vmem] * len(arrays), out_specs=...  5.73 us
  transfers between devices with their start and end apart: 16, of which 14 were waited for; matrix products, arithmetic and copies ran while one was open for 1% of the time, Pallas kernels for 10%

profile of v9, /device:TPU:1, one launch (start us, length us, event | category | flops | bytes accessed | tf_op | source)
XLA Modules:
  0.0 216.4 jit_solution(11568281032296801331)
XLA Ops:
  0.6 2.1 copy.22
  2.8 16.9 %all-to-all-start = ((bf16[1,6,32,16,128]{4,3,1,0,2:T(8,128)(2,1)}), bf16[1,6,32,16,128]{4,3,1,0,2:T(8,128)(2,1)S(1)}, u32[]{:S(2)}, u32[]{:S(2)}) async-start(bf16[1,6,32,16,128]{4,3,1,0,2:T(8,128)(2,1)} %copy.22), calls=%async_computation | async-start | bytes 1572864 | tf_op jit(solution)/shard_map/all_to_all | solution.py:180
  20.5 4.8 %collective-permute-start = (bf16[72,2432]{1,0:T(8,128)(2,1)S(1)}, bf16[72,2432]{1,0:T(8,128)(2,1)S(1)}, u32[]{:S(2)}, u32[]{:S(2)}) collective-permute-start(bf16[72,2432]{1,0:T(8,128)(2,1)S(1)} %get-tuple-element.32), channel_id=1, source_target_pairs={{0,8},{1,9},{2,10},{3,11},{4,12},{5,13},{6,14},{7,15},{8,0},{9,1},... | collective-permute-start | bytes 1050632 | tf_op jit(solution)/shard_map/ppermute | solution.py:110
  25.3 2.3 %collective-permute-start.1 = (bf16[72,2432]{1,0:T(8,128)(2,1)S(1)}, bf16[72,2432]{1,0:T(8,128)(2,1)S(1)}, u32[]{:S(2)}, u32[]{:S(2)}) collective-permute-start(bf16[72,2432]{1,0:T(8,128)(2,1)S(1)} %get-tuple-element.33), channel_id=1, source_target_pairs={{0,4},{1,5},{2,6},{3,7},{4,8},{5,9},{6,10},{7,11},{8,12},{9,13},{1... | collective-permute-start | bytes 1050632 | tf_op jit(solution)/shard_map/ppermute | solution.py:110
  27.6 4.2 %collective-permute-start.2 = (bf16[72,2432]{1,0:T(8,128)(2,1)S(1)}, bf16[72,2432]{1,0:T(8,128)(2,1)S(1)}, u32[]{:S(2)}, u32[]{:S(2)}) collective-permute-start(bf16[72,2432]{1,0:T(8,128)(2,1)S(1)} %get-tuple-element.34), channel_id=1, source_target_pairs={{0,12},{1,13},{2,14},{3,15},{4,0},{5,1},{6,2},{7,3},{8,4},{9,5},{1... | collective-permute-start | bytes 1050632 | tf_op jit(solution)/shard_map/ppermute | solution.py:110
  33.5 8.0 %collective-permute-done.1.refs_2_ = bf16[72,2432]{1,0:T(8,128)(2,1)S(1)} collective-permute-done((bf16[72,2432]{1,0:T(8,128)(2,1)S(1)}, bf16[72,2432]{1,0:T(8,128)(2,1)S(1)}, u32[]{:S(2)}, u32[]{:S(2)}) %collective-permute-start.1) | collective-permute-done | bytes 350240 | tf_op jit(solution)/shard_map/ppermute | solution.py:110
  43.0 4.6 %collective-permute-start.3 = (bf16[4,72,896]{2,1,0:T(8,128)(2,1)S(1)}, bf16[4,72,896]{2,1,0:T(8,128)(2,1)S(1)}, u32[]{:S(2)}, u32[]{:S(2)}) collective-permute-start(bf16[4,72,896]{2,1,0:T(8,128)(2,1)S(1)} %get-tuple-element.35), channel_id=1, source_target_pairs={{0,2},{1,3},{2,0},{3,1},{4,6},{5,7},{6,4},{7,5},{8,10},{9,11},{10,... | collective-permute-start | bytes 1548296 | tf_op jit(solution)/shard_map/ppermute | solution.py:110
  48.4 3.4 %cache_rows.1.rows_ref = s32[192]{0:T(256)} custom-call(s32[192]{0:T(256)} %reshape.28.sessions_ref, s32[192]{0:T(256)} %owners_ref.1, s32[192]{0:T(256)} %slots_ref.1), custom_call_target="tpu_custom_call" | custom-call | tf_op jit(solution)/shard_map/cache_rows/pallas_call | solution.py:145
  51.8 9.6 %all-to-all-done = bf16[1,6,32,16,128]{4,3,1,0,2:T(8,128)(2,1)S(1)} async-done(((bf16[1,6,32,16,128]{4,3,1,0,2:T(8,128)(2,1)}), bf16[1,6,32,16,128]{4,3,1,0,2:T(8,128)(2,1)S(1)}, u32[]{:S(2)}, u32[]{:S(2)}) %all-to-all-start) | async-done | bytes 786464 | tf_op jit(solution)/shard_map/all_to_all | solution.py:180
  62.1 1.7 to_group_order.1
  63.8 8.6 %all-to-all-start.1 = ((bf16[32,6,16,128]{3,2,1,0:T(8,128)(2,1)}), bf16[32,6,16,128]{3,2,1,0:T(8,128)(2,1)S(1)}, u32[]{:S(2)}, u32[]{:S(2)}) async-start(bf16[32,6,16,128]{3,2,1,0:T(8,128)(2,1)} %bitcast.8), calls=%async_computation.1 | async-start | bytes 1572864 | tf_op jit(solution)/shard_map/all_to_all | solution.py:180
  72.4 3.1 %collective-permute-start.4 = (bf16[4,72,896]{2,1,0:T(8,128)(2,1)}, bf16[4,72,896]{2,1,0:T(8,128)(2,1)S(1)}, u32[]{:S(2)}, u32[]{:S(2)}) collective-permute-start(bf16[4,72,896]{2,1,0:T(8,128)(2,1)} %get-tuple-element.38), channel_id=1, source_target_pairs={{0,1},{1,2},{2,3},{3,0},{4,5},{5,6},{6,7},{7,4},{8,9},{9,10},{10,1... | collective-permute-start | bytes 1548296 | tf_op jit(solution)/shard_map/ppermute | solution.py:110
  75.5 3.4 %collective-permute-start.5 = (bf16[4,72,896]{2,1,0:T(8,128)(2,1)S(1)}, bf16[4,72,896]{2,1,0:T(8,128)(2,1)S(1)}, u32[]{:S(2)}, u32[]{:S(2)}) collective-permute-start(bf16[4,72,896]{2,1,0:T(8,128)(2,1)S(1)} %get-tuple-element.40), channel_id=1, source_target_pairs={{0,3},{1,0},{2,1},{3,2},{4,7},{5,4},{6,5},{7,6},{8,11},{9,8},{10,9... | collective-permute-start | bytes 1548296 | tf_op jit(solution)/shard_map/ppermute | solution.py:110
  79.1 9.7 %collective-permute-done.4.refs_1_ = bf16[4,72,896]{2,1,0:T(8,128)(2,1)S(1)} collective-permute-done((bf16[4,72,896]{2,1,0:T(8,128)(2,1)}, bf16[4,72,896]{2,1,0:T(8,128)(2,1)S(1)}, u32[]{:S(2)}, u32[]{:S(2)}) %collective-permute-start.4) | collective-permute-done | bytes 516128 | tf_op jit(solution)/shard_map/ppermute | solution.py:110
  96.2 4.8 %delta_states.1 = (f32[32,6,16,128]{3,2,1,0:T(8,128)}, f32[6,8,128]{2,1,0:T(8,128)S(1)}) custom-call(bf16[1152,896]{1,0:T(8,128)(2,1)S(1)} %bitcast.18, bf16[1152,896]{1,0:T(8,128)(2,1)S(1)} %bitcast.19, f32[6,192,128]{2,1,0:T(8,128)S(1)} %get-tuple-element.41.step_ref, f32[6,192,128]{2,1,0:T(8,128)S(1)} %get-tuple-element.42.cum_ref), custom_call_target="tpu_custom_call" | custom-call | flops 4000000000 | bytes 8388608 | tf_op jit(solution)/shard_map/delta_states/pallas_call | solution.py:323
  102.7 11.4 %all-to-all-done.1.start_ref = bf16[32,6,16,128]{3,2,1,0:T(8,128)(2,1)S(1)} async-done(((bf16[32,6,16,128]{3,2,1,0:T(8,128)(2,1)}), bf16[32,6,16,128]{3,2,1,0:T(8,128)(2,1)S(1)}, u32[]{:S(2)}, u32[]{:S(2)}) %all-to-all-start.1) | async-done | bytes 786464 | tf_op jit(solution)/shard_map/all_to_all | solution.py:180
  114.1 1.7 copy-done.20
  115.8 2.7 %closing_states.1 = bf16[32,6,16,128]{3,2,1,0:T(8,128)(2,1)} custom-call(bf16[32,6,16,128]{3,2,1,0:T(8,128)(2,1)S(1)} %all-to-all-done.1.start_ref, f32[32,6,16,128]{3,2,1,0:T(8,128)S(1)} %copy-done.20, f32[6,8,128]{2,1,0:T(8,128)S(1)} %get-tuple-element.44.kept_ref), custom_call_target="tpu_custom_call" | custom-call | flops 1000000000 | bytes 8388608 | tf_op jit(solution)/shard_map/closing_states/pallas_call | solution.py:323
  118.4 6.0 %all-to-all-start.2 = ((bf16[32,6,16,128]{3,2,1,0:T(8,128)(2,1)}), bf16[32,6,16,128]{3,2,1,0:T(8,128)(2,1)S(1)}, u32[]{:S(2)}, u32[]{:S(2)}) async-start(bf16[32,6,16,128]{3,2,1,0:T(8,128)(2,1)} %closing_states.1), calls=%async_computation.2 | async-start | bytes 1572864 | tf_op jit(solution)/shard_map/all_to_all | solution.py:180
  127.8 5.1 %session_outputs.1 = bf16[1152,512]{1,0:T(8,128)(2,1)S(1)} custom-call(s32[4]{0:T(128)S(1)} %pad_add_fusion.place_ref, s32[192]{0:T(256)S(1)} %copy-done.12, s32[192]{0:T(256)S(1)} %copy-done.15, bf16[1152,896]{1,0:T(8,128)(2,1)S(1)} %bitcast.20, bf16[1152,896]{1,0:T(8,128)(2,1)S(1)} %bitcast.21, bf16[1152,896]{1,0:T(8,128)(2,1)S(1)} %bitcast.22, ...), custom_call_target="tpu_custom_call" | custom-call | flops 10000000000 | bytes 8388608 | tf_op jit(solution)/shard_map/session_outputs/pallas_call | solution.py:323
  133.6 3.1 %collective-permute-start.6 = (bf16[4,72,512]{2,1,0:T(8,128)(2,1)S(1)}, bf16[4,72,512]{2,1,0:T(8,128)(2,1)S(1)}, u32[]{:S(2)}, u32[]{:S(2)}) collective-permute-start(bf16[4,72,512]{2,1,0:T(8,128)(2,1)S(1)} %get-tuple-element.48), channel_id=1, source_target_pairs={{0,1},{1,2},{2,3},{3,0},{4,5},{5,6},{6,7},{7,4},{8,9},{9,10},{10,1... | collective-permute-start | bytes 884744 | tf_op jit(solution)/shard_map/ppermute | solution.py:110
  136.7 4.4 %collective-permute-start.7 = (bf16[4,72,512]{2,1,0:T(8,128)(2,1)S(1)}, bf16[4,72,512]{2,1,0:T(8,128)(2,1)S(1)}, u32[]{:S(2)}, u32[]{:S(2)}) collective-permute-start(bf16[4,72,512]{2,1,0:T(8,128)(2,1)S(1)} %get-tuple-element.49), channel_id=1, source_target_pairs={{0,2},{1,3},{2,0},{3,1},{4,6},{5,7},{6,4},{7,5},{8,10},{9,11},{10,... | collective-permute-start | bytes 884744 | tf_op jit(solution)/shard_map/ppermute | solution.py:110
  141.1 3.1 %collective-permute-start.8 = (bf16[4,72,512]{2,1,0:T(8,128)(2,1)S(1)}, bf16[4,72,512]{2,1,0:T(8,128)(2,1)S(1)}, u32[]{:S(2)}, u32[]{:S(2)}) collective-permute-start(bf16[4,72,512]{2,1,0:T(8,128)(2,1)S(1)} %get-tuple-element.50), channel_id=1, source_target_pairs={{0,3},{1,0},{2,1},{3,2},{4,7},{5,4},{6,5},{7,6},{8,11},{9,8},{10,9... | collective-permute-start | bytes 884744 | tf_op jit(solution)/shard_map/ppermute | solution.py:110
  145.1 7.3 %collective-permute-done.7.refs_2_ = bf16[4,72,512]{2,1,0:T(8,128)(2,1)S(1)} collective-permute-done((bf16[4,72,512]{2,1,0:T(8,128)(2,1)S(1)}, bf16[4,72,512]{2,1,0:T(8,128)(2,1)S(1)}, u32[]{:S(2)}, u32[]{:S(2)}) %collective-permute-start.7) | collective-permute-done | bytes 294944 | tf_op jit(solution)/shard_map/ppermute | solution.py:110
  154.2 11.9 %all-to-all-done.2 = bf16[32,6,16,128]{3,2,1,0:T(8,128)(2,1)S(1)} async-done(((bf16[32,6,16,128]{3,2,1,0:T(8,128)(2,1)}), bf16[32,6,16,128]{3,2,1,0:T(8,128)(2,1)S(1)}, u32[]{:S(2)}, u32[]{:S(2)}) %all-to-all-start.2) | async-done | bytes 786464 | tf_op jit(solution)/shard_map/all_to_all | solution.py:180
  166.1 1.7 to_owner_order.1
  167.8 5.8 %all-to-all-start.3 = ((bf16[32,6,16,128]{3,2,1,0:T(8,128)(2,1)}), bf16[32,6,16,128]{3,2,1,0:T(8,128)(2,1)S(1)}, u32[]{:S(2)}, u32[]{:S(2)}) async-start(bf16[32,6,16,128]{3,2,1,0:T(8,128)(2,1)} %bitcast.12), calls=%async_computation.3 | async-start | bytes 1572864 | tf_op jit(solution)/shard_map/all_to_all | solution.py:180
  173.6 3.2 %collective-permute-start.9 = (bf16[72,2048]{1,0:T(8,128)(2,1)S(1)}, bf16[72,2048]{1,0:T(8,128)(2,1)S(1)}, u32[]{:S(2)}, u32[]{:S(2)}) collective-permute-start(bf16[72,2048]{1,0:T(8,128)(2,1)S(1)} %get-tuple-element.56), channel_id=1, source_target_pairs={{0,4},{1,5},{2,6},{3,7},{4,8},{5,9},{6,10},{7,11},{8,12},{9,13},{1... | collective-permute-start | bytes 884744 | tf_op jit(solution)/shard_map/ppermute | solution.py:110
  176.9 4.1 %collective-permute-start.10 = (bf16[72,2048]{1,0:T(8,128)(2,1)S(1)}, bf16[72,2048]{1,0:T(8,128)(2,1)S(1)}, u32[]{:S(2)}, u32[]{:S(2)}) collective-permute-start(bf16[72,2048]{1,0:T(8,128)(2,1)S(1)} %get-tuple-element.57), channel_id=1, source_target_pairs={{0,8},{1,9},{2,10},{3,11},{4,12},{5,13},{6,14},{7,15},{8,0},{9,1},... | collective-permute-start | bytes 884744 | tf_op jit(solution)/shard_map/ppermute | solution.py:110
  180.9 3.5 %collective-permute-start.11 = (bf16[72,2048]{1,0:T(8,128)(2,1)S(1)}, bf16[72,2048]{1,0:T(8,128)(2,1)S(1)}, u32[]{:S(2)}, u32[]{:S(2)}) collective-permute-start(bf16[72,2048]{1,0:T(8,128)(2,1)S(1)} %get-tuple-element.58), channel_id=1, source_target_pairs={{0,12},{1,13},{2,14},{3,15},{4,0},{5,1},{6,2},{7,3},{8,4},{9,5},{1... | collective-permute-start | bytes 884744 | tf_op jit(solution)/shard_map/ppermute | solution.py:110
  185.1 7.1 %collective-permute-done.10.refs_2_ = bf16[72,2048]{1,0:T(8,128)(2,1)S(1)} collective-permute-done((bf16[72,2048]{1,0:T(8,128)(2,1)S(1)}, bf16[72,2048]{1,0:T(8,128)(2,1)S(1)}, u32[]{:S(2)}, u32[]{:S(2)}) %collective-permute-start.10) | collective-permute-done | bytes 294944 | tf_op jit(solution)/shard_map/ppermute | solution.py:110
  195.3 20.1 %all-to-all-done.3 = bf16[32,6,16,128]{3,2,1,0:T(8,128)(2,1)S(1)} async-done(((bf16[32,6,16,128]{3,2,1,0:T(8,128)(2,1)}), bf16[32,6,16,128]{3,2,1,0:T(8,128)(2,1)S(1)}, u32[]{:S(2)}, u32[]{:S(2)}) %all-to-all-start.3) | async-done | bytes 786464 | tf_op jit(solution)/shard_map/all_to_all | solution.py:180
  (76 shorter events, 26.1 us)
Async XLA Ops:
  2.8 17.0 %copy-start = (bf16[72,8192]{1,0:T(8,128)(2,1)S(1)}, bf16[72,8192]{1,0:T(8,128)(2,1)}, u32[]{:S(2)}) copy-start(bf16[72,8192]{1,0:T(8,128)(2,1)} %x_ref.1) | copy-start | bytes 3538948
  2.8 17.0 %copy-start.9 = (bf16[72,512]{1,0:T(8,128)(2,1)S(1)}, bf16[72,512]{1,0:T(8,128)(2,1)}, u32[]{:S(2)}) copy-start(bf16[72,512]{1,0:T(8,128)(2,1)} %b_ref.1) | copy-start | bytes 221188
  2.8 17.0 %copy-start.10 = (bf16[72,512]{1,0:T(8,128)(2,1)S(1)}, bf16[72,512]{1,0:T(8,128)(2,1)}, u32[]{:S(2)}) copy-start(bf16[72,512]{1,0:T(8,128)(2,1)} %c_ref.1) | copy-start | bytes 221188
  2.8 17.0 %copy-start.11 = (bf16[72,128]{1,0:T(8,128)(2,1)S(1)}, bf16[72,128]{1,0:T(8,128)(2,1)}, u32[]{:S(2)}) copy-start(bf16[72,128]{1,0:T(8,128)(2,1)} %dt_ref.1) | copy-start | bytes 55300
  2.8 58.6 %all-to-all-start = ((bf16[1,6,32,16,128]{4,3,1,0,2:T(8,128)(2,1)}), bf16[1,6,32,16,128]{4,3,1,0,2:T(8,128)(2,1)S(1)}, u32[]{:S(2)}, u32[]{:S(2)}) async-start(bf16[1,6,32,16,128]{4,3,1,0,2:T(8,128)(2,1)} %copy.22), calls=%async_computation | async-start | bytes 1572864 | tf_op jit(solution)/shard_map/all_to_all | solution.py:180
  19.8 27.8 %copy-start.21 = (s32[32,6]{0,1:T(8,128)S(1)}, s32[32,6]{0,1:T(8,128)}, u32[]{:S(2)}) copy-start(s32[32,6]{0,1:T(8,128)} %param.20) | copy-start | bytes 2308
  20.5 13.0 %collective-permute-start = (bf16[72,2432]{1,0:T(8,128)(2,1)S(1)}, bf16[72,2432]{1,0:T(8,128)(2,1)S(1)}, u32[]{:S(2)}, u32[]{:S(2)}) collective-permute-start(bf16[72,2432]{1,0:T(8,128)(2,1)S(1)} %get-tuple-element.32), channel_id=1, source_target_pairs={{0,8},{1,9},{2,10},{3,11},{4,12},{5,13},{6,14},{7,15},{8,0},{9,1},... | collective-permute-start | bytes 1050632 | tf_op jit(solution)/shard_map/ppermute | solution.py:110
  25.3 16.2 %collective-permute-start.1 = (bf16[72,2432]{1,0:T(8,128)(2,1)S(1)}, bf16[72,2432]{1,0:T(8,128)(2,1)S(1)}, u32[]{:S(2)}, u32[]{:S(2)}) collective-permute-start(bf16[72,2432]{1,0:T(8,128)(2,1)S(1)} %get-tuple-element.33), channel_id=1, source_target_pairs={{0,4},{1,5},{2,6},{3,7},{4,8},{5,9},{6,10},{7,11},{8,12},{9,13},{1... | collective-permute-start | bytes 1050632 | tf_op jit(solution)/shard_map/ppermute | solution.py:110
  27.6 13.9 %collective-permute-start.2 = (bf16[72,2432]{1,0:T(8,128)(2,1)S(1)}, bf16[72,2432]{1,0:T(8,128)(2,1)S(1)}, u32[]{:S(2)}, u32[]{:S(2)}) collective-permute-start(bf16[72,2432]{1,0:T(8,128)(2,1)S(1)} %get-tuple-element.34), channel_id=1, source_target_pairs={{0,12},{1,13},{2,14},{3,15},{4,0},{5,1},{6,2},{7,3},{8,4},{9,5},{1... | collective-permute-start | bytes 1050632 | tf_op jit(solution)/shard_map/ppermute | solution.py:110
  43.0 20.8 %collective-permute-start.3 = (bf16[4,72,896]{2,1,0:T(8,128)(2,1)S(1)}, bf16[4,72,896]{2,1,0:T(8,128)(2,1)S(1)}, u32[]{:S(2)}, u32[]{:S(2)}) collective-permute-start(bf16[4,72,896]{2,1,0:T(8,128)(2,1)S(1)} %get-tuple-element.35), channel_id=1, source_target_pairs={{0,2},{1,3},{2,0},{3,1},{4,6},{5,7},{6,4},{7,5},{8,10},{9,11},{10,... | collective-permute-start | bytes 1548296 | tf_op jit(solution)/shard_map/ppermute | solution.py:110
  63.8 15.1 %copy-start.22 = (f32[8]{0:T(128)S(1)}, f32[8]{0:T(128)}, u32[]{:S(2)}) copy-start(f32[8]{0:T(128)} %param.17) | copy-start | bytes 100
  63.8 15.2 %copy-start.23 = (f32[8]{0:T(128)S(1)}, f32[8]{0:T(128)}, u32[]{:S(2)}) copy-start(f32[8]{0:T(128)} %param.16) | copy-start | bytes 100
  63.8 26.4 %copy-start.3 = (bf16[4,72,896]{2,1,0:T(8,128)(2,1)}, bf16[4,72,896]{2,1,0:T(8,128)(2,1)S(1)}, u32[]{:S(2)}) copy-start(bf16[4,72,896]{2,1,0:T(8,128)(2,1)S(1)} %collective-permute-done.3.refs_2_) | copy-start | bytes 1548292
  63.8 50.3 %all-to-all-start.1 = ((bf16[32,6,16,128]{3,2,1,0:T(8,128)(2,1)}), bf16[32,6,16,128]{3,2,1,0:T(8,128)(2,1)S(1)}, u32[]{:S(2)}, u32[]{:S(2)}) async-start(bf16[32,6,16,128]{3,2,1,0:T(8,128)(2,1)} %bitcast.8), calls=%async_computation.1 | async-start | bytes 1572864 | tf_op jit(solution)/shard_map/all_to_all | solution.py:180
  72.4 16.4 %collective-permute-start.4 = (bf16[4,72,896]{2,1,0:T(8,128)(2,1)}, bf16[4,72,896]{2,1,0:T(8,128)(2,1)S(1)}, u32[]{:S(2)}, u32[]{:S(2)}) collective-permute-start(bf16[4,72,896]{2,1,0:T(8,128)(2,1)} %get-tuple-element.38), channel_id=1, source_target_pairs={{0,1},{1,2},{2,3},{3,0},{4,5},{5,6},{6,7},{7,4},{8,9},{9,10},{10,1... | collective-permute-start | bytes 1548296 | tf_op jit(solution)/shard_map/ppermute | solution.py:110
  75.5 14.7 %collective-permute-start.5 = (bf16[4,72,896]{2,1,0:T(8,128)(2,1)S(1)}, bf16[4,72,896]{2,1,0:T(8,128)(2,1)S(1)}, u32[]{:S(2)}, u32[]{:S(2)}) collective-permute-start(bf16[4,72,896]{2,1,0:T(8,128)(2,1)S(1)} %get-tuple-element.40), channel_id=1, source_target_pairs={{0,3},{1,0},{2,1},{3,2},{4,7},{5,4},{6,5},{7,6},{8,11},{9,8},{10,9... | collective-permute-start | bytes 1548296 | tf_op jit(solution)/shard_map/ppermute | solution.py:110
  91.0 1.0 copy-start.4
  114.1 4.4 %copy-start.1 = (bf16[32,6,16,128]{3,2,1,0:T(8,128)(2,1)}, bf16[32,6,16,128]{3,2,1,0:T(8,128)(2,1)S(1)}, u32[]{:S(2)}) copy-start(bf16[32,6,16,128]{3,2,1,0:T(8,128)(2,1)S(1)} %all-to-all-done.1.start_ref) | copy-start | bytes 2359300
  114.1 1.7 copy-start.20
  118.4 6.0 %copy-start.24 = (f32[8]{0:T(128)S(1)}, f32[8]{0:T(128)}, u32[]{:S(2)}) copy-start(f32[8]{0:T(128)} %param.18) | copy-start | bytes 100
  118.4 47.7 %all-to-all-start.2 = ((bf16[32,6,16,128]{3,2,1,0:T(8,128)(2,1)}), bf16[32,6,16,128]{3,2,1,0:T(8,128)(2,1)S(1)}, u32[]{:S(2)}, u32[]{:S(2)}) async-start(bf16[32,6,16,128]{3,2,1,0:T(8,128)(2,1)} %closing_states.1), calls=%async_computation.2 | async-start | bytes 1572864 | tf_op jit(solution)/shard_map/all_to_all | solution.py:180
  124.6 1.1 copy-start.2
  125.7 1.1 copy-start.17
  126.8 1.1 copy-start.19
  132.9 33.2 %copy-start.14 = (s32[192]{0:T(256)S(1)}, s32[192]{0:T(256)}, u32[]{:S(2)}) copy-start(s32[192]{0:T(256)} %cache_rows.1.rows_ref) | copy-start | bytes 2308
  133.6 11.5 %collective-permute-start.6 = (bf16[4,72,512]{2,1,0:T(8,128)(2,1)S(1)}, bf16[4,72,512]{2,1,0:T(8,128)(2,1)S(1)}, u32[]{:S(2)}, u32[]{:S(2)}) collective-permute-start(bf16[4,72,512]{2,1,0:T(8,128)(2,1)S(1)} %get-tuple-element.48), channel_id=1, source_target_pairs={{0,1},{1,2},{2,3},{3,0},{4,5},{5,6},{6,7},{7,4},{8,9},{9,10},{10,1... | collective-permute-start | bytes 884744 | tf_op jit(solution)/shard_map/ppermute | solution.py:110
  136.7 15.7 %collective-permute-start.7 = (bf16[4,72,512]{2,1,0:T(8,128)(2,1)S(1)}, bf16[4,72,512]{2,1,0:T(8,128)(2,1)S(1)}, u32[]{:S(2)}, u32[]{:S(2)}) collective-permute-start(bf16[4,72,512]{2,1,0:T(8,128)(2,1)S(1)} %get-tuple-element.49), channel_id=1, source_target_pairs={{0,2},{1,3},{2,0},{3,1},{4,6},{5,7},{6,4},{7,5},{8,10},{9,11},{10,... | collective-permute-start | bytes 884744 | tf_op jit(solution)/shard_map/ppermute | solution.py:110
  141.1 12.5 %collective-permute-start.8 = (bf16[4,72,512]{2,1,0:T(8,128)(2,1)S(1)}, bf16[4,72,512]{2,1,0:T(8,128)(2,1)S(1)}, u32[]{:S(2)}, u32[]{:S(2)}) collective-permute-start(bf16[4,72,512]{2,1,0:T(8,128)(2,1)S(1)} %get-tuple-element.50), channel_id=1, source_target_pairs={{0,3},{1,0},{2,1},{3,2},{4,7},{5,4},{6,5},{7,6},{8,11},{9,8},{10,9... | collective-permute-start | bytes 884744 | tf_op jit(solution)/shard_map/ppermute | solution.py:110
  167.8 47.5 %all-to-all-start.3 = ((bf16[32,6,16,128]{3,2,1,0:T(8,128)(2,1)}), bf16[32,6,16,128]{3,2,1,0:T(8,128)(2,1)S(1)}, u32[]{:S(2)}, u32[]{:S(2)}) async-start(bf16[32,6,16,128]{3,2,1,0:T(8,128)(2,1)} %bitcast.12), calls=%async_computation.3 | async-start | bytes 1572864 | tf_op jit(solution)/shard_map/all_to_all | solution.py:180
  173.6 11.5 %collective-permute-start.9 = (bf16[72,2048]{1,0:T(8,128)(2,1)S(1)}, bf16[72,2048]{1,0:T(8,128)(2,1)S(1)}, u32[]{:S(2)}, u32[]{:S(2)}) collective-permute-start(bf16[72,2048]{1,0:T(8,128)(2,1)S(1)} %get-tuple-element.56), channel_id=1, source_target_pairs={{0,4},{1,5},{2,6},{3,7},{4,8},{5,9},{6,10},{7,11},{8,12},{9,13},{1... | collective-permute-start | bytes 884744 | tf_op jit(solution)/shard_map/ppermute | solution.py:110
  176.9 15.4 %collective-permute-start.10 = (bf16[72,2048]{1,0:T(8,128)(2,1)S(1)}, bf16[72,2048]{1,0:T(8,128)(2,1)S(1)}, u32[]{:S(2)}, u32[]{:S(2)}) collective-permute-start(bf16[72,2048]{1,0:T(8,128)(2,1)S(1)} %get-tuple-element.57), channel_id=1, source_target_pairs={{0,8},{1,9},{2,10},{3,11},{4,12},{5,13},{6,14},{7,15},{8,0},{9,1},... | collective-permute-start | bytes 884744 | tf_op jit(solution)/shard_map/ppermute | solution.py:110
  180.9 12.7 %collective-permute-start.11 = (bf16[72,2048]{1,0:T(8,128)(2,1)S(1)}, bf16[72,2048]{1,0:T(8,128)(2,1)S(1)}, u32[]{:S(2)}, u32[]{:S(2)}) collective-permute-start(bf16[72,2048]{1,0:T(8,128)(2,1)S(1)} %get-tuple-element.58), channel_id=1, source_target_pairs={{0,12},{1,13},{2,14},{3,15},{4,0},{5,1},{6,2},{7,3},{8,4},{9,5},{1... | collective-permute-start | bytes 884744 | tf_op jit(solution)/shard_map/ppermute | solution.py:110
  (9 other events, 7.4 us)
